TPU v7x, 1024 devices: a whole 4x4x32 slice. The times are simulated.
1024 devices in a mesh: gx: 4 (over x), gy: 8 (over y, core), gz: 32 (over z).
Axes of the slice: x: 4, y: 4, z: 32, core: 2. Of those that a mesh axis runs over, the one named last changes fastest.
Arguments:
- right_side: float32 [3, 16, 64, 4096], P(None, 'gx', 'gy', 'gz'), may hold values from -8 to 8
- block_diag: float32 [3, 16, 64, 4096], P(None, 'gx', 'gy', 'gz'), may hold values from 2 to 4
- block_off: float32 [3, 16, 64, 4096], P(None, 'gx', 'gy', 'gz'), may hold values from -0.6 to 0.6
- mobility: float32 [3, 16, 64, 4096], P(None, 'gx', 'gy', 'gz'), may hold values from 0.1 to 10
- perf_cell: int32 [4, 8, 16384], P('gx', 'gy', 'gz'), may hold values from 0 to 4095
- perf_well: int32 [4, 8, 16384], P('gx', 'gy', 'gz'), may hold values from 0 to 639
- perf_factor: float32 [4, 8, 16384], P('gx', 'gy', 'gz'), may hold values from 0.5 to 8
Outputs:
- solution_field: float32 [3, 16, 64, 4096], P(None, 'gx', 'gy', 'gz')
- residual: float32 [3, 16, 64, 4096], P(None, 'gx', 'gy', 'gz')
All inputs are finite; a program needn't handle non-finite values.
Results may differ from a plain program's by a relative error of at most 0.00012.
Values sent between devices are 32-bit elements; how exact they have to be, the bound alone decides.
No kernel may reach another device: no remote copies, remote signals or barrier semaphores. Data moves between devices by JAX's collectives and lax.ppermute only.
A program may use at most 32 MiB of HBM per device.

v0:
```python
import jax
import jax.numpy as jnp
from jax import lax
from jax.sharding import PartitionSpec as P

W_COL = 640
ITERS = 3


def with_halo(block, sides, width):
    for axis, dim in sides:
        count = lax.axis_size(axis)
        forward = [(i, i + 1) for i in range(count - 1)]
        backward = [(target, source) for source, target in forward]
        low = lax.ppermute(
            lax.slice_in_dim(block, block.shape[dim] - width, None, axis=dim), axis, forward
        )
        high = lax.ppermute(lax.slice_in_dim(block, 0, width, axis=dim), axis, backward)
        block = jnp.concatenate([low, block, high], axis=dim)
    return block


def side_views(padded):
    return [
        padded[:, 2:, 1:-1, 1:-1],
        padded[:, :-2, 1:-1, 1:-1],
        padded[:, 1:-1, 2:, 1:-1],
        padded[:, 1:-1, :-2, 1:-1],
        padded[:, 1:-1, 1:-1, 2:],
        padded[:, 1:-1, 1:-1, :-2],
    ]


def field_sides(field):
    padded = with_halo(field, (("gx", 1), ("gy", 2), ("gz", 3)), 1)
    return side_views(padded)


def well_means(num, den):
    total_num, total_den = lax.psum((num, den), "gz")
    return total_num / (1.0 + total_den)[:, None]


def well_term(field, cell_index, wells, factor):
    flat = field.reshape(3, -1)
    values = flat[:, cell_index]
    num = jax.ops.segment_sum((factor * values).T, wells, num_segments=W_COL)
    den = jax.ops.segment_sum(factor, wells, num_segments=W_COL)
    mean = well_means(num, den)
    delta = factor * (values - mean[wells].T)
    return jnp.zeros_like(flat).at[:, cell_index].add(delta).reshape(field.shape)


def operate(field, conduct, block_diag, block_off, cell_index, wells, factor):
    flow = jnp.zeros_like(field)
    for weight, near_field in zip(conduct, field_sides(field)):
        flow = flow + weight * (field - near_field)
    first = block_diag[0] * field[0] + block_off[0] * field[1] + block_off[1] * field[2]
    second = block_off[0] * field[0] + block_diag[1] * field[1] + block_off[2] * field[2]
    third = block_off[1] * field[0] + block_off[2] * field[1] + block_diag[2] * field[2]
    local = jnp.stack([first, second, third])
    return local + flow + well_term(field, cell_index, wells, factor)


def products(residual, image):
    local = (jnp.sum(residual * residual), jnp.sum(residual * image))
    return lax.psum((local[0], local[1]), ("gx", "gy", "gz"))


def body(right_side, block_diag, block_off, mobility, perf_cell, perf_well, perf_factor):
    padded_mob = with_halo(mobility, (("gx", 1), ("gy", 2), ("gz", 3)), 1)
    conduct = [
        2.0 * mobility * near_mob / (mobility + near_mob) for near_mob in side_views(padded_mob)
    ]
    cell_index = perf_cell.reshape(-1)
    wells = perf_well.reshape(-1)
    factor = perf_factor.reshape(-1)
    solution_field = jnp.zeros_like(right_side)
    residual = right_side
    image = operate(residual, conduct, block_diag, block_off, cell_index, wells, factor)
    norm_now, product = products(residual, image)
    alpha = norm_now / product
    direction, along = (residual, image)
    for index in range(ITERS):
        solution_field = solution_field + alpha * direction
        residual = residual - alpha * along
        if index + 1 < ITERS:
            image = operate(residual, conduct, block_diag, block_off, cell_index, wells, factor)
            norm_next, product = products(residual, image)
            ratio = norm_next / norm_now
            alpha = norm_next / (product - ratio * norm_next / alpha)
            direction = residual + ratio * direction
            along = image + ratio * along
            norm_now = norm_next
    return (solution_field, residual)


def solution(mesh):
    placed = (
        P(None, "gx", "gy", "gz"),
        P(None, "gx", "gy", "gz"),
        P(None, "gx", "gy", "gz"),
        P(None, "gx", "gy", "gz"),
        P("gx", "gy", "gz"),
        P("gx", "gy", "gz"),
        P("gx", "gy", "gz"),
    )
    return jax.shard_map(
        body,
        mesh=mesh,
        in_specs=placed,
        out_specs=(P(None, "gx", "gy", "gz"), P(None, "gx", "gy", "gz")),
        check_vma=False,
    )
```

profile of v0, /device:TPU:1, one launch (start us, length us, event | category | flops | bytes accessed | tf_op | source)
XLA Modules:
  0.0 927.6 jit_solution(15592866201014559725)
XLA Ops:
  1.5 3.9 collective-permute-start.3
  5.4 1.3 collective-permute-start.1
  7.4 4.0 collective-permute-start.2
  11.4 1.4 collective-permute-start
  12.9 1.4 copy.15
  15.4 4.1 scatter_custom_fusion.1
  19.5 2.5 scatter_custom_fusion
  22.0 97.0 %all-reduce.3 = (f32[640,3]{1,0:T(8,128)S(1)}, f32[640]{0:T(1024)S(1)}) all-reduce(f32[640,3]{1,0:T(8,128)S(1)} %scatter_custom_fusion, f32[640]{0:T(1024)S(1)} %scatter_custom_fusion.1), channel_id=1, replica_groups=mesh['gx'=4,'gy'=8,'gz'=32] {'gz'}, use_global_device_ids=true, to_apply=%region_3.0 | all-reduce | flops 2560 | bytes 20480 | tf_op jit(solution)/shard_map/psum | solution.py:40
  119.9 30.4 %collective-permute-start.5 = (f32[3,6,1,128]{3,2,1,0:T(1,128)S(1)}, f32[3,6,1,128]{3,2,1,0:T(1,128)S(1)}, u32[]{:S(2)}, u32[]{:S(2)}) collective-permute-start(f32[3,6,1,128]{3,2,1,0:T(1,128)S(1)} %get-tuple-element.47), channel_id=1, source_target_pairs={{32,0},{64,32},{96,64},{128,96},{160,128},{192,160},{224,192},{33,... | collective-permute-start | bytes 27656 | tf_op jit(solution)/shard_map/ppermute | solution.py:18
  150.3 3.1 collective-permute-start.7
  153.5 1.9 collective-permute-start.4
  155.4 3.6 collective-permute-start.6
  164.6 5.3 collective-permute-start.10
  169.9 4.8 scatter_custom_fusion.2
  175.6 1.7 multiply_reduce_fusion.4
  177.3 156.6 %all-reduce.2 = (f32[]{:T(128)}, f32[]{:T(128)}) all-reduce(f32[]{:T(128)} %get-tuple-element.7, f32[]{:T(128)} %get-tuple-element.6), channel_id=1, replica_groups=mesh['gx'=4,'gy'=8,'gz'=32] {'gx','gy','gz'}, use_global_device_ids=true, to_apply=%region_1.0 | all-reduce | flops 2 | bytes 16 | tf_op jit(solution)/shard_map/psum | solution.py:67
  336.5 4.2 collective-permute-start.13
  342.3 2.6 scatter_custom_fusion.3
  344.9 81.8 %psum.81 = f32[640,3]{1,0:T(8,128)S(1)} all-reduce(f32[640,3]{1,0:T(8,128)S(1)} %scatter_custom_fusion.3), channel_id=1, replica_groups=mesh['gx'=4,'gy'=8,'gz'=32] {'gz'}, use_global_device_ids=true, to_apply=%region_12.0 | all-reduce | flops 1920 | bytes 15360 | tf_op jit(solution)/shard_map/psum | solution.py:40
  426.8 30.3 %collective-permute-start.14 = (f32[3,6,1,128]{3,2,1,0:T(1,128)S(1)}, f32[3,6,1,128]{3,2,1,0:T(1,128)S(1)}, u32[]{:S(2)}, u32[]{:S(2)}) collective-permute-start(f32[3,6,1,128]{3,2,1,0:T(1,128)S(1)} %get-tuple-element.43), channel_id=1, source_target_pairs={{32,0},{64,32},{96,64},{128,96},{160,128},{192,160},{224,192},{33,... | collective-permute-start | bytes 27656 | tf_op jit(solution)/shard_map/ppermute | solution.py:18
  457.1 2.2 collective-permute-start.15
  464.2 4.8 scatter_custom_fusion.4
  470.4 155.8 %all-reduce.1 = (f32[]{:T(128)}, f32[]{:T(128)}) all-reduce(f32[]{:T(128)} %get-tuple-element.5, f32[]{:T(128)} %get-tuple-element.4), channel_id=1, replica_groups=mesh['gx'=4,'gy'=8,'gz'=32] {'gx','gy','gz'}, use_global_device_ids=true, to_apply=%region_10.0 | all-reduce | flops 2 | bytes 16 | tf_op jit(solution)/shard_map/psum | solution.py:67
  632.1 4.0 collective-permute-start.19
  637.8 2.6 scatter_custom_fusion.5
  640.4 82.0 %psum.84 = f32[640,3]{1,0:T(8,128)S(1)} all-reduce(f32[640,3]{1,0:T(8,128)S(1)} %scatter_custom_fusion.5), channel_id=1, replica_groups=mesh['gx'=4,'gy'=8,'gz'=32] {'gz'}, use_global_device_ids=true, to_apply=%region_19.0 | all-reduce | flops 1920 | bytes 15360 | tf_op jit(solution)/shard_map/psum | solution.py:40
  722.4 31.2 %collective-permute-start.20 = (f32[3,6,1,128]{3,2,1,0:T(1,128)S(1)}, f32[3,6,1,128]{3,2,1,0:T(1,128)S(1)}, u32[]{:S(2)}, u32[]{:S(2)}) collective-permute-start(f32[3,6,1,128]{3,2,1,0:T(1,128)S(1)} %get-tuple-element.41), channel_id=1, source_target_pairs={{32,0},{64,32},{96,64},{128,96},{160,128},{192,160},{224,192},{33,... | collective-permute-start | bytes 27656 | tf_op jit(solution)/shard_map/ppermute | solution.py:18
  753.6 1.9 collective-permute-start.21
  758.8 1.5 collective-permute-start.22
  760.3 4.8 scatter_custom_fusion.6
  766.3 1.7 multiply_reduce_fusion
  768.0 155.0 %all-reduce = (f32[]{:T(128)}, f32[]{:T(128)}) all-reduce(f32[]{:T(128)} %get-tuple-element.3, f32[]{:T(128)} %get-tuple-element.2), channel_id=1, replica_groups=mesh['gx'=4,'gy'=8,'gz'=32] {'gx','gy','gz'}, use_global_device_ids=true, to_apply=%region_17.0 | all-reduce | flops 2 | bytes 16 | tf_op jit(solution)/shard_map/psum | solution.py:67
  (139 shorter events, 27.0 us)
Async XLA Ops:
  0.6 118.5 %copy-start = (f32[3,4,8,128]{3,2,1,0:T(8,128)S(1)}, f32[3,4,8,128]{3,2,1,0:T(8,128)}, u32[]{:S(2)}) copy-start(f32[3,4,8,128]{3,2,1,0:T(8,128)} %param.7) | copy-start | bytes 147460
  0.7 118.5 %copy-start.2 = (f32[3,4,8,128]{3,2,1,0:T(8,128)S(1)}, f32[3,4,8,128]{3,2,1,0:T(8,128)}, u32[]{:S(2)}) copy-start(f32[3,4,8,128]{3,2,1,0:T(8,128)} %param.8) | copy-start | bytes 147460
  0.7 118.5 %copy-start.3 = (f32[3,4,8,128]{3,2,1,0:T(8,128)S(1)}, f32[3,4,8,128]{3,2,1,0:T(8,128)}, u32[]{:S(2)}) copy-start(f32[3,4,8,128]{3,2,1,0:T(8,128)} %param.9) | copy-start | bytes 147460
  1.5 118.4 %collective-permute-start.3 = (f32[3,1,8,128]{3,2,1,0:T(8,128)S(1)}, f32[3,1,8,128]{3,2,1,0:T(8,128)S(1)}, u32[]{:S(2)}, u32[]{:S(2)}) collective-permute-start(f32[3,1,8,128]{3,2,1,0:T(8,128)S(1)} %get-tuple-element.57), channel_id=1, source_target_pairs={{0,256},{256,512},{512,768},{1,257},{257,513},{513,769},{2,258},{2... | collective-permute-start | bytes 36872 | tf_op jit(solution)/shard_map/ppermute | solution.py:15
  5.4 114.4 %collective-permute-start.1 = (f32[3,1,8,128]{3,2,1,0:T(8,128)S(1)}, f32[3,1,8,128]{3,2,1,0:T(8,128)S(1)}, u32[]{:S(2)}, u32[]{:S(2)}) collective-permute-start(f32[3,1,8,128]{3,2,1,0:T(8,128)S(1)} %get-tuple-element.56), channel_id=1, source_target_pairs={{256,0},{512,256},{768,512},{257,1},{513,257},{769,513},{258,2},{5... | collective-permute-start | bytes 36872 | tf_op jit(solution)/shard_map/ppermute | solution.py:18
  7.4 145.9 %collective-permute-start.2 = (f32[3,1,8,128]{3,2,1,0:T(8,128)S(1)}, f32[3,1,8,128]{3,2,1,0:T(8,128)S(1)}, u32[]{:S(2)}, u32[]{:S(2)}) collective-permute-start(f32[3,1,8,128]{3,2,1,0:T(8,128)S(1)} %get-tuple-element.55), channel_id=1, source_target_pairs={{0,256},{256,512},{512,768},{1,257},{257,513},{513,769},{2,258},{2... | collective-permute-start | bytes 36872 | tf_op jit(solution)/shard_map/ppermute | solution.py:15
  11.4 142.0 %copy-start.1 = (f32[3,4,8,128]{3,2,1,0:T(8,128)S(1)}, f32[3,4,8,128]{3,2,1,0:T(8,128)}, u32[]{:S(2)}) copy-start(f32[3,4,8,128]{3,2,1,0:T(8,128)} %param.10) | copy-start | bytes 147460
  11.4 142.0 %collective-permute-start = (f32[3,1,8,128]{3,2,1,0:T(8,128)S(1)}, f32[3,1,8,128]{3,2,1,0:T(8,128)S(1)}, u32[]{:S(2)}, u32[]{:S(2)}) collective-permute-start(f32[3,1,8,128]{3,2,1,0:T(8,128)S(1)} %get-tuple-element.54), channel_id=1, source_target_pairs={{256,0},{512,256},{768,512},{257,1},{513,257},{769,513},{258,2},{5... | collective-permute-start | bytes 36872 | tf_op jit(solution)/shard_map/ppermute | solution.py:18
  14.4 104.6 %copy-start.25 = (s32[1024]{0:T(1024)}, s32[1024]{0:T(1024)S(1)}, u32[]{:S(2)}) copy-start(s32[1024]{0:T(1024)S(1)} %pad_clamp_fusion.1) | copy-start | bytes 12292
  119.9 50.1 %copy-start.11 = (f32[3,1,8,128]{3,2,1,0:T(8,128)}, f32[3,1,8,128]{3,2,1,0:T(8,128)S(1)}, u32[]{:S(2)}) copy-start(f32[3,1,8,128]{3,2,1,0:T(8,128)S(1)} %collective-permute-done.1) | copy-start | bytes 36868
  119.9 39.1 %collective-permute-start.5 = (f32[3,6,1,128]{3,2,1,0:T(1,128)S(1)}, f32[3,6,1,128]{3,2,1,0:T(1,128)S(1)}, u32[]{:S(2)}, u32[]{:S(2)}) collective-permute-start(f32[3,6,1,128]{3,2,1,0:T(1,128)S(1)} %get-tuple-element.47), channel_id=1, source_target_pairs={{32,0},{64,32},{96,64},{128,96},{160,128},{192,160},{224,192},{33,... | collective-permute-start | bytes 27656 | tf_op jit(solution)/shard_map/ppermute | solution.py:18
  150.3 8.8 collective-permute-start.7
  153.5 9.0 collective-permute-start.4
  155.4 7.1 collective-permute-start.6
  159.9 15.6 %collective-permute-start.11 = (f32[3,6,10,1]{3,2,1,0:T(8,128)}, f32[3,6,10,1]{3,2,1,0:T(8,128)S(1)}, u32[]{:S(2)}, u32[]{:S(2)}) collective-permute-start(f32[3,6,10,1]{3,2,1,0:T(8,128)} %get-tuple-element.39), channel_id=1, source_target_pairs={{0,1},{1,2},{2,3},{3,4},{4,5},{5,6},{6,7},{7,8},{8,9},{9,10},{10,1... | collective-permute-start | bytes 2168 | tf_op jit(solution)/shard_map/ppermute | solution.py:15
  161.2 14.3 %collective-permute-start.9 = (f32[3,6,10,1]{3,2,1,0:T(8,128)}, f32[3,6,10,1]{3,2,1,0:T(8,128)S(1)}, u32[]{:S(2)}, u32[]{:S(2)}) collective-permute-start(f32[3,6,10,1]{3,2,1,0:T(8,128)} %get-tuple-element.38), channel_id=1, source_target_pairs={{1,0},{2,1},{3,2},{4,3},{5,4},{6,5},{7,6},{8,7},{9,8},{10,9},{11,1... | collective-permute-start | bytes 2168 | tf_op jit(solution)/shard_map/ppermute | solution.py:18
  163.4 12.1 %collective-permute-start.8 = (f32[3,6,10,1]{3,2,1,0:T(8,128)}, f32[3,6,10,1]{3,2,1,0:T(8,128)S(1)}, u32[]{:S(2)}, u32[]{:S(2)}) collective-permute-start(f32[3,6,10,1]{3,2,1,0:T(8,128)} %get-tuple-element.34), channel_id=1, source_target_pairs={{1,0},{2,1},{3,2},{4,3},{5,4},{6,5},{7,6},{8,7},{9,8},{10,9},{11,1... | collective-permute-start | bytes 2168 | tf_op jit(solution)/shard_map/ppermute | solution.py:18
  164.6 10.8 %collective-permute-start.10 = (f32[3,6,10,1]{3,2,1,0:T(8,128)}, f32[3,6,10,1]{3,2,1,0:T(8,128)}, u32[]{:S(2)}, u32[]{:S(2)}) collective-permute-start(f32[3,6,10,1]{3,2,1,0:T(8,128)} %get-tuple-element.33), channel_id=1, source_target_pairs={{0,1},{1,2},{2,3},{3,4},{4,5},{5,6},{6,7},{7,8},{8,9},{9,10},{10,1... | collective-permute-start | bytes 2168 | tf_op jit(solution)/shard_map/ppermute | solution.py:15
  175.5 165.8 %copy-start.26 = (s32[1024]{0:T(1024)S(1)}, s32[1024]{0:T(1024)}, u32[]{:S(2)}) copy-start(s32[1024]{0:T(1024)} %copy-done.25) | copy-start | bytes 12292
  335.2 91.6 %collective-permute-start.12 = (f32[3,1,8,128]{3,2,1,0:T(8,128)S(1)}, f32[3,1,8,128]{3,2,1,0:T(8,128)S(1)}, u32[]{:S(2)}, u32[]{:S(2)}) collective-permute-start(f32[3,1,8,128]{3,2,1,0:T(8,128)S(1)} %get-tuple-element.53), channel_id=1, source_target_pairs={{256,0},{512,256},{768,512},{257,1},{513,257},{769,513},{258,2},{5... | collective-permute-start | bytes 36872 | tf_op jit(solution)/shard_map/ppermute | solution.py:18
  336.5 90.3 %collective-permute-start.13 = (f32[3,1,8,128]{3,2,1,0:T(8,128)S(1)}, f32[3,1,8,128]{3,2,1,0:T(8,128)S(1)}, u32[]{:S(2)}, u32[]{:S(2)}) collective-permute-start(f32[3,1,8,128]{3,2,1,0:T(8,128)S(1)} %get-tuple-element.52), channel_id=1, source_target_pairs={{0,256},{256,512},{512,768},{1,257},{257,513},{513,769},{2,258},{2... | collective-permute-start | bytes 36872 | tf_op jit(solution)/shard_map/ppermute | solution.py:15
  426.8 32.6 %collective-permute-start.14 = (f32[3,6,1,128]{3,2,1,0:T(1,128)S(1)}, f32[3,6,1,128]{3,2,1,0:T(1,128)S(1)}, u32[]{:S(2)}, u32[]{:S(2)}) collective-permute-start(f32[3,6,1,128]{3,2,1,0:T(1,128)S(1)} %get-tuple-element.43), channel_id=1, source_target_pairs={{32,0},{64,32},{96,64},{128,96},{160,128},{192,160},{224,192},{33,... | collective-permute-start | bytes 27656 | tf_op jit(solution)/shard_map/ppermute | solution.py:18
  457.1 3.1 collective-permute-start.15
  460.9 8.7 collective-permute-start.17
  462.2 7.4 collective-permute-start.16
  469.6 167.1 %copy-start.27 = (s32[1024]{0:T(1024)S(1)}, s32[1024]{0:T(1024)}, u32[]{:S(2)}) copy-start(s32[1024]{0:T(1024)} %copy-done.25) | copy-start | bytes 12292
  630.8 91.6 %collective-permute-start.18 = (f32[3,1,8,128]{3,2,1,0:T(8,128)S(1)}, f32[3,1,8,128]{3,2,1,0:T(8,128)S(1)}, u32[]{:S(2)}, u32[]{:S(2)}) collective-permute-start(f32[3,1,8,128]{3,2,1,0:T(8,128)S(1)} %get-tuple-element.51), channel_id=1, source_target_pairs={{256,0},{512,256},{768,512},{257,1},{513,257},{769,513},{258,2},{5... | collective-permute-start | bytes 36872 | tf_op jit(solution)/shard_map/ppermute | solution.py:18
  632.1 90.3 %collective-permute-start.19 = (f32[3,1,8,128]{3,2,1,0:T(8,128)S(1)}, f32[3,1,8,128]{3,2,1,0:T(8,128)S(1)}, u32[]{:S(2)}, u32[]{:S(2)}) collective-permute-start(f32[3,1,8,128]{3,2,1,0:T(8,128)S(1)} %get-tuple-element.50), channel_id=1, source_target_pairs={{0,256},{256,512},{512,768},{1,257},{257,513},{513,769},{2,258},{2... | collective-permute-start | bytes 36872 | tf_op jit(solution)/shard_map/ppermute | solution.py:15
  722.4 33.3 %collective-permute-start.20 = (f32[3,6,1,128]{3,2,1,0:T(1,128)S(1)}, f32[3,6,1,128]{3,2,1,0:T(1,128)S(1)}, u32[]{:S(2)}, u32[]{:S(2)}) collective-permute-start(f32[3,6,1,128]{3,2,1,0:T(1,128)S(1)} %get-tuple-element.41), channel_id=1, source_target_pairs={{32,0},{64,32},{96,64},{128,96},{160,128},{192,160},{224,192},{33,... | collective-permute-start | bytes 27656 | tf_op jit(solution)/shard_map/ppermute | solution.py:18
  753.6 3.1 collective-permute-start.21
  757.5 8.3 collective-permute-start.23
  758.8 7.5 collective-permute-start.22
  (23 other events, 92.8 us)
where the time goes:
time: 929 us; the launch traced here: 928 us
  blocking collectives  728 us (78%)
  starting transfers between devices  140 us (15%)
  other arithmetic  32.8 us (4%)
  local copies, waits for them, and re-layouts  12.5 us (1%)
  between operations  11.4 us (1%)
    psum x3, blocking collectives, products(): return lax.psum((local[0], local[1]), ('gx', 'gy', 'gz'))  467 us
    psum x3, blocking collectives, well_means(): total_num, total_den = lax.psum((num, den), 'gz')  261 us
    ppermute x12, starting transfers between devices, with_halo(): lax.ppermute(lax.slice_in_dim(block, 0, width, axis=dim), axis, backward)  104 us
    ppermute x12, starting transfers between devices, with_halo(): lax.ppermute(lax.slice_in_dim(block, block.shape[dim] - width, None, axis...  36 us
  transfers between devices with their start and end apart: 24, of which 3 were waited for; matrix products, arithmetic and copies ran while one was open for 4% of the time, Pallas kernels for 0%

commit v1 on v0

v1 whole, which is shorter than its diff:
```python
import jax
import jax.numpy as jnp
from jax import lax
from jax.experimental import pallas as pl
from jax.experimental.pallas import tpu as pltpu
from jax.sharding import PartitionSpec as P

W_COL = 640
WELL_ROWS = W_COL // 128
SHIFT = 8.0
F32 = jnp.float32
BF16 = jnp.bfloat16


def split3(a):
    first = a.astype(BF16)
    rest = a - first.astype(F32)
    second = rest.astype(BF16)
    third = (rest - second.astype(F32)).astype(BF16)
    return [first, second, third]


def sum3(a, rows):
    return a[:rows] + a[rows : 2 * rows] + a[2 * rows : 3 * rows]


def one_hot(index, rows):
    ids = lax.broadcasted_iota(jnp.int32, (rows, index.shape[1]), 0)
    return ids == index


def cell_masks(cell):
    row = one_hot(lax.shift_right_logical(cell, 7), 32).astype(F32)
    lane = one_hot(lax.bitwise_and(cell, 127), 128).astype(F32).astype(BF16)
    return row, lane


def well_mask(well):
    return one_hot(well, W_COL).astype(F32).astype(BF16)


def gather_cells(fields, row, lane):
    parts = [part for field in fields for part in split3(field)]
    picked = jnp.dot(jnp.concatenate(parts, 0), lane, preferred_element_type=F32)
    out = []
    for u in range(len(fields)):
        block = sum3(picked[96 * u : 96 * (u + 1)], 32)
        out.append(jnp.sum(block * row, axis=0, keepdims=True))
    return out


def scatter_cells(values, row, lane):
    parts = [part for value in values for part in split3(row * value)]
    placed = lax.dot_general(
        jnp.concatenate(parts, 0), lane, (((1,), (1,)), ((), ())), preferred_element_type=F32
    )
    return [sum3(placed[96 * u : 96 * (u + 1)], 32) for u in range(len(values))]


def scatter_wells(values, wells):
    count = len(values)
    stacked = jnp.concatenate(values + [jnp.zeros_like(values[0])] * (8 - count), 0)
    sums = lax.dot_general(
        jnp.concatenate(split3(stacked), 0), wells, (((1,), (1,)), ((), ())),
        preferred_element_type=F32,
    )
    sums = sum3(sums, 8)
    return [sums[u : u + 1] for u in range(count)]


def gather_wells(rows, wells):
    count = len(rows)
    stacked = jnp.concatenate(rows + [jnp.zeros_like(rows[0])] * (8 - count), 0)
    picked = sum3(jnp.dot(jnp.concatenate(split3(stacked), 0), wells, preferred_element_type=F32), 8)
    return [picked[u : u + 1] for u in range(count)]


def put_well_rows(ref, rows):
    for u, row in enumerate(rows):
        for j in range(WELL_ROWS):
            ref[u * WELL_ROWS + j : u * WELL_ROWS + j + 1, :] = row[:, 128 * j : 128 * (j + 1)]


def get_well_rows(table, count):
    out = []
    for u in range(count):
        pieces = [table[u * WELL_ROWS + j : u * WELL_ROWS + j + 1] for j in range(WELL_ROWS)]
        out.append(jnp.concatenate(pieces, 1))
    return out


def lanes():
    return lax.broadcasted_iota(jnp.int32, (8, 128), 1)


def put_faces(refs, fields):
    gx_high, gx_low, gy_high, gy_low, gz_both = refs
    lane = lanes()
    both = jnp.zeros((8, 128), F32)
    for k, field in enumerate(fields):
        for u in range(3):
            gx_high[3 * k + u] = field[u, 24:32]
            gx_low[3 * k + u] = field[u, 0:8]
            for x in range(4):
                at = 12 * k + 4 * u + x
                gy_high[at : at + 1] = field[u, 8 * x + 7 : 8 * x + 8]
                gy_low[at : at + 1] = field[u, 8 * x : 8 * x + 1]
                value = field[u, 8 * x : 8 * x + 8]
                at = 32 * k + 4 * u + x
                both = jnp.where(lane == at, pltpu.roll(value, (at + 1) % 128, 1), both)
                both = jnp.where(lane == at + 16, pltpu.roll(value, at + 16, 1), both)
    gz_both[...] = both


def low_views(field, k, u, x, halo, lane, sub):
    gx_low, gy_low, gz_low = halo
    value = field[u, 8 * x : 8 * x + 8]
    view_x = field[u, 8 * x - 8 : 8 * x] if x else gx_low[3 * k + u]
    at = 12 * k + 4 * u + x
    edge = jnp.broadcast_to(gy_low[at : at + 1], (8, 128))
    view_y = jnp.where(sub == 0, edge, pltpu.roll(value, 1, 0))
    at = 32 * k + 4 * u + x
    edge = pltpu.roll(gz_low[...], (128 - at) % 128, 1)
    view_z = jnp.where(lane == 0, edge, pltpu.roll(value, 1, 1))
    return [view_x, view_y, view_z]


def high_views(field, k, u, x, halo, lane, sub):
    gx_high, gy_high, gz_high = halo
    value = field[u, 8 * x : 8 * x + 8]
    view_x = field[u, 8 * x + 8 : 8 * x + 16] if x < 3 else gx_high[3 * k + u]
    at = 12 * k + 4 * u + x
    edge = jnp.broadcast_to(gy_high[at : at + 1], (8, 128))
    view_y = jnp.where(sub == 7, edge, pltpu.roll(value, 7, 0))
    at = 32 * k + 4 * u + x + 16
    edge = pltpu.roll(gz_high[...], 127 - at, 1)
    view_z = jnp.where(lane == 127, edge, pltpu.roll(value, 127, 1))
    return [view_x, view_y, view_z]


def block_row(field, diag, off, u, rows):
    pick = ((None, 0, 1), (0, None, 2), (1, 2, None))[u]
    total = (diag[u, rows] - SHIFT) * field[u, rows]
    for t in range(3):
        if pick[t] is not None:
            total = total + off[pick[t], rows] * field[t, rows]
    return total


def first_kernel(right, mobility, cell, well, factor, table, *faces):
    row, lane = cell_masks(cell[0])
    values = gather_cells([right[u] for u in range(3)], row, lane)
    weight = factor[0]
    put_well_rows(table, scatter_wells([weight * v for v in values] + [weight], well_mask(well[0])))
    table[4 * WELL_ROWS : 24] = jnp.zeros((24 - 4 * WELL_ROWS, 128), F32)
    put_faces(faces, [right, mobility])


def first_flow_kernel(
    right, mobility, diag, off, xl, yl, zl, xh, yh, zh, flow, cond_low, cond_high
):
    lane, sub = lanes(), lax.broadcasted_iota(jnp.int32, (8, 128), 0)
    for u in range(3):
        for x in range(4):
            rows = slice(8 * x, 8 * x + 8)
            total = block_row(right, diag, off, u, rows)
            value, own = right[u, rows], mobility[u, rows]
            for views, halo, cond in (
                (low_views, (xl, yl, zl), cond_low),
                (high_views, (xh, yh, zh), cond_high),
            ):
                near = views(right, 0, u, x, halo, lane, sub)
                near_mob = views(mobility, 1, u, x, halo, lane, sub)
                for d in range(3):
                    weight = 2.0 * own * near_mob[d] / (own + near_mob[d])
                    cond[d, u, rows] = weight
                    total = total + weight * (value - near[d])
            flow[u, rows] = total


def flow_kernel(field, diag, off, cond_low, cond_high, xl, yl, zl, xh, yh, zh, flow):
    lane, sub = lanes(), lax.broadcasted_iota(jnp.int32, (8, 128), 0)
    for u in range(3):
        for x in range(4):
            rows = slice(8 * x, 8 * x + 8)
            total = block_row(field, diag, off, u, rows)
            value = field[u, rows]
            low = low_views(field, 0, u, x, (xl, yl, zl), lane, sub)
            high = high_views(field, 0, u, x, (xh, yh, zh), lane, sub)
            for d in range(3):
                total = total + cond_low[d, u, rows] * (value - low[d])
                total = total + cond_high[d, u, rows] * (value - high[d])
            flow[u, rows] = total


def advance(means, flow, field, extra, weight, row, lane, wells):
    picked = gather_wells(means, wells)
    pulled = scatter_cells([weight * m for m in picked], row, lane)
    return [flow[u] + extra * field[u] - pulled[u] for u in range(3)]


def second_kernel(slots, flow, right, cell, well, factor, field, table, inverse, extra, *faces):
    total = jnp.sum(slots[...], axis=0)
    scale = 1.0 / (1.0 + total[3 * WELL_ROWS : 4 * WELL_ROWS])
    inverse[...] = jnp.zeros((8, 128), F32)
    inverse[0:WELL_ROWS] = scale
    rows = get_well_rows(total[: 3 * WELL_ROWS], 3)
    scale_row = get_well_rows(scale, 1)[0]
    row, lane = cell_masks(cell[0])
    wells = well_mask(well[0])
    weight = factor[0]
    own = scatter_cells([weight], row, lane)[0]
    extra[...] = own
    fresh = advance([r * scale_row for r in rows], flow, right, own, weight, row, lane, wells)
    for u in range(3):
        field[u] = fresh[u]
    values = gather_cells(fresh, row, lane)
    put_well_rows(table, scatter_wells([weight * v for v in values], wells))
    table[15:16] = jnp.zeros((1, 128), F32)
    put_faces(faces, [field])


def third_kernel(slots, flow, before, extra, inverse, cell, well, factor, field, table, *faces):
    total = jnp.sum(slots[...], axis=0)
    scale_row = get_well_rows(inverse[...], 1)[0]
    rows = get_well_rows(total, 3)
    row, lane = cell_masks(cell[0])
    wells = well_mask(well[0])
    weight = factor[0]
    fresh = advance([r * scale_row for r in rows], flow, before, extra[...], weight, row, lane, wells)
    for u in range(3):
        field[u] = fresh[u]
    values = gather_cells(fresh, row, lane)
    put_well_rows(table, scatter_wells([weight * v for v in values], wells))
    table[15:16] = jnp.zeros((1, 128), F32)
    put_faces(faces, [field])


def tree(terms):
    while len(terms) > 1:
        pairs = [a + b for a, b in zip(terms[::2], terms[1::2])]
        terms = pairs + ([terms[-1]] if len(terms) % 2 else [])
    return terms[0]


def moment_kernel(wells_table, w0, w1, w2, extra, diag, off, cond_low, xl, yl, zl, table):
    lane, sub = lanes(), lax.broadcasted_iota(jnp.int32, (8, 128), 0)
    sums = [[] for _ in range(6)]
    for u in range(3):
        for x in range(4):
            rows = slice(8 * x, 8 * x + 8)
            a, b, c = w0[u, rows], w1[u, rows], w2[u, rows]
            for k, (p, q) in enumerate(((a, a), (a, b), (b, b), (b, c), (c, c))):
                sums[k].append(p * q)
            energy = c * (block_row(w2, diag, off, u, rows) + extra[rows] * c)
            for d, near in enumerate(low_views(w2, 0, u, x, (xl, yl, zl), lane, sub)):
                energy = energy + cond_low[d, u, rows] * (c - near) * (c - near)
            sums[5].append(energy)
    line = jnp.zeros((1, 128), F32)
    first_lane = lane[0:1]
    for k in range(6):
        both = jnp.sum(tree(sums[k]), axis=0, keepdims=True)
        line = jnp.where(first_lane == k, jnp.sum(both, axis=1, keepdims=True), line)
    table[...] = wells_table[...]
    table[15:16] = line


def scalar_kernel(slots, inverse, moments):
    total = jnp.sum(slots[...], axis=0)
    pull = jnp.zeros((WELL_ROWS, 128), F32)
    scale = inverse[0:WELL_ROWS]
    for u in range(3):
        part = total[u * WELL_ROWS : (u + 1) * WELL_ROWS]
        pull = pull + part * part * scale
    pull = jnp.sum(jnp.sum(pull, axis=0, keepdims=True), axis=1, keepdims=True)
    line = total[15:16]
    lane = lanes()[0:1]
    out = []
    for k in range(6):
        value = jnp.sum(jnp.where(lane == k, line, 0.0), axis=1, keepdims=True)
        if k == 5:
            value = value - pull
        moments[k : k + 1] = jnp.broadcast_to(value, (1, 128))
    moments[6:8] = jnp.zeros((2, 128), F32)


def last_vector_kernel(slots, flow, before, extra, inverse, cell, well, factor, field):
    total = jnp.sum(slots[...], axis=0)
    scale_row = get_well_rows(inverse[...], 1)[0]
    rows = get_well_rows(total, 3)
    row, lane = cell_masks(cell[0])
    fresh = advance(
        [r * scale_row for r in rows], flow, before, extra[...], factor[0], row, lane,
        well_mask(well[0]),
    )
    for u in range(3):
        field[u] = fresh[u]


def plus(a, b, scale):
    size = max(len(a), len(b))
    out = []
    for k in range(size):
        p = a[k] if k < len(a) else None
        q = scale * b[k] if k < len(b) else None
        out.append(q if p is None else p if q is None else p + q)
    return out


def image_of(a):
    raised = [None] + list(a)
    return [
        SHIFT * a[0] if k == 0 else raised[k] + SHIFT * a[k] if k < len(a) else raised[k]
        for k in range(len(a) + 1)
    ]


def inner(a, b, moment):
    by_degree = {}
    for i, p in enumerate(a):
        for j, q in enumerate(b):
            by_degree[i + j] = by_degree.get(i + j, 0.0) + p * q
    return tree([by_degree[k] * moment[k] for k in sorted(by_degree)])


def combine_kernel(slots, w0, w1, w2, w3, solved, rest):
    terms = [slots[k] for k in range(slots.shape[0])]
    total = tree(terms)
    moment = [total[k : k + 1] for k in range(6)]
    one = jnp.ones((1, 128), F32)
    residual, direction, solution_field = [one], [one], []
    norm = moment[0]
    for step in range(3):
        image = image_of(direction)
        alpha = norm / inner(direction, image, moment)
        solution_field = plus(solution_field, direction, alpha)
        residual = plus(residual, image, -alpha)
        if step < 2:
            fresh = inner(residual, residual, moment)
            direction = plus(residual, direction, fresh / norm)
            norm = fresh
    solution_field = [jnp.broadcast_to(c, (8, 128)) for c in solution_field]
    residual = [jnp.broadcast_to(c, (8, 128)) for c in residual]
    for u in range(3):
        for x in range(4):
            rows = slice(8 * x, 8 * x + 8)
            basis = [w0[u, rows], w1[u, rows], w2[u, rows], w3[u, rows]]
            solved[u, rows] = tree([c * w for c, w in zip(solution_field, basis)])
            rest[u, rows] = tree([c * w for c, w in zip(residual, basis)])


def call(kernel, shapes, *args):
    return pl.pallas_call(
        kernel,
        out_shape=[jax.ShapeDtypeStruct(shape, F32) for shape in shapes],
        in_specs=[pl.BlockSpec(memory_space=pltpu.VMEM)] * len(args),
        out_specs=[pl.BlockSpec(memory_space=pltpu.VMEM)] * len(shapes),
        compiler_params=pltpu.CompilerParams(vmem_limit_bytes=32 * 1024 * 1024),
    )(*args)


NEAR = 4


def near_sum(table):
    count = lax.axis_size("gz")
    groups = [[NEAR * g + k for k in range(NEAR)] for g in range(count // NEAR)]
    sent = jnp.broadcast_to(table[None], (NEAR,) + table.shape)
    return jnp.sum(lax.all_to_all(sent, "gz", 0, 0, axis_index_groups=groups), axis=0)


def far_slots(table):
    count = lax.axis_size("gz")
    groups = [[g + NEAR * k for k in range(count // NEAR)] for g in range(NEAR)]
    sent = jnp.broadcast_to(table[None], (count // NEAR,) + table.shape)
    return lax.all_to_all(sent, "gz", 0, 0, axis_index_groups=groups)


def forward(piece, axis):
    count = lax.axis_size(axis)
    return lax.ppermute(piece, axis, [(i, i + 1) for i in range(count - 1)])


def backward(piece, axis):
    count = lax.axis_size(axis)
    return lax.ppermute(piece, axis, [(i + 1, i) for i in range(count - 1)])


def low_halos(faces):
    gx_high, _, gy_high, _, gz_both = faces
    return [forward(gx_high, "gx"), forward(gy_high, "gy"), forward(gz_both, "gz")]


def high_halos(faces):
    _, gx_low, _, gy_low, gz_both = faces
    return [backward(gx_low, "gx"), backward(gy_low, "gy"), backward(gz_both, "gz")]


def after(first, *later):
    return lax.optimization_barrier((first, *later))


def face_shapes(fields):
    return [(3 * fields, 8, 128)] * 2 + [(12 * fields, 128)] * 2 + [(8, 128)]


def body(right_side, block_diag, block_off, mobility, perf_cell, perf_well, perf_factor):
    block = (3, 32, 128)
    right, diag, off, mob = (
        a.reshape(block) for a in (right_side, block_diag, block_off, mobility)
    )
    perfs = (perf_cell, perf_well, perf_factor)

    table, *faces = call(first_kernel, [(24, 128)] + face_shapes(2), right, mob, *perfs)
    table, *faces = after(near_sum(table), *faces)
    slots = far_slots(table)
    flow, cond_low, cond_high = call(
        first_flow_kernel, [block, (3,) + block, (3,) + block],
        right, mob, diag, off, *low_halos(faces), *high_halos(faces),
    )

    w1, table, inverse, extra, *faces = call(
        second_kernel, [block, (16, 128), (8, 128), (32, 128)] + face_shapes(1),
        slots, flow, right, *perfs,
    )
    table, *faces = after(near_sum(table), *faces)
    slots = far_slots(table)
    flow = call(
        flow_kernel, [block],
        w1, diag, off, cond_low, cond_high, *low_halos(faces), *high_halos(faces),
    )[0]

    w2, table, *faces = call(
        third_kernel, [block, (16, 128)] + face_shapes(1), slots, flow, w1, extra, inverse, *perfs
    )
    low = low_halos(faces)
    table = call(
        moment_kernel, [(16, 128)], table, right, w1, w2, extra, diag, off, cond_low, *low
    )[0]
    table, *faces = after(near_sum(table), *faces)
    slots = far_slots(table)
    flow = call(
        flow_kernel, [block], w2, diag, off, cond_low, cond_high, *low, *high_halos(faces)
    )[0]

    moments = call(scalar_kernel, [(8, 128)], slots, inverse)[0]
    count = lax.axis_size("gx") * lax.axis_size("gy")
    sent = jnp.broadcast_to(moments[None], (count, 8, 128))
    moment_slots = lax.all_to_all(sent, ("gx", "gy"), 0, 0)
    w3 = call(last_vector_kernel, [block], slots, flow, w2, extra, inverse, *perfs)[0]
    solved, rest = call(combine_kernel, [block, block], moment_slots, right, w1, w2, w3)
    return solved.reshape(right_side.shape), rest.reshape(right_side.shape)


def solution(mesh):
    field = P(None, "gx", "gy", "gz")
    perf = P("gx", "gy", "gz")
    return jax.shard_map(
        body,
        mesh=mesh,
        in_specs=(field, field, field, field, perf, perf, perf),
        out_specs=(field, field),
        check_vma=False,
    )
```

time: 929 us -> 206 us (0.22)
  blocking collectives: 728 us -> 68.1 us
  other arithmetic: 32.8 us -> 0.02 us
  starting transfers between devices: 140 us -> 111 us
  waiting for transfers between devices: 2.27 us -> 13.4 us
  between operations: 11.4 us -> 0.94 us
    psum x6 -> x0, blocking collectives: 728 us -> none  [the longest x3 467 us: products(): return lax.psum((local[0], local[1]), ('gx', 'gy', 'gz'))]
    ppermute x24 -> x18, starting transfers between devices: 140 us -> 57.1 us  [the longest x9 43.3 us: forward(): return lax.ppermute(piece, axis, [(i, i + 1) for i in range(count - 1)])]
    all_to_all x0 -> x4, blocking collectives: none -> 68.1 us  [the longest x1 41.2 us: far_slots(): return lax.all_to_all(sent, 'gz', 0, 0, axis_index_groups=groups)]
    all_to_all x0 -> x3, starting transfers between devices: none -> 53.6 us  [the longest x2 44.4 us: far_slots(): return lax.all_to_all(sent, 'gz', 0, 0, axis_index_groups=groups)]
    scatter-add x7 -> x0, other arithmetic: 26.1 us -> none  [the longest x3 14.4 us: well_term(): jnp.zeros_like(flat).at[:, cell_index].add(delta).reshape(field.shape)]
  transfers between devices with their start and end apart: 24 -> 21, of which waited for: 3 -> 7; matrix products, arithmetic and copies ran while one was open for 4% -> 0% of each run, Pallas kernels for 0% -> 0%
where the time goes in v1:
time: 206 us; the launch traced here: 203 us
  starting transfers between devices  111 us (54%)
  blocking collectives  68.1 us (33%)
  waiting for transfers between devices  13.4 us (7%)
  local copies, waits for them, and re-layouts  5.64 us (3%)
  Pallas kernels  4.62 us (2%)
    all_to_all x2, starting transfers between devices, far_slots(): return lax.all_to_all(sent, 'gz', 0, 0, axis_index_groups=groups)  44.4 us
    ppermute x9, starting transfers between devices, forward(): return lax.ppermute(piece, axis, [(i, i + 1) for i in range(count - 1)])  43.3 us
    all_to_all x1, blocking collectives, far_slots(): return lax.all_to_all(sent, 'gz', 0, 0, axis_index_groups=groups)  41.2 us
    all_to_all x3, blocking collectives, near_sum(): lax.all_to_all(sent, 'gz', 0, 0, axis_index_groups=groups)  27 us
    ppermute x9, starting transfers between devices, backward(): return lax.ppermute(piece, axis, [(i + 1, i) for i in range(count - 1)])  13.7 us
    all_to_all x1, starting transfers between devices, body(): moment_slots = lax.all_to_all(sent, ('gx', 'gy'), 0, 0)  9.18 us
    ppermute x9, waiting for transfers between devices, backward(): return lax.ppermute(piece, axis, [(i + 1, i) for i in range(count - 1)])  6.57 us
    pallas_call x10, Pallas kernels, call(): pl.pallas_call(kernel, out_shape=[jax.ShapeDtypeStruct(shape, F32) for sh...  4.62 us
  transfers between devices with their start and end apart: 21, of which 7 were waited for; matrix products, arithmetic and copies ran while one was open for 0% of the time, Pallas kernels for 0%

profile of v1, /device:TPU:1, one launch (start us, length us, event | category | flops | bytes accessed | tf_op | source)
XLA Modules:
  0.0 203.4 jit_solution(10806004011043909077)
XLA Ops:
  1.3 0.8 copy-done
  4.8 10.8 %all_to_all.35 = f32[4,24,128]{2,1,0:T(8,128)S(1)} all-to-all(f32[4,24,128]{2,1,0:T(8,128)S(1)} %broadcast_in_dim.14), channel_id=1, replica_groups={{0,1,2,3},{4,5,6,7},{8,9,10,11},{12,13,14,15},{16,17,18,19},{20,21,22,2..., dimensions={0} | all-to-all | bytes 98304 | tf_op jit(solution)/shard_map/all_to_all | solution.py:369
  16.2 25.5 %all-to-all-start.1 = ((f32[8,24,128]{2,1,0:T(8,128)}), f32[8,24,128]{2,1,0:T(8,128)S(1)}, u32[]{:S(2)}, u32[]{:S(2)}) async-start(f32[8,24,128]{2,1,0:T(8,128)} %broadcast_in_dim.15), calls=%async_computation.1 | async-start | bytes 196608 | tf_op jit(solution)/shard_map/all_to_all | solution.py:376
  41.8 3.1 %collective-permute-start = (f32[6,8,128]{2,1,0:T(8,128)S(1)}, f32[6,8,128]{2,1,0:T(8,128)S(1)}, u32[]{:S(2)}, u32[]{:S(2)}) collective-permute-start(f32[6,8,128]{2,1,0:T(8,128)S(1)} %get-tuple-element.52), channel_id=1, source_target_pairs={{0,256},{256,512},{512,768},{1,257},{257,513},{513,769},{2,258},{2... | collective-permute-start | bytes 73736 | tf_op jit(solution)/shard_map/ppermute | solution.py:381
  44.9 1.3 collective-permute-start.3
  46.2 5.8 %collective-permute-start.1 = (f32[24,128]{1,0:T(8,128)S(1)}, f32[24,128]{1,0:T(8,128)S(1)}, u32[]{:S(2)}, u32[]{:S(2)}) collective-permute-start(f32[24,128]{1,0:T(8,128)S(1)} %get-tuple-element.53), channel_id=1, source_target_pairs={{0,32},{32,64},{64,96},{96,128},{128,160},{160,192},{192,224},{1,3... | collective-permute-start | bytes 36872 | tf_op jit(solution)/shard_map/ppermute | solution.py:381
  51.9 1.9 collective-permute-start.4
  53.9 1.3 collective-permute-start.5
  55.2 3.4 %collective-permute-done.5.zh = f32[8,128]{1,0:T(8,128)S(1)} collective-permute-done((f32[8,128]{1,0:T(8,128)S(1)}, f32[8,128]{1,0:T(8,128)S(1)}, u32[]{:S(2)}, u32[]{:S(2)}) %collective-permute-start.5) | collective-permute-done | bytes 4128 | tf_op jit(solution)/shard_map/ppermute | solution.py:386
  58.5 2.4 %collective-permute-start.2 = (f32[8,128]{1,0:T(8,128)S(1)}, f32[8,128]{1,0:T(8,128)S(1)}, u32[]{:S(2)}, u32[]{:S(2)}) collective-permute-start(f32[8,128]{1,0:T(8,128)S(1)} %get-tuple-element.54), channel_id=1, source_target_pairs={{0,1},{1,2},{2,3},{3,4},{4,5},{5,6},{6,7},{7,8},{8,9},{9,10},{10,1... | collective-permute-start | bytes 12296 | tf_op jit(solution)/shard_map/ppermute | solution.py:381
  62.0 3.7 %all-to-all-done.1.slots = f32[8,24,128]{2,1,0:T(8,128)S(1)} async-done(((f32[8,24,128]{2,1,0:T(8,128)}), f32[8,24,128]{2,1,0:T(8,128)S(1)}, u32[]{:S(2)}, u32[]{:S(2)}) %all-to-all-start.1) | async-done | bytes 98336 | tf_op jit(solution)/shard_map/all_to_all | solution.py:376
  65.7 1.2 shard_map.88
  66.9 8.2 %all_to_all.36 = f32[4,16,128]{2,1,0:T(8,128)S(1)} all-to-all(f32[4,16,128]{2,1,0:T(8,128)S(1)} %broadcast_in_dim.16), channel_id=1, replica_groups={{0,1,2,3},{4,5,6,7},{8,9,10,11},{12,13,14,15},{16,17,18,19},{20,21,22,2..., dimensions={0} | all-to-all | bytes 65536 | tf_op jit(solution)/shard_map/all_to_all | solution.py:369
  75.6 18.9 %all-to-all-start.3 = ((f32[8,16,128]{2,1,0:T(8,128)}), f32[8,16,128]{2,1,0:T(8,128)S(1)}, u32[]{:S(2)}, u32[]{:S(2)}) async-start(f32[8,16,128]{2,1,0:T(8,128)} %broadcast_in_dim.17), calls=%async_computation.3 | async-start | bytes 131072 | tf_op jit(solution)/shard_map/all_to_all | solution.py:376
  94.6 4.3 %collective-permute-start.6 = (f32[3,8,128]{2,1,0:T(8,128)S(1)}, f32[3,8,128]{2,1,0:T(8,128)S(1)}, u32[]{:S(2)}, u32[]{:S(2)}) collective-permute-start(f32[3,8,128]{2,1,0:T(8,128)S(1)} %get-tuple-element.68), channel_id=1, source_target_pairs={{0,256},{256,512},{512,768},{1,257},{257,513},{513,769},{2,258},{2... | collective-permute-start | bytes 36872 | tf_op jit(solution)/shard_map/ppermute | solution.py:381
  98.8 1.3 collective-permute-start.9
  100.1 1.3 collective-permute-start.11
  101.4 7.7 %collective-permute-start.7 = (f32[12,128]{1,0:T(8,128)S(1)}, f32[12,128]{1,0:T(8,128)S(1)}, u32[]{:S(2)}, u32[]{:S(2)}) collective-permute-start(f32[12,128]{1,0:T(8,128)S(1)} %get-tuple-element.69), channel_id=1, source_target_pairs={{0,32},{32,64},{64,96},{96,128},{128,160},{160,192},{192,224},{1,3... | collective-permute-start | bytes 18440 | tf_op jit(solution)/shard_map/ppermute | solution.py:381
  109.1 1.9 collective-permute-start.10
  111.0 4.3 %collective-permute-start.8 = (f32[8,128]{1,0:T(8,128)S(1)}, f32[8,128]{1,0:T(8,128)S(1)}, u32[]{:S(2)}, u32[]{:S(2)}) collective-permute-start(f32[8,128]{1,0:T(8,128)S(1)} %get-tuple-element.70), channel_id=1, source_target_pairs={{0,1},{1,2},{2,3},{3,4},{4,5},{5,6},{6,7},{7,8},{8,9},{9,10},{10,1... | collective-permute-start | bytes 12296 | tf_op jit(solution)/shard_map/ppermute | solution.py:381
  116.2 0.8 all-to-all-done.3.slots
  117.0 1.1 shard_map.90
  118.1 4.3 %collective-permute-start.12 = (f32[3,8,128]{2,1,0:T(8,128)S(1)}, f32[3,8,128]{2,1,0:T(8,128)S(1)}, u32[]{:S(2)}, u32[]{:S(2)}) collective-permute-start(f32[3,8,128]{2,1,0:T(8,128)S(1)} %get-tuple-element.77), channel_id=1, source_target_pairs={{0,256},{256,512},{512,768},{1,257},{257,513},{513,769},{2,258},{2... | collective-permute-start | bytes 36872 | tf_op jit(solution)/shard_map/ppermute | solution.py:381
  122.4 8.2 %collective-permute-start.13 = (f32[12,128]{1,0:T(8,128)S(1)}, f32[12,128]{1,0:T(8,128)S(1)}, u32[]{:S(2)}, u32[]{:S(2)}) collective-permute-start(f32[12,128]{1,0:T(8,128)S(1)} %get-tuple-element.78), channel_id=1, source_target_pairs={{0,32},{32,64},{64,96},{96,128},{128,160},{160,192},{192,224},{1,3... | collective-permute-start | bytes 18440 | tf_op jit(solution)/shard_map/ppermute | solution.py:381
  130.6 3.4 %collective-permute-start.14 = (f32[8,128]{1,0:T(8,128)S(1)}, f32[8,128]{1,0:T(8,128)S(1)}, u32[]{:S(2)}, u32[]{:S(2)}) collective-permute-start(f32[8,128]{1,0:T(8,128)S(1)} %get-tuple-element.85), channel_id=1, source_target_pairs={{0,1},{1,2},{2,3},{3,4},{4,5},{5,6},{6,7},{7,8},{8,9},{9,10},{10,1... | collective-permute-start | bytes 12296 | tf_op jit(solution)/shard_map/ppermute | solution.py:381
  134.9 8.0 %all_to_all.37 = f32[4,16,128]{2,1,0:T(8,128)S(1)} all-to-all(f32[4,16,128]{2,1,0:T(8,128)S(1)} %broadcast_in_dim.18), channel_id=1, replica_groups={{0,1,2,3},{4,5,6,7},{8,9,10,11},{12,13,14,15},{16,17,18,19},{20,21,22,2..., dimensions={0} | all-to-all | bytes 65536 | tf_op jit(solution)/shard_map/all_to_all | solution.py:369
  143.0 41.2 %all_to_all.38.slots = f32[8,16,128]{2,1,0:T(8,128)S(1)} all-to-all(f32[8,16,128]{2,1,0:T(8,128)S(1)} %broadcast_in_dim.19), channel_id=1, replica_groups={{0,4,8,12,16,20,24,28},{1,5,9,13,17,21,25,29},{2,6,10,14,18,22,26,30},{..., dimensions={0} | all-to-all | bytes 131072 | tf_op jit(solution)/shard_map/all_to_all | solution.py:376
  184.9 9.2 %all-to-all-start.6 = ((f32[32,8,128]{2,1,0:T(8,128)}), f32[32,8,128]{2,1,0:T(8,128)S(1)}, u32[]{:S(2)}, u32[]{:S(2)}) async-start(f32[32,8,128]{2,1,0:T(8,128)} %broadcast_in_dim.20), calls=%async_computation.6 | async-start | bytes 262144 | tf_op jit(solution)/shard_map/all_to_all | solution.py:449
  194.1 1.3 collective-permute-start.15
  195.4 2.1 %collective-permute-start.16 = (f32[12,128]{1,0:T(8,128)S(1)}, f32[12,128]{1,0:T(8,128)S(1)}, u32[]{:S(2)}, u32[]{:S(2)}) collective-permute-start(f32[12,128]{1,0:T(8,128)S(1)} %get-tuple-element.84), channel_id=1, source_target_pairs={{32,0},{64,32},{96,64},{128,96},{160,128},{192,160},{224,192},{33,... | collective-permute-start | bytes 18440 | tf_op jit(solution)/shard_map/ppermute | solution.py:386
  197.6 1.3 collective-permute-start.17
  198.9 3.2 %collective-permute-done.17.zh = f32[8,128]{1,0:T(8,128)S(1)} collective-permute-done((f32[8,128]{1,0:T(8,128)S(1)}, f32[8,128]{1,0:T(8,128)S(1)}, u32[]{:S(2)}, u32[]{:S(2)}) %collective-permute-start.17) | collective-permute-done | bytes 4128 | tf_op jit(solution)/shard_map/ppermute | solution.py:386
  (56 shorter events, 9.5 us)
Async XLA Ops:
  0.6 0.7 copy-start.6
  1.3 0.8 copy-start
  2.1 0.8 copy-start.4
  2.9 0.7 copy-start.7
  3.6 0.7 copy-start.9
  16.2 45.5 %copy-start.1 = (f32[3,4,8,128]{3,2,1,0:T(8,128)S(1)}, f32[3,4,8,128]{3,2,1,0:T(8,128)}, u32[]{:S(2)}) copy-start(f32[3,4,8,128]{3,2,1,0:T(8,128)} %param.7) | copy-start | bytes 147460
  16.2 45.5 %copy-start.2 = (f32[3,4,8,128]{3,2,1,0:T(8,128)S(1)}, f32[3,4,8,128]{3,2,1,0:T(8,128)}, u32[]{:S(2)}) copy-start(f32[3,4,8,128]{3,2,1,0:T(8,128)} %param.8) | copy-start | bytes 147460
  16.2 45.5 %copy-start.3 = (f32[3,4,8,128]{3,2,1,0:T(8,128)S(1)}, f32[3,4,8,128]{3,2,1,0:T(8,128)}, u32[]{:S(2)}) copy-start(f32[3,4,8,128]{3,2,1,0:T(8,128)} %param.9) | copy-start | bytes 147460
  16.2 45.5 %copy-start.5 = (f32[3,4,8,128]{3,2,1,0:T(8,128)S(1)}, f32[3,4,8,128]{3,2,1,0:T(8,128)}, u32[]{:S(2)}) copy-start(f32[3,4,8,128]{3,2,1,0:T(8,128)} %param.10) | copy-start | bytes 147460
  16.2 49.4 %all-to-all-start.1 = ((f32[8,24,128]{2,1,0:T(8,128)}), f32[8,24,128]{2,1,0:T(8,128)S(1)}, u32[]{:S(2)}, u32[]{:S(2)}) async-start(f32[8,24,128]{2,1,0:T(8,128)} %broadcast_in_dim.15), calls=%async_computation.1 | async-start | bytes 196608 | tf_op jit(solution)/shard_map/all_to_all | solution.py:376
  41.8 19.9 %collective-permute-start = (f32[6,8,128]{2,1,0:T(8,128)S(1)}, f32[6,8,128]{2,1,0:T(8,128)S(1)}, u32[]{:S(2)}, u32[]{:S(2)}) collective-permute-start(f32[6,8,128]{2,1,0:T(8,128)S(1)} %get-tuple-element.52), channel_id=1, source_target_pairs={{0,256},{256,512},{512,768},{1,257},{257,513},{513,769},{2,258},{2... | collective-permute-start | bytes 73736 | tf_op jit(solution)/shard_map/ppermute | solution.py:381
  44.9 16.8 %collective-permute-start.3 = (f32[6,8,128]{2,1,0:T(8,128)S(1)}, f32[6,8,128]{2,1,0:T(8,128)S(1)}, u32[]{:S(2)}, u32[]{:S(2)}) collective-permute-start(f32[6,8,128]{2,1,0:T(8,128)S(1)} %get-tuple-element.55), channel_id=1, source_target_pairs={{256,0},{512,256},{768,512},{257,1},{513,257},{769,513},{258,2},{5... | collective-permute-start | bytes 73736 | tf_op jit(solution)/shard_map/ppermute | solution.py:386
  46.2 15.5 %collective-permute-start.1 = (f32[24,128]{1,0:T(8,128)S(1)}, f32[24,128]{1,0:T(8,128)S(1)}, u32[]{:S(2)}, u32[]{:S(2)}) collective-permute-start(f32[24,128]{1,0:T(8,128)S(1)} %get-tuple-element.53), channel_id=1, source_target_pairs={{0,32},{32,64},{64,96},{96,128},{128,160},{160,192},{192,224},{1,3... | collective-permute-start | bytes 36872 | tf_op jit(solution)/shard_map/ppermute | solution.py:381
  51.9 9.8 %collective-permute-start.4 = (f32[24,128]{1,0:T(8,128)S(1)}, f32[24,128]{1,0:T(8,128)S(1)}, u32[]{:S(2)}, u32[]{:S(2)}) collective-permute-start(f32[24,128]{1,0:T(8,128)S(1)} %get-tuple-element.56), channel_id=1, source_target_pairs={{32,0},{64,32},{96,64},{128,96},{160,128},{192,160},{224,192},{33,... | collective-permute-start | bytes 36872 | tf_op jit(solution)/shard_map/ppermute | solution.py:386
  53.9 4.7 %collective-permute-start.5 = (f32[8,128]{1,0:T(8,128)S(1)}, f32[8,128]{1,0:T(8,128)S(1)}, u32[]{:S(2)}, u32[]{:S(2)}) collective-permute-start(f32[8,128]{1,0:T(8,128)S(1)} %get-tuple-element.54), channel_id=1, source_target_pairs={{1,0},{2,1},{3,2},{4,3},{5,4},{6,5},{7,6},{8,7},{9,8},{10,9},{11,1... | collective-permute-start | bytes 12296 | tf_op jit(solution)/shard_map/ppermute | solution.py:386
  58.5 3.2 %collective-permute-start.2 = (f32[8,128]{1,0:T(8,128)S(1)}, f32[8,128]{1,0:T(8,128)S(1)}, u32[]{:S(2)}, u32[]{:S(2)}) collective-permute-start(f32[8,128]{1,0:T(8,128)S(1)} %get-tuple-element.54), channel_id=1, source_target_pairs={{0,1},{1,2},{2,3},{3,4},{4,5},{5,6},{6,7},{7,8},{8,9},{9,10},{10,1... | collective-permute-start | bytes 12296 | tf_op jit(solution)/shard_map/ppermute | solution.py:381
  61.8 3.9 %copy-start.8 = (s32[1,1,512]{2,1,0:T(1,128)S(1)}, s32[1,1,512]{2,1,0:T(1,128)}, u32[]{:S(2)}) copy-start(s32[1,1,512]{2,1,0:T(1,128)} %well.7) | copy-start | bytes 6148
  61.8 3.9 %copy-start.10 = (f32[1,1,512]{2,1,0:T(1,128)S(1)}, f32[1,1,512]{2,1,0:T(1,128)}, u32[]{:S(2)}) copy-start(f32[1,1,512]{2,1,0:T(1,128)} %factor.7) | copy-start | bytes 6148
  75.6 41.4 %all-to-all-start.3 = ((f32[8,16,128]{2,1,0:T(8,128)}), f32[8,16,128]{2,1,0:T(8,128)S(1)}, u32[]{:S(2)}, u32[]{:S(2)}) async-start(f32[8,16,128]{2,1,0:T(8,128)} %broadcast_in_dim.17), calls=%async_computation.3 | async-start | bytes 131072 | tf_op jit(solution)/shard_map/all_to_all | solution.py:376
  94.6 21.5 %collective-permute-start.6 = (f32[3,8,128]{2,1,0:T(8,128)S(1)}, f32[3,8,128]{2,1,0:T(8,128)S(1)}, u32[]{:S(2)}, u32[]{:S(2)}) collective-permute-start(f32[3,8,128]{2,1,0:T(8,128)S(1)} %get-tuple-element.68), channel_id=1, source_target_pairs={{0,256},{256,512},{512,768},{1,257},{257,513},{513,769},{2,258},{2... | collective-permute-start | bytes 36872 | tf_op jit(solution)/shard_map/ppermute | solution.py:381
  98.8 17.2 %collective-permute-start.9 = (f32[3,8,128]{2,1,0:T(8,128)S(1)}, f32[3,8,128]{2,1,0:T(8,128)S(1)}, u32[]{:S(2)}, u32[]{:S(2)}) collective-permute-start(f32[3,8,128]{2,1,0:T(8,128)S(1)} %get-tuple-element.71), channel_id=1, source_target_pairs={{256,0},{512,256},{768,512},{257,1},{513,257},{769,513},{258,2},{5... | collective-permute-start | bytes 36872 | tf_op jit(solution)/shard_map/ppermute | solution.py:386
  100.1 10.9 %collective-permute-start.11 = (f32[8,128]{1,0:T(8,128)S(1)}, f32[8,128]{1,0:T(8,128)S(1)}, u32[]{:S(2)}, u32[]{:S(2)}) collective-permute-start(f32[8,128]{1,0:T(8,128)S(1)} %get-tuple-element.70), channel_id=1, source_target_pairs={{1,0},{2,1},{3,2},{4,3},{5,4},{6,5},{7,6},{8,7},{9,8},{10,9},{11,1... | collective-permute-start | bytes 12296 | tf_op jit(solution)/shard_map/ppermute | solution.py:386
  101.4 14.6 %collective-permute-start.7 = (f32[12,128]{1,0:T(8,128)S(1)}, f32[12,128]{1,0:T(8,128)S(1)}, u32[]{:S(2)}, u32[]{:S(2)}) collective-permute-start(f32[12,128]{1,0:T(8,128)S(1)} %get-tuple-element.69), channel_id=1, source_target_pairs={{0,32},{32,64},{64,96},{96,128},{128,160},{160,192},{192,224},{1,3... | collective-permute-start | bytes 18440 | tf_op jit(solution)/shard_map/ppermute | solution.py:381
  109.1 7.0 %collective-permute-start.10 = (f32[12,128]{1,0:T(8,128)S(1)}, f32[12,128]{1,0:T(8,128)S(1)}, u32[]{:S(2)}, u32[]{:S(2)}) collective-permute-start(f32[12,128]{1,0:T(8,128)S(1)} %get-tuple-element.72), channel_id=1, source_target_pairs={{32,0},{64,32},{96,64},{128,96},{160,128},{192,160},{224,192},{33,... | collective-permute-start | bytes 18440 | tf_op jit(solution)/shard_map/ppermute | solution.py:386
  111.0 5.0 %collective-permute-start.8 = (f32[8,128]{1,0:T(8,128)S(1)}, f32[8,128]{1,0:T(8,128)S(1)}, u32[]{:S(2)}, u32[]{:S(2)}) collective-permute-start(f32[8,128]{1,0:T(8,128)S(1)} %get-tuple-element.70), channel_id=1, source_target_pairs={{0,1},{1,2},{2,3},{3,4},{4,5},{5,6},{6,7},{7,8},{8,9},{9,10},{10,1... | collective-permute-start | bytes 12296 | tf_op jit(solution)/shard_map/ppermute | solution.py:381
  118.1 16.6 %collective-permute-start.12 = (f32[3,8,128]{2,1,0:T(8,128)S(1)}, f32[3,8,128]{2,1,0:T(8,128)S(1)}, u32[]{:S(2)}, u32[]{:S(2)}) collective-permute-start(f32[3,8,128]{2,1,0:T(8,128)S(1)} %get-tuple-element.77), channel_id=1, source_target_pairs={{0,256},{256,512},{512,768},{1,257},{257,513},{513,769},{2,258},{2... | collective-permute-start | bytes 36872 | tf_op jit(solution)/shard_map/ppermute | solution.py:381
  122.4 12.3 %collective-permute-start.13 = (f32[12,128]{1,0:T(8,128)S(1)}, f32[12,128]{1,0:T(8,128)S(1)}, u32[]{:S(2)}, u32[]{:S(2)}) collective-permute-start(f32[12,128]{1,0:T(8,128)S(1)} %get-tuple-element.78), channel_id=1, source_target_pairs={{0,32},{32,64},{64,96},{96,128},{128,160},{160,192},{192,224},{1,3... | collective-permute-start | bytes 18440 | tf_op jit(solution)/shard_map/ppermute | solution.py:381
  130.6 4.2 %collective-permute-start.14 = (f32[8,128]{1,0:T(8,128)S(1)}, f32[8,128]{1,0:T(8,128)S(1)}, u32[]{:S(2)}, u32[]{:S(2)}) collective-permute-start(f32[8,128]{1,0:T(8,128)S(1)} %get-tuple-element.85), channel_id=1, source_target_pairs={{0,1},{1,2},{2,3},{3,4},{4,5},{5,6},{6,7},{7,8},{8,9},{9,10},{10,1... | collective-permute-start | bytes 12296 | tf_op jit(solution)/shard_map/ppermute | solution.py:381
  184.9 17.7 %all-to-all-start.6 = ((f32[32,8,128]{2,1,0:T(8,128)}), f32[32,8,128]{2,1,0:T(8,128)S(1)}, u32[]{:S(2)}, u32[]{:S(2)}) async-start(f32[32,8,128]{2,1,0:T(8,128)} %broadcast_in_dim.20), calls=%async_computation.6 | async-start | bytes 262144 | tf_op jit(solution)/shard_map/all_to_all | solution.py:449
  194.1 7.9 %collective-permute-start.15 = (f32[3,8,128]{2,1,0:T(8,128)S(1)}, f32[3,8,128]{2,1,0:T(8,128)S(1)}, u32[]{:S(2)}, u32[]{:S(2)}) collective-permute-start(f32[3,8,128]{2,1,0:T(8,128)S(1)} %get-tuple-element.83), channel_id=1, source_target_pairs={{256,0},{512,256},{768,512},{257,1},{513,257},{769,513},{258,2},{5... | collective-permute-start | bytes 36872 | tf_op jit(solution)/shard_map/ppermute | solution.py:386
  195.4 6.6 %collective-permute-start.16 = (f32[12,128]{1,0:T(8,128)S(1)}, f32[12,128]{1,0:T(8,128)S(1)}, u32[]{:S(2)}, u32[]{:S(2)}) collective-permute-start(f32[12,128]{1,0:T(8,128)S(1)} %get-tuple-element.84), channel_id=1, source_target_pairs={{32,0},{64,32},{96,64},{128,96},{160,128},{192,160},{224,192},{33,... | collective-permute-start | bytes 18440 | tf_op jit(solution)/shard_map/ppermute | solution.py:386
  197.6 4.5 %collective-permute-start.17 = (f32[8,128]{1,0:T(8,128)S(1)}, f32[8,128]{1,0:T(8,128)S(1)}, u32[]{:S(2)}, u32[]{:S(2)}) collective-permute-start(f32[8,128]{1,0:T(8,128)S(1)} %get-tuple-element.85), channel_id=1, source_target_pairs={{1,0},{2,1},{3,2},{4,3},{5,4},{6,5},{7,6},{8,7},{9,8},{10,9},{11,1... | collective-permute-start | bytes 12296 | tf_op jit(solution)/shard_map/ppermute | solution.py:386

commit v2 on v1

--- a/solution.py
+++ b/solution.py
@@ -94,9 +94,7 @@
 
 
 def put_faces(refs, fields):
-    gx_high, gx_low, gy_high, gy_low, gz_both = refs
-    lane = lanes()
-    both = jnp.zeros((8, 128), F32)
+    gx_high, gx_low, gy_high, gy_low = refs
     for k, field in enumerate(fields):
         for u in range(3):
             gx_high[3 * k + u] = field[u, 24:32]
@@ -105,37 +103,75 @@
                 at = 12 * k + 4 * u + x
                 gy_high[at : at + 1] = field[u, 8 * x + 7 : 8 * x + 8]
                 gy_low[at : at + 1] = field[u, 8 * x : 8 * x + 1]
-                value = field[u, 8 * x : 8 * x + 8]
-                at = 32 * k + 4 * u + x
-                both = jnp.where(lane == at, pltpu.roll(value, (at + 1) % 128, 1), both)
-                both = jnp.where(lane == at + 16, pltpu.roll(value, at + 16, 1), both)
-    gz_both[...] = both
-
-
-def low_views(field, k, u, x, halo, lane, sub):
-    gx_low, gy_low, gz_low = halo
+
+
+def end_tile(highs, lows):
+    lane = lanes()
+    tile = jnp.zeros((8, 128), F32)
+    for fields, turn in ((highs, 1), (lows, 0)):
+        for field, start in fields:
+            for u in range(3):
+                for x in range(4):
+                    at = start + 4 * u + x
+                    value = pltpu.roll(field[u, 8 * x : 8 * x + 8], at + turn, 1)
+                    tile = jnp.where(lane == at, value, tile)
+    return tile
+
+
+def fold(tile):
+    return jnp.where(lanes()[0:4] < 64, tile[0:4], pltpu.roll(tile, 64, 1)[4:8])
+
+
+def unfold(rows):
+    return jnp.concatenate([rows, pltpu.roll(jnp.concatenate([rows, rows], 0), 64, 1)[0:4]], 0)
+
+
+def low_views(field, k, u, x, halo, sub):
+    gx_low, gy_low = halo
     value = field[u, 8 * x : 8 * x + 8]
     view_x = field[u, 8 * x - 8 : 8 * x] if x else gx_low[3 * k + u]
     at = 12 * k + 4 * u + x
     edge = jnp.broadcast_to(gy_low[at : at + 1], (8, 128))
-    view_y = jnp.where(sub == 0, edge, pltpu.roll(value, 1, 0))
-    at = 32 * k + 4 * u + x
-    edge = pltpu.roll(gz_low[...], (128 - at) % 128, 1)
-    view_z = jnp.where(lane == 0, edge, pltpu.roll(value, 1, 1))
-    return [view_x, view_y, view_z]
-
-
-def high_views(field, k, u, x, halo, lane, sub):
-    gx_high, gy_high, gz_high = halo
+    return [view_x, jnp.where(sub == 0, edge, pltpu.roll(value, 1, 0))]
+
+
+def high_views(field, k, u, x, halo, sub):
+    gx_high, gy_high = halo
     value = field[u, 8 * x : 8 * x + 8]
     view_x = field[u, 8 * x + 8 : 8 * x + 16] if x < 3 else gx_high[3 * k + u]
     at = 12 * k + 4 * u + x
     edge = jnp.broadcast_to(gy_high[at : at + 1], (8, 128))
-    view_y = jnp.where(sub == 7, edge, pltpu.roll(value, 7, 0))
-    at = 32 * k + 4 * u + x + 16
-    edge = pltpu.roll(gz_high[...], 127 - at, 1)
-    view_z = jnp.where(lane == 127, edge, pltpu.roll(value, 127, 1))
-    return [view_x, view_y, view_z]
+    return [view_x, jnp.where(sub == 7, edge, pltpu.roll(value, 7, 0))]
+
+
+def low_along(value, tile, at, lane):
+    return jnp.where(lane == 0, pltpu.roll(tile, (128 - at) % 128, 1), pltpu.roll(value, 1, 1))
+
+
+def high_along(value, tile, at, lane):
+    return jnp.where(lane == 127, pltpu.roll(tile, 127 - at, 1), pltpu.roll(value, 127, 1))
+
+
+def place():
+    at = lax.axis_index("gz")
+    return lax.div(at, NEAR), lax.rem(at, NEAR)
+
+
+def near_tiles(tiles):
+    _, member = place()
+    low, high = tiles[0], tiles[-1]
+    for k in range(1, NEAR - 1):
+        low = jnp.where(member == k + 1, tiles[k], low)
+        high = jnp.where(member == k - 1, tiles[k], high)
+    return low, high
+
+
+def halo_tiles(near, slots, read):
+    group, member = place()
+    last = slots.shape[0] - 1
+    below = jnp.where(group == 0, 0.0, read(slots[jnp.maximum(group - 1, 0)]))
+    above = jnp.where(group == last, 0.0, read(slots[jnp.minimum(group + 1, last)]))
+    return jnp.where(member == 0, below, near[0]), jnp.where(member == NEAR - 1, above, near[1])
 
 
 def block_row(field, diag, off, u, rows):
@@ -147,50 +183,138 @@
     return total
 
 
-def first_kernel(right, mobility, cell, well, factor, table, *faces):
+def first_kernel(right_any, mobility_any, cell_any, well_any, factor_any, table, *rest):
+    faces, (right, mobility, cell, well, factor, sems) = rest[:4], rest[4:]
+    copies = [
+        pltpu.make_async_copy(source, target, sems.at[k])
+        for k, (source, target) in enumerate(
+            (
+                (cell_any, cell),
+                (right_any, right),
+                (factor_any, factor),
+                (well_any, well),
+                (mobility_any, mobility),
+            )
+        )
+    ]
+    for copy in copies:
+        copy.start()
+    for copy in copies:
+        copy.wait()
     row, lane = cell_masks(cell[0])
     values = gather_cells([right[u] for u in range(3)], row, lane)
     weight = factor[0]
     put_well_rows(table, scatter_wells([weight * v for v in values] + [weight], well_mask(well[0])))
-    table[4 * WELL_ROWS : 24] = jnp.zeros((24 - 4 * WELL_ROWS, 128), F32)
+    ends = [(right, 0), (mobility, 32)], [(right, 16), (mobility, 48)]
+    table[4 * WELL_ROWS : 24] = fold(end_tile(*ends))
     put_faces(faces, [right, mobility])
 
 
-def first_flow_kernel(
-    right, mobility, diag, off, xl, yl, zl, xh, yh, zh, flow, cond_low, cond_high
-):
-    lane, sub = lanes(), lax.broadcasted_iota(jnp.int32, (8, 128), 0)
+def first_near_kernel(slots, sent, near):
+    rows = 4 * WELL_ROWS
+    total = jnp.sum(slots[...], axis=0)
+    tiles = [unfold(slots[k, rows:24]) for k in range(NEAR)]
+    low, high = near_tiles(tiles)
+    near[0], near[1] = low, high
+    lane = lanes()
+    ends = fold(jnp.where(lax.bitwise_and(lane, 31) < 16, tiles[-1], tiles[0]))
+    for k in range(sent.shape[0]):
+        sent[k, 0:rows] = total[0:rows]
+        sent[k, rows:24] = ends
+
+
+def near_kernel(slots, sent, near):
+    total = jnp.sum(slots[...], axis=0)
+    tiles = [slots[k, 16:24] for k in range(NEAR)]
+    low, high = near_tiles(tiles)
+    near[0], near[1] = low, high
+    ends = jnp.where(lanes() < 16, tiles[-1], tiles[0])
+    for k in range(sent.shape[0]):
+        sent[k, 0:16] = total[0:16]
+        sent[k, 16:24] = ends
+
+
+def face_energy(below, above):
+    step = pltpu.roll(above, 112, 1) - below
+    return jnp.where(lanes() < 12, pltpu.roll(above, 96, 1) * step * step, 0.0)
+
+
+def whole_sum(a):
+    return jnp.sum(jnp.sum(a, axis=0, keepdims=True), axis=1, keepdims=True)
+
+
+def last_near_kernel(slots, sent, near):
+    total = jnp.sum(slots[...], axis=0)
+    tiles = [slots[k, 16:24] for k in range(NEAR)]
+    low, high = near_tiles(tiles)
+    near[0], near[1] = low, high
+    between = whole_sum(tree([face_energy(a, b) for a, b in zip(tiles, tiles[1:])]))
+    line = total[15:16] + jnp.where(lanes()[0:1] == 5, between, 0.0)
+    ends = jnp.where(lanes() < 16, tiles[-1], tiles[0])
+    for k in range(sent.shape[0]):
+        sent[k, 0:15] = total[0:15]
+        sent[k, 15:16] = line
+        sent[k, 16:24] = ends
+
+
+def first_flow_kernel(right, mobility, diag, off, xl, yl, xh, yh, flow, cond):
+    sub = lax.broadcasted_iota(jnp.int32, (8, 128), 0)
     for u in range(3):
         for x in range(4):
             rows = slice(8 * x, 8 * x + 8)
             total = block_row(right, diag, off, u, rows)
             value, own = right[u, rows], mobility[u, rows]
-            for views, halo, cond in (
-                (low_views, (xl, yl, zl), cond_low),
-                (high_views, (xh, yh, zh), cond_high),
-            ):
-                near = views(right, 0, u, x, halo, lane, sub)
-                near_mob = views(mobility, 1, u, x, halo, lane, sub)
-                for d in range(3):
-                    weight = 2.0 * own * near_mob[d] / (own + near_mob[d])
-                    cond[d, u, rows] = weight
-                    total = total + weight * (value - near[d])
+            near = low_views(right, 0, u, x, (xl, yl), sub)
+            near += high_views(right, 0, u, x, (xh, yh), sub)
+            near_mob = low_views(mobility, 1, u, x, (xl, yl), sub)
+            near_mob += high_views(mobility, 1, u, x, (xh, yh), sub)
+            for d in range(4):
+                weight = 2.0 * own * near_mob[d] / (own + near_mob[d])
+                cond[d, u, rows] = weight
+                total = total + weight * (value - near[d])
             flow[u, rows] = total
 
 
-def flow_kernel(field, diag, off, cond_low, cond_high, xl, yl, zl, xh, yh, zh, flow):
-    lane, sub = lanes(), lax.broadcasted_iota(jnp.int32, (8, 128), 0)
+def flow_kernel(field, diag, off, cond, xl, yl, xh, yh, flow):
+    sub = lax.broadcasted_iota(jnp.int32, (8, 128), 0)
     for u in range(3):
         for x in range(4):
             rows = slice(8 * x, 8 * x + 8)
             total = block_row(field, diag, off, u, rows)
             value = field[u, rows]
-            low = low_views(field, 0, u, x, (xl, yl, zl), lane, sub)
-            high = high_views(field, 0, u, x, (xh, yh, zh), lane, sub)
-            for d in range(3):
-                total = total + cond_low[d, u, rows] * (value - low[d])
-                total = total + cond_high[d, u, rows] * (value - high[d])
+            near = low_views(field, 0, u, x, (xl, yl), sub)
+            near += high_views(field, 0, u, x, (xh, yh), sub)
+            for d in range(4):
+                total = total + cond[d, u, rows] * (value - near[d])
             flow[u, rows] = total
+
+
+def flow_along(field, flow, cond, low, high):
+    lane = lanes()
+    out = []
+    for u in range(3):
+        blocks = []
+        for x in range(4):
+            rows = slice(8 * x, 8 * x + 8)
+            value = field[u, rows]
+            step_low = value - low_along(value, low, 4 * u + x, lane)
+            step_high = value - high_along(value, high, 16 + 4 * u + x, lane)
+            total = flow[u, rows] + cond[0, u, rows] * step_low
+            blocks.append(total + cond[1, u, rows] * step_high)
+        out.append(jnp.concatenate(blocks, 0))
+    return out
+
+
+def put_cond_along(cond, mobility, low, high):
+    lane = lanes()
+    for u in range(3):
+        for x in range(4):
+            rows = slice(8 * x, 8 * x + 8)
+            own = mobility[u, rows]
+            near = low_along(own, low, 32 + 4 * u + x, lane)
+            cond[0, u, rows] = 2.0 * own * near / (own + near)
+            near = high_along(own, high, 48 + 4 * u + x, lane)
+            cond[1, u, rows] = 2.0 * own * near / (own + near)
 
 
 def advance(means, flow, field, extra, weight, row, lane, wells):
@@ -199,8 +323,14 @@
     return [flow[u] + extra * field[u] - pulled[u] for u in range(3)]
 
 
-def second_kernel(slots, flow, right, cell, well, factor, field, table, inverse, extra, *faces):
+def second_kernel(
+    slots, near, flow, right, mobility, cell, well, factor,
+    field, table, inverse, extra, cond, *faces
+):
     total = jnp.sum(slots[...], axis=0)
+    low, high = halo_tiles(near, slots, lambda a: unfold(a[4 * WELL_ROWS : 24]))
+    put_cond_along(cond, mobility, low, high)
+    whole = flow_along(right, flow, cond, low, high)
     scale = 1.0 / (1.0 + total[3 * WELL_ROWS : 4 * WELL_ROWS])
     inverse[...] = jnp.zeros((8, 128), F32)
     inverse[0:WELL_ROWS] = scale
@@ -211,28 +341,34 @@
     weight = factor[0]
     own = scatter_cells([weight], row, lane)[0]
     extra[...] = own
-    fresh = advance([r * scale_row for r in rows], flow, right, own, weight, row, lane, wells)
+    fresh = advance([r * scale_row for r in rows], whole, right, own, weight, row, lane, wells)
     for u in range(3):
         field[u] = fresh[u]
     values = gather_cells(fresh, row, lane)
     put_well_rows(table, scatter_wells([weight * v for v in values], wells))
     table[15:16] = jnp.zeros((1, 128), F32)
+    table[16:24] = end_tile([(field, 0)], [(field, 16)])
     put_faces(faces, [field])
 
 
-def third_kernel(slots, flow, before, extra, inverse, cell, well, factor, field, table, *faces):
+def third_kernel(
+    slots, near, flow, before, extra, inverse, cond, cell, well, factor, field, table, *faces
+):
     total = jnp.sum(slots[...], axis=0)
+    low, high = halo_tiles(near, slots, lambda a: a[16:24])
+    whole = flow_along(before, flow, cond, low, high)
     scale_row = get_well_rows(inverse[...], 1)[0]
     rows = get_well_rows(total, 3)
     row, lane = cell_masks(cell[0])
     wells = well_mask(well[0])
     weight = factor[0]
-    fresh = advance([r * scale_row for r in rows], flow, before, extra[...], weight, row, lane, wells)
+    fresh = advance([r * scale_row for r in rows], whole, before, extra[...], weight, row, lane, wells)
     for u in range(3):
         field[u] = fresh[u]
     values = gather_cells(fresh, row, lane)
     put_well_rows(table, scatter_wells([weight * v for v in values], wells))
     table[15:16] = jnp.zeros((1, 128), F32)
+    table[16:24] = end_tile([(field, 0)], [(field, 16), (cond.at[0], 32)])
     put_faces(faces, [field])
 
 
@@ -243,7 +379,7 @@
     return terms[0]
 
 
-def moment_kernel(wells_table, w0, w1, w2, extra, diag, off, cond_low, xl, yl, zl, table):
+def moment_kernel(wells_table, w0, w1, w2, extra, diag, off, cond, cond_along, xl, yl, table):
     lane, sub = lanes(), lax.broadcasted_iota(jnp.int32, (8, 128), 0)
     sums = [[] for _ in range(6)]
     for u in range(3):
@@ -253,14 +389,13 @@
             for k, (p, q) in enumerate(((a, a), (a, b), (b, b), (b, c), (c, c))):
                 sums[k].append(p * q)
             energy = c * (block_row(w2, diag, off, u, rows) + extra[rows] * c)
-            for d, near in enumerate(low_views(w2, 0, u, x, (xl, yl, zl), lane, sub)):
-                energy = energy + cond_low[d, u, rows] * (c - near) * (c - near)
-            sums[5].append(energy)
+            for d, near in enumerate(low_views(w2, 0, u, x, (xl, yl), sub)):
+                energy = energy + cond[d, u, rows] * (c - near) * (c - near)
+            step = jnp.where(lane == 0, 0.0, c - pltpu.roll(c, 1, 1))
+            sums[5].append(energy + cond_along[0, u, rows] * step * step)
     line = jnp.zeros((1, 128), F32)
-    first_lane = lane[0:1]
     for k in range(6):
-        both = jnp.sum(tree(sums[k]), axis=0, keepdims=True)
-        line = jnp.where(first_lane == k, jnp.sum(both, axis=1, keepdims=True), line)
+        line = jnp.where(lane[0:1] == k, whole_sum(tree(sums[k])), line)
     table[...] = wells_table[...]
     table[15:16] = line
 
@@ -272,25 +407,29 @@
     for u in range(3):
         part = total[u * WELL_ROWS : (u + 1) * WELL_ROWS]
         pull = pull + part * part * scale
-    pull = jnp.sum(jnp.sum(pull, axis=0, keepdims=True), axis=1, keepdims=True)
+    tiles = [slots[k, 16:24] for k in range(slots.shape[0])]
+    between = tree([face_energy(a, b) for a, b in zip(tiles, tiles[1:])])
     line = total[15:16]
     lane = lanes()[0:1]
-    out = []
     for k in range(6):
         value = jnp.sum(jnp.where(lane == k, line, 0.0), axis=1, keepdims=True)
         if k == 5:
-            value = value - pull
+            value = value + (whole_sum(between) - whole_sum(pull))
         moments[k : k + 1] = jnp.broadcast_to(value, (1, 128))
     moments[6:8] = jnp.zeros((2, 128), F32)
 
 
-def last_vector_kernel(slots, flow, before, extra, inverse, cell, well, factor, field):
+def last_vector_kernel(
+    slots, near, flow, before, extra, inverse, cond, cell, well, factor, field
+):
     total = jnp.sum(slots[...], axis=0)
+    low, high = halo_tiles(near, slots, lambda a: a[16:24])
+    whole = flow_along(before, flow, cond, low, high)
     scale_row = get_well_rows(inverse[...], 1)[0]
     rows = get_well_rows(total, 3)
     row, lane = cell_masks(cell[0])
     fresh = advance(
-        [r * scale_row for r in rows], flow, before, extra[...], factor[0], row, lane,
+        [r * scale_row for r in rows], whole, before, extra[...], factor[0], row, lane,
         well_mask(well[0]),
     )
     for u in range(3):
@@ -349,30 +488,30 @@
             rest[u, rows] = tree([c * w for c, w in zip(residual, basis)])
 
 
-def call(kernel, shapes, *args):
+def call(kernel, shapes, *args, space=pltpu.VMEM, scratch=(), mib=32):
     return pl.pallas_call(
         kernel,
         out_shape=[jax.ShapeDtypeStruct(shape, F32) for shape in shapes],
-        in_specs=[pl.BlockSpec(memory_space=pltpu.VMEM)] * len(args),
+        in_specs=[pl.BlockSpec(memory_space=space)] * len(args),
         out_specs=[pl.BlockSpec(memory_space=pltpu.VMEM)] * len(shapes),
-        compiler_params=pltpu.CompilerParams(vmem_limit_bytes=32 * 1024 * 1024),
+        scratch_shapes=list(scratch),
+        compiler_params=pltpu.CompilerParams(vmem_limit_bytes=mib * 1024 * 1024),
     )(*args)
 
 
 NEAR = 4
 
 
-def near_sum(table):
+def near_slots(table):
     count = lax.axis_size("gz")
     groups = [[NEAR * g + k for k in range(NEAR)] for g in range(count // NEAR)]
     sent = jnp.broadcast_to(table[None], (NEAR,) + table.shape)
-    return jnp.sum(lax.all_to_all(sent, "gz", 0, 0, axis_index_groups=groups), axis=0)
-
-
-def far_slots(table):
+    return lax.all_to_all(sent, "gz", 0, 0, axis_index_groups=groups)
+
+
+def far_slots(sent):
     count = lax.axis_size("gz")
     groups = [[g + NEAR * k for k in range(count // NEAR)] for g in range(NEAR)]
-    sent = jnp.broadcast_to(table[None], (count // NEAR,) + table.shape)
     return lax.all_to_all(sent, "gz", 0, 0, axis_index_groups=groups)
 
 
@@ -387,13 +526,11 @@
 
 
 def low_halos(faces):
-    gx_high, _, gy_high, _, gz_both = faces
-    return [forward(gx_high, "gx"), forward(gy_high, "gy"), forward(gz_both, "gz")]
+    return [forward(faces[0], "gx"), forward(faces[2], "gy")]
 
 
 def high_halos(faces):
-    _, gx_low, _, gy_low, gz_both = faces
-    return [backward(gx_low, "gx"), backward(gy_low, "gy"), backward(gz_both, "gz")]
+    return [backward(faces[1], "gx"), backward(faces[3], "gy")]
 
 
 def after(first, *later):
@@ -401,7 +538,7 @@
 
 
 def face_shapes(fields):
-    return [(3 * fields, 8, 128)] * 2 + [(12 * fields, 128)] * 2 + [(8, 128)]
+    return [(3 * fields, 8, 128)] * 2 + [(12 * fields, 128)] * 2
 
 
 def body(right_side, block_diag, block_off, mobility, perf_cell, perf_well, perf_factor):
@@ -410,44 +547,57 @@
         a.reshape(block) for a in (right_side, block_diag, block_off, mobility)
     )
     perfs = (perf_cell, perf_well, perf_factor)
-
-    table, *faces = call(first_kernel, [(24, 128)] + face_shapes(2), right, mob, *perfs)
-    table, *faces = after(near_sum(table), *faces)
-    slots = far_slots(table)
-    flow, cond_low, cond_high = call(
-        first_flow_kernel, [block, (3,) + block, (3,) + block],
+    sent_shapes = [(lax.axis_size("gz") // NEAR, 24, 128), (2, 8, 128)]
+
+    table, *faces = call(
+        first_kernel, [(24, 128)] + face_shapes(2), right, mob, *perfs,
+        space=pltpu.HBM, mib=60,
+        scratch=[pltpu.VMEM(block, F32)] * 2
+        + [pltpu.VMEM(a.shape, a.dtype) for a in perfs]
+        + [pltpu.SemaphoreType.DMA((5,))],
+    )
+    sent, near = call(first_near_kernel, sent_shapes, near_slots(table))
+    sent, *faces = after(sent, *faces)
+    slots = far_slots(sent)
+    flow, cond = call(
+        first_flow_kernel, [block, (4,) + block],
         right, mob, diag, off, *low_halos(faces), *high_halos(faces),
     )
-
-    w1, table, inverse, extra, *faces = call(
-        second_kernel, [block, (16, 128), (8, 128), (32, 128)] + face_shapes(1),
-        slots, flow, right, *perfs,
-    )
-    table, *faces = after(near_sum(table), *faces)
-    slots = far_slots(table)
+    w1, table, inverse, extra, cond_along, *faces = call(
+        second_kernel,
+        [block, (24, 128), (8, 128), (32, 128), (2,) + block] + face_shapes(1),
+        slots, near, flow, right, mob, *perfs,
+    )
+
+    sent, near = call(near_kernel, sent_shapes, near_slots(table))
+    sent, *faces = after(sent, *faces)
+    slots = far_slots(sent)
     flow = call(
-        flow_kernel, [block],
-        w1, diag, off, cond_low, cond_high, *low_halos(faces), *high_halos(faces),
+        flow_kernel, [block], w1, diag, off, cond, *low_halos(faces), *high_halos(faces)
     )[0]
-
     w2, table, *faces = call(
-        third_kernel, [block, (16, 128)] + face_shapes(1), slots, flow, w1, extra, inverse, *perfs
-    )
+        third_kernel, [block, (24, 128)] + face_shapes(1),
+        slots, near, flow, w1, extra, inverse, cond_along, *perfs,
+    )
+
     low = low_halos(faces)
     table = call(
-        moment_kernel, [(16, 128)], table, right, w1, w2, extra, diag, off, cond_low, *low
+        moment_kernel, [(24, 128)],
+        table, right, w1, w2, extra, diag, off, cond, cond_along, *low,
     )[0]
-    table, *faces = after(near_sum(table), *faces)
-    slots = far_slots(table)
-    flow = call(
-        flow_kernel, [block], w2, diag, off, cond_low, cond_high, *low, *high_halos(faces)
-    )[0]
+    sent, near = call(last_near_kernel, sent_shapes, near_slots(table))
+    sent, *faces = after(sent, *faces)
+    slots, *high = after(far_slots(sent), *high_halos(faces))
+    flow = call(flow_kernel, [block], w2, diag, off, cond, *low, *high)[0]
 
     moments = call(scalar_kernel, [(8, 128)], slots, inverse)[0]
     count = lax.axis_size("gx") * lax.axis_size("gy")
     sent = jnp.broadcast_to(moments[None], (count, 8, 128))
     moment_slots = lax.all_to_all(sent, ("gx", "gy"), 0, 0)
-    w3 = call(last_vector_kernel, [block], slots, flow, w2, extra, inverse, *perfs)[0]
+    w3 = call(
+        last_vector_kernel, [block],
+        slots, near, flow, w2, extra, inverse, cond_along, *perfs,
+    )[0]
     solved, rest = call(combine_kernel, [block, block], moment_slots, right, w1, w2, w3)
     return solved.reshape(right_side.shape), rest.reshape(right_side.shape)
 

time: 206 us -> 183 us (0.89)
  blocking collectives: 68.1 us -> 25.3 us
  waiting for transfers between devices: 13.4 us -> 53.2 us
  starting transfers between devices: 111 us -> 92.6 us
  local copies, waits for them, and re-layouts: 5.64 us -> 1.48 us
  Pallas kernels: 4.62 us -> 8.17 us
    all_to_all x4 -> x3, blocking collectives: 68.1 us -> 25.3 us  [near_slots(): return lax.all_to_all(sent, 'gz', 0, 0, axis_index_groups=groups)]
    all_to_all x2 -> x3, waiting for transfers between devices: 4.56 us -> 34.8 us  [far_slots(): return lax.all_to_all(sent, 'gz', 0, 0, axis_index_groups=groups)]
    ppermute x9 -> x6, starting transfers between devices: 43.3 us -> 25.3 us  [forward(): return lax.ppermute(piece, axis, [(i, i + 1) for i in range(count - 1)])]
    all_to_all x1, waiting for transfers between devices: 0.01 us -> 7.18 us  [body(): moment_slots = lax.all_to_all(sent, ('gx', 'gy'), 0, 0)]
    ppermute x9 -> x6, waiting for transfers between devices: 6.57 us -> 10.4 us  [backward(): return lax.ppermute(piece, axis, [(i + 1, i) for i in range(count - 1)])]
    unnamed x22, local copies, waits for them, and re-layouts: 3.66 us -> 0.05 us
    pallas_call x10 -> x13, Pallas kernels: 4.62 us -> 8.17 us  [call(): pl.pallas_call(kernel, out_shape=[jax.ShapeDtypeStruct(shape, F32) for sh...]
    ppermute x9 -> x6, starting transfers between devices: 13.7 us -> 11.2 us  [backward(): return lax.ppermute(piece, axis, [(i + 1, i) for i in range(count - 1)])]
  transfers between devices with their start and end apart: 21 -> 16, of which waited for: 7 -> 8; matrix products, arithmetic and copies ran while one was open for 0% -> 0% of each run, Pallas kernels for 0% -> 0%
where the time goes in v2:
time: 183 us; the launch traced here: 182 us
  starting transfers between devices  92.6 us (51%)
  waiting for transfers between devices  53.2 us (29%)
  blocking collectives  25.3 us (14%)
  Pallas kernels  8.17 us (4%)
    all_to_all x3, starting transfers between devices, far_slots(): return lax.all_to_all(sent, 'gz', 0, 0, axis_index_groups=groups)  45.5 us
    all_to_all x3, waiting for transfers between devices, far_slots(): return lax.all_to_all(sent, 'gz', 0, 0, axis_index_groups=groups)  34.8 us
    ppermute x6, starting transfers between devices, forward(): return lax.ppermute(piece, axis, [(i, i + 1) for i in range(count - 1)])  25.3 us
    all_to_all x3, blocking collectives, near_slots(): return lax.all_to_all(sent, 'gz', 0, 0, axis_index_groups=groups)  25.3 us
    ppermute x6, starting transfers between devices, backward(): return lax.ppermute(piece, axis, [(i + 1, i) for i in range(count - 1)])  11.2 us
    all_to_all x1, starting transfers between devices, body(): moment_slots = lax.all_to_all(sent, ('gx', 'gy'), 0, 0)  10.6 us
    ppermute x6, waiting for transfers between devices, backward(): return lax.ppermute(piece, axis, [(i + 1, i) for i in range(count - 1)])  10.4 us
    pallas_call x13, Pallas kernels, call(): pl.pallas_call(kernel, out_shape=[jax.ShapeDtypeStruct(shape, F32) for sh...  8.17 us
  transfers between devices with their start and end apart: 16, of which 8 were waited for; matrix products, arithmetic and copies ran while one was open for 0% of the time, Pallas kernels for 0%

profile of v2, /device:TPU:1, one launch (start us, length us, event | category | flops | bytes accessed | tf_op | source)
XLA Modules:
  0.0 181.6 jit_solution(2047502567771246473)
XLA Ops:
  0.6 2.0 %shard_map.86 = (f32[24,128]{1,0:T(8,128)}, f32[6,8,128]{2,1,0:T(8,128)}, f32[6,8,128]{2,1,0:T(8,128)}, f32[24,128]{1,0:T(8,128)}, f32[24,128]{1,0:T(8,128)}) custom-call(f32[3,32,128]{2,1,0:T(8,128)} %bitcast.6, f32[3,32,128]{2,1,0:T(8,128)} %bitcast.19, s32[1,1,512]{2,1,0:T(1,128)} %cell.5, s32[1,1,512]{2,1,0:T(1,128)} %well.5, f32[1,1,512]{2,1,0:T(1,128)} %factor.5), custom_call_target="tpu_custom_call" | custom-call | tf_op jit(solution)/shard_map/pallas_call | solution.py:492
  3.4 10.9 %all_to_all.35.slots = f32[4,24,128]{2,1,0:T(8,128)S(1)} all-to-all(f32[4,24,128]{2,1,0:T(8,128)S(1)} %broadcast_in_dim.8), channel_id=1, replica_groups={{0,1,2,3},{4,5,6,7},{8,9,10,11},{12,13,14,15},{16,17,18,19},{20,21,22,2..., dimensions={0} | all-to-all | bytes 98304 | tf_op jit(solution)/shard_map/all_to_all | solution.py:509
  14.3 0.8 shard_map.87
  15.1 25.5 %all-to-all-start.1 = ((f32[8,24,128]{2,1,0:T(8,128)}), f32[8,24,128]{2,1,0:T(8,128)S(1)}, u32[]{:S(2)}, u32[]{:S(2)}) async-start(f32[8,24,128]{2,1,0:T(8,128)} %get-tuple-element.54), calls=%async_computation.1 | async-start | bytes 196608 | tf_op jit(solution)/shard_map/all_to_all | solution.py:515
  40.6 3.1 %collective-permute-start = (f32[6,8,128]{2,1,0:T(8,128)S(1)}, f32[6,8,128]{2,1,0:T(8,128)S(1)}, u32[]{:S(2)}, u32[]{:S(2)}) collective-permute-start(f32[6,8,128]{2,1,0:T(8,128)S(1)} %copy-done.8), channel_id=1, source_target_pairs={{0,256},{256,512},{512,768},{1,257},{257,513},{513,769},{2,258},{2... | collective-permute-start | bytes 73736 | tf_op jit(solution)/shard_map/ppermute | solution.py:520
  43.7 1.3 collective-permute-start.2
  45.0 5.8 %collective-permute-start.1 = (f32[24,128]{1,0:T(8,128)S(1)}, f32[24,128]{1,0:T(8,128)S(1)}, u32[]{:S(2)}, u32[]{:S(2)}) collective-permute-start(f32[24,128]{1,0:T(8,128)S(1)} %copy-done.10), channel_id=1, source_target_pairs={{0,32},{32,64},{64,96},{96,128},{128,160},{160,192},{192,224},{1,3... | collective-permute-start | bytes 36872 | tf_op jit(solution)/shard_map/ppermute | solution.py:520
  50.8 1.9 %collective-permute-start.3 = (f32[24,128]{1,0:T(8,128)S(1)}, f32[24,128]{1,0:T(8,128)S(1)}, u32[]{:S(2)}, u32[]{:S(2)}) collective-permute-start(f32[24,128]{1,0:T(8,128)S(1)} %copy-done.9), channel_id=1, source_target_pairs={{32,0},{64,32},{96,64},{128,96},{160,128},{192,160},{224,192},{33,... | collective-permute-start | bytes 36872 | tf_op jit(solution)/shard_map/ppermute | solution.py:525
  52.7 3.4 %collective-permute-done.3.yh = f32[24,128]{1,0:T(8,128)S(1)} collective-permute-done((f32[24,128]{1,0:T(8,128)S(1)}, f32[24,128]{1,0:T(8,128)S(1)}, u32[]{:S(2)}, u32[]{:S(2)}) %collective-permute-start.3) | collective-permute-done | bytes 12320 | tf_op jit(solution)/shard_map/ppermute | solution.py:525
  56.3 8.3 %all-to-all-done.1.slots = f32[8,24,128]{2,1,0:T(8,128)S(1)} async-done(((f32[8,24,128]{2,1,0:T(8,128)}), f32[8,24,128]{2,1,0:T(8,128)S(1)}, u32[]{:S(2)}, u32[]{:S(2)}) %all-to-all-start.1) | async-done | bytes 98336 | tf_op jit(solution)/shard_map/all_to_all | solution.py:515
  64.5 1.2 shard_map.89
  65.8 6.9 %all_to_all.36.slots = f32[4,24,128]{2,1,0:T(8,128)S(1)} all-to-all(f32[4,24,128]{2,1,0:T(8,128)S(1)} %broadcast_in_dim.9), channel_id=1, replica_groups={{0,1,2,3},{4,5,6,7},{8,9,10,11},{12,13,14,15},{16,17,18,19},{20,21,22,2..., dimensions={0} | all-to-all | bytes 98304 | tf_op jit(solution)/shard_map/all_to_all | solution.py:509
  73.3 13.4 %all-to-all-start.3 = ((f32[8,24,128]{2,1,0:T(8,128)}), f32[8,24,128]{2,1,0:T(8,128)S(1)}, u32[]{:S(2)}, u32[]{:S(2)}) async-start(f32[8,24,128]{2,1,0:T(8,128)} %get-tuple-element.67), calls=%async_computation.3 | async-start | bytes 196608 | tf_op jit(solution)/shard_map/all_to_all | solution.py:515
  86.8 4.3 %collective-permute-start.4 = (f32[3,8,128]{2,1,0:T(8,128)S(1)}, f32[3,8,128]{2,1,0:T(8,128)S(1)}, u32[]{:S(2)}, u32[]{:S(2)}) collective-permute-start(f32[3,8,128]{2,1,0:T(8,128)S(1)} %get-tuple-element.71), channel_id=1, source_target_pairs={{0,256},{256,512},{512,768},{1,257},{257,513},{513,769},{2,258},{2... | collective-permute-start | bytes 36872 | tf_op jit(solution)/shard_map/ppermute | solution.py:520
  91.0 1.3 collective-permute-start.6
  92.3 3.7 %collective-permute-start.5 = (f32[12,128]{1,0:T(8,128)S(1)}, f32[12,128]{1,0:T(8,128)S(1)}, u32[]{:S(2)}, u32[]{:S(2)}) collective-permute-start(f32[12,128]{1,0:T(8,128)S(1)} %get-tuple-element.72), channel_id=1, source_target_pairs={{0,32},{32,64},{64,96},{96,128},{128,160},{160,192},{192,224},{1,3... | collective-permute-start | bytes 18440 | tf_op jit(solution)/shard_map/ppermute | solution.py:520
  96.0 1.9 %collective-permute-start.7 = (f32[12,128]{1,0:T(8,128)S(1)}, f32[12,128]{1,0:T(8,128)S(1)}, u32[]{:S(2)}, u32[]{:S(2)}) collective-permute-start(f32[12,128]{1,0:T(8,128)S(1)} %get-tuple-element.74), channel_id=1, source_target_pairs={{32,0},{64,32},{96,64},{128,96},{160,128},{192,160},{224,192},{33,... | collective-permute-start | bytes 18440 | tf_op jit(solution)/shard_map/ppermute | solution.py:525
  98.0 3.3 %collective-permute-done.7.yh = f32[12,128]{1,0:T(8,128)S(1)} collective-permute-done((f32[12,128]{1,0:T(8,128)S(1)}, f32[12,128]{1,0:T(8,128)S(1)}, u32[]{:S(2)}, u32[]{:S(2)}) %collective-permute-start.7) | collective-permute-done | bytes 6176 | tf_op jit(solution)/shard_map/ppermute | solution.py:525
  101.3 12.1 %all-to-all-done.3.slots = f32[8,24,128]{2,1,0:T(8,128)S(1)} async-done(((f32[8,24,128]{2,1,0:T(8,128)}), f32[8,24,128]{2,1,0:T(8,128)S(1)}, u32[]{:S(2)}, u32[]{:S(2)}) %all-to-all-start.3) | async-done | bytes 98336 | tf_op jit(solution)/shard_map/all_to_all | solution.py:515
  113.5 1.1 shard_map.92
  114.5 4.3 %collective-permute-start.8 = (f32[3,8,128]{2,1,0:T(8,128)S(1)}, f32[3,8,128]{2,1,0:T(8,128)S(1)}, u32[]{:S(2)}, u32[]{:S(2)}) collective-permute-start(f32[3,8,128]{2,1,0:T(8,128)S(1)} %get-tuple-element.80), channel_id=1, source_target_pairs={{0,256},{256,512},{512,768},{1,257},{257,513},{513,769},{2,258},{2... | collective-permute-start | bytes 36872 | tf_op jit(solution)/shard_map/ppermute | solution.py:520
  118.8 4.2 %collective-permute-start.9 = (f32[12,128]{1,0:T(8,128)S(1)}, f32[12,128]{1,0:T(8,128)S(1)}, u32[]{:S(2)}, u32[]{:S(2)}) collective-permute-start(f32[12,128]{1,0:T(8,128)S(1)} %get-tuple-element.81), channel_id=1, source_target_pairs={{0,32},{32,64},{64,96},{96,128},{128,160},{160,192},{192,224},{1,3... | collective-permute-start | bytes 18440 | tf_op jit(solution)/shard_map/ppermute | solution.py:520
  123.0 0.8 collective-permute-done.9.yl
  124.0 7.5 %all_to_all.37.slots = f32[4,24,128]{2,1,0:T(8,128)S(1)} all-to-all(f32[4,24,128]{2,1,0:T(8,128)S(1)} %broadcast_in_dim.10), channel_id=1, replica_groups={{0,1,2,3},{4,5,6,7},{8,9,10,11},{12,13,14,15},{16,17,18,19},{20,21,22,2..., dimensions={0} | all-to-all | bytes 98304 | tf_op jit(solution)/shard_map/all_to_all | solution.py:509
  131.4 0.8 shard_map.94
  132.2 6.5 %all-to-all-start.5 = ((f32[8,24,128]{2,1,0:T(8,128)}), f32[8,24,128]{2,1,0:T(8,128)S(1)}, u32[]{:S(2)}, u32[]{:S(2)}) async-start(f32[8,24,128]{2,1,0:T(8,128)} %get-tuple-element.85), calls=%async_computation.5 | async-start | bytes 196608 | tf_op jit(solution)/shard_map/all_to_all | solution.py:515
  138.7 1.3 collective-permute-start.10
  140.0 3.5 %collective-permute-start.11 = (f32[12,128]{1,0:T(8,128)S(1)}, f32[12,128]{1,0:T(8,128)S(1)}, u32[]{:S(2)}, u32[]{:S(2)}) collective-permute-start(f32[12,128]{1,0:T(8,128)S(1)} %get-tuple-element.87), channel_id=1, source_target_pairs={{32,0},{64,32},{96,64},{128,96},{160,128},{192,160},{224,192},{33,... | collective-permute-start | bytes 18440 | tf_op jit(solution)/shard_map/ppermute | solution.py:525
  143.5 3.7 %collective-permute-done.11.yh = f32[12,128]{1,0:T(8,128)S(1)} collective-permute-done((f32[12,128]{1,0:T(8,128)S(1)}, f32[12,128]{1,0:T(8,128)S(1)}, u32[]{:S(2)}, u32[]{:S(2)}) %collective-permute-start.11) | collective-permute-done | bytes 6176 | tf_op jit(solution)/shard_map/ppermute | solution.py:525
  147.2 14.5 %all-to-all-done.5.slots = f32[8,24,128]{2,1,0:T(8,128)S(1)} async-done(((f32[8,24,128]{2,1,0:T(8,128)}), f32[8,24,128]{2,1,0:T(8,128)S(1)}, u32[]{:S(2)}, u32[]{:S(2)}) %all-to-all-start.5) | async-done | bytes 98336 | tf_op jit(solution)/shard_map/all_to_all | solution.py:515
  162.5 10.6 %all-to-all-start.6 = ((f32[32,8,128]{2,1,0:T(8,128)}), f32[32,8,128]{2,1,0:T(8,128)S(1)}, u32[]{:S(2)}, u32[]{:S(2)}) async-start(f32[32,8,128]{2,1,0:T(8,128)} %broadcast_in_dim.11), calls=%async_computation.6 | async-start | bytes 262144 | tf_op jit(solution)/shard_map/all_to_all | solution.py:596
  173.7 7.2 %all-to-all-done.6.slots = f32[32,8,128]{2,1,0:T(8,128)S(1)} async-done(((f32[32,8,128]{2,1,0:T(8,128)}), f32[32,8,128]{2,1,0:T(8,128)S(1)}, u32[]{:S(2)}, u32[]{:S(2)}) %all-to-all-start.6) | async-done | bytes 131104 | tf_op jit(solution)/shard_map/all_to_all | solution.py:596
  (42 shorter events, 3.9 us)
Async XLA Ops:
  3.4 41.7 %copy-start.10 = (f32[24,128]{1,0:T(8,128)S(1)}, f32[24,128]{1,0:T(8,128)}, u32[]{:S(2)}) copy-start(f32[24,128]{1,0:T(8,128)} %get-tuple-element.57) | copy-start | bytes 36868
  14.3 26.3 %copy-start.8 = (f32[6,8,128]{2,1,0:T(8,128)S(1)}, f32[6,8,128]{2,1,0:T(8,128)}, u32[]{:S(2)}) copy-start(f32[6,8,128]{2,1,0:T(8,128)} %get-tuple-element.56) | copy-start | bytes 73732
  14.3 29.4 %copy-start.7 = (f32[6,8,128]{2,1,0:T(8,128)S(1)}, f32[6,8,128]{2,1,0:T(8,128)}, u32[]{:S(2)}) copy-start(f32[6,8,128]{2,1,0:T(8,128)} %get-tuple-element.58) | copy-start | bytes 73732
  14.3 36.5 %copy-start.9 = (f32[24,128]{1,0:T(8,128)S(1)}, f32[24,128]{1,0:T(8,128)}, u32[]{:S(2)}) copy-start(f32[24,128]{1,0:T(8,128)} %get-tuple-element.59) | copy-start | bytes 36868
  15.1 41.1 %copy-start = (f32[3,4,8,128]{3,2,1,0:T(8,128)S(1)}, f32[3,4,8,128]{3,2,1,0:T(8,128)}, u32[]{:S(2)}) copy-start(f32[3,4,8,128]{3,2,1,0:T(8,128)} %param.7) | copy-start | bytes 147460
  15.1 41.1 %copy-start.1 = (f32[3,4,8,128]{3,2,1,0:T(8,128)S(1)}, f32[3,4,8,128]{3,2,1,0:T(8,128)}, u32[]{:S(2)}) copy-start(f32[3,4,8,128]{3,2,1,0:T(8,128)} %param.8) | copy-start | bytes 147460
  15.1 41.1 %copy-start.2 = (f32[3,4,8,128]{3,2,1,0:T(8,128)S(1)}, f32[3,4,8,128]{3,2,1,0:T(8,128)}, u32[]{:S(2)}) copy-start(f32[3,4,8,128]{3,2,1,0:T(8,128)} %param.9) | copy-start | bytes 147460
  15.1 41.1 %copy-start.3 = (f32[3,4,8,128]{3,2,1,0:T(8,128)S(1)}, f32[3,4,8,128]{3,2,1,0:T(8,128)}, u32[]{:S(2)}) copy-start(f32[3,4,8,128]{3,2,1,0:T(8,128)} %param.10) | copy-start | bytes 147460
  15.1 49.5 %all-to-all-start.1 = ((f32[8,24,128]{2,1,0:T(8,128)}), f32[8,24,128]{2,1,0:T(8,128)S(1)}, u32[]{:S(2)}, u32[]{:S(2)}) async-start(f32[8,24,128]{2,1,0:T(8,128)} %get-tuple-element.54), calls=%async_computation.1 | async-start | bytes 196608 | tf_op jit(solution)/shard_map/all_to_all | solution.py:515
  40.6 15.5 %collective-permute-start = (f32[6,8,128]{2,1,0:T(8,128)S(1)}, f32[6,8,128]{2,1,0:T(8,128)S(1)}, u32[]{:S(2)}, u32[]{:S(2)}) collective-permute-start(f32[6,8,128]{2,1,0:T(8,128)S(1)} %copy-done.8), channel_id=1, source_target_pairs={{0,256},{256,512},{512,768},{1,257},{257,513},{513,769},{2,258},{2... | collective-permute-start | bytes 73736 | tf_op jit(solution)/shard_map/ppermute | solution.py:520
  43.7 12.4 %collective-permute-start.2 = (f32[6,8,128]{2,1,0:T(8,128)S(1)}, f32[6,8,128]{2,1,0:T(8,128)S(1)}, u32[]{:S(2)}, u32[]{:S(2)}) collective-permute-start(f32[6,8,128]{2,1,0:T(8,128)S(1)} %copy-done.7), channel_id=1, source_target_pairs={{256,0},{512,256},{768,512},{257,1},{513,257},{769,513},{258,2},{5... | collective-permute-start | bytes 73736 | tf_op jit(solution)/shard_map/ppermute | solution.py:525
  45.0 7.7 %collective-permute-start.1 = (f32[24,128]{1,0:T(8,128)S(1)}, f32[24,128]{1,0:T(8,128)S(1)}, u32[]{:S(2)}, u32[]{:S(2)}) collective-permute-start(f32[24,128]{1,0:T(8,128)S(1)} %copy-done.10), channel_id=1, source_target_pairs={{0,32},{32,64},{64,96},{96,128},{128,160},{160,192},{192,224},{1,3... | collective-permute-start | bytes 36872 | tf_op jit(solution)/shard_map/ppermute | solution.py:520
  50.8 5.3 %collective-permute-start.3 = (f32[24,128]{1,0:T(8,128)S(1)}, f32[24,128]{1,0:T(8,128)S(1)}, u32[]{:S(2)}, u32[]{:S(2)}) collective-permute-start(f32[24,128]{1,0:T(8,128)S(1)} %copy-done.9), channel_id=1, source_target_pairs={{32,0},{64,32},{96,64},{128,96},{160,128},{192,160},{224,192},{33,... | collective-permute-start | bytes 36872 | tf_op jit(solution)/shard_map/ppermute | solution.py:525
  56.2 8.4 %copy-start.5 = (s32[1,1,512]{2,1,0:T(1,128)S(1)}, s32[1,1,512]{2,1,0:T(1,128)}, u32[]{:S(2)}) copy-start(s32[1,1,512]{2,1,0:T(1,128)} %well.5) | copy-start | bytes 6148
  56.2 8.4 %copy-start.6 = (f32[1,1,512]{2,1,0:T(1,128)S(1)}, f32[1,1,512]{2,1,0:T(1,128)}, u32[]{:S(2)}) copy-start(f32[1,1,512]{2,1,0:T(1,128)} %factor.5) | copy-start | bytes 6148
  56.3 8.3 %copy-start.4 = (s32[1,1,512]{2,1,0:T(1,128)S(1)}, s32[1,1,512]{2,1,0:T(1,128)}, u32[]{:S(2)}) copy-start(s32[1,1,512]{2,1,0:T(1,128)} %cell.5) | copy-start | bytes 6148
  73.3 40.1 %all-to-all-start.3 = ((f32[8,24,128]{2,1,0:T(8,128)}), f32[8,24,128]{2,1,0:T(8,128)S(1)}, u32[]{:S(2)}, u32[]{:S(2)}) async-start(f32[8,24,128]{2,1,0:T(8,128)} %get-tuple-element.67), calls=%async_computation.3 | async-start | bytes 196608 | tf_op jit(solution)/shard_map/all_to_all | solution.py:515
  86.8 14.5 %collective-permute-start.4 = (f32[3,8,128]{2,1,0:T(8,128)S(1)}, f32[3,8,128]{2,1,0:T(8,128)S(1)}, u32[]{:S(2)}, u32[]{:S(2)}) collective-permute-start(f32[3,8,128]{2,1,0:T(8,128)S(1)} %get-tuple-element.71), channel_id=1, source_target_pairs={{0,256},{256,512},{512,768},{1,257},{257,513},{513,769},{2,258},{2... | collective-permute-start | bytes 36872 | tf_op jit(solution)/shard_map/ppermute | solution.py:520
  91.0 10.3 %collective-permute-start.6 = (f32[3,8,128]{2,1,0:T(8,128)S(1)}, f32[3,8,128]{2,1,0:T(8,128)S(1)}, u32[]{:S(2)}, u32[]{:S(2)}) collective-permute-start(f32[3,8,128]{2,1,0:T(8,128)S(1)} %get-tuple-element.73), channel_id=1, source_target_pairs={{256,0},{512,256},{768,512},{257,1},{513,257},{769,513},{258,2},{5... | collective-permute-start | bytes 36872 | tf_op jit(solution)/shard_map/ppermute | solution.py:525
  92.3 5.6 %collective-permute-start.5 = (f32[12,128]{1,0:T(8,128)S(1)}, f32[12,128]{1,0:T(8,128)S(1)}, u32[]{:S(2)}, u32[]{:S(2)}) collective-permute-start(f32[12,128]{1,0:T(8,128)S(1)} %get-tuple-element.72), channel_id=1, source_target_pairs={{0,32},{32,64},{64,96},{96,128},{128,160},{160,192},{192,224},{1,3... | collective-permute-start | bytes 18440 | tf_op jit(solution)/shard_map/ppermute | solution.py:520
  96.0 5.3 %collective-permute-start.7 = (f32[12,128]{1,0:T(8,128)S(1)}, f32[12,128]{1,0:T(8,128)S(1)}, u32[]{:S(2)}, u32[]{:S(2)}) collective-permute-start(f32[12,128]{1,0:T(8,128)S(1)} %get-tuple-element.74), channel_id=1, source_target_pairs={{32,0},{64,32},{96,64},{128,96},{160,128},{192,160},{224,192},{33,... | collective-permute-start | bytes 18440 | tf_op jit(solution)/shard_map/ppermute | solution.py:525
  114.5 9.2 %collective-permute-start.8 = (f32[3,8,128]{2,1,0:T(8,128)S(1)}, f32[3,8,128]{2,1,0:T(8,128)S(1)}, u32[]{:S(2)}, u32[]{:S(2)}) collective-permute-start(f32[3,8,128]{2,1,0:T(8,128)S(1)} %get-tuple-element.80), channel_id=1, source_target_pairs={{0,256},{256,512},{512,768},{1,257},{257,513},{513,769},{2,258},{2... | collective-permute-start | bytes 36872 | tf_op jit(solution)/shard_map/ppermute | solution.py:520
  118.8 4.9 %collective-permute-start.9 = (f32[12,128]{1,0:T(8,128)S(1)}, f32[12,128]{1,0:T(8,128)S(1)}, u32[]{:S(2)}, u32[]{:S(2)}) collective-permute-start(f32[12,128]{1,0:T(8,128)S(1)} %get-tuple-element.81), channel_id=1, source_target_pairs={{0,32},{32,64},{64,96},{96,128},{128,160},{160,192},{192,224},{1,3... | collective-permute-start | bytes 18440 | tf_op jit(solution)/shard_map/ppermute | solution.py:520
  132.2 29.5 %all-to-all-start.5 = ((f32[8,24,128]{2,1,0:T(8,128)}), f32[8,24,128]{2,1,0:T(8,128)S(1)}, u32[]{:S(2)}, u32[]{:S(2)}) async-start(f32[8,24,128]{2,1,0:T(8,128)} %get-tuple-element.85), calls=%async_computation.5 | async-start | bytes 196608 | tf_op jit(solution)/shard_map/all_to_all | solution.py:515
  138.7 8.5 %collective-permute-start.10 = (f32[3,8,128]{2,1,0:T(8,128)S(1)}, f32[3,8,128]{2,1,0:T(8,128)S(1)}, u32[]{:S(2)}, u32[]{:S(2)}) collective-permute-start(f32[3,8,128]{2,1,0:T(8,128)S(1)} %get-tuple-element.86), channel_id=1, source_target_pairs={{256,0},{512,256},{768,512},{257,1},{513,257},{769,513},{258,2},{5... | collective-permute-start | bytes 36872 | tf_op jit(solution)/shard_map/ppermute | solution.py:525
  140.0 7.2 %collective-permute-start.11 = (f32[12,128]{1,0:T(8,128)S(1)}, f32[12,128]{1,0:T(8,128)S(1)}, u32[]{:S(2)}, u32[]{:S(2)}) collective-permute-start(f32[12,128]{1,0:T(8,128)S(1)} %get-tuple-element.87), channel_id=1, source_target_pairs={{32,0},{64,32},{96,64},{128,96},{160,128},{192,160},{224,192},{33,... | collective-permute-start | bytes 18440 | tf_op jit(solution)/shard_map/ppermute | solution.py:525
  162.5 18.3 %all-to-all-start.6 = ((f32[32,8,128]{2,1,0:T(8,128)}), f32[32,8,128]{2,1,0:T(8,128)S(1)}, u32[]{:S(2)}, u32[]{:S(2)}) async-start(f32[32,8,128]{2,1,0:T(8,128)} %broadcast_in_dim.11), calls=%async_computation.6 | async-start | bytes 262144 | tf_op jit(solution)/shard_map/all_to_all | solution.py:596

commit v3 on v2

--- a/solution.py
+++ b/solution.py
@@ -400,7 +400,7 @@
     table[15:16] = line
 
 
-def scalar_kernel(slots, inverse, moments):
+def scalar_kernel(slots, inverse, sent):
     total = jnp.sum(slots[...], axis=0)
     pull = jnp.zeros((WELL_ROWS, 128), F32)
     scale = inverse[0:WELL_ROWS]
@@ -411,12 +411,15 @@
     between = tree([face_energy(a, b) for a, b in zip(tiles, tiles[1:])])
     line = total[15:16]
     lane = lanes()[0:1]
+    out = []
     for k in range(6):
         value = jnp.sum(jnp.where(lane == k, line, 0.0), axis=1, keepdims=True)
         if k == 5:
             value = value + (whole_sum(between) - whole_sum(pull))
-        moments[k : k + 1] = jnp.broadcast_to(value, (1, 128))
-    moments[6:8] = jnp.zeros((2, 128), F32)
+        out.append(jnp.broadcast_to(value, (1, 128)))
+    moments = jnp.concatenate(out + [jnp.zeros((2, 128), F32)], 0)
+    for k in range(sent.shape[0]):
+        sent[k] = moments
 
 
 def last_vector_kernel(
@@ -556,12 +559,11 @@
         + [pltpu.VMEM(a.shape, a.dtype) for a in perfs]
         + [pltpu.SemaphoreType.DMA((5,))],
     )
-    sent, near = call(first_near_kernel, sent_shapes, near_slots(table))
-    sent, *faces = after(sent, *faces)
+    slots, *halos = after(near_slots(table), *low_halos(faces), *high_halos(faces))
+    sent, near = call(first_near_kernel, sent_shapes, slots)
     slots = far_slots(sent)
     flow, cond = call(
-        first_flow_kernel, [block, (4,) + block],
-        right, mob, diag, off, *low_halos(faces), *high_halos(faces),
+        first_flow_kernel, [block, (4,) + block], right, mob, diag, off, *halos
     )
     w1, table, inverse, extra, cond_along, *faces = call(
         second_kernel,
@@ -569,30 +571,28 @@
         slots, near, flow, right, mob, *perfs,
     )
 
-    sent, near = call(near_kernel, sent_shapes, near_slots(table))
-    sent, *faces = after(sent, *faces)
+    slots, *halos = after(near_slots(table), *low_halos(faces), *high_halos(faces))
+    sent, near = call(near_kernel, sent_shapes, slots)
     slots = far_slots(sent)
-    flow = call(
-        flow_kernel, [block], w1, diag, off, cond, *low_halos(faces), *high_halos(faces)
-    )[0]
+    flow = call(flow_kernel, [block], w1, diag, off, cond, *halos)[0]
     w2, table, *faces = call(
         third_kernel, [block, (24, 128)] + face_shapes(1),
         slots, near, flow, w1, extra, inverse, cond_along, *perfs,
     )
 
     low = low_halos(faces)
+    high = high_halos(faces)
     table = call(
         moment_kernel, [(24, 128)],
         table, right, w1, w2, extra, diag, off, cond, cond_along, *low,
     )[0]
-    sent, near = call(last_near_kernel, sent_shapes, near_slots(table))
-    sent, *faces = after(sent, *faces)
-    slots, *high = after(far_slots(sent), *high_halos(faces))
+    slots, *high = after(near_slots(table), *high)
+    sent, near = call(last_near_kernel, sent_shapes, slots)
+    slots = far_slots(sent)
     flow = call(flow_kernel, [block], w2, diag, off, cond, *low, *high)[0]
 
-    moments = call(scalar_kernel, [(8, 128)], slots, inverse)[0]
     count = lax.axis_size("gx") * lax.axis_size("gy")
-    sent = jnp.broadcast_to(moments[None], (count, 8, 128))
+    sent = call(scalar_kernel, [(count, 8, 128)], slots, inverse)[0]
     moment_slots = lax.all_to_all(sent, ("gx", "gy"), 0, 0)
     w3 = call(
         last_vector_kernel, [block],

time: 183 us -> 199 us (1.087)
  waiting for transfers between devices: 53.2 us -> 66.4 us
  blocking collectives: 25.3 us -> 28.8 us
  starting transfers between devices: 92.6 us -> 90.6 us
    all_to_all x3 -> x2, starting transfers between devices: 45.5 us -> 25.1 us  [far_slots(): return lax.all_to_all(sent, 'gz', 0, 0, axis_index_groups=groups)]
    all_to_all x0 -> x3, starting transfers between devices: none -> 18.7 us  [near_slots(): return lax.all_to_all(sent, 'gz', 0, 0, axis_index_groups=groups)]
    all_to_all x3 -> x2, waiting for transfers between devices: 34.8 us -> 50.7 us  [far_slots(): return lax.all_to_all(sent, 'gz', 0, 0, axis_index_groups=groups)]
    ppermute x6, starting transfers between devices: 11.2 us -> 15.8 us  [backward(): return lax.ppermute(piece, axis, [(i + 1, i) for i in range(count - 1)])]
    all_to_all x1, starting transfers between devices: 10.6 us -> 6.81 us  [body(): moment_slots = lax.all_to_all(sent, ('gx', 'gy'), 0, 0)]
    all_to_all x3 -> x1, blocking collectives: 25.3 us -> 28.8 us  [far_slots(): return lax.all_to_all(sent, 'gz', 0, 0, axis_index_groups=groups)]
    ppermute x6, waiting for transfers between devices: 10.4 us -> 7.71 us  [backward(): return lax.ppermute(piece, axis, [(i + 1, i) for i in range(count - 1)])]
  transfers between devices with their start and end apart: 16 -> 18, of which waited for: 8 -> 7; matrix products, arithmetic and copies ran while one was open for 0% -> 0% of each run, Pallas kernels for 0% -> 0%
where the time goes in v3:
time: 199 us; the launch traced here: 198 us
  starting transfers between devices  90.6 us (46%)
  waiting for transfers between devices  66.4 us (33%)
  blocking collectives  28.8 us (14%)
  Pallas kernels  8.23 us (4%)
  local copies, waits for them, and re-layouts  2.68 us (1%)
    all_to_all x2, waiting for transfers between devices, far_slots(): return lax.all_to_all(sent, 'gz', 0, 0, axis_index_groups=groups)  50.7 us
    all_to_all x1, blocking collectives, far_slots(): return lax.all_to_all(sent, 'gz', 0, 0, axis_index_groups=groups)  28.8 us
    all_to_all x2, starting transfers between devices, far_slots(): return lax.all_to_all(sent, 'gz', 0, 0, axis_index_groups=groups)  25.1 us
    ppermute x6, starting transfers between devices, forward(): return lax.ppermute(piece, axis, [(i, i + 1) for i in range(count - 1)])  24.2 us
    all_to_all x3, starting transfers between devices, near_slots(): return lax.all_to_all(sent, 'gz', 0, 0, axis_index_groups=groups)  18.7 us
    ppermute x6, starting transfers between devices, backward(): return lax.ppermute(piece, axis, [(i + 1, i) for i in range(count - 1)])  15.8 us
    pallas_call x13, Pallas kernels, call(): pl.pallas_call(kernel, out_shape=[jax.ShapeDtypeStruct(shape, F32) for sh...  8.23 us
    ppermute x6, waiting for transfers between devices, backward(): return lax.ppermute(piece, axis, [(i + 1, i) for i in range(count - 1)])  7.71 us
  transfers between devices with their start and end apart: 18, of which 7 were waited for; matrix products, arithmetic and copies ran while one was open for 0% of the time, Pallas kernels for 0%

profile of v3, /device:TPU:1, one launch (start us, length us, event | category | flops | bytes accessed | tf_op | source)
XLA Modules:
  0.0 197.7 jit_solution(2604697942984431462)
XLA Ops:
  0.6 2.0 %shard_map.86 = (f32[24,128]{1,0:T(8,128)}, f32[6,8,128]{2,1,0:T(8,128)}, f32[6,8,128]{2,1,0:T(8,128)}, f32[24,128]{1,0:T(8,128)}, f32[24,128]{1,0:T(8,128)}) custom-call(f32[3,32,128]{2,1,0:T(8,128)} %bitcast.6, f32[3,32,128]{2,1,0:T(8,128)} %bitcast.19, s32[1,1,512]{2,1,0:T(1,128)} %cell.5, s32[1,1,512]{2,1,0:T(1,128)} %well.5, f32[1,1,512]{2,1,0:T(1,128)} %factor.5), custom_call_target="tpu_custom_call" | custom-call | tf_op jit(solution)/shard_map/pallas_call | solution.py:495
  2.6 1.3 broadcast_in_dim.6
  4.0 6.6 %all-to-all-start = ((f32[4,24,128]{2,1,0:T(8,128)}), f32[4,24,128]{2,1,0:T(8,128)S(1)}, u32[]{:S(2)}, u32[]{:S(2)}) async-start(f32[4,24,128]{2,1,0:T(8,128)} %broadcast_in_dim.6), calls=%async_computation | async-start | bytes 98304 | tf_op jit(solution)/shard_map/all_to_all | solution.py:512
  10.6 3.1 %collective-permute-start = (f32[6,8,128]{2,1,0:T(8,128)S(1)}, f32[6,8,128]{2,1,0:T(8,128)S(1)}, u32[]{:S(2)}, u32[]{:S(2)}) collective-permute-start(f32[6,8,128]{2,1,0:T(8,128)S(1)} %copy-done.8), channel_id=1, source_target_pairs={{0,256},{256,512},{512,768},{1,257},{257,513},{513,769},{2,258},{2... | collective-permute-start | bytes 73736 | tf_op jit(solution)/shard_map/ppermute | solution.py:523
  13.7 1.3 collective-permute-start.2
  15.0 4.3 %collective-permute-start.1 = (f32[24,128]{1,0:T(8,128)S(1)}, f32[24,128]{1,0:T(8,128)S(1)}, u32[]{:S(2)}, u32[]{:S(2)}) collective-permute-start(f32[24,128]{1,0:T(8,128)S(1)} %copy-done.10), channel_id=1, source_target_pairs={{0,32},{32,64},{64,96},{96,128},{128,160},{160,192},{192,224},{1,3... | collective-permute-start | bytes 36872 | tf_op jit(solution)/shard_map/ppermute | solution.py:523
  19.4 8.1 %collective-permute-start.3 = (f32[24,128]{1,0:T(8,128)S(1)}, f32[24,128]{1,0:T(8,128)S(1)}, u32[]{:S(2)}, u32[]{:S(2)}) collective-permute-start(f32[24,128]{1,0:T(8,128)S(1)} %copy-done.9), channel_id=1, source_target_pairs={{32,0},{64,32},{96,64},{128,96},{160,128},{192,160},{224,192},{33,... | collective-permute-start | bytes 36872 | tf_op jit(solution)/shard_map/ppermute | solution.py:528
  27.4 0.8 collective-permute-done.3.yh
  28.2 0.8 shard_map.87
  29.0 21.7 %all-to-all-start.1 = ((f32[8,24,128]{2,1,0:T(8,128)}), f32[8,24,128]{2,1,0:T(8,128)S(1)}, u32[]{:S(2)}, u32[]{:S(2)}) async-start(f32[8,24,128]{2,1,0:T(8,128)} %get-tuple-element.51), calls=%async_computation.1 | async-start | bytes 196608 | tf_op jit(solution)/shard_map/all_to_all | solution.py:518
  51.0 25.7 %all-to-all-done.1.slots = f32[8,24,128]{2,1,0:T(8,128)S(1)} async-done(((f32[8,24,128]{2,1,0:T(8,128)}), f32[8,24,128]{2,1,0:T(8,128)S(1)}, u32[]{:S(2)}, u32[]{:S(2)}) %all-to-all-start.1) | async-done | bytes 98336 | tf_op jit(solution)/shard_map/all_to_all | solution.py:518
  76.7 1.2 shard_map.89
  78.5 5.0 %all-to-all-start.2 = ((f32[4,24,128]{2,1,0:T(8,128)}), f32[4,24,128]{2,1,0:T(8,128)S(1)}, u32[]{:S(2)}, u32[]{:S(2)}) async-start(f32[4,24,128]{2,1,0:T(8,128)} %broadcast_in_dim.7), calls=%async_computation.2 | async-start | bytes 98304 | tf_op jit(solution)/shard_map/all_to_all | solution.py:512
  83.5 4.3 %collective-permute-start.4 = (f32[3,8,128]{2,1,0:T(8,128)S(1)}, f32[3,8,128]{2,1,0:T(8,128)S(1)}, u32[]{:S(2)}, u32[]{:S(2)}) collective-permute-start(f32[3,8,128]{2,1,0:T(8,128)S(1)} %get-tuple-element.59), channel_id=1, source_target_pairs={{0,256},{256,512},{512,768},{1,257},{257,513},{513,769},{2,258},{2... | collective-permute-start | bytes 36872 | tf_op jit(solution)/shard_map/ppermute | solution.py:523
  87.8 1.3 collective-permute-start.6
  89.1 4.9 %collective-permute-start.5 = (f32[12,128]{1,0:T(8,128)S(1)}, f32[12,128]{1,0:T(8,128)S(1)}, u32[]{:S(2)}, u32[]{:S(2)}) collective-permute-start(f32[12,128]{1,0:T(8,128)S(1)} %get-tuple-element.60), channel_id=1, source_target_pairs={{0,32},{32,64},{64,96},{96,128},{128,160},{160,192},{192,224},{1,3... | collective-permute-start | bytes 18440 | tf_op jit(solution)/shard_map/ppermute | solution.py:523
  94.0 1.9 collective-permute-start.7
  95.9 3.0 %collective-permute-done.7.yh = f32[12,128]{1,0:T(8,128)S(1)} collective-permute-done((f32[12,128]{1,0:T(8,128)S(1)}, f32[12,128]{1,0:T(8,128)S(1)}, u32[]{:S(2)}, u32[]{:S(2)}) %collective-permute-start.7) | collective-permute-done | bytes 6176 | tf_op jit(solution)/shard_map/ppermute | solution.py:528
  99.6 3.4 %all-to-all-start.3 = ((f32[8,24,128]{2,1,0:T(8,128)}), f32[8,24,128]{2,1,0:T(8,128)S(1)}, u32[]{:S(2)}, u32[]{:S(2)}) async-start(f32[8,24,128]{2,1,0:T(8,128)} %get-tuple-element.64), calls=%async_computation.3 | async-start | bytes 196608 | tf_op jit(solution)/shard_map/all_to_all | solution.py:518
  103.0 25.1 %all-to-all-done.3.slots = f32[8,24,128]{2,1,0:T(8,128)S(1)} async-done(((f32[8,24,128]{2,1,0:T(8,128)}), f32[8,24,128]{2,1,0:T(8,128)S(1)}, u32[]{:S(2)}, u32[]{:S(2)}) %all-to-all-start.3) | async-done | bytes 98336 | tf_op jit(solution)/shard_map/all_to_all | solution.py:518
  128.1 1.1 shard_map.92
  129.2 4.3 %collective-permute-start.8 = (f32[3,8,128]{2,1,0:T(8,128)S(1)}, f32[3,8,128]{2,1,0:T(8,128)S(1)}, u32[]{:S(2)}, u32[]{:S(2)}) collective-permute-start(f32[3,8,128]{2,1,0:T(8,128)S(1)} %get-tuple-element.77), channel_id=1, source_target_pairs={{0,256},{256,512},{512,768},{1,257},{257,513},{513,769},{2,258},{2... | collective-permute-start | bytes 36872 | tf_op jit(solution)/shard_map/ppermute | solution.py:523
  133.5 3.4 %collective-permute-start.9 = (f32[12,128]{1,0:T(8,128)S(1)}, f32[12,128]{1,0:T(8,128)S(1)}, u32[]{:S(2)}, u32[]{:S(2)}) collective-permute-start(f32[12,128]{1,0:T(8,128)S(1)} %get-tuple-element.78), channel_id=1, source_target_pairs={{0,32},{32,64},{64,96},{96,128},{128,160},{160,192},{192,224},{1,3... | collective-permute-start | bytes 18440 | tf_op jit(solution)/shard_map/ppermute | solution.py:523
  136.9 0.8 collective-permute-done.9.yl
  138.4 7.1 %all-to-all-start.4 = ((f32[4,24,128]{2,1,0:T(8,128)}), f32[4,24,128]{2,1,0:T(8,128)S(1)}, u32[]{:S(2)}, u32[]{:S(2)}) async-start(f32[4,24,128]{2,1,0:T(8,128)} %broadcast_in_dim.8), calls=%async_computation.4 | async-start | bytes 98304 | tf_op jit(solution)/shard_map/all_to_all | solution.py:512
  145.5 1.3 collective-permute-start.10
  146.8 1.9 collective-permute-start.11
  148.7 3.9 %collective-permute-done.11.yh = f32[12,128]{1,0:T(8,128)S(1)} collective-permute-done((f32[12,128]{1,0:T(8,128)S(1)}, f32[12,128]{1,0:T(8,128)S(1)}, u32[]{:S(2)}, u32[]{:S(2)}) %collective-permute-start.11) | collective-permute-done | bytes 6176 | tf_op jit(solution)/shard_map/ppermute | solution.py:528
  152.8 28.8 %all_to_all.35.slots = f32[8,24,128]{2,1,0:T(8,128)S(1)} all-to-all(f32[8,24,128]{2,1,0:T(8,128)S(1)} %get-tuple-element.82), channel_id=1, replica_groups={{0,4,8,12,16,20,24,28},{1,5,9,13,17,21,25,29},{2,6,10,14,18,22,26,30},{..., dimensions={0} | all-to-all | bytes 196608 | tf_op jit(solution)/shard_map/all_to_all | solution.py:518
  181.6 0.8 shard_map.95
  182.4 6.8 %all-to-all-start.6 = ((f32[32,8,128]{2,1,0:T(8,128)}), f32[32,8,128]{2,1,0:T(8,128)S(1)}, u32[]{:S(2)}, u32[]{:S(2)}) async-start(f32[32,8,128]{2,1,0:T(8,128)} %shard_map.95), calls=%async_computation.6 | async-start | bytes 262144 | tf_op jit(solution)/shard_map/all_to_all | solution.py:596
  189.8 7.2 %all-to-all-done.6.slots = f32[32,8,128]{2,1,0:T(8,128)S(1)} async-done(((f32[32,8,128]{2,1,0:T(8,128)}), f32[32,8,128]{2,1,0:T(8,128)S(1)}, u32[]{:S(2)}, u32[]{:S(2)}) %all-to-all-start.6) | async-done | bytes 131104 | tf_op jit(solution)/shard_map/all_to_all | solution.py:596
  (43 shorter events, 3.7 us)
Async XLA Ops:
  4.0 6.6 %copy-start.8 = (f32[6,8,128]{2,1,0:T(8,128)S(1)}, f32[6,8,128]{2,1,0:T(8,128)}, u32[]{:S(2)}) copy-start(f32[6,8,128]{2,1,0:T(8,128)} %get-tuple-element.46) | copy-start | bytes 73732
  4.0 9.7 %copy-start.7 = (f32[6,8,128]{2,1,0:T(8,128)S(1)}, f32[6,8,128]{2,1,0:T(8,128)}, u32[]{:S(2)}) copy-start(f32[6,8,128]{2,1,0:T(8,128)} %get-tuple-element.48) | copy-start | bytes 73732
  4.0 11.0 %copy-start.10 = (f32[24,128]{1,0:T(8,128)S(1)}, f32[24,128]{1,0:T(8,128)}, u32[]{:S(2)}) copy-start(f32[24,128]{1,0:T(8,128)} %get-tuple-element.47) | copy-start | bytes 36868
  4.0 15.4 %copy-start.9 = (f32[24,128]{1,0:T(8,128)S(1)}, f32[24,128]{1,0:T(8,128)}, u32[]{:S(2)}) copy-start(f32[24,128]{1,0:T(8,128)} %get-tuple-element.49) | copy-start | bytes 36868
  4.0 24.3 %all-to-all-start = ((f32[4,24,128]{2,1,0:T(8,128)}), f32[4,24,128]{2,1,0:T(8,128)S(1)}, u32[]{:S(2)}, u32[]{:S(2)}) async-start(f32[4,24,128]{2,1,0:T(8,128)} %broadcast_in_dim.6), calls=%async_computation | async-start | bytes 98304 | tf_op jit(solution)/shard_map/all_to_all | solution.py:512
  10.6 17.7 %collective-permute-start = (f32[6,8,128]{2,1,0:T(8,128)S(1)}, f32[6,8,128]{2,1,0:T(8,128)S(1)}, u32[]{:S(2)}, u32[]{:S(2)}) collective-permute-start(f32[6,8,128]{2,1,0:T(8,128)S(1)} %copy-done.8), channel_id=1, source_target_pairs={{0,256},{256,512},{512,768},{1,257},{257,513},{513,769},{2,258},{2... | collective-permute-start | bytes 73736 | tf_op jit(solution)/shard_map/ppermute | solution.py:523
  13.7 14.5 %collective-permute-start.2 = (f32[6,8,128]{2,1,0:T(8,128)S(1)}, f32[6,8,128]{2,1,0:T(8,128)S(1)}, u32[]{:S(2)}, u32[]{:S(2)}) collective-permute-start(f32[6,8,128]{2,1,0:T(8,128)S(1)} %copy-done.7), channel_id=1, source_target_pairs={{256,0},{512,256},{768,512},{257,1},{513,257},{769,513},{258,2},{5... | collective-permute-start | bytes 73736 | tf_op jit(solution)/shard_map/ppermute | solution.py:528
  15.0 12.4 %collective-permute-start.1 = (f32[24,128]{1,0:T(8,128)S(1)}, f32[24,128]{1,0:T(8,128)S(1)}, u32[]{:S(2)}, u32[]{:S(2)}) collective-permute-start(f32[24,128]{1,0:T(8,128)S(1)} %copy-done.10), channel_id=1, source_target_pairs={{0,32},{32,64},{64,96},{96,128},{128,160},{160,192},{192,224},{1,3... | collective-permute-start | bytes 36872 | tf_op jit(solution)/shard_map/ppermute | solution.py:523
  19.4 8.9 %collective-permute-start.3 = (f32[24,128]{1,0:T(8,128)S(1)}, f32[24,128]{1,0:T(8,128)S(1)}, u32[]{:S(2)}, u32[]{:S(2)}) collective-permute-start(f32[24,128]{1,0:T(8,128)S(1)} %copy-done.9), channel_id=1, source_target_pairs={{32,0},{64,32},{96,64},{128,96},{160,128},{192,160},{224,192},{33,... | collective-permute-start | bytes 36872 | tf_op jit(solution)/shard_map/ppermute | solution.py:528
  29.0 21.8 %copy-start = (f32[3,4,8,128]{3,2,1,0:T(8,128)S(1)}, f32[3,4,8,128]{3,2,1,0:T(8,128)}, u32[]{:S(2)}) copy-start(f32[3,4,8,128]{3,2,1,0:T(8,128)} %param.7) | copy-start | bytes 147460
  29.0 21.8 %copy-start.1 = (f32[3,4,8,128]{3,2,1,0:T(8,128)S(1)}, f32[3,4,8,128]{3,2,1,0:T(8,128)}, u32[]{:S(2)}) copy-start(f32[3,4,8,128]{3,2,1,0:T(8,128)} %param.8) | copy-start | bytes 147460
  29.0 21.8 %copy-start.2 = (f32[3,4,8,128]{3,2,1,0:T(8,128)S(1)}, f32[3,4,8,128]{3,2,1,0:T(8,128)}, u32[]{:S(2)}) copy-start(f32[3,4,8,128]{3,2,1,0:T(8,128)} %param.9) | copy-start | bytes 147460
  29.0 21.8 %copy-start.3 = (f32[3,4,8,128]{3,2,1,0:T(8,128)S(1)}, f32[3,4,8,128]{3,2,1,0:T(8,128)}, u32[]{:S(2)}) copy-start(f32[3,4,8,128]{3,2,1,0:T(8,128)} %param.10) | copy-start | bytes 147460
  29.0 47.6 %all-to-all-start.1 = ((f32[8,24,128]{2,1,0:T(8,128)}), f32[8,24,128]{2,1,0:T(8,128)S(1)}, u32[]{:S(2)}, u32[]{:S(2)}) async-start(f32[8,24,128]{2,1,0:T(8,128)} %get-tuple-element.51), calls=%async_computation.1 | async-start | bytes 196608 | tf_op jit(solution)/shard_map/all_to_all | solution.py:518
  50.8 25.8 %copy-start.5 = (s32[1,1,512]{2,1,0:T(1,128)S(1)}, s32[1,1,512]{2,1,0:T(1,128)}, u32[]{:S(2)}) copy-start(s32[1,1,512]{2,1,0:T(1,128)} %well.5) | copy-start | bytes 6148
  50.8 25.8 %copy-start.6 = (f32[1,1,512]{2,1,0:T(1,128)S(1)}, f32[1,1,512]{2,1,0:T(1,128)}, u32[]{:S(2)}) copy-start(f32[1,1,512]{2,1,0:T(1,128)} %factor.5) | copy-start | bytes 6148
  50.9 25.7 %copy-start.4 = (s32[1,1,512]{2,1,0:T(1,128)S(1)}, s32[1,1,512]{2,1,0:T(1,128)}, u32[]{:S(2)}) copy-start(s32[1,1,512]{2,1,0:T(1,128)} %cell.5) | copy-start | bytes 6148
  78.5 20.5 %all-to-all-start.2 = ((f32[4,24,128]{2,1,0:T(8,128)}), f32[4,24,128]{2,1,0:T(8,128)S(1)}, u32[]{:S(2)}, u32[]{:S(2)}) async-start(f32[4,24,128]{2,1,0:T(8,128)} %broadcast_in_dim.7), calls=%async_computation.2 | async-start | bytes 98304 | tf_op jit(solution)/shard_map/all_to_all | solution.py:512
  83.5 15.4 %collective-permute-start.4 = (f32[3,8,128]{2,1,0:T(8,128)S(1)}, f32[3,8,128]{2,1,0:T(8,128)S(1)}, u32[]{:S(2)}, u32[]{:S(2)}) collective-permute-start(f32[3,8,128]{2,1,0:T(8,128)S(1)} %get-tuple-element.59), channel_id=1, source_target_pairs={{0,256},{256,512},{512,768},{1,257},{257,513},{513,769},{2,258},{2... | collective-permute-start | bytes 36872 | tf_op jit(solution)/shard_map/ppermute | solution.py:523
  87.8 11.2 %collective-permute-start.6 = (f32[3,8,128]{2,1,0:T(8,128)S(1)}, f32[3,8,128]{2,1,0:T(8,128)S(1)}, u32[]{:S(2)}, u32[]{:S(2)}) collective-permute-start(f32[3,8,128]{2,1,0:T(8,128)S(1)} %get-tuple-element.61), channel_id=1, source_target_pairs={{256,0},{512,256},{768,512},{257,1},{513,257},{769,513},{258,2},{5... | collective-permute-start | bytes 36872 | tf_op jit(solution)/shard_map/ppermute | solution.py:528
  89.1 6.8 %collective-permute-start.5 = (f32[12,128]{1,0:T(8,128)S(1)}, f32[12,128]{1,0:T(8,128)S(1)}, u32[]{:S(2)}, u32[]{:S(2)}) collective-permute-start(f32[12,128]{1,0:T(8,128)S(1)} %get-tuple-element.60), channel_id=1, source_target_pairs={{0,32},{32,64},{64,96},{96,128},{128,160},{160,192},{192,224},{1,3... | collective-permute-start | bytes 18440 | tf_op jit(solution)/shard_map/ppermute | solution.py:523
  94.0 5.0 %collective-permute-start.7 = (f32[12,128]{1,0:T(8,128)S(1)}, f32[12,128]{1,0:T(8,128)S(1)}, u32[]{:S(2)}, u32[]{:S(2)}) collective-permute-start(f32[12,128]{1,0:T(8,128)S(1)} %get-tuple-element.62), channel_id=1, source_target_pairs={{32,0},{64,32},{96,64},{128,96},{160,128},{192,160},{224,192},{33,... | collective-permute-start | bytes 18440 | tf_op jit(solution)/shard_map/ppermute | solution.py:528
  99.6 28.5 %all-to-all-start.3 = ((f32[8,24,128]{2,1,0:T(8,128)}), f32[8,24,128]{2,1,0:T(8,128)S(1)}, u32[]{:S(2)}, u32[]{:S(2)}) async-start(f32[8,24,128]{2,1,0:T(8,128)} %get-tuple-element.64), calls=%async_computation.3 | async-start | bytes 196608 | tf_op jit(solution)/shard_map/all_to_all | solution.py:518
  129.2 8.5 %collective-permute-start.8 = (f32[3,8,128]{2,1,0:T(8,128)S(1)}, f32[3,8,128]{2,1,0:T(8,128)S(1)}, u32[]{:S(2)}, u32[]{:S(2)}) collective-permute-start(f32[3,8,128]{2,1,0:T(8,128)S(1)} %get-tuple-element.77), channel_id=1, source_target_pairs={{0,256},{256,512},{512,768},{1,257},{257,513},{513,769},{2,258},{2... | collective-permute-start | bytes 36872 | tf_op jit(solution)/shard_map/ppermute | solution.py:523
  133.5 4.2 %collective-permute-start.9 = (f32[12,128]{1,0:T(8,128)S(1)}, f32[12,128]{1,0:T(8,128)S(1)}, u32[]{:S(2)}, u32[]{:S(2)}) collective-permute-start(f32[12,128]{1,0:T(8,128)S(1)} %get-tuple-element.78), channel_id=1, source_target_pairs={{0,32},{32,64},{64,96},{96,128},{128,160},{160,192},{192,224},{1,3... | collective-permute-start | bytes 18440 | tf_op jit(solution)/shard_map/ppermute | solution.py:523
  138.4 14.2 %all-to-all-start.4 = ((f32[4,24,128]{2,1,0:T(8,128)}), f32[4,24,128]{2,1,0:T(8,128)S(1)}, u32[]{:S(2)}, u32[]{:S(2)}) async-start(f32[4,24,128]{2,1,0:T(8,128)} %broadcast_in_dim.8), calls=%async_computation.4 | async-start | bytes 98304 | tf_op jit(solution)/shard_map/all_to_all | solution.py:512
  145.5 7.1 %collective-permute-start.10 = (f32[3,8,128]{2,1,0:T(8,128)S(1)}, f32[3,8,128]{2,1,0:T(8,128)S(1)}, u32[]{:S(2)}, u32[]{:S(2)}) collective-permute-start(f32[3,8,128]{2,1,0:T(8,128)S(1)} %get-tuple-element.79), channel_id=1, source_target_pairs={{256,0},{512,256},{768,512},{257,1},{513,257},{769,513},{258,2},{5... | collective-permute-start | bytes 36872 | tf_op jit(solution)/shard_map/ppermute | solution.py:528
  146.8 5.8 %collective-permute-start.11 = (f32[12,128]{1,0:T(8,128)S(1)}, f32[12,128]{1,0:T(8,128)S(1)}, u32[]{:S(2)}, u32[]{:S(2)}) collective-permute-start(f32[12,128]{1,0:T(8,128)S(1)} %get-tuple-element.80), channel_id=1, source_target_pairs={{32,0},{64,32},{96,64},{128,96},{160,128},{192,160},{224,192},{33,... | collective-permute-start | bytes 18440 | tf_op jit(solution)/shard_map/ppermute | solution.py:528
  182.4 14.5 %all-to-all-start.6 = ((f32[32,8,128]{2,1,0:T(8,128)}), f32[32,8,128]{2,1,0:T(8,128)S(1)}, u32[]{:S(2)}, u32[]{:S(2)}) async-start(f32[32,8,128]{2,1,0:T(8,128)} %shard_map.95), calls=%async_computation.6 | async-start | bytes 262144 | tf_op jit(solution)/shard_map/all_to_all | solution.py:596

commit v4 on v2

--- a/solution.py
+++ b/solution.py
@@ -204,9 +204,11 @@
     row, lane = cell_masks(cell[0])
     values = gather_cells([right[u] for u in range(3)], row, lane)
     weight = factor[0]
-    put_well_rows(table, scatter_wells([weight * v for v in values] + [weight], well_mask(well[0])))
-    ends = [(right, 0), (mobility, 32)], [(right, 16), (mobility, 48)]
-    table[4 * WELL_ROWS : 24] = fold(end_tile(*ends))
+    sums = scatter_wells([weight * v for v in values] + [weight], well_mask(well[0]))
+    ends = fold(end_tile([(right, 0), (mobility, 32)], [(right, 16), (mobility, 48)]))
+    for k in range(NEAR):
+        put_well_rows(table.at[k], sums)
+        table[k, 4 * WELL_ROWS : 24] = ends
     put_faces(faces, [right, mobility])
 
 
@@ -400,7 +402,7 @@
     table[15:16] = line
 
 
-def scalar_kernel(slots, inverse, moments):
+def scalar_kernel(slots, inverse, sent):
     total = jnp.sum(slots[...], axis=0)
     pull = jnp.zeros((WELL_ROWS, 128), F32)
     scale = inverse[0:WELL_ROWS]
@@ -409,31 +411,10 @@
         pull = pull + part * part * scale
     tiles = [slots[k, 16:24] for k in range(slots.shape[0])]
     between = tree([face_energy(a, b) for a, b in zip(tiles, tiles[1:])])
-    line = total[15:16]
-    lane = lanes()[0:1]
-    for k in range(6):
-        value = jnp.sum(jnp.where(lane == k, line, 0.0), axis=1, keepdims=True)
-        if k == 5:
-            value = value + (whole_sum(between) - whole_sum(pull))
-        moments[k : k + 1] = jnp.broadcast_to(value, (1, 128))
-    moments[6:8] = jnp.zeros((2, 128), F32)
-
-
-def last_vector_kernel(
-    slots, near, flow, before, extra, inverse, cond, cell, well, factor, field
-):
-    total = jnp.sum(slots[...], axis=0)
-    low, high = halo_tiles(near, slots, lambda a: a[16:24])
-    whole = flow_along(before, flow, cond, low, high)
-    scale_row = get_well_rows(inverse[...], 1)[0]
-    rows = get_well_rows(total, 3)
-    row, lane = cell_masks(cell[0])
-    fresh = advance(
-        [r * scale_row for r in rows], whole, before, extra[...], factor[0], row, lane,
-        well_mask(well[0]),
-    )
-    for u in range(3):
-        field[u] = fresh[u]
+    last = whole_sum(between) - whole_sum(pull)
+    line = total[15:16] + jnp.where(lanes()[0:1] == 5, last, 0.0)
+    for k in range(sent.shape[0]):
+        sent[k] = line
 
 
 def plus(a, b, scale):
@@ -462,10 +443,23 @@
     return tree([by_degree[k] * moment[k] for k in sorted(by_degree)])
 
 
-def combine_kernel(slots, w0, w1, w2, w3, solved, rest):
-    terms = [slots[k] for k in range(slots.shape[0])]
-    total = tree(terms)
-    moment = [total[k : k + 1] for k in range(6)]
+def combine_kernel(
+    lines, slots, near, flow, extra, inverse, cond, cell, well, factor, w0, w1, w2, solved, rest
+):
+    total = jnp.sum(slots[...], axis=0)
+    low, high = halo_tiles(near, slots, lambda a: a[16:24])
+    whole = flow_along(w2, flow, cond, low, high)
+    scale_row = get_well_rows(inverse[...], 1)[0]
+    means = [r * scale_row for r in get_well_rows(total, 3)]
+    row, lane = cell_masks(cell[0])
+    w3 = advance(means, whole, w2, extra[...], factor[0], row, lane, well_mask(well[0]))
+
+    line = tree([lines[k] for k in range(lines.shape[0])])
+    first = lanes()[0:1]
+    moment = [
+        jnp.broadcast_to(jnp.sum(jnp.where(first == k, line, 0.0), axis=1, keepdims=True), (1, 128))
+        for k in range(6)
+    ]
     one = jnp.ones((1, 128), F32)
     residual, direction, solution_field = [one], [one], []
     norm = moment[0]
@@ -483,7 +477,7 @@
     for u in range(3):
         for x in range(4):
             rows = slice(8 * x, 8 * x + 8)
-            basis = [w0[u, rows], w1[u, rows], w2[u, rows], w3[u, rows]]
+            basis = [w0[u, rows], w1[u, rows], w2[u, rows], w3[u][rows]]
             solved[u, rows] = tree([c * w for c, w in zip(solution_field, basis)])
             rest[u, rows] = tree([c * w for c, w in zip(residual, basis)])
 
@@ -502,11 +496,14 @@
 NEAR = 4
 
 
-def near_slots(table):
+def near_slots(sent):
     count = lax.axis_size("gz")
     groups = [[NEAR * g + k for k in range(NEAR)] for g in range(count // NEAR)]
-    sent = jnp.broadcast_to(table[None], (NEAR,) + table.shape)
     return lax.all_to_all(sent, "gz", 0, 0, axis_index_groups=groups)
+
+
+def copies(table):
+    return jnp.broadcast_to(table[None], (NEAR,) + table.shape)
 
 
 def far_slots(sent):
@@ -550,7 +547,7 @@
     sent_shapes = [(lax.axis_size("gz") // NEAR, 24, 128), (2, 8, 128)]
 
     table, *faces = call(
-        first_kernel, [(24, 128)] + face_shapes(2), right, mob, *perfs,
+        first_kernel, [(NEAR, 24, 128)] + face_shapes(2), right, mob, *perfs,
         space=pltpu.HBM, mib=60,
         scratch=[pltpu.VMEM(block, F32)] * 2
         + [pltpu.VMEM(a.shape, a.dtype) for a in perfs]
@@ -569,7 +566,7 @@
         slots, near, flow, right, mob, *perfs,
     )
 
-    sent, near = call(near_kernel, sent_shapes, near_slots(table))
+    sent, near = call(near_kernel, sent_shapes, near_slots(copies(table)))
     sent, *faces = after(sent, *faces)
     slots = far_slots(sent)
     flow = call(
@@ -585,20 +582,20 @@
         moment_kernel, [(24, 128)],
         table, right, w1, w2, extra, diag, off, cond, cond_along, *low,
     )[0]
-    sent, near = call(last_near_kernel, sent_shapes, near_slots(table))
+    sent, near = call(last_near_kernel, sent_shapes, near_slots(copies(table)))
     sent, *faces = after(sent, *faces)
-    slots, *high = after(far_slots(sent), *high_halos(faces))
+    slots = far_slots(sent)
+    high = high_halos(faces)
     flow = call(flow_kernel, [block], w2, diag, off, cond, *low, *high)[0]
-
-    moments = call(scalar_kernel, [(8, 128)], slots, inverse)[0]
+    slots, flow = after(slots, flow)
+
     count = lax.axis_size("gx") * lax.axis_size("gy")
-    sent = jnp.broadcast_to(moments[None], (count, 8, 128))
-    moment_slots = lax.all_to_all(sent, ("gx", "gy"), 0, 0)
-    w3 = call(
-        last_vector_kernel, [block],
-        slots, near, flow, w2, extra, inverse, cond_along, *perfs,
-    )[0]
-    solved, rest = call(combine_kernel, [block, block], moment_slots, right, w1, w2, w3)
+    sent = call(scalar_kernel, [(count, 1, 128)], slots, inverse)[0]
+    lines = lax.all_to_all(sent, ("gx", "gy"), 0, 0)
+    solved, rest = call(
+        combine_kernel, [block, block],
+        lines, slots, near, flow, extra, inverse, cond_along, *perfs, right, w1, w2,
+    )
     return solved.reshape(right_side.shape), rest.reshape(right_side.shape)
 
 

time: 183 us -> 181 us (0.989)
  blocking collectives: 25.3 us -> 42.8 us
  starting transfers between devices: 92.6 us -> 82.2 us
  waiting for transfers between devices: 53.2 us -> 45.7 us
    all_to_all x0 -> x1, blocking collectives: none -> 17.4 us  [body(): lines = lax.all_to_all(sent, ('gx', 'gy'), 0, 0)]
    all_to_all x1 -> x0, starting transfers between devices: 10.6 us -> none  [body(): moment_slots = lax.all_to_all(sent, ('gx', 'gy'), 0, 0)]
    all_to_all x1 -> x0, waiting for transfers between devices: 7.18 us -> none  [body(): moment_slots = lax.all_to_all(sent, ('gx', 'gy'), 0, 0)]
    pallas_call x13 -> x12, Pallas kernels: 8.17 us -> 8.13 us  [call(): pl.pallas_call(kernel, out_shape=[jax.ShapeDtypeStruct(shape, F32) for sh...]
  transfers between devices with their start and end apart: 16 -> 15, of which waited for: 8 -> 7; matrix products, arithmetic and copies ran while one was open for 0% -> 0% of each run, Pallas kernels for 0% -> 0%
where the time goes in v4:
time: 181 us; the launch traced here: 180 us
  starting transfers between devices  82.2 us (45%)
  waiting for transfers between devices  45.7 us (25%)
  blocking collectives  42.8 us (24%)
  Pallas kernels  8.13 us (4%)
    all_to_all x3, starting transfers between devices, far_slots(): return lax.all_to_all(sent, 'gz', 0, 0, axis_index_groups=groups)  46 us
    all_to_all x3, waiting for transfers between devices, far_slots(): return lax.all_to_all(sent, 'gz', 0, 0, axis_index_groups=groups)  34.5 us
    all_to_all x3, blocking collectives, near_slots(): return lax.all_to_all(sent, 'gz', 0, 0, axis_index_groups=groups)  25.5 us
    ppermute x6, starting transfers between devices, forward(): return lax.ppermute(piece, axis, [(i, i + 1) for i in range(count - 1)])  25 us
    all_to_all x1, blocking collectives, body(): lines = lax.all_to_all(sent, ('gx', 'gy'), 0, 0)  17.4 us
    ppermute x6, starting transfers between devices, backward(): return lax.ppermute(piece, axis, [(i + 1, i) for i in range(count - 1)])  11.2 us
    ppermute x6, waiting for transfers between devices, backward(): return lax.ppermute(piece, axis, [(i + 1, i) for i in range(count - 1)])  10.4 us
    pallas_call x12, Pallas kernels, call(): pl.pallas_call(kernel, out_shape=[jax.ShapeDtypeStruct(shape, F32) for sh...  8.13 us
  transfers between devices with their start and end apart: 15, of which 7 were waited for; matrix products, arithmetic and copies ran while one was open for 0% of the time, Pallas kernels for 0%

profile of v4, /device:TPU:1, one launch (start us, length us, event | category | flops | bytes accessed | tf_op | source)
XLA Modules:
  0.0 179.8 jit_solution(6354507843569177599)
XLA Ops:
  0.6 2.0 %shard_map.86 = (f32[4,24,128]{2,1,0:T(8,128)}, f32[6,8,128]{2,1,0:T(8,128)}, f32[6,8,128]{2,1,0:T(8,128)}, f32[24,128]{1,0:T(8,128)}, f32[24,128]{1,0:T(8,128)}) custom-call(f32[3,32,128]{2,1,0:T(8,128)} %bitcast.6, f32[3,32,128]{2,1,0:T(8,128)} %bitcast.19, s32[1,1,512]{2,1,0:T(1,128)} %cell.5, s32[1,1,512]{2,1,0:T(1,128)} %well.5, f32[1,1,512]{2,1,0:T(1,128)} %factor.5), custom_call_target="tpu_custom_call" | custom-call | tf_op jit(solution)/shard_map/pallas_call | solution.py:486
  2.7 11.0 %all_to_all.35.slots = f32[4,24,128]{2,1,0:T(8,128)S(1)} all-to-all(f32[4,24,128]{2,1,0:T(8,128)} %get-tuple-element.47), channel_id=1, replica_groups={{0,1,2,3},{4,5,6,7},{8,9,10,11},{12,13,14,15},{16,17,18,19},{20,21,22,2..., dimensions={0} | all-to-all | bytes 98304 | tf_op jit(solution)/shard_map/all_to_all | solution.py:502
  13.7 0.8 shard_map.87
  14.5 25.8 %all-to-all-start.1 = ((f32[8,24,128]{2,1,0:T(8,128)}), f32[8,24,128]{2,1,0:T(8,128)S(1)}, u32[]{:S(2)}, u32[]{:S(2)}) async-start(f32[8,24,128]{2,1,0:T(8,128)} %get-tuple-element.53), calls=%async_computation.1 | async-start | bytes 196608 | tf_op jit(solution)/shard_map/all_to_all | solution.py:512
  40.3 3.1 %collective-permute-start = (f32[6,8,128]{2,1,0:T(8,128)S(1)}, f32[6,8,128]{2,1,0:T(8,128)S(1)}, u32[]{:S(2)}, u32[]{:S(2)}) collective-permute-start(f32[6,8,128]{2,1,0:T(8,128)S(1)} %copy-done.8), channel_id=1, source_target_pairs={{0,256},{256,512},{512,768},{1,257},{257,513},{513,769},{2,258},{2... | collective-permute-start | bytes 73736 | tf_op jit(solution)/shard_map/ppermute | solution.py:517
  43.5 1.3 collective-permute-start.2
  44.8 5.5 %collective-permute-start.1 = (f32[24,128]{1,0:T(8,128)S(1)}, f32[24,128]{1,0:T(8,128)S(1)}, u32[]{:S(2)}, u32[]{:S(2)}) collective-permute-start(f32[24,128]{1,0:T(8,128)S(1)} %copy-done.10), channel_id=1, source_target_pairs={{0,32},{32,64},{64,96},{96,128},{128,160},{160,192},{192,224},{1,3... | collective-permute-start | bytes 36872 | tf_op jit(solution)/shard_map/ppermute | solution.py:517
  50.3 1.9 %collective-permute-start.3 = (f32[24,128]{1,0:T(8,128)S(1)}, f32[24,128]{1,0:T(8,128)S(1)}, u32[]{:S(2)}, u32[]{:S(2)}) collective-permute-start(f32[24,128]{1,0:T(8,128)S(1)} %copy-done.9), channel_id=1, source_target_pairs={{32,0},{64,32},{96,64},{128,96},{160,128},{192,160},{224,192},{33,... | collective-permute-start | bytes 36872 | tf_op jit(solution)/shard_map/ppermute | solution.py:522
  52.2 3.4 %collective-permute-done.3.yh = f32[24,128]{1,0:T(8,128)S(1)} collective-permute-done((f32[24,128]{1,0:T(8,128)S(1)}, f32[24,128]{1,0:T(8,128)S(1)}, u32[]{:S(2)}, u32[]{:S(2)}) %collective-permute-start.3) | collective-permute-done | bytes 12320 | tf_op jit(solution)/shard_map/ppermute | solution.py:522
  55.7 8.0 %all-to-all-done.1.slots = f32[8,24,128]{2,1,0:T(8,128)S(1)} async-done(((f32[8,24,128]{2,1,0:T(8,128)}), f32[8,24,128]{2,1,0:T(8,128)S(1)}, u32[]{:S(2)}, u32[]{:S(2)}) %all-to-all-start.1) | async-done | bytes 98336 | tf_op jit(solution)/shard_map/all_to_all | solution.py:512
  63.7 1.2 shard_map.89
  65.0 7.0 %all_to_all.36.slots = f32[4,24,128]{2,1,0:T(8,128)S(1)} all-to-all(f32[4,24,128]{2,1,0:T(8,128)S(1)} %broadcast_in_dim.4), channel_id=1, replica_groups={{0,1,2,3},{4,5,6,7},{8,9,10,11},{12,13,14,15},{16,17,18,19},{20,21,22,2..., dimensions={0} | all-to-all | bytes 98304 | tf_op jit(solution)/shard_map/all_to_all | solution.py:502
  72.6 13.6 %all-to-all-start.3 = ((f32[8,24,128]{2,1,0:T(8,128)}), f32[8,24,128]{2,1,0:T(8,128)S(1)}, u32[]{:S(2)}, u32[]{:S(2)}) async-start(f32[8,24,128]{2,1,0:T(8,128)} %get-tuple-element.66), calls=%async_computation.3 | async-start | bytes 196608 | tf_op jit(solution)/shard_map/all_to_all | solution.py:512
  86.2 4.3 %collective-permute-start.4 = (f32[3,8,128]{2,1,0:T(8,128)S(1)}, f32[3,8,128]{2,1,0:T(8,128)S(1)}, u32[]{:S(2)}, u32[]{:S(2)}) collective-permute-start(f32[3,8,128]{2,1,0:T(8,128)S(1)} %get-tuple-element.70), channel_id=1, source_target_pairs={{0,256},{256,512},{512,768},{1,257},{257,513},{513,769},{2,258},{2... | collective-permute-start | bytes 36872 | tf_op jit(solution)/shard_map/ppermute | solution.py:517
  90.5 1.3 collective-permute-start.6
  91.8 3.7 %collective-permute-start.5 = (f32[12,128]{1,0:T(8,128)S(1)}, f32[12,128]{1,0:T(8,128)S(1)}, u32[]{:S(2)}, u32[]{:S(2)}) collective-permute-start(f32[12,128]{1,0:T(8,128)S(1)} %get-tuple-element.71), channel_id=1, source_target_pairs={{0,32},{32,64},{64,96},{96,128},{128,160},{160,192},{192,224},{1,3... | collective-permute-start | bytes 18440 | tf_op jit(solution)/shard_map/ppermute | solution.py:517
  95.5 1.9 %collective-permute-start.7 = (f32[12,128]{1,0:T(8,128)S(1)}, f32[12,128]{1,0:T(8,128)S(1)}, u32[]{:S(2)}, u32[]{:S(2)}) collective-permute-start(f32[12,128]{1,0:T(8,128)S(1)} %get-tuple-element.73), channel_id=1, source_target_pairs={{32,0},{64,32},{96,64},{128,96},{160,128},{192,160},{224,192},{33,... | collective-permute-start | bytes 18440 | tf_op jit(solution)/shard_map/ppermute | solution.py:522
  97.4 3.3 %collective-permute-done.7.yh = f32[12,128]{1,0:T(8,128)S(1)} collective-permute-done((f32[12,128]{1,0:T(8,128)S(1)}, f32[12,128]{1,0:T(8,128)S(1)}, u32[]{:S(2)}, u32[]{:S(2)}) %collective-permute-start.7) | collective-permute-done | bytes 6176 | tf_op jit(solution)/shard_map/ppermute | solution.py:522
  100.8 12.1 %all-to-all-done.3.slots = f32[8,24,128]{2,1,0:T(8,128)S(1)} async-done(((f32[8,24,128]{2,1,0:T(8,128)}), f32[8,24,128]{2,1,0:T(8,128)S(1)}, u32[]{:S(2)}, u32[]{:S(2)}) %all-to-all-start.3) | async-done | bytes 98336 | tf_op jit(solution)/shard_map/all_to_all | solution.py:512
  112.9 1.1 shard_map.92
  114.0 4.3 %collective-permute-start.8 = (f32[3,8,128]{2,1,0:T(8,128)S(1)}, f32[3,8,128]{2,1,0:T(8,128)S(1)}, u32[]{:S(2)}, u32[]{:S(2)}) collective-permute-start(f32[3,8,128]{2,1,0:T(8,128)S(1)} %get-tuple-element.79), channel_id=1, source_target_pairs={{0,256},{256,512},{512,768},{1,257},{257,513},{513,769},{2,258},{2... | collective-permute-start | bytes 36872 | tf_op jit(solution)/shard_map/ppermute | solution.py:517
  118.3 4.2 %collective-permute-start.9 = (f32[12,128]{1,0:T(8,128)S(1)}, f32[12,128]{1,0:T(8,128)S(1)}, u32[]{:S(2)}, u32[]{:S(2)}) collective-permute-start(f32[12,128]{1,0:T(8,128)S(1)} %get-tuple-element.80), channel_id=1, source_target_pairs={{0,32},{32,64},{64,96},{96,128},{128,160},{160,192},{192,224},{1,3... | collective-permute-start | bytes 18440 | tf_op jit(solution)/shard_map/ppermute | solution.py:517
  122.5 0.8 collective-permute-done.9.yl
  123.4 7.5 %all_to_all.37.slots = f32[4,24,128]{2,1,0:T(8,128)S(1)} all-to-all(f32[4,24,128]{2,1,0:T(8,128)S(1)} %broadcast_in_dim.5), channel_id=1, replica_groups={{0,1,2,3},{4,5,6,7},{8,9,10,11},{12,13,14,15},{16,17,18,19},{20,21,22,2..., dimensions={0} | all-to-all | bytes 98304 | tf_op jit(solution)/shard_map/all_to_all | solution.py:502
  130.9 0.8 shard_map.94
  131.7 6.5 %all-to-all-start.5 = ((f32[8,24,128]{2,1,0:T(8,128)}), f32[8,24,128]{2,1,0:T(8,128)S(1)}, u32[]{:S(2)}, u32[]{:S(2)}) async-start(f32[8,24,128]{2,1,0:T(8,128)} %get-tuple-element.84), calls=%async_computation.5 | async-start | bytes 196608 | tf_op jit(solution)/shard_map/all_to_all | solution.py:512
  138.2 1.3 collective-permute-start.10
  139.5 3.5 %collective-permute-start.11 = (f32[12,128]{1,0:T(8,128)S(1)}, f32[12,128]{1,0:T(8,128)S(1)}, u32[]{:S(2)}, u32[]{:S(2)}) collective-permute-start(f32[12,128]{1,0:T(8,128)S(1)} %get-tuple-element.86), channel_id=1, source_target_pairs={{32,0},{64,32},{96,64},{128,96},{160,128},{192,160},{224,192},{33,... | collective-permute-start | bytes 18440 | tf_op jit(solution)/shard_map/ppermute | solution.py:522
  143.0 3.7 %collective-permute-done.11.yh = f32[12,128]{1,0:T(8,128)S(1)} collective-permute-done((f32[12,128]{1,0:T(8,128)S(1)}, f32[12,128]{1,0:T(8,128)S(1)}, u32[]{:S(2)}, u32[]{:S(2)}) %collective-permute-start.11) | collective-permute-done | bytes 6176 | tf_op jit(solution)/shard_map/ppermute | solution.py:522
  146.7 14.4 %all-to-all-done.5.slots = f32[8,24,128]{2,1,0:T(8,128)S(1)} async-done(((f32[8,24,128]{2,1,0:T(8,128)}), f32[8,24,128]{2,1,0:T(8,128)S(1)}, u32[]{:S(2)}, u32[]{:S(2)}) %all-to-all-start.5) | async-done | bytes 98336 | tf_op jit(solution)/shard_map/all_to_all | solution.py:512
  161.4 17.4 %all_to_all.38.lines = f32[32,1,128]{2,1,0:T(1,128)S(1)} all-to-all(f32[32,1,128]{2,1,0:T(1,128)S(1)} %shard_map.96), channel_id=1, replica_groups=mesh['gx'=4,'gy'=8,'gz'=32] {'gx','gy'}, dimensions={0} | all-to-all | bytes 32768 | tf_op jit(solution)/shard_map/all_to_all | solution.py:594
  178.7 1.1 shard_map.97
  (38 shorter events, 1.3 us)
Async XLA Ops:
  2.7 42.1 %copy-start.10 = (f32[24,128]{1,0:T(8,128)S(1)}, f32[24,128]{1,0:T(8,128)}, u32[]{:S(2)}) copy-start(f32[24,128]{1,0:T(8,128)} %get-tuple-element.56) | copy-start | bytes 36868
  13.7 26.6 %copy-start.8 = (f32[6,8,128]{2,1,0:T(8,128)S(1)}, f32[6,8,128]{2,1,0:T(8,128)}, u32[]{:S(2)}) copy-start(f32[6,8,128]{2,1,0:T(8,128)} %get-tuple-element.55) | copy-start | bytes 73732
  13.7 29.8 %copy-start.7 = (f32[6,8,128]{2,1,0:T(8,128)S(1)}, f32[6,8,128]{2,1,0:T(8,128)}, u32[]{:S(2)}) copy-start(f32[6,8,128]{2,1,0:T(8,128)} %get-tuple-element.57) | copy-start | bytes 73732
  13.7 36.6 %copy-start.9 = (f32[24,128]{1,0:T(8,128)S(1)}, f32[24,128]{1,0:T(8,128)}, u32[]{:S(2)}) copy-start(f32[24,128]{1,0:T(8,128)} %get-tuple-element.58) | copy-start | bytes 36868
  14.5 41.1 %copy-start = (f32[3,4,8,128]{3,2,1,0:T(8,128)S(1)}, f32[3,4,8,128]{3,2,1,0:T(8,128)}, u32[]{:S(2)}) copy-start(f32[3,4,8,128]{3,2,1,0:T(8,128)} %param.7) | copy-start | bytes 147460
  14.5 41.1 %copy-start.1 = (f32[3,4,8,128]{3,2,1,0:T(8,128)S(1)}, f32[3,4,8,128]{3,2,1,0:T(8,128)}, u32[]{:S(2)}) copy-start(f32[3,4,8,128]{3,2,1,0:T(8,128)} %param.8) | copy-start | bytes 147460
  14.5 41.1 %copy-start.2 = (f32[3,4,8,128]{3,2,1,0:T(8,128)S(1)}, f32[3,4,8,128]{3,2,1,0:T(8,128)}, u32[]{:S(2)}) copy-start(f32[3,4,8,128]{3,2,1,0:T(8,128)} %param.9) | copy-start | bytes 147460
  14.5 41.1 %copy-start.3 = (f32[3,4,8,128]{3,2,1,0:T(8,128)S(1)}, f32[3,4,8,128]{3,2,1,0:T(8,128)}, u32[]{:S(2)}) copy-start(f32[3,4,8,128]{3,2,1,0:T(8,128)} %param.10) | copy-start | bytes 147460
  14.5 49.2 %all-to-all-start.1 = ((f32[8,24,128]{2,1,0:T(8,128)}), f32[8,24,128]{2,1,0:T(8,128)S(1)}, u32[]{:S(2)}, u32[]{:S(2)}) async-start(f32[8,24,128]{2,1,0:T(8,128)} %get-tuple-element.53), calls=%async_computation.1 | async-start | bytes 196608 | tf_op jit(solution)/shard_map/all_to_all | solution.py:512
  40.3 15.2 %collective-permute-start = (f32[6,8,128]{2,1,0:T(8,128)S(1)}, f32[6,8,128]{2,1,0:T(8,128)S(1)}, u32[]{:S(2)}, u32[]{:S(2)}) collective-permute-start(f32[6,8,128]{2,1,0:T(8,128)S(1)} %copy-done.8), channel_id=1, source_target_pairs={{0,256},{256,512},{512,768},{1,257},{257,513},{513,769},{2,258},{2... | collective-permute-start | bytes 73736 | tf_op jit(solution)/shard_map/ppermute | solution.py:517
  43.5 12.1 %collective-permute-start.2 = (f32[6,8,128]{2,1,0:T(8,128)S(1)}, f32[6,8,128]{2,1,0:T(8,128)S(1)}, u32[]{:S(2)}, u32[]{:S(2)}) collective-permute-start(f32[6,8,128]{2,1,0:T(8,128)S(1)} %copy-done.7), channel_id=1, source_target_pairs={{256,0},{512,256},{768,512},{257,1},{513,257},{769,513},{258,2},{5... | collective-permute-start | bytes 73736 | tf_op jit(solution)/shard_map/ppermute | solution.py:522
  44.8 7.4 %collective-permute-start.1 = (f32[24,128]{1,0:T(8,128)S(1)}, f32[24,128]{1,0:T(8,128)S(1)}, u32[]{:S(2)}, u32[]{:S(2)}) collective-permute-start(f32[24,128]{1,0:T(8,128)S(1)} %copy-done.10), channel_id=1, source_target_pairs={{0,32},{32,64},{64,96},{96,128},{128,160},{160,192},{192,224},{1,3... | collective-permute-start | bytes 36872 | tf_op jit(solution)/shard_map/ppermute | solution.py:517
  50.3 5.3 %collective-permute-start.3 = (f32[24,128]{1,0:T(8,128)S(1)}, f32[24,128]{1,0:T(8,128)S(1)}, u32[]{:S(2)}, u32[]{:S(2)}) collective-permute-start(f32[24,128]{1,0:T(8,128)S(1)} %copy-done.9), channel_id=1, source_target_pairs={{32,0},{64,32},{96,64},{128,96},{160,128},{192,160},{224,192},{33,... | collective-permute-start | bytes 36872 | tf_op jit(solution)/shard_map/ppermute | solution.py:522
  55.6 8.1 %copy-start.5 = (s32[1,1,512]{2,1,0:T(1,128)S(1)}, s32[1,1,512]{2,1,0:T(1,128)}, u32[]{:S(2)}) copy-start(s32[1,1,512]{2,1,0:T(1,128)} %well.5) | copy-start | bytes 6148
  55.6 8.1 %copy-start.6 = (f32[1,1,512]{2,1,0:T(1,128)S(1)}, f32[1,1,512]{2,1,0:T(1,128)}, u32[]{:S(2)}) copy-start(f32[1,1,512]{2,1,0:T(1,128)} %factor.5) | copy-start | bytes 6148
  55.7 8.0 %copy-start.4 = (s32[1,1,512]{2,1,0:T(1,128)S(1)}, s32[1,1,512]{2,1,0:T(1,128)}, u32[]{:S(2)}) copy-start(s32[1,1,512]{2,1,0:T(1,128)} %cell.5) | copy-start | bytes 6148
  72.6 40.3 %all-to-all-start.3 = ((f32[8,24,128]{2,1,0:T(8,128)}), f32[8,24,128]{2,1,0:T(8,128)S(1)}, u32[]{:S(2)}, u32[]{:S(2)}) async-start(f32[8,24,128]{2,1,0:T(8,128)} %get-tuple-element.66), calls=%async_computation.3 | async-start | bytes 196608 | tf_op jit(solution)/shard_map/all_to_all | solution.py:512
  86.2 14.5 %collective-permute-start.4 = (f32[3,8,128]{2,1,0:T(8,128)S(1)}, f32[3,8,128]{2,1,0:T(8,128)S(1)}, u32[]{:S(2)}, u32[]{:S(2)}) collective-permute-start(f32[3,8,128]{2,1,0:T(8,128)S(1)} %get-tuple-element.70), channel_id=1, source_target_pairs={{0,256},{256,512},{512,768},{1,257},{257,513},{513,769},{2,258},{2... | collective-permute-start | bytes 36872 | tf_op jit(solution)/shard_map/ppermute | solution.py:517
  90.5 10.3 %collective-permute-start.6 = (f32[3,8,128]{2,1,0:T(8,128)S(1)}, f32[3,8,128]{2,1,0:T(8,128)S(1)}, u32[]{:S(2)}, u32[]{:S(2)}) collective-permute-start(f32[3,8,128]{2,1,0:T(8,128)S(1)} %get-tuple-element.72), channel_id=1, source_target_pairs={{256,0},{512,256},{768,512},{257,1},{513,257},{769,513},{258,2},{5... | collective-permute-start | bytes 36872 | tf_op jit(solution)/shard_map/ppermute | solution.py:522
  91.8 5.6 %collective-permute-start.5 = (f32[12,128]{1,0:T(8,128)S(1)}, f32[12,128]{1,0:T(8,128)S(1)}, u32[]{:S(2)}, u32[]{:S(2)}) collective-permute-start(f32[12,128]{1,0:T(8,128)S(1)} %get-tuple-element.71), channel_id=1, source_target_pairs={{0,32},{32,64},{64,96},{96,128},{128,160},{160,192},{192,224},{1,3... | collective-permute-start | bytes 18440 | tf_op jit(solution)/shard_map/ppermute | solution.py:517
  95.5 5.3 %collective-permute-start.7 = (f32[12,128]{1,0:T(8,128)S(1)}, f32[12,128]{1,0:T(8,128)S(1)}, u32[]{:S(2)}, u32[]{:S(2)}) collective-permute-start(f32[12,128]{1,0:T(8,128)S(1)} %get-tuple-element.73), channel_id=1, source_target_pairs={{32,0},{64,32},{96,64},{128,96},{160,128},{192,160},{224,192},{33,... | collective-permute-start | bytes 18440 | tf_op jit(solution)/shard_map/ppermute | solution.py:522
  114.0 9.3 %collective-permute-start.8 = (f32[3,8,128]{2,1,0:T(8,128)S(1)}, f32[3,8,128]{2,1,0:T(8,128)S(1)}, u32[]{:S(2)}, u32[]{:S(2)}) collective-permute-start(f32[3,8,128]{2,1,0:T(8,128)S(1)} %get-tuple-element.79), channel_id=1, source_target_pairs={{0,256},{256,512},{512,768},{1,257},{257,513},{513,769},{2,258},{2... | collective-permute-start | bytes 36872 | tf_op jit(solution)/shard_map/ppermute | solution.py:517
  118.3 4.9 %collective-permute-start.9 = (f32[12,128]{1,0:T(8,128)S(1)}, f32[12,128]{1,0:T(8,128)S(1)}, u32[]{:S(2)}, u32[]{:S(2)}) collective-permute-start(f32[12,128]{1,0:T(8,128)S(1)} %get-tuple-element.80), channel_id=1, source_target_pairs={{0,32},{32,64},{64,96},{96,128},{128,160},{160,192},{192,224},{1,3... | collective-permute-start | bytes 18440 | tf_op jit(solution)/shard_map/ppermute | solution.py:517
  131.7 29.5 %all-to-all-start.5 = ((f32[8,24,128]{2,1,0:T(8,128)}), f32[8,24,128]{2,1,0:T(8,128)S(1)}, u32[]{:S(2)}, u32[]{:S(2)}) async-start(f32[8,24,128]{2,1,0:T(8,128)} %get-tuple-element.84), calls=%async_computation.5 | async-start | bytes 196608 | tf_op jit(solution)/shard_map/all_to_all | solution.py:512
  138.2 8.5 %collective-permute-start.10 = (f32[3,8,128]{2,1,0:T(8,128)S(1)}, f32[3,8,128]{2,1,0:T(8,128)S(1)}, u32[]{:S(2)}, u32[]{:S(2)}) collective-permute-start(f32[3,8,128]{2,1,0:T(8,128)S(1)} %get-tuple-element.85), channel_id=1, source_target_pairs={{256,0},{512,256},{768,512},{257,1},{513,257},{769,513},{258,2},{5... | collective-permute-start | bytes 36872 | tf_op jit(solution)/shard_map/ppermute | solution.py:522
  139.5 7.2 %collective-permute-start.11 = (f32[12,128]{1,0:T(8,128)S(1)}, f32[12,128]{1,0:T(8,128)S(1)}, u32[]{:S(2)}, u32[]{:S(2)}) collective-permute-start(f32[12,128]{1,0:T(8,128)S(1)} %get-tuple-element.86), channel_id=1, source_target_pairs={{32,0},{64,32},{96,64},{128,96},{160,128},{192,160},{224,192},{33,... | collective-permute-start | bytes 18440 | tf_op jit(solution)/shard_map/ppermute | solution.py:522

commit v5 on v4

--- a/solution.py
+++ b/solution.py
@@ -157,6 +157,10 @@
     return lax.div(at, NEAR), lax.rem(at, NEAR)
 
 
+def slot_of(group, count):
+    return (group + count - count // 2) % count
+
+
 def near_tiles(tiles):
     _, member = place()
     low, high = tiles[0], tiles[-1]
@@ -169,8 +173,8 @@
 def halo_tiles(near, slots, read):
     group, member = place()
     last = slots.shape[0] - 1
-    below = jnp.where(group == 0, 0.0, read(slots[jnp.maximum(group - 1, 0)]))
-    above = jnp.where(group == last, 0.0, read(slots[jnp.minimum(group + 1, last)]))
+    below = jnp.where(group == 0, 0.0, read(slots[slot_of(jnp.maximum(group - 1, 0), last + 1)]))
+    above = jnp.where(group == last, 0.0, read(slots[slot_of(jnp.minimum(group + 1, last), last + 1)]))
     return jnp.where(member == 0, below, near[0]), jnp.where(member == NEAR - 1, above, near[1])
 
 
@@ -409,7 +413,8 @@
     for u in range(3):
         part = total[u * WELL_ROWS : (u + 1) * WELL_ROWS]
         pull = pull + part * part * scale
-    tiles = [slots[k, 16:24] for k in range(slots.shape[0])]
+    count = slots.shape[0]
+    tiles = [slots[slot_of(k, count), 16:24] for k in range(count)]
     between = tree([face_energy(a, b) for a, b in zip(tiles, tiles[1:])])
     last = whole_sum(between) - whole_sum(pull)
     line = total[15:16] + jnp.where(lanes()[0:1] == 5, last, 0.0)
@@ -508,7 +513,9 @@
 
 def far_slots(sent):
     count = lax.axis_size("gz")
-    groups = [[g + NEAR * k for k in range(count // NEAR)] for g in range(NEAR)]
+    slots = count // NEAR
+    order = sorted(range(slots), key=lambda group: slot_of(group, slots))
+    groups = [[g + NEAR * k for k in order] for g in range(NEAR)]
     return lax.all_to_all(sent, "gz", 0, 0, axis_index_groups=groups)
 
 

time: 181 us -> 170 us (0.939)
  waiting for transfers between devices: 45.7 us -> 10.6 us
  starting transfers between devices: 82.2 us -> 109 us
  blocking collectives: 42.8 us -> 39.3 us
    all_to_all x3, waiting for transfers between devices: 34.5 us -> 0.01 us  [far_slots(): return lax.all_to_all(sent, 'gz', 0, 0, axis_index_groups=groups)]
    all_to_all x3, starting transfers between devices: 46 us -> 73.7 us  [far_slots(): return lax.all_to_all(sent, 'gz', 0, 0, axis_index_groups=groups)]
    all_to_all x1, blocking collectives: 17.4 us -> 14.5 us  [body(): lines = lax.all_to_all(sent, ('gx', 'gy'), 0, 0)]
  transfers between devices with their start and end apart: 15 -> 15, of which waited for: 7 -> 4; matrix products, arithmetic and copies ran while one was open for 0% -> 0% of each run, Pallas kernels for 0% -> 0%
where the time goes in v5:
time: 170 us; the launch traced here: 169 us
  starting transfers between devices  109 us (64%)
  blocking collectives  39.3 us (23%)
  waiting for transfers between devices  10.6 us (6%)
  Pallas kernels  8.13 us (5%)
    all_to_all x3, starting transfers between devices, far_slots(): return lax.all_to_all(sent, 'gz', 0, 0, axis_index_groups=groups)  73.7 us
    all_to_all x3, blocking collectives, near_slots(): return lax.all_to_all(sent, 'gz', 0, 0, axis_index_groups=groups)  24.8 us
    ppermute x6, starting transfers between devices, forward(): return lax.ppermute(piece, axis, [(i, i + 1) for i in range(count - 1)])  23.6 us
    all_to_all x1, blocking collectives, body(): lines = lax.all_to_all(sent, ('gx', 'gy'), 0, 0)  14.5 us
    ppermute x6, starting transfers between devices, backward(): return lax.ppermute(piece, axis, [(i + 1, i) for i in range(count - 1)])  11.5 us
    ppermute x6, waiting for transfers between devices, backward(): return lax.ppermute(piece, axis, [(i + 1, i) for i in range(count - 1)])  9.78 us
    pallas_call x12, Pallas kernels, call(): pl.pallas_call(kernel, out_shape=[jax.ShapeDtypeStruct(shape, F32) for sh...  8.13 us
  transfers between devices with their start and end apart: 15, of which 4 were waited for; matrix products, arithmetic and copies ran while one was open for 0% of the time, Pallas kernels for 0%

profile of v5, /device:TPU:1, one launch (start us, length us, event | category | flops | bytes accessed | tf_op | source)
XLA Modules:
  0.0 168.5 jit_solution(10798528144382740702)
XLA Ops:
  0.6 2.0 %shard_map.86 = (f32[4,24,128]{2,1,0:T(8,128)}, f32[6,8,128]{2,1,0:T(8,128)}, f32[6,8,128]{2,1,0:T(8,128)}, f32[24,128]{1,0:T(8,128)}, f32[24,128]{1,0:T(8,128)}) custom-call(f32[3,32,128]{2,1,0:T(8,128)} %bitcast.6, f32[3,32,128]{2,1,0:T(8,128)} %bitcast.19, s32[1,1,512]{2,1,0:T(1,128)} %cell.5, s32[1,1,512]{2,1,0:T(1,128)} %well.5, f32[1,1,512]{2,1,0:T(1,128)} %factor.5), custom_call_target="tpu_custom_call" | custom-call | tf_op jit(solution)/shard_map/pallas_call | solution.py:491
  2.7 11.0 %all_to_all.35.slots = f32[4,24,128]{2,1,0:T(8,128)S(1)} all-to-all(f32[4,24,128]{2,1,0:T(8,128)} %get-tuple-element.47), channel_id=1, replica_groups={{0,1,2,3},{4,5,6,7},{8,9,10,11},{12,13,14,15},{16,17,18,19},{20,21,22,2..., dimensions={0} | all-to-all | bytes 98304 | tf_op jit(solution)/shard_map/all_to_all | solution.py:507
  13.7 0.8 shard_map.87
  14.5 31.6 %all-to-all-start.1 = ((f32[8,24,128]{2,1,0:T(8,128)}), f32[8,24,128]{2,1,0:T(8,128)S(1)}, u32[]{:S(2)}, u32[]{:S(2)}) async-start(f32[8,24,128]{2,1,0:T(8,128)} %get-tuple-element.53), calls=%async_computation.1 | async-start | bytes 196608 | tf_op jit(solution)/shard_map/all_to_all | solution.py:519
  46.1 3.1 %collective-permute-start = (f32[6,8,128]{2,1,0:T(8,128)S(1)}, f32[6,8,128]{2,1,0:T(8,128)S(1)}, u32[]{:S(2)}, u32[]{:S(2)}) collective-permute-start(f32[6,8,128]{2,1,0:T(8,128)S(1)} %copy-done.8), channel_id=1, source_target_pairs={{0,256},{256,512},{512,768},{1,257},{257,513},{513,769},{2,258},{2... | collective-permute-start | bytes 73736 | tf_op jit(solution)/shard_map/ppermute | solution.py:524
  49.2 1.3 collective-permute-start.2
  50.5 5.8 %collective-permute-start.1 = (f32[24,128]{1,0:T(8,128)S(1)}, f32[24,128]{1,0:T(8,128)S(1)}, u32[]{:S(2)}, u32[]{:S(2)}) collective-permute-start(f32[24,128]{1,0:T(8,128)S(1)} %copy-done.10), channel_id=1, source_target_pairs={{0,32},{32,64},{64,96},{96,128},{128,160},{160,192},{192,224},{1,3... | collective-permute-start | bytes 36872 | tf_op jit(solution)/shard_map/ppermute | solution.py:524
  56.3 1.9 %collective-permute-start.3 = (f32[24,128]{1,0:T(8,128)S(1)}, f32[24,128]{1,0:T(8,128)S(1)}, u32[]{:S(2)}, u32[]{:S(2)}) collective-permute-start(f32[24,128]{1,0:T(8,128)S(1)} %copy-done.9), channel_id=1, source_target_pairs={{32,0},{64,32},{96,64},{128,96},{160,128},{192,160},{224,192},{33,... | collective-permute-start | bytes 36872 | tf_op jit(solution)/shard_map/ppermute | solution.py:529
  58.2 3.1 %collective-permute-done.3.yh = f32[24,128]{1,0:T(8,128)S(1)} collective-permute-done((f32[24,128]{1,0:T(8,128)S(1)}, f32[24,128]{1,0:T(8,128)S(1)}, u32[]{:S(2)}, u32[]{:S(2)}) %collective-permute-start.3) | collective-permute-done | bytes 12320 | tf_op jit(solution)/shard_map/ppermute | solution.py:529
  61.5 0.6 copy-done.5
  62.1 1.2 shard_map.89
  63.3 6.9 %all_to_all.36.slots = f32[4,24,128]{2,1,0:T(8,128)S(1)} all-to-all(f32[4,24,128]{2,1,0:T(8,128)S(1)} %broadcast_in_dim.4), channel_id=1, replica_groups={{0,1,2,3},{4,5,6,7},{8,9,10,11},{12,13,14,15},{16,17,18,19},{20,21,22,2..., dimensions={0} | all-to-all | bytes 98304 | tf_op jit(solution)/shard_map/all_to_all | solution.py:507
  70.2 0.6 shard_map.90
  70.9 21.1 %all-to-all-start.3 = ((f32[8,24,128]{2,1,0:T(8,128)}), f32[8,24,128]{2,1,0:T(8,128)S(1)}, u32[]{:S(2)}, u32[]{:S(2)}) async-start(f32[8,24,128]{2,1,0:T(8,128)} %get-tuple-element.66), calls=%async_computation.3 | async-start | bytes 196608 | tf_op jit(solution)/shard_map/all_to_all | solution.py:519
  92.0 4.3 %collective-permute-start.4 = (f32[3,8,128]{2,1,0:T(8,128)S(1)}, f32[3,8,128]{2,1,0:T(8,128)S(1)}, u32[]{:S(2)}, u32[]{:S(2)}) collective-permute-start(f32[3,8,128]{2,1,0:T(8,128)S(1)} %get-tuple-element.70), channel_id=1, source_target_pairs={{0,256},{256,512},{512,768},{1,257},{257,513},{513,769},{2,258},{2... | collective-permute-start | bytes 36872 | tf_op jit(solution)/shard_map/ppermute | solution.py:524
  96.2 1.3 collective-permute-start.6
  97.5 4.0 %collective-permute-start.5 = (f32[12,128]{1,0:T(8,128)S(1)}, f32[12,128]{1,0:T(8,128)S(1)}, u32[]{:S(2)}, u32[]{:S(2)}) collective-permute-start(f32[12,128]{1,0:T(8,128)S(1)} %get-tuple-element.71), channel_id=1, source_target_pairs={{0,32},{32,64},{64,96},{96,128},{128,160},{160,192},{192,224},{1,3... | collective-permute-start | bytes 18440 | tf_op jit(solution)/shard_map/ppermute | solution.py:524
  101.5 1.9 %collective-permute-start.7 = (f32[12,128]{1,0:T(8,128)S(1)}, f32[12,128]{1,0:T(8,128)S(1)}, u32[]{:S(2)}, u32[]{:S(2)}) collective-permute-start(f32[12,128]{1,0:T(8,128)S(1)} %get-tuple-element.73), channel_id=1, source_target_pairs={{32,0},{64,32},{96,64},{128,96},{160,128},{192,160},{224,192},{33,... | collective-permute-start | bytes 18440 | tf_op jit(solution)/shard_map/ppermute | solution.py:529
  103.4 3.0 %collective-permute-done.7.yh = f32[12,128]{1,0:T(8,128)S(1)} collective-permute-done((f32[12,128]{1,0:T(8,128)S(1)}, f32[12,128]{1,0:T(8,128)S(1)}, u32[]{:S(2)}, u32[]{:S(2)}) %collective-permute-start.7) | collective-permute-done | bytes 6176 | tf_op jit(solution)/shard_map/ppermute | solution.py:529
  106.5 1.1 shard_map.92
  107.6 4.3 %collective-permute-start.8 = (f32[3,8,128]{2,1,0:T(8,128)S(1)}, f32[3,8,128]{2,1,0:T(8,128)S(1)}, u32[]{:S(2)}, u32[]{:S(2)}) collective-permute-start(f32[3,8,128]{2,1,0:T(8,128)S(1)} %get-tuple-element.79), channel_id=1, source_target_pairs={{0,256},{256,512},{512,768},{1,257},{257,513},{513,769},{2,258},{2... | collective-permute-start | bytes 36872 | tf_op jit(solution)/shard_map/ppermute | solution.py:524
  111.9 2.2 %collective-permute-start.9 = (f32[12,128]{1,0:T(8,128)S(1)}, f32[12,128]{1,0:T(8,128)S(1)}, u32[]{:S(2)}, u32[]{:S(2)}) collective-permute-start(f32[12,128]{1,0:T(8,128)S(1)} %get-tuple-element.80), channel_id=1, source_target_pairs={{0,32},{32,64},{64,96},{96,128},{128,160},{160,192},{192,224},{1,3... | collective-permute-start | bytes 18440 | tf_op jit(solution)/shard_map/ppermute | solution.py:524
  114.2 0.8 collective-permute-done.9.yl
  115.2 6.9 %all_to_all.37.slots = f32[4,24,128]{2,1,0:T(8,128)S(1)} all-to-all(f32[4,24,128]{2,1,0:T(8,128)S(1)} %broadcast_in_dim.5), channel_id=1, replica_groups={{0,1,2,3},{4,5,6,7},{8,9,10,11},{12,13,14,15},{16,17,18,19},{20,21,22,2..., dimensions={0} | all-to-all | bytes 98304 | tf_op jit(solution)/shard_map/all_to_all | solution.py:507
  122.1 0.8 shard_map.94
  122.9 21.1 %all-to-all-start.5 = ((f32[8,24,128]{2,1,0:T(8,128)}), f32[8,24,128]{2,1,0:T(8,128)S(1)}, u32[]{:S(2)}, u32[]{:S(2)}) async-start(f32[8,24,128]{2,1,0:T(8,128)} %get-tuple-element.84), calls=%async_computation.5 | async-start | bytes 196608 | tf_op jit(solution)/shard_map/all_to_all | solution.py:519
  144.0 1.3 collective-permute-start.10
  145.2 3.8 %collective-permute-start.11 = (f32[12,128]{1,0:T(8,128)S(1)}, f32[12,128]{1,0:T(8,128)S(1)}, u32[]{:S(2)}, u32[]{:S(2)}) collective-permute-start(f32[12,128]{1,0:T(8,128)S(1)} %get-tuple-element.86), channel_id=1, source_target_pairs={{32,0},{64,32},{96,64},{128,96},{160,128},{192,160},{224,192},{33,... | collective-permute-start | bytes 18440 | tf_op jit(solution)/shard_map/ppermute | solution.py:529
  149.0 3.7 %collective-permute-done.11.yh = f32[12,128]{1,0:T(8,128)S(1)} collective-permute-done((f32[12,128]{1,0:T(8,128)S(1)}, f32[12,128]{1,0:T(8,128)S(1)}, u32[]{:S(2)}, u32[]{:S(2)}) %collective-permute-start.11) | collective-permute-done | bytes 6176 | tf_op jit(solution)/shard_map/ppermute | solution.py:529
  152.8 0.2 shard_map.96
  152.9 14.5 %all_to_all.38.lines = f32[32,1,128]{2,1,0:T(1,128)S(1)} all-to-all(f32[32,1,128]{2,1,0:T(1,128)S(1)} %shard_map.96), channel_id=1, replica_groups=mesh['gx'=4,'gy'=8,'gz'=32] {'gx','gy'}, dimensions={0} | all-to-all | bytes 32768 | tf_op jit(solution)/shard_map/all_to_all | solution.py:601
  167.4 1.1 shard_map.97
  (38 shorter events, 0.6 us)
Async XLA Ops:
  2.7 47.8 %copy-start.10 = (f32[24,128]{1,0:T(8,128)S(1)}, f32[24,128]{1,0:T(8,128)}, u32[]{:S(2)}) copy-start(f32[24,128]{1,0:T(8,128)} %get-tuple-element.56) | copy-start | bytes 36868
  13.7 32.4 %copy-start.8 = (f32[6,8,128]{2,1,0:T(8,128)S(1)}, f32[6,8,128]{2,1,0:T(8,128)}, u32[]{:S(2)}) copy-start(f32[6,8,128]{2,1,0:T(8,128)} %get-tuple-element.55) | copy-start | bytes 73732
  13.7 35.5 %copy-start.7 = (f32[6,8,128]{2,1,0:T(8,128)S(1)}, f32[6,8,128]{2,1,0:T(8,128)}, u32[]{:S(2)}) copy-start(f32[6,8,128]{2,1,0:T(8,128)} %get-tuple-element.57) | copy-start | bytes 73732
  13.7 42.6 %copy-start.9 = (f32[24,128]{1,0:T(8,128)S(1)}, f32[24,128]{1,0:T(8,128)}, u32[]{:S(2)}) copy-start(f32[24,128]{1,0:T(8,128)} %get-tuple-element.58) | copy-start | bytes 36868
  14.5 46.8 %copy-start = (f32[3,4,8,128]{3,2,1,0:T(8,128)S(1)}, f32[3,4,8,128]{3,2,1,0:T(8,128)}, u32[]{:S(2)}) copy-start(f32[3,4,8,128]{3,2,1,0:T(8,128)} %param.7) | copy-start | bytes 147460
  14.5 46.8 %copy-start.1 = (f32[3,4,8,128]{3,2,1,0:T(8,128)S(1)}, f32[3,4,8,128]{3,2,1,0:T(8,128)}, u32[]{:S(2)}) copy-start(f32[3,4,8,128]{3,2,1,0:T(8,128)} %param.8) | copy-start | bytes 147460
  14.5 46.8 %copy-start.2 = (f32[3,4,8,128]{3,2,1,0:T(8,128)S(1)}, f32[3,4,8,128]{3,2,1,0:T(8,128)}, u32[]{:S(2)}) copy-start(f32[3,4,8,128]{3,2,1,0:T(8,128)} %param.9) | copy-start | bytes 147460
  14.5 46.8 %copy-start.3 = (f32[3,4,8,128]{3,2,1,0:T(8,128)S(1)}, f32[3,4,8,128]{3,2,1,0:T(8,128)}, u32[]{:S(2)}) copy-start(f32[3,4,8,128]{3,2,1,0:T(8,128)} %param.10) | copy-start | bytes 147460
  14.5 47.0 %all-to-all-start.1 = ((f32[8,24,128]{2,1,0:T(8,128)}), f32[8,24,128]{2,1,0:T(8,128)S(1)}, u32[]{:S(2)}, u32[]{:S(2)}) async-start(f32[8,24,128]{2,1,0:T(8,128)} %get-tuple-element.53), calls=%async_computation.1 | async-start | bytes 196608 | tf_op jit(solution)/shard_map/all_to_all | solution.py:519
  46.1 15.2 %collective-permute-start = (f32[6,8,128]{2,1,0:T(8,128)S(1)}, f32[6,8,128]{2,1,0:T(8,128)S(1)}, u32[]{:S(2)}, u32[]{:S(2)}) collective-permute-start(f32[6,8,128]{2,1,0:T(8,128)S(1)} %copy-done.8), channel_id=1, source_target_pairs={{0,256},{256,512},{512,768},{1,257},{257,513},{513,769},{2,258},{2... | collective-permute-start | bytes 73736 | tf_op jit(solution)/shard_map/ppermute | solution.py:524
  49.2 12.1 %collective-permute-start.2 = (f32[6,8,128]{2,1,0:T(8,128)S(1)}, f32[6,8,128]{2,1,0:T(8,128)S(1)}, u32[]{:S(2)}, u32[]{:S(2)}) collective-permute-start(f32[6,8,128]{2,1,0:T(8,128)S(1)} %copy-done.7), channel_id=1, source_target_pairs={{256,0},{512,256},{768,512},{257,1},{513,257},{769,513},{258,2},{5... | collective-permute-start | bytes 73736 | tf_op jit(solution)/shard_map/ppermute | solution.py:529
  50.5 7.7 %collective-permute-start.1 = (f32[24,128]{1,0:T(8,128)S(1)}, f32[24,128]{1,0:T(8,128)S(1)}, u32[]{:S(2)}, u32[]{:S(2)}) collective-permute-start(f32[24,128]{1,0:T(8,128)S(1)} %copy-done.10), channel_id=1, source_target_pairs={{0,32},{32,64},{64,96},{96,128},{128,160},{160,192},{192,224},{1,3... | collective-permute-start | bytes 36872 | tf_op jit(solution)/shard_map/ppermute | solution.py:524
  56.3 5.0 %collective-permute-start.3 = (f32[24,128]{1,0:T(8,128)S(1)}, f32[24,128]{1,0:T(8,128)S(1)}, u32[]{:S(2)}, u32[]{:S(2)}) collective-permute-start(f32[24,128]{1,0:T(8,128)S(1)} %copy-done.9), channel_id=1, source_target_pairs={{32,0},{64,32},{96,64},{128,96},{160,128},{192,160},{224,192},{33,... | collective-permute-start | bytes 36872 | tf_op jit(solution)/shard_map/ppermute | solution.py:529
  61.3 0.7 copy-start.5
  61.3 0.7 copy-start.6
  61.4 0.7 copy-start.4
  70.9 35.6 %all-to-all-start.3 = ((f32[8,24,128]{2,1,0:T(8,128)}), f32[8,24,128]{2,1,0:T(8,128)S(1)}, u32[]{:S(2)}, u32[]{:S(2)}) async-start(f32[8,24,128]{2,1,0:T(8,128)} %get-tuple-element.66), calls=%async_computation.3 | async-start | bytes 196608 | tf_op jit(solution)/shard_map/all_to_all | solution.py:519
  92.0 14.5 %collective-permute-start.4 = (f32[3,8,128]{2,1,0:T(8,128)S(1)}, f32[3,8,128]{2,1,0:T(8,128)S(1)}, u32[]{:S(2)}, u32[]{:S(2)}) collective-permute-start(f32[3,8,128]{2,1,0:T(8,128)S(1)} %get-tuple-element.70), channel_id=1, source_target_pairs={{0,256},{256,512},{512,768},{1,257},{257,513},{513,769},{2,258},{2... | collective-permute-start | bytes 36872 | tf_op jit(solution)/shard_map/ppermute | solution.py:524
  96.2 10.3 %collective-permute-start.6 = (f32[3,8,128]{2,1,0:T(8,128)S(1)}, f32[3,8,128]{2,1,0:T(8,128)S(1)}, u32[]{:S(2)}, u32[]{:S(2)}) collective-permute-start(f32[3,8,128]{2,1,0:T(8,128)S(1)} %get-tuple-element.72), channel_id=1, source_target_pairs={{256,0},{512,256},{768,512},{257,1},{513,257},{769,513},{258,2},{5... | collective-permute-start | bytes 36872 | tf_op jit(solution)/shard_map/ppermute | solution.py:529
  97.5 5.9 %collective-permute-start.5 = (f32[12,128]{1,0:T(8,128)S(1)}, f32[12,128]{1,0:T(8,128)S(1)}, u32[]{:S(2)}, u32[]{:S(2)}) collective-permute-start(f32[12,128]{1,0:T(8,128)S(1)} %get-tuple-element.71), channel_id=1, source_target_pairs={{0,32},{32,64},{64,96},{96,128},{128,160},{160,192},{192,224},{1,3... | collective-permute-start | bytes 18440 | tf_op jit(solution)/shard_map/ppermute | solution.py:524
  101.5 5.0 %collective-permute-start.7 = (f32[12,128]{1,0:T(8,128)S(1)}, f32[12,128]{1,0:T(8,128)S(1)}, u32[]{:S(2)}, u32[]{:S(2)}) collective-permute-start(f32[12,128]{1,0:T(8,128)S(1)} %get-tuple-element.73), channel_id=1, source_target_pairs={{32,0},{64,32},{96,64},{128,96},{160,128},{192,160},{224,192},{33,... | collective-permute-start | bytes 18440 | tf_op jit(solution)/shard_map/ppermute | solution.py:529
  107.6 7.4 %collective-permute-start.8 = (f32[3,8,128]{2,1,0:T(8,128)S(1)}, f32[3,8,128]{2,1,0:T(8,128)S(1)}, u32[]{:S(2)}, u32[]{:S(2)}) collective-permute-start(f32[3,8,128]{2,1,0:T(8,128)S(1)} %get-tuple-element.79), channel_id=1, source_target_pairs={{0,256},{256,512},{512,768},{1,257},{257,513},{513,769},{2,258},{2... | collective-permute-start | bytes 36872 | tf_op jit(solution)/shard_map/ppermute | solution.py:524
  111.9 3.1 %collective-permute-start.9 = (f32[12,128]{1,0:T(8,128)S(1)}, f32[12,128]{1,0:T(8,128)S(1)}, u32[]{:S(2)}, u32[]{:S(2)}) collective-permute-start(f32[12,128]{1,0:T(8,128)S(1)} %get-tuple-element.80), channel_id=1, source_target_pairs={{0,32},{32,64},{64,96},{96,128},{128,160},{160,192},{192,224},{1,3... | collective-permute-start | bytes 18440 | tf_op jit(solution)/shard_map/ppermute | solution.py:524
  122.9 29.9 %all-to-all-start.5 = ((f32[8,24,128]{2,1,0:T(8,128)}), f32[8,24,128]{2,1,0:T(8,128)S(1)}, u32[]{:S(2)}, u32[]{:S(2)}) async-start(f32[8,24,128]{2,1,0:T(8,128)} %get-tuple-element.84), calls=%async_computation.5 | async-start | bytes 196608 | tf_op jit(solution)/shard_map/all_to_all | solution.py:519
  144.0 8.8 %collective-permute-start.10 = (f32[3,8,128]{2,1,0:T(8,128)S(1)}, f32[3,8,128]{2,1,0:T(8,128)S(1)}, u32[]{:S(2)}, u32[]{:S(2)}) collective-permute-start(f32[3,8,128]{2,1,0:T(8,128)S(1)} %get-tuple-element.85), channel_id=1, source_target_pairs={{256,0},{512,256},{768,512},{257,1},{513,257},{769,513},{258,2},{5... | collective-permute-start | bytes 36872 | tf_op jit(solution)/shard_map/ppermute | solution.py:529
  145.2 7.5 %collective-permute-start.11 = (f32[12,128]{1,0:T(8,128)S(1)}, f32[12,128]{1,0:T(8,128)S(1)}, u32[]{:S(2)}, u32[]{:S(2)}) collective-permute-start(f32[12,128]{1,0:T(8,128)S(1)} %get-tuple-element.86), channel_id=1, source_target_pairs={{32,0},{64,32},{96,64},{128,96},{160,128},{192,160},{224,192},{33,... | collective-permute-start | bytes 18440 | tf_op jit(solution)/shard_map/ppermute | solution.py:529

commit v6 on v5

--- a/solution.py
+++ b/solution.py
@@ -157,8 +157,11 @@
     return lax.div(at, NEAR), lax.rem(at, NEAR)
 
 
-def slot_of(group, count):
-    return (group + count - count // 2) % count
+FIRST = (5, 3, 4)
+
+
+def slot_of(group, count, step):
+    return (group + count - FIRST[step] % count) % count
 
 
 def near_tiles(tiles):
@@ -170,11 +173,11 @@
     return low, high
 
 
-def halo_tiles(near, slots, read):
+def halo_tiles(near, slots, read, step):
     group, member = place()
     last = slots.shape[0] - 1
-    below = jnp.where(group == 0, 0.0, read(slots[slot_of(jnp.maximum(group - 1, 0), last + 1)]))
-    above = jnp.where(group == last, 0.0, read(slots[slot_of(jnp.minimum(group + 1, last), last + 1)]))
+    below = jnp.where(group == 0, 0.0, read(slots[slot_of(jnp.maximum(group - 1, 0), last + 1, step)]))
+    above = jnp.where(group == last, 0.0, read(slots[slot_of(jnp.minimum(group + 1, last), last + 1, step)]))
     return jnp.where(member == 0, below, near[0]), jnp.where(member == NEAR - 1, above, near[1])
 
 
@@ -334,7 +337,7 @@
     field, table, inverse, extra, cond, *faces
 ):
     total = jnp.sum(slots[...], axis=0)
-    low, high = halo_tiles(near, slots, lambda a: unfold(a[4 * WELL_ROWS : 24]))
+    low, high = halo_tiles(near, slots, lambda a: unfold(a[4 * WELL_ROWS : 24]), 0)
     put_cond_along(cond, mobility, low, high)
     whole = flow_along(right, flow, cond, low, high)
     scale = 1.0 / (1.0 + total[3 * WELL_ROWS : 4 * WELL_ROWS])
@@ -361,7 +364,7 @@
     slots, near, flow, before, extra, inverse, cond, cell, well, factor, field, table, *faces
 ):
     total = jnp.sum(slots[...], axis=0)
-    low, high = halo_tiles(near, slots, lambda a: a[16:24])
+    low, high = halo_tiles(near, slots, lambda a: a[16:24], 1)
     whole = flow_along(before, flow, cond, low, high)
     scale_row = get_well_rows(inverse[...], 1)[0]
     rows = get_well_rows(total, 3)
@@ -414,7 +417,7 @@
         part = total[u * WELL_ROWS : (u + 1) * WELL_ROWS]
         pull = pull + part * part * scale
     count = slots.shape[0]
-    tiles = [slots[slot_of(k, count), 16:24] for k in range(count)]
+    tiles = [slots[slot_of(k, count, 2), 16:24] for k in range(count)]
     between = tree([face_energy(a, b) for a, b in zip(tiles, tiles[1:])])
     last = whole_sum(between) - whole_sum(pull)
     line = total[15:16] + jnp.where(lanes()[0:1] == 5, last, 0.0)
@@ -452,7 +455,7 @@
     lines, slots, near, flow, extra, inverse, cond, cell, well, factor, w0, w1, w2, solved, rest
 ):
     total = jnp.sum(slots[...], axis=0)
-    low, high = halo_tiles(near, slots, lambda a: a[16:24])
+    low, high = halo_tiles(near, slots, lambda a: a[16:24], 2)
     whole = flow_along(w2, flow, cond, low, high)
     scale_row = get_well_rows(inverse[...], 1)[0]
     means = [r * scale_row for r in get_well_rows(total, 3)]
@@ -511,10 +514,10 @@
     return jnp.broadcast_to(table[None], (NEAR,) + table.shape)
 
 
-def far_slots(sent):
+def far_slots(sent, step):
     count = lax.axis_size("gz")
     slots = count // NEAR
-    order = sorted(range(slots), key=lambda group: slot_of(group, slots))
+    order = sorted(range(slots), key=lambda group: slot_of(group, slots, step))
     groups = [[g + NEAR * k for k in order] for g in range(NEAR)]
     return lax.all_to_all(sent, "gz", 0, 0, axis_index_groups=groups)
 
@@ -562,7 +565,7 @@
     )
     sent, near = call(first_near_kernel, sent_shapes, near_slots(table))
     sent, *faces = after(sent, *faces)
-    slots = far_slots(sent)
+    slots = far_slots(sent, 0)
     flow, cond = call(
         first_flow_kernel, [block, (4,) + block],
         right, mob, diag, off, *low_halos(faces), *high_halos(faces),
@@ -575,7 +578,7 @@
 
     sent, near = call(near_kernel, sent_shapes, near_slots(copies(table)))
     sent, *faces = after(sent, *faces)
-    slots = far_slots(sent)
+    slots = far_slots(sent, 1)
     flow = call(
         flow_kernel, [block], w1, diag, off, cond, *low_halos(faces), *high_halos(faces)
     )[0]
@@ -591,7 +594,7 @@
     )[0]
     sent, near = call(last_near_kernel, sent_shapes, near_slots(copies(table)))
     sent, *faces = after(sent, *faces)
-    slots = far_slots(sent)
+    slots = far_slots(sent, 2)
     high = high_halos(faces)
     flow = call(flow_kernel, [block], w2, diag, off, cond, *low, *high)[0]
     slots, flow = after(slots, flow)

time: 170 us -> 164 us (0.965)
  starting transfers between devices: 109 us -> 103 us
    all_to_all x3, starting transfers between devices: 73.7 us -> 65.6 us  [far_slots(): return lax.all_to_all(sent, 'gz', 0, 0, axis_index_groups=groups)]
    ppermute x6, starting transfers between devices: 23.6 us -> 26.2 us  [forward(): return lax.ppermute(piece, axis, [(i, i + 1) for i in range(count - 1)])]
where the time goes in v6:
time: 164 us; the launch traced here: 163 us
  starting transfers between devices  103 us (63%)
  blocking collectives  39.3 us (24%)
  waiting for transfers between devices  10.6 us (6%)
  Pallas kernels  8.13 us (5%)
    all_to_all x3, starting transfers between devices, far_slots(): return lax.all_to_all(sent, 'gz', 0, 0, axis_index_groups=groups)  65.6 us
    ppermute x6, starting transfers between devices, forward(): return lax.ppermute(piece, axis, [(i, i + 1) for i in range(count - 1)])  26.2 us
    all_to_all x3, blocking collectives, near_slots(): return lax.all_to_all(sent, 'gz', 0, 0, axis_index_groups=groups)  24.8 us
    all_to_all x1, blocking collectives, body(): lines = lax.all_to_all(sent, ('gx', 'gy'), 0, 0)  14.5 us
    ppermute x6, starting transfers between devices, backward(): return lax.ppermute(piece, axis, [(i + 1, i) for i in range(count - 1)])  11.5 us
    ppermute x6, waiting for transfers between devices, backward(): return lax.ppermute(piece, axis, [(i + 1, i) for i in range(count - 1)])  9.78 us
    pallas_call x12, Pallas kernels, call(): pl.pallas_call(kernel, out_shape=[jax.ShapeDtypeStruct(shape, F32) for sh...  8.13 us
  transfers between devices with their start and end apart: 15, of which 4 were waited for; matrix products, arithmetic and copies ran while one was open for 0% of the time, Pallas kernels for 0%

profile of v6, /device:TPU:1, one launch (start us, length us, event | category | flops | bytes accessed | tf_op | source)
XLA Modules:
  0.0 163.0 jit_solution(8478446097678255927)
XLA Ops:
  0.6 2.0 %shard_map.86 = (f32[4,24,128]{2,1,0:T(8,128)}, f32[6,8,128]{2,1,0:T(8,128)}, f32[6,8,128]{2,1,0:T(8,128)}, f32[24,128]{1,0:T(8,128)}, f32[24,128]{1,0:T(8,128)}) custom-call(f32[3,32,128]{2,1,0:T(8,128)} %bitcast.6, f32[3,32,128]{2,1,0:T(8,128)} %bitcast.19, s32[1,1,512]{2,1,0:T(1,128)} %cell.5, s32[1,1,512]{2,1,0:T(1,128)} %well.5, f32[1,1,512]{2,1,0:T(1,128)} %factor.5), custom_call_target="tpu_custom_call" | custom-call | tf_op jit(solution)/shard_map/pallas_call | solution.py:494
  2.7 11.0 %all_to_all.35.slots = f32[4,24,128]{2,1,0:T(8,128)S(1)} all-to-all(f32[4,24,128]{2,1,0:T(8,128)} %get-tuple-element.47), channel_id=1, replica_groups={{0,1,2,3},{4,5,6,7},{8,9,10,11},{12,13,14,15},{16,17,18,19},{20,21,22,2..., dimensions={0} | all-to-all | bytes 98304 | tf_op jit(solution)/shard_map/all_to_all | solution.py:510
  13.7 0.8 shard_map.87
  14.5 26.8 %all-to-all-start.1 = ((f32[8,24,128]{2,1,0:T(8,128)}), f32[8,24,128]{2,1,0:T(8,128)S(1)}, u32[]{:S(2)}, u32[]{:S(2)}) async-start(f32[8,24,128]{2,1,0:T(8,128)} %get-tuple-element.53), calls=%async_computation.1 | async-start | bytes 196608 | tf_op jit(solution)/shard_map/all_to_all | solution.py:522
  41.3 3.1 %collective-permute-start = (f32[6,8,128]{2,1,0:T(8,128)S(1)}, f32[6,8,128]{2,1,0:T(8,128)S(1)}, u32[]{:S(2)}, u32[]{:S(2)}) collective-permute-start(f32[6,8,128]{2,1,0:T(8,128)S(1)} %copy-done.8), channel_id=1, source_target_pairs={{0,256},{256,512},{512,768},{1,257},{257,513},{513,769},{2,258},{2... | collective-permute-start | bytes 73736 | tf_op jit(solution)/shard_map/ppermute | solution.py:527
  44.4 1.3 collective-permute-start.2
  45.7 5.9 %collective-permute-start.1 = (f32[24,128]{1,0:T(8,128)S(1)}, f32[24,128]{1,0:T(8,128)S(1)}, u32[]{:S(2)}, u32[]{:S(2)}) collective-permute-start(f32[24,128]{1,0:T(8,128)S(1)} %copy-done.10), channel_id=1, source_target_pairs={{0,32},{32,64},{64,96},{96,128},{128,160},{160,192},{192,224},{1,3... | collective-permute-start | bytes 36872 | tf_op jit(solution)/shard_map/ppermute | solution.py:527
  51.6 1.9 %collective-permute-start.3 = (f32[24,128]{1,0:T(8,128)S(1)}, f32[24,128]{1,0:T(8,128)S(1)}, u32[]{:S(2)}, u32[]{:S(2)}) collective-permute-start(f32[24,128]{1,0:T(8,128)S(1)} %copy-done.9), channel_id=1, source_target_pairs={{32,0},{64,32},{96,64},{128,96},{160,128},{192,160},{224,192},{33,... | collective-permute-start | bytes 36872 | tf_op jit(solution)/shard_map/ppermute | solution.py:532
  53.6 3.1 %collective-permute-done.3.yh = f32[24,128]{1,0:T(8,128)S(1)} collective-permute-done((f32[24,128]{1,0:T(8,128)S(1)}, f32[24,128]{1,0:T(8,128)S(1)}, u32[]{:S(2)}, u32[]{:S(2)}) %collective-permute-start.3) | collective-permute-done | bytes 12320 | tf_op jit(solution)/shard_map/ppermute | solution.py:532
  56.8 0.6 copy-done.5
  57.5 1.2 shard_map.89
  58.7 6.9 %all_to_all.36.slots = f32[4,24,128]{2,1,0:T(8,128)S(1)} all-to-all(f32[4,24,128]{2,1,0:T(8,128)S(1)} %broadcast_in_dim.4), channel_id=1, replica_groups={{0,1,2,3},{4,5,6,7},{8,9,10,11},{12,13,14,15},{16,17,18,19},{20,21,22,2..., dimensions={0} | all-to-all | bytes 98304 | tf_op jit(solution)/shard_map/all_to_all | solution.py:510
  65.6 0.6 shard_map.90
  66.3 17.7 %all-to-all-start.3 = ((f32[8,24,128]{2,1,0:T(8,128)}), f32[8,24,128]{2,1,0:T(8,128)S(1)}, u32[]{:S(2)}, u32[]{:S(2)}) async-start(f32[8,24,128]{2,1,0:T(8,128)} %get-tuple-element.66), calls=%async_computation.3 | async-start | bytes 196608 | tf_op jit(solution)/shard_map/all_to_all | solution.py:522
  84.0 3.1 %collective-permute-start.4 = (f32[3,8,128]{2,1,0:T(8,128)S(1)}, f32[3,8,128]{2,1,0:T(8,128)S(1)}, u32[]{:S(2)}, u32[]{:S(2)}) collective-permute-start(f32[3,8,128]{2,1,0:T(8,128)S(1)} %get-tuple-element.70), channel_id=1, source_target_pairs={{0,256},{256,512},{512,768},{1,257},{257,513},{513,769},{2,258},{2... | collective-permute-start | bytes 36872 | tf_op jit(solution)/shard_map/ppermute | solution.py:527
  87.1 1.3 collective-permute-start.6
  88.4 7.5 %collective-permute-start.5 = (f32[12,128]{1,0:T(8,128)S(1)}, f32[12,128]{1,0:T(8,128)S(1)}, u32[]{:S(2)}, u32[]{:S(2)}) collective-permute-start(f32[12,128]{1,0:T(8,128)S(1)} %get-tuple-element.71), channel_id=1, source_target_pairs={{0,32},{32,64},{64,96},{96,128},{128,160},{160,192},{192,224},{1,3... | collective-permute-start | bytes 18440 | tf_op jit(solution)/shard_map/ppermute | solution.py:527
  96.0 1.9 %collective-permute-start.7 = (f32[12,128]{1,0:T(8,128)S(1)}, f32[12,128]{1,0:T(8,128)S(1)}, u32[]{:S(2)}, u32[]{:S(2)}) collective-permute-start(f32[12,128]{1,0:T(8,128)S(1)} %get-tuple-element.73), channel_id=1, source_target_pairs={{32,0},{64,32},{96,64},{128,96},{160,128},{192,160},{224,192},{33,... | collective-permute-start | bytes 18440 | tf_op jit(solution)/shard_map/ppermute | solution.py:532
  97.9 3.0 %collective-permute-done.7.yh = f32[12,128]{1,0:T(8,128)S(1)} collective-permute-done((f32[12,128]{1,0:T(8,128)S(1)}, f32[12,128]{1,0:T(8,128)S(1)}, u32[]{:S(2)}, u32[]{:S(2)}) %collective-permute-start.7) | collective-permute-done | bytes 6176 | tf_op jit(solution)/shard_map/ppermute | solution.py:532
  101.0 1.1 shard_map.92
  102.1 4.3 %collective-permute-start.8 = (f32[3,8,128]{2,1,0:T(8,128)S(1)}, f32[3,8,128]{2,1,0:T(8,128)S(1)}, u32[]{:S(2)}, u32[]{:S(2)}) collective-permute-start(f32[3,8,128]{2,1,0:T(8,128)S(1)} %get-tuple-element.79), channel_id=1, source_target_pairs={{0,256},{256,512},{512,768},{1,257},{257,513},{513,769},{2,258},{2... | collective-permute-start | bytes 36872 | tf_op jit(solution)/shard_map/ppermute | solution.py:527
  106.4 2.2 %collective-permute-start.9 = (f32[12,128]{1,0:T(8,128)S(1)}, f32[12,128]{1,0:T(8,128)S(1)}, u32[]{:S(2)}, u32[]{:S(2)}) collective-permute-start(f32[12,128]{1,0:T(8,128)S(1)} %get-tuple-element.80), channel_id=1, source_target_pairs={{0,32},{32,64},{64,96},{96,128},{128,160},{160,192},{192,224},{1,3... | collective-permute-start | bytes 18440 | tf_op jit(solution)/shard_map/ppermute | solution.py:527
  108.6 0.8 collective-permute-done.9.yl
  109.6 6.9 %all_to_all.37.slots = f32[4,24,128]{2,1,0:T(8,128)S(1)} all-to-all(f32[4,24,128]{2,1,0:T(8,128)S(1)} %broadcast_in_dim.5), channel_id=1, replica_groups={{0,1,2,3},{4,5,6,7},{8,9,10,11},{12,13,14,15},{16,17,18,19},{20,21,22,2..., dimensions={0} | all-to-all | bytes 98304 | tf_op jit(solution)/shard_map/all_to_all | solution.py:510
  116.5 0.8 shard_map.94
  117.3 21.1 %all-to-all-start.5 = ((f32[8,24,128]{2,1,0:T(8,128)}), f32[8,24,128]{2,1,0:T(8,128)S(1)}, u32[]{:S(2)}, u32[]{:S(2)}) async-start(f32[8,24,128]{2,1,0:T(8,128)} %get-tuple-element.84), calls=%async_computation.5 | async-start | bytes 196608 | tf_op jit(solution)/shard_map/all_to_all | solution.py:522
  138.4 1.3 collective-permute-start.10
  139.7 3.8 %collective-permute-start.11 = (f32[12,128]{1,0:T(8,128)S(1)}, f32[12,128]{1,0:T(8,128)S(1)}, u32[]{:S(2)}, u32[]{:S(2)}) collective-permute-start(f32[12,128]{1,0:T(8,128)S(1)} %get-tuple-element.86), channel_id=1, source_target_pairs={{32,0},{64,32},{96,64},{128,96},{160,128},{192,160},{224,192},{33,... | collective-permute-start | bytes 18440 | tf_op jit(solution)/shard_map/ppermute | solution.py:532
  143.5 3.7 %collective-permute-done.11.yh = f32[12,128]{1,0:T(8,128)S(1)} collective-permute-done((f32[12,128]{1,0:T(8,128)S(1)}, f32[12,128]{1,0:T(8,128)S(1)}, u32[]{:S(2)}, u32[]{:S(2)}) %collective-permute-start.11) | collective-permute-done | bytes 6176 | tf_op jit(solution)/shard_map/ppermute | solution.py:532
  147.2 0.2 shard_map.96
  147.4 14.5 %all_to_all.38.lines = f32[32,1,128]{2,1,0:T(1,128)S(1)} all-to-all(f32[32,1,128]{2,1,0:T(1,128)S(1)} %shard_map.96), channel_id=1, replica_groups=mesh['gx'=4,'gy'=8,'gz'=32] {'gx','gy'}, dimensions={0} | all-to-all | bytes 32768 | tf_op jit(solution)/shard_map/all_to_all | solution.py:604
  161.9 1.1 shard_map.97
  (38 shorter events, 0.6 us)
Async XLA Ops:
  2.7 43.0 %copy-start.10 = (f32[24,128]{1,0:T(8,128)S(1)}, f32[24,128]{1,0:T(8,128)}, u32[]{:S(2)}) copy-start(f32[24,128]{1,0:T(8,128)} %get-tuple-element.56) | copy-start | bytes 36868
  13.7 27.6 %copy-start.8 = (f32[6,8,128]{2,1,0:T(8,128)S(1)}, f32[6,8,128]{2,1,0:T(8,128)}, u32[]{:S(2)}) copy-start(f32[6,8,128]{2,1,0:T(8,128)} %get-tuple-element.55) | copy-start | bytes 73732
  13.7 30.7 %copy-start.7 = (f32[6,8,128]{2,1,0:T(8,128)S(1)}, f32[6,8,128]{2,1,0:T(8,128)}, u32[]{:S(2)}) copy-start(f32[6,8,128]{2,1,0:T(8,128)} %get-tuple-element.57) | copy-start | bytes 73732
  13.7 37.9 %copy-start.9 = (f32[24,128]{1,0:T(8,128)S(1)}, f32[24,128]{1,0:T(8,128)}, u32[]{:S(2)}) copy-start(f32[24,128]{1,0:T(8,128)} %get-tuple-element.58) | copy-start | bytes 36868
  14.5 42.2 %copy-start = (f32[3,4,8,128]{3,2,1,0:T(8,128)S(1)}, f32[3,4,8,128]{3,2,1,0:T(8,128)}, u32[]{:S(2)}) copy-start(f32[3,4,8,128]{3,2,1,0:T(8,128)} %param.7) | copy-start | bytes 147460
  14.5 42.2 %copy-start.1 = (f32[3,4,8,128]{3,2,1,0:T(8,128)S(1)}, f32[3,4,8,128]{3,2,1,0:T(8,128)}, u32[]{:S(2)}) copy-start(f32[3,4,8,128]{3,2,1,0:T(8,128)} %param.8) | copy-start | bytes 147460
  14.5 42.2 %copy-start.2 = (f32[3,4,8,128]{3,2,1,0:T(8,128)S(1)}, f32[3,4,8,128]{3,2,1,0:T(8,128)}, u32[]{:S(2)}) copy-start(f32[3,4,8,128]{3,2,1,0:T(8,128)} %param.9) | copy-start | bytes 147460
  14.5 42.2 %copy-start.3 = (f32[3,4,8,128]{3,2,1,0:T(8,128)S(1)}, f32[3,4,8,128]{3,2,1,0:T(8,128)}, u32[]{:S(2)}) copy-start(f32[3,4,8,128]{3,2,1,0:T(8,128)} %param.10) | copy-start | bytes 147460
  14.5 42.3 %all-to-all-start.1 = ((f32[8,24,128]{2,1,0:T(8,128)}), f32[8,24,128]{2,1,0:T(8,128)S(1)}, u32[]{:S(2)}, u32[]{:S(2)}) async-start(f32[8,24,128]{2,1,0:T(8,128)} %get-tuple-element.53), calls=%async_computation.1 | async-start | bytes 196608 | tf_op jit(solution)/shard_map/all_to_all | solution.py:522
  41.3 15.4 %collective-permute-start = (f32[6,8,128]{2,1,0:T(8,128)S(1)}, f32[6,8,128]{2,1,0:T(8,128)S(1)}, u32[]{:S(2)}, u32[]{:S(2)}) collective-permute-start(f32[6,8,128]{2,1,0:T(8,128)S(1)} %copy-done.8), channel_id=1, source_target_pairs={{0,256},{256,512},{512,768},{1,257},{257,513},{513,769},{2,258},{2... | collective-permute-start | bytes 73736 | tf_op jit(solution)/shard_map/ppermute | solution.py:527
  44.4 12.3 %collective-permute-start.2 = (f32[6,8,128]{2,1,0:T(8,128)S(1)}, f32[6,8,128]{2,1,0:T(8,128)S(1)}, u32[]{:S(2)}, u32[]{:S(2)}) collective-permute-start(f32[6,8,128]{2,1,0:T(8,128)S(1)} %copy-done.7), channel_id=1, source_target_pairs={{256,0},{512,256},{768,512},{257,1},{513,257},{769,513},{258,2},{5... | collective-permute-start | bytes 73736 | tf_op jit(solution)/shard_map/ppermute | solution.py:532
  45.7 7.9 %collective-permute-start.1 = (f32[24,128]{1,0:T(8,128)S(1)}, f32[24,128]{1,0:T(8,128)S(1)}, u32[]{:S(2)}, u32[]{:S(2)}) collective-permute-start(f32[24,128]{1,0:T(8,128)S(1)} %copy-done.10), channel_id=1, source_target_pairs={{0,32},{32,64},{64,96},{96,128},{128,160},{160,192},{192,224},{1,3... | collective-permute-start | bytes 36872 | tf_op jit(solution)/shard_map/ppermute | solution.py:527
  51.6 5.0 %collective-permute-start.3 = (f32[24,128]{1,0:T(8,128)S(1)}, f32[24,128]{1,0:T(8,128)S(1)}, u32[]{:S(2)}, u32[]{:S(2)}) collective-permute-start(f32[24,128]{1,0:T(8,128)S(1)} %copy-done.9), channel_id=1, source_target_pairs={{32,0},{64,32},{96,64},{128,96},{160,128},{192,160},{224,192},{33,... | collective-permute-start | bytes 36872 | tf_op jit(solution)/shard_map/ppermute | solution.py:532
  56.7 0.7 copy-start.5
  56.7 0.7 copy-start.6
  56.8 0.7 copy-start.4
  66.3 34.7 %all-to-all-start.3 = ((f32[8,24,128]{2,1,0:T(8,128)}), f32[8,24,128]{2,1,0:T(8,128)S(1)}, u32[]{:S(2)}, u32[]{:S(2)}) async-start(f32[8,24,128]{2,1,0:T(8,128)} %get-tuple-element.66), calls=%async_computation.3 | async-start | bytes 196608 | tf_op jit(solution)/shard_map/all_to_all | solution.py:522
  84.0 16.9 %collective-permute-start.4 = (f32[3,8,128]{2,1,0:T(8,128)S(1)}, f32[3,8,128]{2,1,0:T(8,128)S(1)}, u32[]{:S(2)}, u32[]{:S(2)}) collective-permute-start(f32[3,8,128]{2,1,0:T(8,128)S(1)} %get-tuple-element.70), channel_id=1, source_target_pairs={{0,256},{256,512},{512,768},{1,257},{257,513},{513,769},{2,258},{2... | collective-permute-start | bytes 36872 | tf_op jit(solution)/shard_map/ppermute | solution.py:527
  87.1 13.8 %collective-permute-start.6 = (f32[3,8,128]{2,1,0:T(8,128)S(1)}, f32[3,8,128]{2,1,0:T(8,128)S(1)}, u32[]{:S(2)}, u32[]{:S(2)}) collective-permute-start(f32[3,8,128]{2,1,0:T(8,128)S(1)} %get-tuple-element.72), channel_id=1, source_target_pairs={{256,0},{512,256},{768,512},{257,1},{513,257},{769,513},{258,2},{5... | collective-permute-start | bytes 36872 | tf_op jit(solution)/shard_map/ppermute | solution.py:532
  88.4 9.5 %collective-permute-start.5 = (f32[12,128]{1,0:T(8,128)S(1)}, f32[12,128]{1,0:T(8,128)S(1)}, u32[]{:S(2)}, u32[]{:S(2)}) collective-permute-start(f32[12,128]{1,0:T(8,128)S(1)} %get-tuple-element.71), channel_id=1, source_target_pairs={{0,32},{32,64},{64,96},{96,128},{128,160},{160,192},{192,224},{1,3... | collective-permute-start | bytes 18440 | tf_op jit(solution)/shard_map/ppermute | solution.py:527
  96.0 5.0 %collective-permute-start.7 = (f32[12,128]{1,0:T(8,128)S(1)}, f32[12,128]{1,0:T(8,128)S(1)}, u32[]{:S(2)}, u32[]{:S(2)}) collective-permute-start(f32[12,128]{1,0:T(8,128)S(1)} %get-tuple-element.73), channel_id=1, source_target_pairs={{32,0},{64,32},{96,64},{128,96},{160,128},{192,160},{224,192},{33,... | collective-permute-start | bytes 18440 | tf_op jit(solution)/shard_map/ppermute | solution.py:532
  102.1 7.4 %collective-permute-start.8 = (f32[3,8,128]{2,1,0:T(8,128)S(1)}, f32[3,8,128]{2,1,0:T(8,128)S(1)}, u32[]{:S(2)}, u32[]{:S(2)}) collective-permute-start(f32[3,8,128]{2,1,0:T(8,128)S(1)} %get-tuple-element.79), channel_id=1, source_target_pairs={{0,256},{256,512},{512,768},{1,257},{257,513},{513,769},{2,258},{2... | collective-permute-start | bytes 36872 | tf_op jit(solution)/shard_map/ppermute | solution.py:527
  106.4 3.1 %collective-permute-start.9 = (f32[12,128]{1,0:T(8,128)S(1)}, f32[12,128]{1,0:T(8,128)S(1)}, u32[]{:S(2)}, u32[]{:S(2)}) collective-permute-start(f32[12,128]{1,0:T(8,128)S(1)} %get-tuple-element.80), channel_id=1, source_target_pairs={{0,32},{32,64},{64,96},{96,128},{128,160},{160,192},{192,224},{1,3... | collective-permute-start | bytes 18440 | tf_op jit(solution)/shard_map/ppermute | solution.py:527
  117.3 29.9 %all-to-all-start.5 = ((f32[8,24,128]{2,1,0:T(8,128)}), f32[8,24,128]{2,1,0:T(8,128)S(1)}, u32[]{:S(2)}, u32[]{:S(2)}) async-start(f32[8,24,128]{2,1,0:T(8,128)} %get-tuple-element.84), calls=%async_computation.5 | async-start | bytes 196608 | tf_op jit(solution)/shard_map/all_to_all | solution.py:522
  138.4 8.8 %collective-permute-start.10 = (f32[3,8,128]{2,1,0:T(8,128)S(1)}, f32[3,8,128]{2,1,0:T(8,128)S(1)}, u32[]{:S(2)}, u32[]{:S(2)}) collective-permute-start(f32[3,8,128]{2,1,0:T(8,128)S(1)} %get-tuple-element.85), channel_id=1, source_target_pairs={{256,0},{512,256},{768,512},{257,1},{513,257},{769,513},{258,2},{5... | collective-permute-start | bytes 36872 | tf_op jit(solution)/shard_map/ppermute | solution.py:532
  139.7 7.5 %collective-permute-start.11 = (f32[12,128]{1,0:T(8,128)S(1)}, f32[12,128]{1,0:T(8,128)S(1)}, u32[]{:S(2)}, u32[]{:S(2)}) collective-permute-start(f32[12,128]{1,0:T(8,128)S(1)} %get-tuple-element.86), channel_id=1, source_target_pairs={{32,0},{64,32},{96,64},{128,96},{160,128},{192,160},{224,192},{33,... | collective-permute-start | bytes 18440 | tf_op jit(solution)/shard_map/ppermute | solution.py:532

commit v7 on v6

--- a/solution.py
+++ b/solution.py
@@ -126,6 +126,39 @@
     return jnp.concatenate([rows, pltpu.roll(jnp.concatenate([rows, rows], 0), 64, 1)[0:4]], 0)
 
 
+def fold_narrow(tile):
+    kept = jnp.where(lanes() < 32, tile, 0.0)
+    turned = [kept[0:2]] + [pltpu.roll(kept, 32 * k, 1)[2 * k : 2 * k + 2] for k in (1, 2, 3)]
+    return tree(turned)
+
+
+def unfold_narrow(rows):
+    sub = lax.broadcasted_iota(jnp.int32, (8, 128), 0)
+    spread = jnp.concatenate(rows * 4, 0)
+    tile = spread
+    for k in (1, 2, 3):
+        tile = jnp.where(sub >= 2 * k, pltpu.roll(spread, 128 - 32 * k, 1), tile)
+    return tile
+
+
+def slot_rows(slots, first, last):
+    return [tree([slots[k, r] for k in range(slots.shape[0])]) for r in range(first, last)]
+
+
+def well_rows(rows):
+    return [
+        jnp.concatenate(rows[u * WELL_ROWS : (u + 1) * WELL_ROWS], 1) for u in range(3)
+    ]
+
+
+def narrow_tile(slots):
+    return lambda k: unfold_narrow([slots[k, 15], slots[k, 16]])
+
+
+def wide_tile(slots):
+    return lambda k: unfold(jnp.concatenate([slots[k, r] for r in range(16, 20)], 0))
+
+
 def low_views(field, k, u, x, halo, sub):
     gx_low, gy_low = halo
     value = field[u, 8 * x : 8 * x + 8]
@@ -157,7 +190,7 @@
     return lax.div(at, NEAR), lax.rem(at, NEAR)
 
 
-FIRST = (5, 3, 4)
+FIRST = (5, 6, 4)
 
 
 def slot_of(group, count, step):
@@ -176,8 +209,10 @@
 def halo_tiles(near, slots, read, step):
     group, member = place()
     last = slots.shape[0] - 1
-    below = jnp.where(group == 0, 0.0, read(slots[slot_of(jnp.maximum(group - 1, 0), last + 1, step)]))
-    above = jnp.where(group == last, 0.0, read(slots[slot_of(jnp.minimum(group + 1, last), last + 1, step)]))
+    below = jnp.where(group == 0, 0.0, read(slot_of(jnp.maximum(group - 1, 0), last + 1, step)))
+    above = jnp.where(
+        group == last, 0.0, read(slot_of(jnp.minimum(group + 1, last), last + 1, step))
+    )
     return jnp.where(member == 0, below, near[0]), jnp.where(member == NEAR - 1, above, near[1])
 
 
@@ -238,9 +273,12 @@
     low, high = near_tiles(tiles)
     near[0], near[1] = low, high
     ends = jnp.where(lanes() < 16, tiles[-1], tiles[0])
+    ends = fold_narrow(ends)
     for k in range(sent.shape[0]):
-        sent[k, 0:16] = total[0:16]
-        sent[k, 16:24] = ends
+        for r in range(15):
+            sent[k, r] = total[r : r + 1]
+        for r in range(2):
+            sent[k, 15 + r] = ends[r : r + 1]
 
 
 def face_energy(below, above):
@@ -260,10 +298,13 @@
     between = whole_sum(tree([face_energy(a, b) for a, b in zip(tiles, tiles[1:])]))
     line = total[15:16] + jnp.where(lanes()[0:1] == 5, between, 0.0)
     ends = jnp.where(lanes() < 16, tiles[-1], tiles[0])
+    ends = fold(ends)
     for k in range(sent.shape[0]):
-        sent[k, 0:15] = total[0:15]
-        sent[k, 15:16] = line
-        sent[k, 16:24] = ends
+        for r in range(15):
+            sent[k, r] = total[r : r + 1]
+        sent[k, 15] = line
+        for r in range(4):
+            sent[k, 16 + r] = ends[r : r + 1]
 
 
 def first_flow_kernel(right, mobility, diag, off, xl, yl, xh, yh, flow, cond):
@@ -337,7 +378,7 @@
     field, table, inverse, extra, cond, *faces
 ):
     total = jnp.sum(slots[...], axis=0)
-    low, high = halo_tiles(near, slots, lambda a: unfold(a[4 * WELL_ROWS : 24]), 0)
+    low, high = halo_tiles(near, slots, lambda k: unfold(slots[k, 4 * WELL_ROWS : 24]), 0)
     put_cond_along(cond, mobility, low, high)
     whole = flow_along(right, flow, cond, low, high)
     scale = 1.0 / (1.0 + total[3 * WELL_ROWS : 4 * WELL_ROWS])
@@ -363,11 +404,10 @@
 def third_kernel(
     slots, near, flow, before, extra, inverse, cond, cell, well, factor, field, table, *faces
 ):
-    total = jnp.sum(slots[...], axis=0)
-    low, high = halo_tiles(near, slots, lambda a: a[16:24], 1)
+    low, high = halo_tiles(near, slots, narrow_tile(slots), 1)
     whole = flow_along(before, flow, cond, low, high)
     scale_row = get_well_rows(inverse[...], 1)[0]
-    rows = get_well_rows(total, 3)
+    rows = well_rows(slot_rows(slots, 0, 15))
     row, lane = cell_masks(cell[0])
     wells = well_mask(well[0])
     weight = factor[0]
@@ -410,17 +450,13 @@
 
 
 def scalar_kernel(slots, inverse, sent):
-    total = jnp.sum(slots[...], axis=0)
-    pull = jnp.zeros((WELL_ROWS, 128), F32)
-    scale = inverse[0:WELL_ROWS]
-    for u in range(3):
-        part = total[u * WELL_ROWS : (u + 1) * WELL_ROWS]
-        pull = pull + part * part * scale
+    rows = slot_rows(slots, 0, 16)
+    pull = tree([row * row * inverse[k % WELL_ROWS : k % WELL_ROWS + 1] for k, row in enumerate(rows[:15])])
     count = slots.shape[0]
-    tiles = [slots[slot_of(k, count, 2), 16:24] for k in range(count)]
+    tiles = [wide_tile(slots)(slot_of(k, count, 2)) for k in range(count)]
     between = tree([face_energy(a, b) for a, b in zip(tiles, tiles[1:])])
     last = whole_sum(between) - whole_sum(pull)
-    line = total[15:16] + jnp.where(lanes()[0:1] == 5, last, 0.0)
+    line = rows[15] + jnp.where(lanes()[0:1] == 5, last, 0.0)
     for k in range(sent.shape[0]):
         sent[k] = line
 
@@ -454,11 +490,10 @@
 def combine_kernel(
     lines, slots, near, flow, extra, inverse, cond, cell, well, factor, w0, w1, w2, solved, rest
 ):
-    total = jnp.sum(slots[...], axis=0)
-    low, high = halo_tiles(near, slots, lambda a: a[16:24], 2)
+    low, high = halo_tiles(near, slots, wide_tile(slots), 2)
     whole = flow_along(w2, flow, cond, low, high)
     scale_row = get_well_rows(inverse[...], 1)[0]
-    means = [r * scale_row for r in get_well_rows(total, 3)]
+    means = [r * scale_row for r in well_rows(slot_rows(slots, 0, 15))]
     row, lane = cell_masks(cell[0])
     w3 = advance(means, whole, w2, extra[...], factor[0], row, lane, well_mask(well[0]))
 
@@ -554,7 +589,8 @@
         a.reshape(block) for a in (right_side, block_diag, block_off, mobility)
     )
     perfs = (perf_cell, perf_well, perf_factor)
-    sent_shapes = [(lax.axis_size("gz") // NEAR, 24, 128), (2, 8, 128)]
+    groups = lax.axis_size("gz") // NEAR
+    near_shape = (2, 8, 128)
 
     table, *faces = call(
         first_kernel, [(NEAR, 24, 128)] + face_shapes(2), right, mob, *perfs,
@@ -563,7 +599,7 @@
         + [pltpu.VMEM(a.shape, a.dtype) for a in perfs]
         + [pltpu.SemaphoreType.DMA((5,))],
     )
-    sent, near = call(first_near_kernel, sent_shapes, near_slots(table))
+    sent, near = call(first_near_kernel, [(groups, 24, 128), near_shape], near_slots(table))
     sent, *faces = after(sent, *faces)
     slots = far_slots(sent, 0)
     flow, cond = call(
@@ -576,7 +612,7 @@
         slots, near, flow, right, mob, *perfs,
     )
 
-    sent, near = call(near_kernel, sent_shapes, near_slots(copies(table)))
+    sent, near = call(near_kernel, [(groups, 17, 1, 128), near_shape], near_slots(copies(table)))
     sent, *faces = after(sent, *faces)
     slots = far_slots(sent, 1)
     flow = call(
@@ -592,7 +628,7 @@
         moment_kernel, [(24, 128)],
         table, right, w1, w2, extra, diag, off, cond, cond_along, *low,
     )[0]
-    sent, near = call(last_near_kernel, sent_shapes, near_slots(copies(table)))
+    sent, near = call(last_near_kernel, [(groups, 20, 1, 128), near_shape], near_slots(copies(table)))
     sent, *faces = after(sent, *faces)
     slots = far_slots(sent, 2)
     high = high_halos(faces)

time: 164 us -> 163 us (level)
  waiting for transfers between devices: 10.6 us -> 12.4 us
  transfers between devices with their start and end apart: 15 -> 15, of which waited for: 4 -> 5; matrix products, arithmetic and copies ran while one was open for 0% -> 0% of each run, Pallas kernels for 0% -> 0%
where the time goes in v7:
time: 163 us; the launch traced here: 162 us
  starting transfers between devices  102 us (63%)
  blocking collectives  38.4 us (24%)
  waiting for transfers between devices  12.4 us (8%)
  Pallas kernels  8.32 us (5%)
    all_to_all x3, starting transfers between devices, far_slots(): return lax.all_to_all(sent, 'gz', 0, 0, axis_index_groups=groups)  64.1 us
    ppermute x6, starting transfers between devices, forward(): return lax.ppermute(piece, axis, [(i, i + 1) for i in range(count - 1)])  27.6 us
    all_to_all x3, blocking collectives, near_slots(): return lax.all_to_all(sent, 'gz', 0, 0, axis_index_groups=groups)  24.8 us
    all_to_all x1, blocking collectives, body(): lines = lax.all_to_all(sent, ('gx', 'gy'), 0, 0)  13.6 us
    ppermute x6, waiting for transfers between devices, backward(): return lax.ppermute(piece, axis, [(i + 1, i) for i in range(count - 1)])  11.4 us
    ppermute x6, starting transfers between devices, backward(): return lax.ppermute(piece, axis, [(i + 1, i) for i in range(count - 1)])  9.97 us
    pallas_call x12, Pallas kernels, call(): pl.pallas_call(kernel, out_shape=[jax.ShapeDtypeStruct(shape, F32) for sh...  8.32 us
  transfers between devices with their start and end apart: 15, of which 5 were waited for; matrix products, arithmetic and copies ran while one was open for 0% of the time, Pallas kernels for 0%

profile of v7, /device:TPU:1, one launch (start us, length us, event | category | flops | bytes accessed | tf_op | source)
XLA Modules:
  0.0 162.3 jit_solution(17411635636427439999)
XLA Ops:
  0.6 2.0 %shard_map.86 = (f32[4,24,128]{2,1,0:T(8,128)}, f32[6,8,128]{2,1,0:T(8,128)}, f32[6,8,128]{2,1,0:T(8,128)}, f32[24,128]{1,0:T(8,128)}, f32[24,128]{1,0:T(8,128)}) custom-call(f32[3,32,128]{2,1,0:T(8,128)} %bitcast.6, f32[3,32,128]{2,1,0:T(8,128)} %bitcast.19, s32[1,1,512]{2,1,0:T(1,128)} %cell.5, s32[1,1,512]{2,1,0:T(1,128)} %well.5, f32[1,1,512]{2,1,0:T(1,128)} %factor.5), custom_call_target="tpu_custom_call" | custom-call | tf_op jit(solution)/shard_map/pallas_call | solution.py:529
  2.7 11.0 %all_to_all.35.slots = f32[4,24,128]{2,1,0:T(8,128)S(1)} all-to-all(f32[4,24,128]{2,1,0:T(8,128)} %get-tuple-element.47), channel_id=1, replica_groups={{0,1,2,3},{4,5,6,7},{8,9,10,11},{12,13,14,15},{16,17,18,19},{20,21,22,2..., dimensions={0} | all-to-all | bytes 98304 | tf_op jit(solution)/shard_map/all_to_all | solution.py:545
  13.7 0.8 shard_map.87
  14.5 26.8 %all-to-all-start.1 = ((f32[8,24,128]{2,1,0:T(8,128)}), f32[8,24,128]{2,1,0:T(8,128)S(1)}, u32[]{:S(2)}, u32[]{:S(2)}) async-start(f32[8,24,128]{2,1,0:T(8,128)} %get-tuple-element.53), calls=%async_computation.1 | async-start | bytes 196608 | tf_op jit(solution)/shard_map/all_to_all | solution.py:557
  41.3 3.1 %collective-permute-start = (f32[6,8,128]{2,1,0:T(8,128)S(1)}, f32[6,8,128]{2,1,0:T(8,128)S(1)}, u32[]{:S(2)}, u32[]{:S(2)}) collective-permute-start(f32[6,8,128]{2,1,0:T(8,128)S(1)} %copy-done.8), channel_id=1, source_target_pairs={{0,256},{256,512},{512,768},{1,257},{257,513},{513,769},{2,258},{2... | collective-permute-start | bytes 73736 | tf_op jit(solution)/shard_map/ppermute | solution.py:562
  44.4 1.3 collective-permute-start.2
  45.7 5.9 %collective-permute-start.1 = (f32[24,128]{1,0:T(8,128)S(1)}, f32[24,128]{1,0:T(8,128)S(1)}, u32[]{:S(2)}, u32[]{:S(2)}) collective-permute-start(f32[24,128]{1,0:T(8,128)S(1)} %copy-done.10), channel_id=1, source_target_pairs={{0,32},{32,64},{64,96},{96,128},{128,160},{160,192},{192,224},{1,3... | collective-permute-start | bytes 36872 | tf_op jit(solution)/shard_map/ppermute | solution.py:562
  51.6 1.9 %collective-permute-start.3 = (f32[24,128]{1,0:T(8,128)S(1)}, f32[24,128]{1,0:T(8,128)S(1)}, u32[]{:S(2)}, u32[]{:S(2)}) collective-permute-start(f32[24,128]{1,0:T(8,128)S(1)} %copy-done.9), channel_id=1, source_target_pairs={{32,0},{64,32},{96,64},{128,96},{160,128},{192,160},{224,192},{33,... | collective-permute-start | bytes 36872 | tf_op jit(solution)/shard_map/ppermute | solution.py:567
  53.6 3.1 %collective-permute-done.3.yh = f32[24,128]{1,0:T(8,128)S(1)} collective-permute-done((f32[24,128]{1,0:T(8,128)S(1)}, f32[24,128]{1,0:T(8,128)S(1)}, u32[]{:S(2)}, u32[]{:S(2)}) %collective-permute-start.3) | collective-permute-done | bytes 12320 | tf_op jit(solution)/shard_map/ppermute | solution.py:567
  56.8 0.6 copy-done.5
  57.5 1.2 shard_map.89
  58.7 6.9 %all_to_all.36.slots = f32[4,24,128]{2,1,0:T(8,128)S(1)} all-to-all(f32[4,24,128]{2,1,0:T(8,128)S(1)} %broadcast_in_dim.4), channel_id=1, replica_groups={{0,1,2,3},{4,5,6,7},{8,9,10,11},{12,13,14,15},{16,17,18,19},{20,21,22,2..., dimensions={0} | all-to-all | bytes 98304 | tf_op jit(solution)/shard_map/all_to_all | solution.py:545
  65.6 0.7 shard_map.90
  66.3 16.3 %all-to-all-start.3 = ((f32[8,17,1,128]{3,2,1,0:T(1,128)}), f32[8,17,1,128]{3,2,1,0:T(1,128)S(1)}, u32[]{:S(2)}, u32[]{:S(2)}) async-start(f32[8,17,1,128]{3,2,1,0:T(1,128)} %get-tuple-element.66), calls=%async_computation.3 | async-start | bytes 139264 | tf_op jit(solution)/shard_map/all_to_all | solution.py:557
  82.6 4.3 %collective-permute-start.4 = (f32[3,8,128]{2,1,0:T(8,128)S(1)}, f32[3,8,128]{2,1,0:T(8,128)S(1)}, u32[]{:S(2)}, u32[]{:S(2)}) collective-permute-start(f32[3,8,128]{2,1,0:T(8,128)S(1)} %get-tuple-element.70), channel_id=1, source_target_pairs={{0,256},{256,512},{512,768},{1,257},{257,513},{513,769},{2,258},{2... | collective-permute-start | bytes 36872 | tf_op jit(solution)/shard_map/ppermute | solution.py:562
  86.9 1.3 collective-permute-start.6
  88.2 4.0 %collective-permute-start.5 = (f32[12,128]{1,0:T(8,128)S(1)}, f32[12,128]{1,0:T(8,128)S(1)}, u32[]{:S(2)}, u32[]{:S(2)}) collective-permute-start(f32[12,128]{1,0:T(8,128)S(1)} %get-tuple-element.71), channel_id=1, source_target_pairs={{0,32},{32,64},{64,96},{96,128},{128,160},{160,192},{192,224},{1,3... | collective-permute-start | bytes 18440 | tf_op jit(solution)/shard_map/ppermute | solution.py:562
  92.1 1.9 %collective-permute-start.7 = (f32[12,128]{1,0:T(8,128)S(1)}, f32[12,128]{1,0:T(8,128)S(1)}, u32[]{:S(2)}, u32[]{:S(2)}) collective-permute-start(f32[12,128]{1,0:T(8,128)S(1)} %get-tuple-element.73), channel_id=1, source_target_pairs={{32,0},{64,32},{96,64},{128,96},{160,128},{192,160},{224,192},{33,... | collective-permute-start | bytes 18440 | tf_op jit(solution)/shard_map/ppermute | solution.py:567
  94.1 3.3 %collective-permute-done.7.yh = f32[12,128]{1,0:T(8,128)S(1)} collective-permute-done((f32[12,128]{1,0:T(8,128)S(1)}, f32[12,128]{1,0:T(8,128)S(1)}, u32[]{:S(2)}, u32[]{:S(2)}) %collective-permute-start.7) | collective-permute-done | bytes 6176 | tf_op jit(solution)/shard_map/ppermute | solution.py:567
  97.7 1.1 shard_map.92
  98.8 6.5 %collective-permute-start.8 = (f32[3,8,128]{2,1,0:T(8,128)S(1)}, f32[3,8,128]{2,1,0:T(8,128)S(1)}, u32[]{:S(2)}, u32[]{:S(2)}) collective-permute-start(f32[3,8,128]{2,1,0:T(8,128)S(1)} %get-tuple-element.79), channel_id=1, source_target_pairs={{0,256},{256,512},{512,768},{1,257},{257,513},{513,769},{2,258},{2... | collective-permute-start | bytes 36872 | tf_op jit(solution)/shard_map/ppermute | solution.py:562
  105.2 3.8 %collective-permute-start.9 = (f32[12,128]{1,0:T(8,128)S(1)}, f32[12,128]{1,0:T(8,128)S(1)}, u32[]{:S(2)}, u32[]{:S(2)}) collective-permute-start(f32[12,128]{1,0:T(8,128)S(1)} %get-tuple-element.80), channel_id=1, source_target_pairs={{0,32},{32,64},{64,96},{96,128},{128,160},{160,192},{192,224},{1,3... | collective-permute-start | bytes 18440 | tf_op jit(solution)/shard_map/ppermute | solution.py:562
  109.1 0.8 collective-permute-done.9.yl
  110.0 6.9 %all_to_all.37.slots = f32[4,24,128]{2,1,0:T(8,128)S(1)} all-to-all(f32[4,24,128]{2,1,0:T(8,128)S(1)} %broadcast_in_dim.5), channel_id=1, replica_groups={{0,1,2,3},{4,5,6,7},{8,9,10,11},{12,13,14,15},{16,17,18,19},{20,21,22,2..., dimensions={0} | all-to-all | bytes 98304 | tf_op jit(solution)/shard_map/all_to_all | solution.py:545
  116.9 0.8 shard_map.94
  117.7 21.1 %all-to-all-start.5 = ((f32[8,20,1,128]{3,2,1,0:T(1,128)}), f32[8,20,1,128]{3,2,1,0:T(1,128)S(1)}, u32[]{:S(2)}, u32[]{:S(2)}) async-start(f32[8,20,1,128]{3,2,1,0:T(1,128)} %get-tuple-element.84), calls=%async_computation.5 | async-start | bytes 163840 | tf_op jit(solution)/shard_map/all_to_all | solution.py:557
  138.8 1.3 collective-permute-start.10
  140.1 2.3 %collective-permute-start.11 = (f32[12,128]{1,0:T(8,128)S(1)}, f32[12,128]{1,0:T(8,128)S(1)}, u32[]{:S(2)}, u32[]{:S(2)}) collective-permute-start(f32[12,128]{1,0:T(8,128)S(1)} %get-tuple-element.86), channel_id=1, source_target_pairs={{32,0},{64,32},{96,64},{128,96},{160,128},{192,160},{224,192},{33,... | collective-permute-start | bytes 18440 | tf_op jit(solution)/shard_map/ppermute | solution.py:567
  142.4 5.0 %collective-permute-done.11.yh = f32[12,128]{1,0:T(8,128)S(1)} collective-permute-done((f32[12,128]{1,0:T(8,128)S(1)}, f32[12,128]{1,0:T(8,128)S(1)}, u32[]{:S(2)}, u32[]{:S(2)}) %collective-permute-start.11) | collective-permute-done | bytes 6176 | tf_op jit(solution)/shard_map/ppermute | solution.py:567
  147.4 0.2 shard_map.96
  147.6 13.6 %all_to_all.38.lines = f32[32,1,128]{2,1,0:T(1,128)S(1)} all-to-all(f32[32,1,128]{2,1,0:T(1,128)S(1)} %shard_map.96), channel_id=1, replica_groups=mesh['gx'=4,'gy'=8,'gz'=32] {'gx','gy'}, dimensions={0} | all-to-all | bytes 32768 | tf_op jit(solution)/shard_map/all_to_all | solution.py:640
  161.2 1.2 shard_map.97
  (38 shorter events, 0.8 us)
Async XLA Ops:
  2.7 43.0 %copy-start.10 = (f32[24,128]{1,0:T(8,128)S(1)}, f32[24,128]{1,0:T(8,128)}, u32[]{:S(2)}) copy-start(f32[24,128]{1,0:T(8,128)} %get-tuple-element.56) | copy-start | bytes 36868
  13.7 27.6 %copy-start.8 = (f32[6,8,128]{2,1,0:T(8,128)S(1)}, f32[6,8,128]{2,1,0:T(8,128)}, u32[]{:S(2)}) copy-start(f32[6,8,128]{2,1,0:T(8,128)} %get-tuple-element.55) | copy-start | bytes 73732
  13.7 30.7 %copy-start.7 = (f32[6,8,128]{2,1,0:T(8,128)S(1)}, f32[6,8,128]{2,1,0:T(8,128)}, u32[]{:S(2)}) copy-start(f32[6,8,128]{2,1,0:T(8,128)} %get-tuple-element.57) | copy-start | bytes 73732
  13.7 37.9 %copy-start.9 = (f32[24,128]{1,0:T(8,128)S(1)}, f32[24,128]{1,0:T(8,128)}, u32[]{:S(2)}) copy-start(f32[24,128]{1,0:T(8,128)} %get-tuple-element.58) | copy-start | bytes 36868
  14.5 42.2 %copy-start = (f32[3,4,8,128]{3,2,1,0:T(8,128)S(1)}, f32[3,4,8,128]{3,2,1,0:T(8,128)}, u32[]{:S(2)}) copy-start(f32[3,4,8,128]{3,2,1,0:T(8,128)} %param.7) | copy-start | bytes 147460
  14.5 42.2 %copy-start.1 = (f32[3,4,8,128]{3,2,1,0:T(8,128)S(1)}, f32[3,4,8,128]{3,2,1,0:T(8,128)}, u32[]{:S(2)}) copy-start(f32[3,4,8,128]{3,2,1,0:T(8,128)} %param.8) | copy-start | bytes 147460
  14.5 42.2 %copy-start.2 = (f32[3,4,8,128]{3,2,1,0:T(8,128)S(1)}, f32[3,4,8,128]{3,2,1,0:T(8,128)}, u32[]{:S(2)}) copy-start(f32[3,4,8,128]{3,2,1,0:T(8,128)} %param.9) | copy-start | bytes 147460
  14.5 42.2 %copy-start.3 = (f32[3,4,8,128]{3,2,1,0:T(8,128)S(1)}, f32[3,4,8,128]{3,2,1,0:T(8,128)}, u32[]{:S(2)}) copy-start(f32[3,4,8,128]{3,2,1,0:T(8,128)} %param.10) | copy-start | bytes 147460
  14.5 42.3 %all-to-all-start.1 = ((f32[8,24,128]{2,1,0:T(8,128)}), f32[8,24,128]{2,1,0:T(8,128)S(1)}, u32[]{:S(2)}, u32[]{:S(2)}) async-start(f32[8,24,128]{2,1,0:T(8,128)} %get-tuple-element.53), calls=%async_computation.1 | async-start | bytes 196608 | tf_op jit(solution)/shard_map/all_to_all | solution.py:557
  41.3 15.4 %collective-permute-start = (f32[6,8,128]{2,1,0:T(8,128)S(1)}, f32[6,8,128]{2,1,0:T(8,128)S(1)}, u32[]{:S(2)}, u32[]{:S(2)}) collective-permute-start(f32[6,8,128]{2,1,0:T(8,128)S(1)} %copy-done.8), channel_id=1, source_target_pairs={{0,256},{256,512},{512,768},{1,257},{257,513},{513,769},{2,258},{2... | collective-permute-start | bytes 73736 | tf_op jit(solution)/shard_map/ppermute | solution.py:562
  44.4 12.3 %collective-permute-start.2 = (f32[6,8,128]{2,1,0:T(8,128)S(1)}, f32[6,8,128]{2,1,0:T(8,128)S(1)}, u32[]{:S(2)}, u32[]{:S(2)}) collective-permute-start(f32[6,8,128]{2,1,0:T(8,128)S(1)} %copy-done.7), channel_id=1, source_target_pairs={{256,0},{512,256},{768,512},{257,1},{513,257},{769,513},{258,2},{5... | collective-permute-start | bytes 73736 | tf_op jit(solution)/shard_map/ppermute | solution.py:567
  45.7 7.9 %collective-permute-start.1 = (f32[24,128]{1,0:T(8,128)S(1)}, f32[24,128]{1,0:T(8,128)S(1)}, u32[]{:S(2)}, u32[]{:S(2)}) collective-permute-start(f32[24,128]{1,0:T(8,128)S(1)} %copy-done.10), channel_id=1, source_target_pairs={{0,32},{32,64},{64,96},{96,128},{128,160},{160,192},{192,224},{1,3... | collective-permute-start | bytes 36872 | tf_op jit(solution)/shard_map/ppermute | solution.py:562
  51.6 5.0 %collective-permute-start.3 = (f32[24,128]{1,0:T(8,128)S(1)}, f32[24,128]{1,0:T(8,128)S(1)}, u32[]{:S(2)}, u32[]{:S(2)}) collective-permute-start(f32[24,128]{1,0:T(8,128)S(1)} %copy-done.9), channel_id=1, source_target_pairs={{32,0},{64,32},{96,64},{128,96},{160,128},{192,160},{224,192},{33,... | collective-permute-start | bytes 36872 | tf_op jit(solution)/shard_map/ppermute | solution.py:567
  56.7 0.7 copy-start.5
  56.7 0.7 copy-start.6
  56.8 0.7 copy-start.4
  66.3 31.3 %all-to-all-start.3 = ((f32[8,17,1,128]{3,2,1,0:T(1,128)}), f32[8,17,1,128]{3,2,1,0:T(1,128)S(1)}, u32[]{:S(2)}, u32[]{:S(2)}) async-start(f32[8,17,1,128]{3,2,1,0:T(1,128)} %get-tuple-element.66), calls=%async_computation.3 | async-start | bytes 139264 | tf_op jit(solution)/shard_map/all_to_all | solution.py:557
  82.6 14.8 %collective-permute-start.4 = (f32[3,8,128]{2,1,0:T(8,128)S(1)}, f32[3,8,128]{2,1,0:T(8,128)S(1)}, u32[]{:S(2)}, u32[]{:S(2)}) collective-permute-start(f32[3,8,128]{2,1,0:T(8,128)S(1)} %get-tuple-element.70), channel_id=1, source_target_pairs={{0,256},{256,512},{512,768},{1,257},{257,513},{513,769},{2,258},{2... | collective-permute-start | bytes 36872 | tf_op jit(solution)/shard_map/ppermute | solution.py:562
  86.9 10.6 %collective-permute-start.6 = (f32[3,8,128]{2,1,0:T(8,128)S(1)}, f32[3,8,128]{2,1,0:T(8,128)S(1)}, u32[]{:S(2)}, u32[]{:S(2)}) collective-permute-start(f32[3,8,128]{2,1,0:T(8,128)S(1)} %get-tuple-element.72), channel_id=1, source_target_pairs={{256,0},{512,256},{768,512},{257,1},{513,257},{769,513},{258,2},{5... | collective-permute-start | bytes 36872 | tf_op jit(solution)/shard_map/ppermute | solution.py:567
  88.2 5.9 %collective-permute-start.5 = (f32[12,128]{1,0:T(8,128)S(1)}, f32[12,128]{1,0:T(8,128)S(1)}, u32[]{:S(2)}, u32[]{:S(2)}) collective-permute-start(f32[12,128]{1,0:T(8,128)S(1)} %get-tuple-element.71), channel_id=1, source_target_pairs={{0,32},{32,64},{64,96},{96,128},{128,160},{160,192},{192,224},{1,3... | collective-permute-start | bytes 18440 | tf_op jit(solution)/shard_map/ppermute | solution.py:562
  92.1 5.3 %collective-permute-start.7 = (f32[12,128]{1,0:T(8,128)S(1)}, f32[12,128]{1,0:T(8,128)S(1)}, u32[]{:S(2)}, u32[]{:S(2)}) collective-permute-start(f32[12,128]{1,0:T(8,128)S(1)} %get-tuple-element.73), channel_id=1, source_target_pairs={{32,0},{64,32},{96,64},{128,96},{160,128},{192,160},{224,192},{33,... | collective-permute-start | bytes 18440 | tf_op jit(solution)/shard_map/ppermute | solution.py:567
  98.8 11.1 %collective-permute-start.8 = (f32[3,8,128]{2,1,0:T(8,128)S(1)}, f32[3,8,128]{2,1,0:T(8,128)S(1)}, u32[]{:S(2)}, u32[]{:S(2)}) collective-permute-start(f32[3,8,128]{2,1,0:T(8,128)S(1)} %get-tuple-element.79), channel_id=1, source_target_pairs={{0,256},{256,512},{512,768},{1,257},{257,513},{513,769},{2,258},{2... | collective-permute-start | bytes 36872 | tf_op jit(solution)/shard_map/ppermute | solution.py:562
  105.2 4.6 %collective-permute-start.9 = (f32[12,128]{1,0:T(8,128)S(1)}, f32[12,128]{1,0:T(8,128)S(1)}, u32[]{:S(2)}, u32[]{:S(2)}) collective-permute-start(f32[12,128]{1,0:T(8,128)S(1)} %get-tuple-element.80), channel_id=1, source_target_pairs={{0,32},{32,64},{64,96},{96,128},{128,160},{160,192},{192,224},{1,3... | collective-permute-start | bytes 18440 | tf_op jit(solution)/shard_map/ppermute | solution.py:562
  117.7 29.6 %all-to-all-start.5 = ((f32[8,20,1,128]{3,2,1,0:T(1,128)}), f32[8,20,1,128]{3,2,1,0:T(1,128)S(1)}, u32[]{:S(2)}, u32[]{:S(2)}) async-start(f32[8,20,1,128]{3,2,1,0:T(1,128)} %get-tuple-element.84), calls=%async_computation.5 | async-start | bytes 163840 | tf_op jit(solution)/shard_map/all_to_all | solution.py:557
  138.8 8.5 %collective-permute-start.10 = (f32[3,8,128]{2,1,0:T(8,128)S(1)}, f32[3,8,128]{2,1,0:T(8,128)S(1)}, u32[]{:S(2)}, u32[]{:S(2)}) collective-permute-start(f32[3,8,128]{2,1,0:T(8,128)S(1)} %get-tuple-element.85), channel_id=1, source_target_pairs={{256,0},{512,256},{768,512},{257,1},{513,257},{769,513},{258,2},{5... | collective-permute-start | bytes 36872 | tf_op jit(solution)/shard_map/ppermute | solution.py:567
  140.1 7.2 %collective-permute-start.11 = (f32[12,128]{1,0:T(8,128)S(1)}, f32[12,128]{1,0:T(8,128)S(1)}, u32[]{:S(2)}, u32[]{:S(2)}) collective-permute-start(f32[12,128]{1,0:T(8,128)S(1)} %get-tuple-element.86), channel_id=1, source_target_pairs={{32,0},{64,32},{96,64},{128,96},{160,128},{192,160},{224,192},{33,... | collective-permute-start | bytes 18440 | tf_op jit(solution)/shard_map/ppermute | solution.py:567

commit v8 on v7

--- a/solution.py
+++ b/solution.py
@@ -428,7 +428,9 @@
     return terms[0]
 
 
-def moment_kernel(wells_table, w0, w1, w2, extra, diag, off, cond, cond_along, xl, yl, table):
+def moment_kernel(
+    wells_table, w0, w1, w2, extra, diag, off, cond, cond_along, xl, yl, xh, yh, table, flow
+):
     lane, sub = lanes(), lax.broadcasted_iota(jnp.int32, (8, 128), 0)
     sums = [[] for _ in range(6)]
     for u in range(3):
@@ -437,9 +439,13 @@
             a, b, c = w0[u, rows], w1[u, rows], w2[u, rows]
             for k, (p, q) in enumerate(((a, a), (a, b), (b, b), (b, c), (c, c))):
                 sums[k].append(p * q)
-            energy = c * (block_row(w2, diag, off, u, rows) + extra[rows] * c)
-            for d, near in enumerate(low_views(w2, 0, u, x, (xl, yl), sub)):
-                energy = energy + cond[d, u, rows] * (c - near) * (c - near)
+            total = block_row(w2, diag, off, u, rows)
+            near = low_views(w2, 0, u, x, (xl, yl), sub)
+            near += high_views(w2, 0, u, x, (xh, yh), sub)
+            for d in range(4):
+                total = total + cond[d, u, rows] * (c - near[d])
+            flow[u, rows] = total
+            energy = c * (total + extra[rows] * c)
             step = jnp.where(lane == 0, 0.0, c - pltpu.roll(c, 1, 1))
             sums[5].append(energy + cond_along[0, u, rows] * step * step)
     line = jnp.zeros((1, 128), F32)
@@ -623,17 +629,15 @@
         slots, near, flow, w1, extra, inverse, cond_along, *perfs,
     )
 
-    low = low_halos(faces)
-    table = call(
-        moment_kernel, [(24, 128)],
-        table, right, w1, w2, extra, diag, off, cond, cond_along, *low,
-    )[0]
-    sent, near = call(last_near_kernel, [(groups, 20, 1, 128), near_shape], near_slots(copies(table)))
-    sent, *faces = after(sent, *faces)
+    table, flow = call(
+        moment_kernel, [(24, 128), block],
+        table, right, w1, w2, extra, diag, off, cond, cond_along,
+        *low_halos(faces), *high_halos(faces),
+    )
+    sent, near = call(
+        last_near_kernel, [(groups, 20, 1, 128), near_shape], near_slots(copies(table))
+    )
     slots = far_slots(sent, 2)
-    high = high_halos(faces)
-    flow = call(flow_kernel, [block], w2, diag, off, cond, *low, *high)[0]
-    slots, flow = after(slots, flow)
 
     count = lax.axis_size("gx") * lax.axis_size("gy")
     sent = call(scalar_kernel, [(count, 1, 128)], slots, inverse)[0]

time: 163 us -> 168 us (1.031)
  blocking collectives: 38.4 us -> 67.6 us
  starting transfers between devices: 102 us -> 80.2 us
  waiting for transfers between devices: 12.4 us -> 9.66 us
    all_to_all x0 -> x1, blocking collectives: none -> 29.1 us  [far_slots(): return lax.all_to_all(sent, 'gz', 0, 0, axis_index_groups=groups)]
    all_to_all x3 -> x2, starting transfers between devices: 64.1 us -> 43 us  [far_slots(): return lax.all_to_all(sent, 'gz', 0, 0, axis_index_groups=groups)]
    ppermute x6, waiting for transfers between devices: 11.4 us -> 9.44 us  [backward(): return lax.ppermute(piece, axis, [(i + 1, i) for i in range(count - 1)])]
    pallas_call x12 -> x11, Pallas kernels: 8.32 us -> 7.63 us  [call(): pl.pallas_call(kernel, out_shape=[jax.ShapeDtypeStruct(shape, F32) for sh...]
  transfers between devices with their start and end apart: 15 -> 14, of which waited for: 5 -> 4; matrix products, arithmetic and copies ran while one was open for 0% -> 0% of each run, Pallas kernels for 0% -> 0%
where the time goes in v8:
time: 168 us; the launch traced here: 167 us
  starting transfers between devices  80.2 us (48%)
  blocking collectives  67.6 us (40%)
  waiting for transfers between devices  9.66 us (6%)
  Pallas kernels  7.63 us (5%)
    all_to_all x2, starting transfers between devices, far_slots(): return lax.all_to_all(sent, 'gz', 0, 0, axis_index_groups=groups)  43 us
    all_to_all x1, blocking collectives, far_slots(): return lax.all_to_all(sent, 'gz', 0, 0, axis_index_groups=groups)  29.1 us
    ppermute x6, starting transfers between devices, forward(): return lax.ppermute(piece, axis, [(i, i + 1) for i in range(count - 1)])  27.6 us
    all_to_all x3, blocking collectives, near_slots(): return lax.all_to_all(sent, 'gz', 0, 0, axis_index_groups=groups)  24.8 us
    all_to_all x1, blocking collectives, body(): lines = lax.all_to_all(sent, ('gx', 'gy'), 0, 0)  13.7 us
    ppermute x6, starting transfers between devices, backward(): return lax.ppermute(piece, axis, [(i + 1, i) for i in range(count - 1)])  9.64 us
    ppermute x6, waiting for transfers between devices, backward(): return lax.ppermute(piece, axis, [(i + 1, i) for i in range(count - 1)])  9.44 us
    pallas_call x11, Pallas kernels, call(): pl.pallas_call(kernel, out_shape=[jax.ShapeDtypeStruct(shape, F32) for sh...  7.63 us
  transfers between devices with their start and end apart: 14, of which 4 were waited for; matrix products, arithmetic and copies ran while one was open for 0% of the time, Pallas kernels for 0%

profile of v8, /device:TPU:1, one launch (start us, length us, event | category | flops | bytes accessed | tf_op | source)
XLA Modules:
  0.0 166.8 jit_solution(15311008466213103213)
XLA Ops:
  0.6 2.0 %shard_map.86 = (f32[4,24,128]{2,1,0:T(8,128)}, f32[6,8,128]{2,1,0:T(8,128)}, f32[6,8,128]{2,1,0:T(8,128)}, f32[24,128]{1,0:T(8,128)}, f32[24,128]{1,0:T(8,128)}) custom-call(f32[3,32,128]{2,1,0:T(8,128)} %bitcast.6, f32[3,32,128]{2,1,0:T(8,128)} %bitcast.17, s32[1,1,512]{2,1,0:T(1,128)} %cell.5, s32[1,1,512]{2,1,0:T(1,128)} %well.5, f32[1,1,512]{2,1,0:T(1,128)} %factor.5), custom_call_target="tpu_custom_call" | custom-call | tf_op jit(solution)/shard_map/pallas_call | solution.py:535
  2.7 11.0 %all_to_all.35.slots = f32[4,24,128]{2,1,0:T(8,128)S(1)} all-to-all(f32[4,24,128]{2,1,0:T(8,128)} %get-tuple-element.44), channel_id=1, replica_groups={{0,1,2,3},{4,5,6,7},{8,9,10,11},{12,13,14,15},{16,17,18,19},{20,21,22,2..., dimensions={0} | all-to-all | bytes 98304 | tf_op jit(solution)/shard_map/all_to_all | solution.py:551
  13.7 0.8 shard_map.87
  14.5 26.8 %all-to-all-start.1 = ((f32[8,24,128]{2,1,0:T(8,128)}), f32[8,24,128]{2,1,0:T(8,128)S(1)}, u32[]{:S(2)}, u32[]{:S(2)}) async-start(f32[8,24,128]{2,1,0:T(8,128)} %get-tuple-element.50), calls=%async_computation.1 | async-start | bytes 196608 | tf_op jit(solution)/shard_map/all_to_all | solution.py:563
  41.3 3.1 %collective-permute-start = (f32[6,8,128]{2,1,0:T(8,128)S(1)}, f32[6,8,128]{2,1,0:T(8,128)S(1)}, u32[]{:S(2)}, u32[]{:S(2)}) collective-permute-start(f32[6,8,128]{2,1,0:T(8,128)S(1)} %copy-done.8), channel_id=1, source_target_pairs={{0,256},{256,512},{512,768},{1,257},{257,513},{513,769},{2,258},{2... | collective-permute-start | bytes 73736 | tf_op jit(solution)/shard_map/ppermute | solution.py:568
  44.4 1.3 collective-permute-start.2
  45.7 5.9 %collective-permute-start.1 = (f32[24,128]{1,0:T(8,128)S(1)}, f32[24,128]{1,0:T(8,128)S(1)}, u32[]{:S(2)}, u32[]{:S(2)}) collective-permute-start(f32[24,128]{1,0:T(8,128)S(1)} %copy-done.10), channel_id=1, source_target_pairs={{0,32},{32,64},{64,96},{96,128},{128,160},{160,192},{192,224},{1,3... | collective-permute-start | bytes 36872 | tf_op jit(solution)/shard_map/ppermute | solution.py:568
  51.6 1.9 %collective-permute-start.3 = (f32[24,128]{1,0:T(8,128)S(1)}, f32[24,128]{1,0:T(8,128)S(1)}, u32[]{:S(2)}, u32[]{:S(2)}) collective-permute-start(f32[24,128]{1,0:T(8,128)S(1)} %copy-done.9), channel_id=1, source_target_pairs={{32,0},{64,32},{96,64},{128,96},{160,128},{192,160},{224,192},{33,... | collective-permute-start | bytes 36872 | tf_op jit(solution)/shard_map/ppermute | solution.py:573
  53.6 3.1 %collective-permute-done.3.yh = f32[24,128]{1,0:T(8,128)S(1)} collective-permute-done((f32[24,128]{1,0:T(8,128)S(1)}, f32[24,128]{1,0:T(8,128)S(1)}, u32[]{:S(2)}, u32[]{:S(2)}) %collective-permute-start.3) | collective-permute-done | bytes 12320 | tf_op jit(solution)/shard_map/ppermute | solution.py:573
  56.8 0.6 copy-done.5
  57.5 1.2 shard_map.89
  58.7 6.9 %all_to_all.36.slots = f32[4,24,128]{2,1,0:T(8,128)S(1)} all-to-all(f32[4,24,128]{2,1,0:T(8,128)S(1)} %broadcast_in_dim.4), channel_id=1, replica_groups={{0,1,2,3},{4,5,6,7},{8,9,10,11},{12,13,14,15},{16,17,18,19},{20,21,22,2..., dimensions={0} | all-to-all | bytes 98304 | tf_op jit(solution)/shard_map/all_to_all | solution.py:551
  65.6 0.7 shard_map.90
  66.3 16.3 %all-to-all-start.3 = ((f32[8,17,1,128]{3,2,1,0:T(1,128)}), f32[8,17,1,128]{3,2,1,0:T(1,128)S(1)}, u32[]{:S(2)}, u32[]{:S(2)}) async-start(f32[8,17,1,128]{3,2,1,0:T(1,128)} %get-tuple-element.63), calls=%async_computation.3 | async-start | bytes 139264 | tf_op jit(solution)/shard_map/all_to_all | solution.py:563
  82.6 4.3 %collective-permute-start.4 = (f32[3,8,128]{2,1,0:T(8,128)S(1)}, f32[3,8,128]{2,1,0:T(8,128)S(1)}, u32[]{:S(2)}, u32[]{:S(2)}) collective-permute-start(f32[3,8,128]{2,1,0:T(8,128)S(1)} %get-tuple-element.67), channel_id=1, source_target_pairs={{0,256},{256,512},{512,768},{1,257},{257,513},{513,769},{2,258},{2... | collective-permute-start | bytes 36872 | tf_op jit(solution)/shard_map/ppermute | solution.py:568
  86.8 1.3 collective-permute-start.6
  88.1 4.0 %collective-permute-start.5 = (f32[12,128]{1,0:T(8,128)S(1)}, f32[12,128]{1,0:T(8,128)S(1)}, u32[]{:S(2)}, u32[]{:S(2)}) collective-permute-start(f32[12,128]{1,0:T(8,128)S(1)} %get-tuple-element.68), channel_id=1, source_target_pairs={{0,32},{32,64},{64,96},{96,128},{128,160},{160,192},{192,224},{1,3... | collective-permute-start | bytes 18440 | tf_op jit(solution)/shard_map/ppermute | solution.py:568
  92.1 1.9 %collective-permute-start.7 = (f32[12,128]{1,0:T(8,128)S(1)}, f32[12,128]{1,0:T(8,128)S(1)}, u32[]{:S(2)}, u32[]{:S(2)}) collective-permute-start(f32[12,128]{1,0:T(8,128)S(1)} %get-tuple-element.70), channel_id=1, source_target_pairs={{32,0},{64,32},{96,64},{128,96},{160,128},{192,160},{224,192},{33,... | collective-permute-start | bytes 18440 | tf_op jit(solution)/shard_map/ppermute | solution.py:573
  94.1 3.3 %collective-permute-done.7.yh = f32[12,128]{1,0:T(8,128)S(1)} collective-permute-done((f32[12,128]{1,0:T(8,128)S(1)}, f32[12,128]{1,0:T(8,128)S(1)}, u32[]{:S(2)}, u32[]{:S(2)}) %collective-permute-start.7) | collective-permute-done | bytes 6176 | tf_op jit(solution)/shard_map/ppermute | solution.py:573
  97.4 0.2 all-to-all-done.3.slots
  97.6 1.1 shard_map.92
  98.7 6.5 %collective-permute-start.8 = (f32[3,8,128]{2,1,0:T(8,128)S(1)}, f32[3,8,128]{2,1,0:T(8,128)S(1)}, u32[]{:S(2)}, u32[]{:S(2)}) collective-permute-start(f32[3,8,128]{2,1,0:T(8,128)S(1)} %get-tuple-element.76), channel_id=1, source_target_pairs={{0,256},{256,512},{512,768},{1,257},{257,513},{513,769},{2,258},{2... | collective-permute-start | bytes 36872 | tf_op jit(solution)/shard_map/ppermute | solution.py:568
  105.2 1.3 collective-permute-start.10
  106.5 3.8 %collective-permute-start.9 = (f32[12,128]{1,0:T(8,128)S(1)}, f32[12,128]{1,0:T(8,128)S(1)}, u32[]{:S(2)}, u32[]{:S(2)}) collective-permute-start(f32[12,128]{1,0:T(8,128)S(1)} %get-tuple-element.77), channel_id=1, source_target_pairs={{0,32},{32,64},{64,96},{96,128},{128,160},{160,192},{192,224},{1,3... | collective-permute-start | bytes 18440 | tf_op jit(solution)/shard_map/ppermute | solution.py:568
  110.4 1.9 %collective-permute-start.11 = (f32[12,128]{1,0:T(8,128)S(1)}, f32[12,128]{1,0:T(8,128)S(1)}, u32[]{:S(2)}, u32[]{:S(2)}) collective-permute-start(f32[12,128]{1,0:T(8,128)S(1)} %get-tuple-element.79), channel_id=1, source_target_pairs={{32,0},{64,32},{96,64},{128,96},{160,128},{192,160},{224,192},{33,... | collective-permute-start | bytes 18440 | tf_op jit(solution)/shard_map/ppermute | solution.py:573
  112.3 3.0 %collective-permute-done.11.yh = f32[12,128]{1,0:T(8,128)S(1)} collective-permute-done((f32[12,128]{1,0:T(8,128)S(1)}, f32[12,128]{1,0:T(8,128)S(1)}, u32[]{:S(2)}, u32[]{:S(2)}) %collective-permute-start.11) | collective-permute-done | bytes 6176 | tf_op jit(solution)/shard_map/ppermute | solution.py:573
  115.3 0.2 shard_map.93
  115.5 6.9 %all_to_all.37.slots = f32[4,24,128]{2,1,0:T(8,128)S(1)} all-to-all(f32[4,24,128]{2,1,0:T(8,128)S(1)} %broadcast_in_dim.5), channel_id=1, replica_groups={{0,1,2,3},{4,5,6,7},{8,9,10,11},{12,13,14,15},{16,17,18,19},{20,21,22,2..., dimensions={0} | all-to-all | bytes 98304 | tf_op jit(solution)/shard_map/all_to_all | solution.py:551
  122.6 29.1 %all_to_all.38.slots = f32[8,20,1,128]{3,2,1,0:T(1,128)S(1)} all-to-all(f32[8,20,1,128]{3,2,1,0:T(1,128)S(1)} %get-tuple-element.81), channel_id=1, replica_groups={{16,20,24,28,0,4,8,12},{17,21,25,29,1,5,9,13},{18,22,26,30,2,6,10,14},{..., dimensions={0} | all-to-all | bytes 163840 | tf_op jit(solution)/shard_map/all_to_all | solution.py:563
  151.7 0.2 shard_map.95
  151.9 13.7 %all_to_all.39.lines = f32[32,1,128]{2,1,0:T(1,128)S(1)} all-to-all(f32[32,1,128]{2,1,0:T(1,128)S(1)} %shard_map.95), channel_id=1, replica_groups=mesh['gx'=4,'gy'=8,'gz'=32] {'gx','gy'}, dimensions={0} | all-to-all | bytes 32768 | tf_op jit(solution)/shard_map/all_to_all | solution.py:644
  165.6 1.2 shard_map.96
  (36 shorter events, 0.5 us)
Async XLA Ops:
  2.7 43.0 %copy-start.10 = (f32[24,128]{1,0:T(8,128)S(1)}, f32[24,128]{1,0:T(8,128)}, u32[]{:S(2)}) copy-start(f32[24,128]{1,0:T(8,128)} %get-tuple-element.53) | copy-start | bytes 36868
  13.7 27.6 %copy-start.8 = (f32[6,8,128]{2,1,0:T(8,128)S(1)}, f32[6,8,128]{2,1,0:T(8,128)}, u32[]{:S(2)}) copy-start(f32[6,8,128]{2,1,0:T(8,128)} %get-tuple-element.52) | copy-start | bytes 73732
  13.7 30.7 %copy-start.7 = (f32[6,8,128]{2,1,0:T(8,128)S(1)}, f32[6,8,128]{2,1,0:T(8,128)}, u32[]{:S(2)}) copy-start(f32[6,8,128]{2,1,0:T(8,128)} %get-tuple-element.54) | copy-start | bytes 73732
  13.7 37.9 %copy-start.9 = (f32[24,128]{1,0:T(8,128)S(1)}, f32[24,128]{1,0:T(8,128)}, u32[]{:S(2)}) copy-start(f32[24,128]{1,0:T(8,128)} %get-tuple-element.55) | copy-start | bytes 36868
  14.5 42.2 %copy-start = (f32[3,4,8,128]{3,2,1,0:T(8,128)S(1)}, f32[3,4,8,128]{3,2,1,0:T(8,128)}, u32[]{:S(2)}) copy-start(f32[3,4,8,128]{3,2,1,0:T(8,128)} %param.7) | copy-start | bytes 147460
  14.5 42.2 %copy-start.1 = (f32[3,4,8,128]{3,2,1,0:T(8,128)S(1)}, f32[3,4,8,128]{3,2,1,0:T(8,128)}, u32[]{:S(2)}) copy-start(f32[3,4,8,128]{3,2,1,0:T(8,128)} %param.8) | copy-start | bytes 147460
  14.5 42.2 %copy-start.2 = (f32[3,4,8,128]{3,2,1,0:T(8,128)S(1)}, f32[3,4,8,128]{3,2,1,0:T(8,128)}, u32[]{:S(2)}) copy-start(f32[3,4,8,128]{3,2,1,0:T(8,128)} %param.9) | copy-start | bytes 147460
  14.5 42.2 %copy-start.3 = (f32[3,4,8,128]{3,2,1,0:T(8,128)S(1)}, f32[3,4,8,128]{3,2,1,0:T(8,128)}, u32[]{:S(2)}) copy-start(f32[3,4,8,128]{3,2,1,0:T(8,128)} %param.10) | copy-start | bytes 147460
  14.5 42.3 %all-to-all-start.1 = ((f32[8,24,128]{2,1,0:T(8,128)}), f32[8,24,128]{2,1,0:T(8,128)S(1)}, u32[]{:S(2)}, u32[]{:S(2)}) async-start(f32[8,24,128]{2,1,0:T(8,128)} %get-tuple-element.50), calls=%async_computation.1 | async-start | bytes 196608 | tf_op jit(solution)/shard_map/all_to_all | solution.py:563
  41.3 15.4 %collective-permute-start = (f32[6,8,128]{2,1,0:T(8,128)S(1)}, f32[6,8,128]{2,1,0:T(8,128)S(1)}, u32[]{:S(2)}, u32[]{:S(2)}) collective-permute-start(f32[6,8,128]{2,1,0:T(8,128)S(1)} %copy-done.8), channel_id=1, source_target_pairs={{0,256},{256,512},{512,768},{1,257},{257,513},{513,769},{2,258},{2... | collective-permute-start | bytes 73736 | tf_op jit(solution)/shard_map/ppermute | solution.py:568
  44.4 12.3 %collective-permute-start.2 = (f32[6,8,128]{2,1,0:T(8,128)S(1)}, f32[6,8,128]{2,1,0:T(8,128)S(1)}, u32[]{:S(2)}, u32[]{:S(2)}) collective-permute-start(f32[6,8,128]{2,1,0:T(8,128)S(1)} %copy-done.7), channel_id=1, source_target_pairs={{256,0},{512,256},{768,512},{257,1},{513,257},{769,513},{258,2},{5... | collective-permute-start | bytes 73736 | tf_op jit(solution)/shard_map/ppermute | solution.py:573
  45.7 7.9 %collective-permute-start.1 = (f32[24,128]{1,0:T(8,128)S(1)}, f32[24,128]{1,0:T(8,128)S(1)}, u32[]{:S(2)}, u32[]{:S(2)}) collective-permute-start(f32[24,128]{1,0:T(8,128)S(1)} %copy-done.10), channel_id=1, source_target_pairs={{0,32},{32,64},{64,96},{96,128},{128,160},{160,192},{192,224},{1,3... | collective-permute-start | bytes 36872 | tf_op jit(solution)/shard_map/ppermute | solution.py:568
  51.6 5.0 %collective-permute-start.3 = (f32[24,128]{1,0:T(8,128)S(1)}, f32[24,128]{1,0:T(8,128)S(1)}, u32[]{:S(2)}, u32[]{:S(2)}) collective-permute-start(f32[24,128]{1,0:T(8,128)S(1)} %copy-done.9), channel_id=1, source_target_pairs={{32,0},{64,32},{96,64},{128,96},{160,128},{192,160},{224,192},{33,... | collective-permute-start | bytes 36872 | tf_op jit(solution)/shard_map/ppermute | solution.py:573
  56.7 0.7 copy-start.5
  56.7 0.7 copy-start.6
  56.8 0.7 copy-start.4
  66.3 31.3 %all-to-all-start.3 = ((f32[8,17,1,128]{3,2,1,0:T(1,128)}), f32[8,17,1,128]{3,2,1,0:T(1,128)S(1)}, u32[]{:S(2)}, u32[]{:S(2)}) async-start(f32[8,17,1,128]{3,2,1,0:T(1,128)} %get-tuple-element.63), calls=%async_computation.3 | async-start | bytes 139264 | tf_op jit(solution)/shard_map/all_to_all | solution.py:563
  82.6 14.8 %collective-permute-start.4 = (f32[3,8,128]{2,1,0:T(8,128)S(1)}, f32[3,8,128]{2,1,0:T(8,128)S(1)}, u32[]{:S(2)}, u32[]{:S(2)}) collective-permute-start(f32[3,8,128]{2,1,0:T(8,128)S(1)} %get-tuple-element.67), channel_id=1, source_target_pairs={{0,256},{256,512},{512,768},{1,257},{257,513},{513,769},{2,258},{2... | collective-permute-start | bytes 36872 | tf_op jit(solution)/shard_map/ppermute | solution.py:568
  86.8 10.6 %collective-permute-start.6 = (f32[3,8,128]{2,1,0:T(8,128)S(1)}, f32[3,8,128]{2,1,0:T(8,128)S(1)}, u32[]{:S(2)}, u32[]{:S(2)}) collective-permute-start(f32[3,8,128]{2,1,0:T(8,128)S(1)} %get-tuple-element.69), channel_id=1, source_target_pairs={{256,0},{512,256},{768,512},{257,1},{513,257},{769,513},{258,2},{5... | collective-permute-start | bytes 36872 | tf_op jit(solution)/shard_map/ppermute | solution.py:573
  88.1 5.9 %collective-permute-start.5 = (f32[12,128]{1,0:T(8,128)S(1)}, f32[12,128]{1,0:T(8,128)S(1)}, u32[]{:S(2)}, u32[]{:S(2)}) collective-permute-start(f32[12,128]{1,0:T(8,128)S(1)} %get-tuple-element.68), channel_id=1, source_target_pairs={{0,32},{32,64},{64,96},{96,128},{128,160},{160,192},{192,224},{1,3... | collective-permute-start | bytes 18440 | tf_op jit(solution)/shard_map/ppermute | solution.py:568
  92.1 5.3 %collective-permute-start.7 = (f32[12,128]{1,0:T(8,128)S(1)}, f32[12,128]{1,0:T(8,128)S(1)}, u32[]{:S(2)}, u32[]{:S(2)}) collective-permute-start(f32[12,128]{1,0:T(8,128)S(1)} %get-tuple-element.70), channel_id=1, source_target_pairs={{32,0},{64,32},{96,64},{128,96},{160,128},{192,160},{224,192},{33,... | collective-permute-start | bytes 18440 | tf_op jit(solution)/shard_map/ppermute | solution.py:573
  98.7 16.6 %collective-permute-start.8 = (f32[3,8,128]{2,1,0:T(8,128)S(1)}, f32[3,8,128]{2,1,0:T(8,128)S(1)}, u32[]{:S(2)}, u32[]{:S(2)}) collective-permute-start(f32[3,8,128]{2,1,0:T(8,128)S(1)} %get-tuple-element.76), channel_id=1, source_target_pairs={{0,256},{256,512},{512,768},{1,257},{257,513},{513,769},{2,258},{2... | collective-permute-start | bytes 36872 | tf_op jit(solution)/shard_map/ppermute | solution.py:568
  105.2 10.1 %collective-permute-start.10 = (f32[3,8,128]{2,1,0:T(8,128)S(1)}, f32[3,8,128]{2,1,0:T(8,128)S(1)}, u32[]{:S(2)}, u32[]{:S(2)}) collective-permute-start(f32[3,8,128]{2,1,0:T(8,128)S(1)} %get-tuple-element.78), channel_id=1, source_target_pairs={{256,0},{512,256},{768,512},{257,1},{513,257},{769,513},{258,2},{5... | collective-permute-start | bytes 36872 | tf_op jit(solution)/shard_map/ppermute | solution.py:573
  106.5 5.8 %collective-permute-start.9 = (f32[12,128]{1,0:T(8,128)S(1)}, f32[12,128]{1,0:T(8,128)S(1)}, u32[]{:S(2)}, u32[]{:S(2)}) collective-permute-start(f32[12,128]{1,0:T(8,128)S(1)} %get-tuple-element.77), channel_id=1, source_target_pairs={{0,32},{32,64},{64,96},{96,128},{128,160},{160,192},{192,224},{1,3... | collective-permute-start | bytes 18440 | tf_op jit(solution)/shard_map/ppermute | solution.py:568
  110.4 5.0 %collective-permute-start.11 = (f32[12,128]{1,0:T(8,128)S(1)}, f32[12,128]{1,0:T(8,128)S(1)}, u32[]{:S(2)}, u32[]{:S(2)}) collective-permute-start(f32[12,128]{1,0:T(8,128)S(1)} %get-tuple-element.79), channel_id=1, source_target_pairs={{32,0},{64,32},{96,64},{128,96},{160,128},{192,160},{224,192},{33,... | collective-permute-start | bytes 18440 | tf_op jit(solution)/shard_map/ppermute | solution.py:573

commit v9 on v7

--- a/solution.py
+++ b/solution.py
@@ -637,7 +637,8 @@
 
     count = lax.axis_size("gx") * lax.axis_size("gy")
     sent = call(scalar_kernel, [(count, 1, 128)], slots, inverse)[0]
-    lines = lax.all_to_all(sent, ("gx", "gy"), 0, 0)
+    order = [[(k + count // 2 + lax.axis_size("gy") // 2) % count for k in range(count)]]
+    lines = lax.all_to_all(sent, ("gx", "gy"), 0, 0, axis_index_groups=order)
     solved, rest = call(
         combine_kernel, [block, block],
         lines, slots, near, flow, extra, inverse, cond_along, *perfs, right, w1, w2,

time: 163 us -> 161 us (0.988)
  blocking collectives: 38.4 us -> 35.5 us
    all_to_all x1, blocking collectives: 13.6 us -> 10.7 us  [body(): lines = lax.all_to_all(sent, ('gx', 'gy'), 0, 0, axis_index_groups=order)]
where the time goes in v9:
time: 161 us; the launch traced here: 160 us
  starting transfers between devices  102 us (63%)
  blocking collectives  35.5 us (22%)
  waiting for transfers between devices  12.4 us (8%)
  Pallas kernels  8.33 us (5%)
    all_to_all x3, starting transfers between devices, far_slots(): return lax.all_to_all(sent, 'gz', 0, 0, axis_index_groups=groups)  64.1 us
    ppermute x6, starting transfers between devices, forward(): return lax.ppermute(piece, axis, [(i, i + 1) for i in range(count - 1)])  27.6 us
    all_to_all x3, blocking collectives, near_slots(): return lax.all_to_all(sent, 'gz', 0, 0, axis_index_groups=groups)  24.8 us
    ppermute x6, waiting for transfers between devices, backward(): return lax.ppermute(piece, axis, [(i + 1, i) for i in range(count - 1)])  11.4 us
    all_to_all x1, blocking collectives, body(): lines = lax.all_to_all(sent, ('gx', 'gy'), 0, 0, axis_index_groups=order)  10.7 us
    ppermute x6, starting transfers between devices, backward(): return lax.ppermute(piece, axis, [(i + 1, i) for i in range(count - 1)])  9.97 us
    pallas_call x12, Pallas kernels, call(): pl.pallas_call(kernel, out_shape=[jax.ShapeDtypeStruct(shape, F32) for sh...  8.33 us
  transfers between devices with their start and end apart: 15, of which 5 were waited for; matrix products, arithmetic and copies ran while one was open for 0% of the time, Pallas kernels for 0%

profile of v9, /device:TPU:1, one launch (start us, length us, event | category | flops | bytes accessed | tf_op | source)
XLA Modules:
  0.0 159.5 jit_solution(12323424809417634681)
XLA Ops:
  0.6 2.0 %shard_map.86 = (f32[4,24,128]{2,1,0:T(8,128)}, f32[6,8,128]{2,1,0:T(8,128)}, f32[6,8,128]{2,1,0:T(8,128)}, f32[24,128]{1,0:T(8,128)}, f32[24,128]{1,0:T(8,128)}) custom-call(f32[3,32,128]{2,1,0:T(8,128)} %bitcast.6, f32[3,32,128]{2,1,0:T(8,128)} %bitcast.19, s32[1,1,512]{2,1,0:T(1,128)} %cell.5, s32[1,1,512]{2,1,0:T(1,128)} %well.5, f32[1,1,512]{2,1,0:T(1,128)} %factor.5), custom_call_target="tpu_custom_call" | custom-call | tf_op jit(solution)/shard_map/pallas_call | solution.py:529
  2.7 11.0 %all_to_all.35.slots = f32[4,24,128]{2,1,0:T(8,128)S(1)} all-to-all(f32[4,24,128]{2,1,0:T(8,128)} %get-tuple-element.47), channel_id=1, replica_groups={{0,1,2,3},{4,5,6,7},{8,9,10,11},{12,13,14,15},{16,17,18,19},{20,21,22,2..., dimensions={0} | all-to-all | bytes 98304 | tf_op jit(solution)/shard_map/all_to_all | solution.py:545
  13.7 0.8 shard_map.87
  14.5 26.8 %all-to-all-start.1 = ((f32[8,24,128]{2,1,0:T(8,128)}), f32[8,24,128]{2,1,0:T(8,128)S(1)}, u32[]{:S(2)}, u32[]{:S(2)}) async-start(f32[8,24,128]{2,1,0:T(8,128)} %get-tuple-element.53), calls=%async_computation.1 | async-start | bytes 196608 | tf_op jit(solution)/shard_map/all_to_all | solution.py:557
  41.3 3.1 %collective-permute-start = (f32[6,8,128]{2,1,0:T(8,128)S(1)}, f32[6,8,128]{2,1,0:T(8,128)S(1)}, u32[]{:S(2)}, u32[]{:S(2)}) collective-permute-start(f32[6,8,128]{2,1,0:T(8,128)S(1)} %copy-done.8), channel_id=1, source_target_pairs={{0,256},{256,512},{512,768},{1,257},{257,513},{513,769},{2,258},{2... | collective-permute-start | bytes 73736 | tf_op jit(solution)/shard_map/ppermute | solution.py:562
  44.4 1.3 collective-permute-start.2
  45.7 5.9 %collective-permute-start.1 = (f32[24,128]{1,0:T(8,128)S(1)}, f32[24,128]{1,0:T(8,128)S(1)}, u32[]{:S(2)}, u32[]{:S(2)}) collective-permute-start(f32[24,128]{1,0:T(8,128)S(1)} %copy-done.10), channel_id=1, source_target_pairs={{0,32},{32,64},{64,96},{96,128},{128,160},{160,192},{192,224},{1,3... | collective-permute-start | bytes 36872 | tf_op jit(solution)/shard_map/ppermute | solution.py:562
  51.6 1.9 %collective-permute-start.3 = (f32[24,128]{1,0:T(8,128)S(1)}, f32[24,128]{1,0:T(8,128)S(1)}, u32[]{:S(2)}, u32[]{:S(2)}) collective-permute-start(f32[24,128]{1,0:T(8,128)S(1)} %copy-done.9), channel_id=1, source_target_pairs={{32,0},{64,32},{96,64},{128,96},{160,128},{192,160},{224,192},{33,... | collective-permute-start | bytes 36872 | tf_op jit(solution)/shard_map/ppermute | solution.py:567
  53.6 3.1 %collective-permute-done.3.yh = f32[24,128]{1,0:T(8,128)S(1)} collective-permute-done((f32[24,128]{1,0:T(8,128)S(1)}, f32[24,128]{1,0:T(8,128)S(1)}, u32[]{:S(2)}, u32[]{:S(2)}) %collective-permute-start.3) | collective-permute-done | bytes 12320 | tf_op jit(solution)/shard_map/ppermute | solution.py:567
  56.8 0.6 copy-done.5
  57.5 1.2 shard_map.89
  58.7 6.9 %all_to_all.36.slots = f32[4,24,128]{2,1,0:T(8,128)S(1)} all-to-all(f32[4,24,128]{2,1,0:T(8,128)S(1)} %broadcast_in_dim.4), channel_id=1, replica_groups={{0,1,2,3},{4,5,6,7},{8,9,10,11},{12,13,14,15},{16,17,18,19},{20,21,22,2..., dimensions={0} | all-to-all | bytes 98304 | tf_op jit(solution)/shard_map/all_to_all | solution.py:545
  65.6 0.7 shard_map.90
  66.3 16.3 %all-to-all-start.3 = ((f32[8,17,1,128]{3,2,1,0:T(1,128)}), f32[8,17,1,128]{3,2,1,0:T(1,128)S(1)}, u32[]{:S(2)}, u32[]{:S(2)}) async-start(f32[8,17,1,128]{3,2,1,0:T(1,128)} %get-tuple-element.66), calls=%async_computation.3 | async-start | bytes 139264 | tf_op jit(solution)/shard_map/all_to_all | solution.py:557
  82.6 4.3 %collective-permute-start.4 = (f32[3,8,128]{2,1,0:T(8,128)S(1)}, f32[3,8,128]{2,1,0:T(8,128)S(1)}, u32[]{:S(2)}, u32[]{:S(2)}) collective-permute-start(f32[3,8,128]{2,1,0:T(8,128)S(1)} %get-tuple-element.70), channel_id=1, source_target_pairs={{0,256},{256,512},{512,768},{1,257},{257,513},{513,769},{2,258},{2... | collective-permute-start | bytes 36872 | tf_op jit(solution)/shard_map/ppermute | solution.py:562
  86.9 1.3 collective-permute-start.6
  88.2 4.0 %collective-permute-start.5 = (f32[12,128]{1,0:T(8,128)S(1)}, f32[12,128]{1,0:T(8,128)S(1)}, u32[]{:S(2)}, u32[]{:S(2)}) collective-permute-start(f32[12,128]{1,0:T(8,128)S(1)} %get-tuple-element.71), channel_id=1, source_target_pairs={{0,32},{32,64},{64,96},{96,128},{128,160},{160,192},{192,224},{1,3... | collective-permute-start | bytes 18440 | tf_op jit(solution)/shard_map/ppermute | solution.py:562
  92.1 1.9 %collective-permute-start.7 = (f32[12,128]{1,0:T(8,128)S(1)}, f32[12,128]{1,0:T(8,128)S(1)}, u32[]{:S(2)}, u32[]{:S(2)}) collective-permute-start(f32[12,128]{1,0:T(8,128)S(1)} %get-tuple-element.73), channel_id=1, source_target_pairs={{32,0},{64,32},{96,64},{128,96},{160,128},{192,160},{224,192},{33,... | collective-permute-start | bytes 18440 | tf_op jit(solution)/shard_map/ppermute | solution.py:567
  94.1 3.3 %collective-permute-done.7.yh = f32[12,128]{1,0:T(8,128)S(1)} collective-permute-done((f32[12,128]{1,0:T(8,128)S(1)}, f32[12,128]{1,0:T(8,128)S(1)}, u32[]{:S(2)}, u32[]{:S(2)}) %collective-permute-start.7) | collective-permute-done | bytes 6176 | tf_op jit(solution)/shard_map/ppermute | solution.py:567
  97.7 1.1 shard_map.92
  98.8 6.5 %collective-permute-start.8 = (f32[3,8,128]{2,1,0:T(8,128)S(1)}, f32[3,8,128]{2,1,0:T(8,128)S(1)}, u32[]{:S(2)}, u32[]{:S(2)}) collective-permute-start(f32[3,8,128]{2,1,0:T(8,128)S(1)} %get-tuple-element.79), channel_id=1, source_target_pairs={{0,256},{256,512},{512,768},{1,257},{257,513},{513,769},{2,258},{2... | collective-permute-start | bytes 36872 | tf_op jit(solution)/shard_map/ppermute | solution.py:562
  105.2 3.8 %collective-permute-start.9 = (f32[12,128]{1,0:T(8,128)S(1)}, f32[12,128]{1,0:T(8,128)S(1)}, u32[]{:S(2)}, u32[]{:S(2)}) collective-permute-start(f32[12,128]{1,0:T(8,128)S(1)} %get-tuple-element.80), channel_id=1, source_target_pairs={{0,32},{32,64},{64,96},{96,128},{128,160},{160,192},{192,224},{1,3... | collective-permute-start | bytes 18440 | tf_op jit(solution)/shard_map/ppermute | solution.py:562
  109.1 0.8 collective-permute-done.9.yl
  110.0 6.9 %all_to_all.37.slots = f32[4,24,128]{2,1,0:T(8,128)S(1)} all-to-all(f32[4,24,128]{2,1,0:T(8,128)S(1)} %broadcast_in_dim.5), channel_id=1, replica_groups={{0,1,2,3},{4,5,6,7},{8,9,10,11},{12,13,14,15},{16,17,18,19},{20,21,22,2..., dimensions={0} | all-to-all | bytes 98304 | tf_op jit(solution)/shard_map/all_to_all | solution.py:545
  116.9 0.8 shard_map.94
  117.7 21.1 %all-to-all-start.5 = ((f32[8,20,1,128]{3,2,1,0:T(1,128)}), f32[8,20,1,128]{3,2,1,0:T(1,128)S(1)}, u32[]{:S(2)}, u32[]{:S(2)}) async-start(f32[8,20,1,128]{3,2,1,0:T(1,128)} %get-tuple-element.84), calls=%async_computation.5 | async-start | bytes 163840 | tf_op jit(solution)/shard_map/all_to_all | solution.py:557
  138.8 1.3 collective-permute-start.10
  140.1 2.3 %collective-permute-start.11 = (f32[12,128]{1,0:T(8,128)S(1)}, f32[12,128]{1,0:T(8,128)S(1)}, u32[]{:S(2)}, u32[]{:S(2)}) collective-permute-start(f32[12,128]{1,0:T(8,128)S(1)} %get-tuple-element.86), channel_id=1, source_target_pairs={{32,0},{64,32},{96,64},{128,96},{160,128},{192,160},{224,192},{33,... | collective-permute-start | bytes 18440 | tf_op jit(solution)/shard_map/ppermute | solution.py:567
  142.4 5.0 %collective-permute-done.11.yh = f32[12,128]{1,0:T(8,128)S(1)} collective-permute-done((f32[12,128]{1,0:T(8,128)S(1)}, f32[12,128]{1,0:T(8,128)S(1)}, u32[]{:S(2)}, u32[]{:S(2)}) %collective-permute-start.11) | collective-permute-done | bytes 6176 | tf_op jit(solution)/shard_map/ppermute | solution.py:567
  147.4 0.2 shard_map.96
  147.6 10.7 %all_to_all.38.lines = f32[32,1,128]{2,1,0:T(1,128)S(1)} all-to-all(f32[32,1,128]{2,1,0:T(1,128)S(1)} %shard_map.96), channel_id=1, replica_groups={{640,672,704,736,768,800,832,864,896,928,960,992,0,32,64,96,128,160,192..., dimensions={0} | all-to-all | bytes 32768 | tf_op jit(solution)/shard_map/all_to_all | solution.py:641
  158.3 1.2 shard_map.97
  (38 shorter events, 0.8 us)
Async XLA Ops:
  2.7 43.0 %copy-start.10 = (f32[24,128]{1,0:T(8,128)S(1)}, f32[24,128]{1,0:T(8,128)}, u32[]{:S(2)}) copy-start(f32[24,128]{1,0:T(8,128)} %get-tuple-element.56) | copy-start | bytes 36868
  13.7 27.6 %copy-start.8 = (f32[6,8,128]{2,1,0:T(8,128)S(1)}, f32[6,8,128]{2,1,0:T(8,128)}, u32[]{:S(2)}) copy-start(f32[6,8,128]{2,1,0:T(8,128)} %get-tuple-element.55) | copy-start | bytes 73732
  13.7 30.7 %copy-start.7 = (f32[6,8,128]{2,1,0:T(8,128)S(1)}, f32[6,8,128]{2,1,0:T(8,128)}, u32[]{:S(2)}) copy-start(f32[6,8,128]{2,1,0:T(8,128)} %get-tuple-element.57) | copy-start | bytes 73732
  13.7 37.9 %copy-start.9 = (f32[24,128]{1,0:T(8,128)S(1)}, f32[24,128]{1,0:T(8,128)}, u32[]{:S(2)}) copy-start(f32[24,128]{1,0:T(8,128)} %get-tuple-element.58) | copy-start | bytes 36868
  14.5 42.2 %copy-start = (f32[3,4,8,128]{3,2,1,0:T(8,128)S(1)}, f32[3,4,8,128]{3,2,1,0:T(8,128)}, u32[]{:S(2)}) copy-start(f32[3,4,8,128]{3,2,1,0:T(8,128)} %param.7) | copy-start | bytes 147460
  14.5 42.2 %copy-start.1 = (f32[3,4,8,128]{3,2,1,0:T(8,128)S(1)}, f32[3,4,8,128]{3,2,1,0:T(8,128)}, u32[]{:S(2)}) copy-start(f32[3,4,8,128]{3,2,1,0:T(8,128)} %param.8) | copy-start | bytes 147460
  14.5 42.2 %copy-start.2 = (f32[3,4,8,128]{3,2,1,0:T(8,128)S(1)}, f32[3,4,8,128]{3,2,1,0:T(8,128)}, u32[]{:S(2)}) copy-start(f32[3,4,8,128]{3,2,1,0:T(8,128)} %param.9) | copy-start | bytes 147460
  14.5 42.2 %copy-start.3 = (f32[3,4,8,128]{3,2,1,0:T(8,128)S(1)}, f32[3,4,8,128]{3,2,1,0:T(8,128)}, u32[]{:S(2)}) copy-start(f32[3,4,8,128]{3,2,1,0:T(8,128)} %param.10) | copy-start | bytes 147460
  14.5 42.3 %all-to-all-start.1 = ((f32[8,24,128]{2,1,0:T(8,128)}), f32[8,24,128]{2,1,0:T(8,128)S(1)}, u32[]{:S(2)}, u32[]{:S(2)}) async-start(f32[8,24,128]{2,1,0:T(8,128)} %get-tuple-element.53), calls=%async_computation.1 | async-start | bytes 196608 | tf_op jit(solution)/shard_map/all_to_all | solution.py:557
  41.3 15.4 %collective-permute-start = (f32[6,8,128]{2,1,0:T(8,128)S(1)}, f32[6,8,128]{2,1,0:T(8,128)S(1)}, u32[]{:S(2)}, u32[]{:S(2)}) collective-permute-start(f32[6,8,128]{2,1,0:T(8,128)S(1)} %copy-done.8), channel_id=1, source_target_pairs={{0,256},{256,512},{512,768},{1,257},{257,513},{513,769},{2,258},{2... | collective-permute-start | bytes 73736 | tf_op jit(solution)/shard_map/ppermute | solution.py:562
  44.4 12.3 %collective-permute-start.2 = (f32[6,8,128]{2,1,0:T(8,128)S(1)}, f32[6,8,128]{2,1,0:T(8,128)S(1)}, u32[]{:S(2)}, u32[]{:S(2)}) collective-permute-start(f32[6,8,128]{2,1,0:T(8,128)S(1)} %copy-done.7), channel_id=1, source_target_pairs={{256,0},{512,256},{768,512},{257,1},{513,257},{769,513},{258,2},{5... | collective-permute-start | bytes 73736 | tf_op jit(solution)/shard_map/ppermute | solution.py:567
  45.7 7.9 %collective-permute-start.1 = (f32[24,128]{1,0:T(8,128)S(1)}, f32[24,128]{1,0:T(8,128)S(1)}, u32[]{:S(2)}, u32[]{:S(2)}) collective-permute-start(f32[24,128]{1,0:T(8,128)S(1)} %copy-done.10), channel_id=1, source_target_pairs={{0,32},{32,64},{64,96},{96,128},{128,160},{160,192},{192,224},{1,3... | collective-permute-start | bytes 36872 | tf_op jit(solution)/shard_map/ppermute | solution.py:562
  51.6 5.0 %collective-permute-start.3 = (f32[24,128]{1,0:T(8,128)S(1)}, f32[24,128]{1,0:T(8,128)S(1)}, u32[]{:S(2)}, u32[]{:S(2)}) collective-permute-start(f32[24,128]{1,0:T(8,128)S(1)} %copy-done.9), channel_id=1, source_target_pairs={{32,0},{64,32},{96,64},{128,96},{160,128},{192,160},{224,192},{33,... | collective-permute-start | bytes 36872 | tf_op jit(solution)/shard_map/ppermute | solution.py:567
  56.7 0.7 copy-start.5
  56.7 0.7 copy-start.6
  56.8 0.7 copy-start.4
  66.3 31.3 %all-to-all-start.3 = ((f32[8,17,1,128]{3,2,1,0:T(1,128)}), f32[8,17,1,128]{3,2,1,0:T(1,128)S(1)}, u32[]{:S(2)}, u32[]{:S(2)}) async-start(f32[8,17,1,128]{3,2,1,0:T(1,128)} %get-tuple-element.66), calls=%async_computation.3 | async-start | bytes 139264 | tf_op jit(solution)/shard_map/all_to_all | solution.py:557
  82.6 14.8 %collective-permute-start.4 = (f32[3,8,128]{2,1,0:T(8,128)S(1)}, f32[3,8,128]{2,1,0:T(8,128)S(1)}, u32[]{:S(2)}, u32[]{:S(2)}) collective-permute-start(f32[3,8,128]{2,1,0:T(8,128)S(1)} %get-tuple-element.70), channel_id=1, source_target_pairs={{0,256},{256,512},{512,768},{1,257},{257,513},{513,769},{2,258},{2... | collective-permute-start | bytes 36872 | tf_op jit(solution)/shard_map/ppermute | solution.py:562
  86.9 10.6 %collective-permute-start.6 = (f32[3,8,128]{2,1,0:T(8,128)S(1)}, f32[3,8,128]{2,1,0:T(8,128)S(1)}, u32[]{:S(2)}, u32[]{:S(2)}) collective-permute-start(f32[3,8,128]{2,1,0:T(8,128)S(1)} %get-tuple-element.72), channel_id=1, source_target_pairs={{256,0},{512,256},{768,512},{257,1},{513,257},{769,513},{258,2},{5... | collective-permute-start | bytes 36872 | tf_op jit(solution)/shard_map/ppermute | solution.py:567
  88.2 5.9 %collective-permute-start.5 = (f32[12,128]{1,0:T(8,128)S(1)}, f32[12,128]{1,0:T(8,128)S(1)}, u32[]{:S(2)}, u32[]{:S(2)}) collective-permute-start(f32[12,128]{1,0:T(8,128)S(1)} %get-tuple-element.71), channel_id=1, source_target_pairs={{0,32},{32,64},{64,96},{96,128},{128,160},{160,192},{192,224},{1,3... | collective-permute-start | bytes 18440 | tf_op jit(solution)/shard_map/ppermute | solution.py:562
  92.1 5.3 %collective-permute-start.7 = (f32[12,128]{1,0:T(8,128)S(1)}, f32[12,128]{1,0:T(8,128)S(1)}, u32[]{:S(2)}, u32[]{:S(2)}) collective-permute-start(f32[12,128]{1,0:T(8,128)S(1)} %get-tuple-element.73), channel_id=1, source_target_pairs={{32,0},{64,32},{96,64},{128,96},{160,128},{192,160},{224,192},{33,... | collective-permute-start | bytes 18440 | tf_op jit(solution)/shard_map/ppermute | solution.py:567
  98.8 11.1 %collective-permute-start.8 = (f32[3,8,128]{2,1,0:T(8,128)S(1)}, f32[3,8,128]{2,1,0:T(8,128)S(1)}, u32[]{:S(2)}, u32[]{:S(2)}) collective-permute-start(f32[3,8,128]{2,1,0:T(8,128)S(1)} %get-tuple-element.79), channel_id=1, source_target_pairs={{0,256},{256,512},{512,768},{1,257},{257,513},{513,769},{2,258},{2... | collective-permute-start | bytes 36872 | tf_op jit(solution)/shard_map/ppermute | solution.py:562
  105.2 4.6 %collective-permute-start.9 = (f32[12,128]{1,0:T(8,128)S(1)}, f32[12,128]{1,0:T(8,128)S(1)}, u32[]{:S(2)}, u32[]{:S(2)}) collective-permute-start(f32[12,128]{1,0:T(8,128)S(1)} %get-tuple-element.80), channel_id=1, source_target_pairs={{0,32},{32,64},{64,96},{96,128},{128,160},{160,192},{192,224},{1,3... | collective-permute-start | bytes 18440 | tf_op jit(solution)/shard_map/ppermute | solution.py:562
  117.7 29.6 %all-to-all-start.5 = ((f32[8,20,1,128]{3,2,1,0:T(1,128)}), f32[8,20,1,128]{3,2,1,0:T(1,128)S(1)}, u32[]{:S(2)}, u32[]{:S(2)}) async-start(f32[8,20,1,128]{3,2,1,0:T(1,128)} %get-tuple-element.84), calls=%async_computation.5 | async-start | bytes 163840 | tf_op jit(solution)/shard_map/all_to_all | solution.py:557
  138.8 8.5 %collective-permute-start.10 = (f32[3,8,128]{2,1,0:T(8,128)S(1)}, f32[3,8,128]{2,1,0:T(8,128)S(1)}, u32[]{:S(2)}, u32[]{:S(2)}) collective-permute-start(f32[3,8,128]{2,1,0:T(8,128)S(1)} %get-tuple-element.85), channel_id=1, source_target_pairs={{256,0},{512,256},{768,512},{257,1},{513,257},{769,513},{258,2},{5... | collective-permute-start | bytes 36872 | tf_op jit(solution)/shard_map/ppermute | solution.py:567
  140.1 7.2 %collective-permute-start.11 = (f32[12,128]{1,0:T(8,128)S(1)}, f32[12,128]{1,0:T(8,128)S(1)}, u32[]{:S(2)}, u32[]{:S(2)}) collective-permute-start(f32[12,128]{1,0:T(8,128)S(1)} %get-tuple-element.86), channel_id=1, source_target_pairs={{32,0},{64,32},{96,64},{128,96},{160,128},{192,160},{224,192},{33,... | collective-permute-start | bytes 18440 | tf_op jit(solution)/shard_map/ppermute | solution.py:567

commit v10 on v9

--- a/solution.py
+++ b/solution.py
@@ -632,13 +632,13 @@
     sent, *faces = after(sent, *faces)
     slots = far_slots(sent, 2)
     high = high_halos(faces)
-    flow = call(flow_kernel, [block], w2, diag, off, cond, *low, *high)[0]
-    slots, flow = after(slots, flow)
 
     count = lax.axis_size("gx") * lax.axis_size("gy")
     sent = call(scalar_kernel, [(count, 1, 128)], slots, inverse)[0]
     order = [[(k + count // 2 + lax.axis_size("gy") // 2) % count for k in range(count)]]
     lines = lax.all_to_all(sent, ("gx", "gy"), 0, 0, axis_index_groups=order)
+    lines, *high = after(lines, *high)
+    flow = call(flow_kernel, [block], w2, diag, off, cond, *low, *high)[0]
     solved, rest = call(
         combine_kernel, [block, block],
         lines, slots, near, flow, extra, inverse, cond_along, *perfs, right, w1, w2,

time: 161 us -> 164 us (1.019)
  blocking collectives: 35.5 us -> 52.1 us
  starting transfers between devices: 102 us -> 90.5 us
  waiting for transfers between devices: 12.4 us -> 10.1 us
    all_to_all x3 -> x2, starting transfers between devices: 64.1 us -> 43 us  [far_slots(): return lax.all_to_all(sent, 'gz', 0, 0, axis_index_groups=groups)]
    all_to_all x1, blocking collectives: 10.7 us -> 27.3 us  [far_slots(): return lax.all_to_all(sent, 'gz', 0, 0, axis_index_groups=groups)]
    all_to_all x0 -> x1, starting transfers between devices: none -> 9.95 us  [body(): lines = lax.all_to_all(sent, ('gx', 'gy'), 0, 0, axis_index_groups=order)]
    ppermute x6, waiting for transfers between devices: 11.4 us -> 9.1 us  [backward(): return lax.ppermute(piece, axis, [(i + 1, i) for i in range(count - 1)])]
where the time goes in v10:
time: 164 us; the launch traced here: 163 us
  starting transfers between devices  90.5 us (55%)
  blocking collectives  52.1 us (32%)
  waiting for transfers between devices  10.1 us (6%)
  Pallas kernels  8.31 us (5%)
    all_to_all x2, starting transfers between devices, far_slots(): return lax.all_to_all(sent, 'gz', 0, 0, axis_index_groups=groups)  43 us
    ppermute x6, starting transfers between devices, forward(): return lax.ppermute(piece, axis, [(i, i + 1) for i in range(count - 1)])  27.6 us
    all_to_all x1, blocking collectives, far_slots(): return lax.all_to_all(sent, 'gz', 0, 0, axis_index_groups=groups)  27.3 us
    all_to_all x3, blocking collectives, near_slots(): return lax.all_to_all(sent, 'gz', 0, 0, axis_index_groups=groups)  24.8 us
    ppermute x6, starting transfers between devices, backward(): return lax.ppermute(piece, axis, [(i + 1, i) for i in range(count - 1)])  9.99 us
    all_to_all x1, starting transfers between devices, body(): lines = lax.all_to_all(sent, ('gx', 'gy'), 0, 0, axis_index_groups=order)  9.95 us
    ppermute x6, waiting for transfers between devices, backward(): return lax.ppermute(piece, axis, [(i + 1, i) for i in range(count - 1)])  9.1 us
    pallas_call x12, Pallas kernels, call(): pl.pallas_call(kernel, out_shape=[jax.ShapeDtypeStruct(shape, F32) for sh...  8.31 us
  transfers between devices with their start and end apart: 15, of which 5 were waited for; matrix products, arithmetic and copies ran while one was open for 0% of the time, Pallas kernels for 0%

profile of v10, /device:TPU:1, one launch (start us, length us, event | category | flops | bytes accessed | tf_op | source)
XLA Modules:
  0.0 162.7 jit_solution(9255148698492424280)
XLA Ops:
  0.6 2.0 %shard_map.86 = (f32[4,24,128]{2,1,0:T(8,128)}, f32[6,8,128]{2,1,0:T(8,128)}, f32[6,8,128]{2,1,0:T(8,128)}, f32[24,128]{1,0:T(8,128)}, f32[24,128]{1,0:T(8,128)}) custom-call(f32[3,32,128]{2,1,0:T(8,128)} %bitcast.6, f32[3,32,128]{2,1,0:T(8,128)} %bitcast.19, s32[1,1,512]{2,1,0:T(1,128)} %cell.5, s32[1,1,512]{2,1,0:T(1,128)} %well.5, f32[1,1,512]{2,1,0:T(1,128)} %factor.5), custom_call_target="tpu_custom_call" | custom-call | tf_op jit(solution)/shard_map/pallas_call | solution.py:529
  2.7 11.0 %all_to_all.35.slots = f32[4,24,128]{2,1,0:T(8,128)S(1)} all-to-all(f32[4,24,128]{2,1,0:T(8,128)} %get-tuple-element.48), channel_id=1, replica_groups={{0,1,2,3},{4,5,6,7},{8,9,10,11},{12,13,14,15},{16,17,18,19},{20,21,22,2..., dimensions={0} | all-to-all | bytes 98304 | tf_op jit(solution)/shard_map/all_to_all | solution.py:545
  13.7 0.8 shard_map.87
  14.5 26.8 %all-to-all-start.1 = ((f32[8,24,128]{2,1,0:T(8,128)}), f32[8,24,128]{2,1,0:T(8,128)S(1)}, u32[]{:S(2)}, u32[]{:S(2)}) async-start(f32[8,24,128]{2,1,0:T(8,128)} %get-tuple-element.54), calls=%async_computation.1 | async-start | bytes 196608 | tf_op jit(solution)/shard_map/all_to_all | solution.py:557
  41.3 3.1 %collective-permute-start = (f32[6,8,128]{2,1,0:T(8,128)S(1)}, f32[6,8,128]{2,1,0:T(8,128)S(1)}, u32[]{:S(2)}, u32[]{:S(2)}) collective-permute-start(f32[6,8,128]{2,1,0:T(8,128)S(1)} %copy-done.8), channel_id=1, source_target_pairs={{0,256},{256,512},{512,768},{1,257},{257,513},{513,769},{2,258},{2... | collective-permute-start | bytes 73736 | tf_op jit(solution)/shard_map/ppermute | solution.py:562
  44.4 1.3 collective-permute-start.2
  45.7 5.9 %collective-permute-start.1 = (f32[24,128]{1,0:T(8,128)S(1)}, f32[24,128]{1,0:T(8,128)S(1)}, u32[]{:S(2)}, u32[]{:S(2)}) collective-permute-start(f32[24,128]{1,0:T(8,128)S(1)} %copy-done.10), channel_id=1, source_target_pairs={{0,32},{32,64},{64,96},{96,128},{128,160},{160,192},{192,224},{1,3... | collective-permute-start | bytes 36872 | tf_op jit(solution)/shard_map/ppermute | solution.py:562
  51.6 1.9 %collective-permute-start.3 = (f32[24,128]{1,0:T(8,128)S(1)}, f32[24,128]{1,0:T(8,128)S(1)}, u32[]{:S(2)}, u32[]{:S(2)}) collective-permute-start(f32[24,128]{1,0:T(8,128)S(1)} %copy-done.9), channel_id=1, source_target_pairs={{32,0},{64,32},{96,64},{128,96},{160,128},{192,160},{224,192},{33,... | collective-permute-start | bytes 36872 | tf_op jit(solution)/shard_map/ppermute | solution.py:567
  53.6 3.1 %collective-permute-done.3.yh = f32[24,128]{1,0:T(8,128)S(1)} collective-permute-done((f32[24,128]{1,0:T(8,128)S(1)}, f32[24,128]{1,0:T(8,128)S(1)}, u32[]{:S(2)}, u32[]{:S(2)}) %collective-permute-start.3) | collective-permute-done | bytes 12320 | tf_op jit(solution)/shard_map/ppermute | solution.py:567
  56.8 0.6 copy-done.5
  57.5 1.2 shard_map.89
  58.7 6.9 %all_to_all.36.slots = f32[4,24,128]{2,1,0:T(8,128)S(1)} all-to-all(f32[4,24,128]{2,1,0:T(8,128)S(1)} %broadcast_in_dim.4), channel_id=1, replica_groups={{0,1,2,3},{4,5,6,7},{8,9,10,11},{12,13,14,15},{16,17,18,19},{20,21,22,2..., dimensions={0} | all-to-all | bytes 98304 | tf_op jit(solution)/shard_map/all_to_all | solution.py:545
  65.6 0.7 shard_map.90
  66.3 16.3 %all-to-all-start.3 = ((f32[8,17,1,128]{3,2,1,0:T(1,128)}), f32[8,17,1,128]{3,2,1,0:T(1,128)S(1)}, u32[]{:S(2)}, u32[]{:S(2)}) async-start(f32[8,17,1,128]{3,2,1,0:T(1,128)} %get-tuple-element.67), calls=%async_computation.3 | async-start | bytes 139264 | tf_op jit(solution)/shard_map/all_to_all | solution.py:557
  82.6 4.3 %collective-permute-start.4 = (f32[3,8,128]{2,1,0:T(8,128)S(1)}, f32[3,8,128]{2,1,0:T(8,128)S(1)}, u32[]{:S(2)}, u32[]{:S(2)}) collective-permute-start(f32[3,8,128]{2,1,0:T(8,128)S(1)} %get-tuple-element.71), channel_id=1, source_target_pairs={{0,256},{256,512},{512,768},{1,257},{257,513},{513,769},{2,258},{2... | collective-permute-start | bytes 36872 | tf_op jit(solution)/shard_map/ppermute | solution.py:562
  86.9 1.3 collective-permute-start.6
  88.2 4.0 %collective-permute-start.5 = (f32[12,128]{1,0:T(8,128)S(1)}, f32[12,128]{1,0:T(8,128)S(1)}, u32[]{:S(2)}, u32[]{:S(2)}) collective-permute-start(f32[12,128]{1,0:T(8,128)S(1)} %get-tuple-element.72), channel_id=1, source_target_pairs={{0,32},{32,64},{64,96},{96,128},{128,160},{160,192},{192,224},{1,3... | collective-permute-start | bytes 18440 | tf_op jit(solution)/shard_map/ppermute | solution.py:562
  92.1 1.9 %collective-permute-start.7 = (f32[12,128]{1,0:T(8,128)S(1)}, f32[12,128]{1,0:T(8,128)S(1)}, u32[]{:S(2)}, u32[]{:S(2)}) collective-permute-start(f32[12,128]{1,0:T(8,128)S(1)} %get-tuple-element.74), channel_id=1, source_target_pairs={{32,0},{64,32},{96,64},{128,96},{160,128},{192,160},{224,192},{33,... | collective-permute-start | bytes 18440 | tf_op jit(solution)/shard_map/ppermute | solution.py:567
  94.1 3.3 %collective-permute-done.7.yh = f32[12,128]{1,0:T(8,128)S(1)} collective-permute-done((f32[12,128]{1,0:T(8,128)S(1)}, f32[12,128]{1,0:T(8,128)S(1)}, u32[]{:S(2)}, u32[]{:S(2)}) %collective-permute-start.7) | collective-permute-done | bytes 6176 | tf_op jit(solution)/shard_map/ppermute | solution.py:567
  97.5 0.2 all-to-all-done.3.slots
  97.7 1.1 shard_map.92
  98.8 6.5 %collective-permute-start.8 = (f32[3,8,128]{2,1,0:T(8,128)S(1)}, f32[3,8,128]{2,1,0:T(8,128)S(1)}, u32[]{:S(2)}, u32[]{:S(2)}) collective-permute-start(f32[3,8,128]{2,1,0:T(8,128)S(1)} %get-tuple-element.80), channel_id=1, source_target_pairs={{0,256},{256,512},{512,768},{1,257},{257,513},{513,769},{2,258},{2... | collective-permute-start | bytes 36872 | tf_op jit(solution)/shard_map/ppermute | solution.py:562
  105.2 3.8 %collective-permute-start.9 = (f32[12,128]{1,0:T(8,128)S(1)}, f32[12,128]{1,0:T(8,128)S(1)}, u32[]{:S(2)}, u32[]{:S(2)}) collective-permute-start(f32[12,128]{1,0:T(8,128)S(1)} %get-tuple-element.81), channel_id=1, source_target_pairs={{0,32},{32,64},{64,96},{96,128},{128,160},{160,192},{192,224},{1,3... | collective-permute-start | bytes 18440 | tf_op jit(solution)/shard_map/ppermute | solution.py:562
  109.1 0.8 collective-permute-done.9.yl
  110.0 6.9 %all_to_all.37.slots = f32[4,24,128]{2,1,0:T(8,128)S(1)} all-to-all(f32[4,24,128]{2,1,0:T(8,128)S(1)} %broadcast_in_dim.5), channel_id=1, replica_groups={{0,1,2,3},{4,5,6,7},{8,9,10,11},{12,13,14,15},{16,17,18,19},{20,21,22,2..., dimensions={0} | all-to-all | bytes 98304 | tf_op jit(solution)/shard_map/all_to_all | solution.py:545
  117.1 27.3 %all_to_all.38.slots = f32[8,20,1,128]{3,2,1,0:T(1,128)S(1)} all-to-all(f32[8,20,1,128]{3,2,1,0:T(1,128)S(1)} %get-tuple-element.85), channel_id=1, replica_groups={{16,20,24,28,0,4,8,12},{17,21,25,29,1,5,9,13},{18,22,26,30,2,6,10,14},{..., dimensions={0} | all-to-all | bytes 163840 | tf_op jit(solution)/shard_map/all_to_all | solution.py:557
  144.4 0.9 shard_map.95
  145.2 10.0 %all-to-all-start.6 = ((f32[32,1,128]{2,1,0:T(1,128)}), f32[32,1,128]{2,1,0:T(1,128)S(1)}, u32[]{:S(2)}, u32[]{:S(2)}) async-start(f32[32,1,128]{2,1,0:T(1,128)} %shard_map.95), calls=%async_computation.6 | async-start | bytes 32768 | tf_op jit(solution)/shard_map/all_to_all | solution.py:639
  155.2 1.3 collective-permute-start.10
  156.5 2.3 %collective-permute-start.11 = (f32[12,128]{1,0:T(8,128)S(1)}, f32[12,128]{1,0:T(8,128)S(1)}, u32[]{:S(2)}, u32[]{:S(2)}) collective-permute-start(f32[12,128]{1,0:T(8,128)S(1)} %get-tuple-element.87), channel_id=1, source_target_pairs={{32,0},{64,32},{96,64},{128,96},{160,128},{192,160},{224,192},{33,... | collective-permute-start | bytes 18440 | tf_op jit(solution)/shard_map/ppermute | solution.py:567
  158.8 2.7 %collective-permute-done.11.yh = f32[12,128]{1,0:T(8,128)S(1)} collective-permute-done((f32[12,128]{1,0:T(8,128)S(1)}, f32[12,128]{1,0:T(8,128)S(1)}, u32[]{:S(2)}, u32[]{:S(2)}) %collective-permute-start.11) | collective-permute-done | bytes 6176 | tf_op jit(solution)/shard_map/ppermute | solution.py:567
  161.5 1.2 shard_map.97
  (38 shorter events, 0.7 us)
Async XLA Ops:
  2.7 43.0 %copy-start.10 = (f32[24,128]{1,0:T(8,128)S(1)}, f32[24,128]{1,0:T(8,128)}, u32[]{:S(2)}) copy-start(f32[24,128]{1,0:T(8,128)} %get-tuple-element.57) | copy-start | bytes 36868
  13.7 27.6 %copy-start.8 = (f32[6,8,128]{2,1,0:T(8,128)S(1)}, f32[6,8,128]{2,1,0:T(8,128)}, u32[]{:S(2)}) copy-start(f32[6,8,128]{2,1,0:T(8,128)} %get-tuple-element.56) | copy-start | bytes 73732
  13.7 30.7 %copy-start.7 = (f32[6,8,128]{2,1,0:T(8,128)S(1)}, f32[6,8,128]{2,1,0:T(8,128)}, u32[]{:S(2)}) copy-start(f32[6,8,128]{2,1,0:T(8,128)} %get-tuple-element.58) | copy-start | bytes 73732
  13.7 37.9 %copy-start.9 = (f32[24,128]{1,0:T(8,128)S(1)}, f32[24,128]{1,0:T(8,128)}, u32[]{:S(2)}) copy-start(f32[24,128]{1,0:T(8,128)} %get-tuple-element.59) | copy-start | bytes 36868
  14.5 42.2 %copy-start = (f32[3,4,8,128]{3,2,1,0:T(8,128)S(1)}, f32[3,4,8,128]{3,2,1,0:T(8,128)}, u32[]{:S(2)}) copy-start(f32[3,4,8,128]{3,2,1,0:T(8,128)} %param.7) | copy-start | bytes 147460
  14.5 42.2 %copy-start.1 = (f32[3,4,8,128]{3,2,1,0:T(8,128)S(1)}, f32[3,4,8,128]{3,2,1,0:T(8,128)}, u32[]{:S(2)}) copy-start(f32[3,4,8,128]{3,2,1,0:T(8,128)} %param.8) | copy-start | bytes 147460
  14.5 42.2 %copy-start.2 = (f32[3,4,8,128]{3,2,1,0:T(8,128)S(1)}, f32[3,4,8,128]{3,2,1,0:T(8,128)}, u32[]{:S(2)}) copy-start(f32[3,4,8,128]{3,2,1,0:T(8,128)} %param.9) | copy-start | bytes 147460
  14.5 42.2 %copy-start.3 = (f32[3,4,8,128]{3,2,1,0:T(8,128)S(1)}, f32[3,4,8,128]{3,2,1,0:T(8,128)}, u32[]{:S(2)}) copy-start(f32[3,4,8,128]{3,2,1,0:T(8,128)} %param.10) | copy-start | bytes 147460
  14.5 42.3 %all-to-all-start.1 = ((f32[8,24,128]{2,1,0:T(8,128)}), f32[8,24,128]{2,1,0:T(8,128)S(1)}, u32[]{:S(2)}, u32[]{:S(2)}) async-start(f32[8,24,128]{2,1,0:T(8,128)} %get-tuple-element.54), calls=%async_computation.1 | async-start | bytes 196608 | tf_op jit(solution)/shard_map/all_to_all | solution.py:557
  41.3 15.4 %collective-permute-start = (f32[6,8,128]{2,1,0:T(8,128)S(1)}, f32[6,8,128]{2,1,0:T(8,128)S(1)}, u32[]{:S(2)}, u32[]{:S(2)}) collective-permute-start(f32[6,8,128]{2,1,0:T(8,128)S(1)} %copy-done.8), channel_id=1, source_target_pairs={{0,256},{256,512},{512,768},{1,257},{257,513},{513,769},{2,258},{2... | collective-permute-start | bytes 73736 | tf_op jit(solution)/shard_map/ppermute | solution.py:562
  44.4 12.3 %collective-permute-start.2 = (f32[6,8,128]{2,1,0:T(8,128)S(1)}, f32[6,8,128]{2,1,0:T(8,128)S(1)}, u32[]{:S(2)}, u32[]{:S(2)}) collective-permute-start(f32[6,8,128]{2,1,0:T(8,128)S(1)} %copy-done.7), channel_id=1, source_target_pairs={{256,0},{512,256},{768,512},{257,1},{513,257},{769,513},{258,2},{5... | collective-permute-start | bytes 73736 | tf_op jit(solution)/shard_map/ppermute | solution.py:567
  45.7 7.9 %collective-permute-start.1 = (f32[24,128]{1,0:T(8,128)S(1)}, f32[24,128]{1,0:T(8,128)S(1)}, u32[]{:S(2)}, u32[]{:S(2)}) collective-permute-start(f32[24,128]{1,0:T(8,128)S(1)} %copy-done.10), channel_id=1, source_target_pairs={{0,32},{32,64},{64,96},{96,128},{128,160},{160,192},{192,224},{1,3... | collective-permute-start | bytes 36872 | tf_op jit(solution)/shard_map/ppermute | solution.py:562
  51.6 5.0 %collective-permute-start.3 = (f32[24,128]{1,0:T(8,128)S(1)}, f32[24,128]{1,0:T(8,128)S(1)}, u32[]{:S(2)}, u32[]{:S(2)}) collective-permute-start(f32[24,128]{1,0:T(8,128)S(1)} %copy-done.9), channel_id=1, source_target_pairs={{32,0},{64,32},{96,64},{128,96},{160,128},{192,160},{224,192},{33,... | collective-permute-start | bytes 36872 | tf_op jit(solution)/shard_map/ppermute | solution.py:567
  56.7 0.7 copy-start.5
  56.7 0.7 copy-start.6
  56.8 0.7 copy-start.4
  66.3 31.3 %all-to-all-start.3 = ((f32[8,17,1,128]{3,2,1,0:T(1,128)}), f32[8,17,1,128]{3,2,1,0:T(1,128)S(1)}, u32[]{:S(2)}, u32[]{:S(2)}) async-start(f32[8,17,1,128]{3,2,1,0:T(1,128)} %get-tuple-element.67), calls=%async_computation.3 | async-start | bytes 139264 | tf_op jit(solution)/shard_map/all_to_all | solution.py:557
  82.6 14.8 %collective-permute-start.4 = (f32[3,8,128]{2,1,0:T(8,128)S(1)}, f32[3,8,128]{2,1,0:T(8,128)S(1)}, u32[]{:S(2)}, u32[]{:S(2)}) collective-permute-start(f32[3,8,128]{2,1,0:T(8,128)S(1)} %get-tuple-element.71), channel_id=1, source_target_pairs={{0,256},{256,512},{512,768},{1,257},{257,513},{513,769},{2,258},{2... | collective-permute-start | bytes 36872 | tf_op jit(solution)/shard_map/ppermute | solution.py:562
  86.9 10.6 %collective-permute-start.6 = (f32[3,8,128]{2,1,0:T(8,128)S(1)}, f32[3,8,128]{2,1,0:T(8,128)S(1)}, u32[]{:S(2)}, u32[]{:S(2)}) collective-permute-start(f32[3,8,128]{2,1,0:T(8,128)S(1)} %get-tuple-element.73), channel_id=1, source_target_pairs={{256,0},{512,256},{768,512},{257,1},{513,257},{769,513},{258,2},{5... | collective-permute-start | bytes 36872 | tf_op jit(solution)/shard_map/ppermute | solution.py:567
  88.2 5.9 %collective-permute-start.5 = (f32[12,128]{1,0:T(8,128)S(1)}, f32[12,128]{1,0:T(8,128)S(1)}, u32[]{:S(2)}, u32[]{:S(2)}) collective-permute-start(f32[12,128]{1,0:T(8,128)S(1)} %get-tuple-element.72), channel_id=1, source_target_pairs={{0,32},{32,64},{64,96},{96,128},{128,160},{160,192},{192,224},{1,3... | collective-permute-start | bytes 18440 | tf_op jit(solution)/shard_map/ppermute | solution.py:562
  92.1 5.3 %collective-permute-start.7 = (f32[12,128]{1,0:T(8,128)S(1)}, f32[12,128]{1,0:T(8,128)S(1)}, u32[]{:S(2)}, u32[]{:S(2)}) collective-permute-start(f32[12,128]{1,0:T(8,128)S(1)} %get-tuple-element.74), channel_id=1, source_target_pairs={{32,0},{64,32},{96,64},{128,96},{160,128},{192,160},{224,192},{33,... | collective-permute-start | bytes 18440 | tf_op jit(solution)/shard_map/ppermute | solution.py:567
  98.8 11.1 %collective-permute-start.8 = (f32[3,8,128]{2,1,0:T(8,128)S(1)}, f32[3,8,128]{2,1,0:T(8,128)S(1)}, u32[]{:S(2)}, u32[]{:S(2)}) collective-permute-start(f32[3,8,128]{2,1,0:T(8,128)S(1)} %get-tuple-element.80), channel_id=1, source_target_pairs={{0,256},{256,512},{512,768},{1,257},{257,513},{513,769},{2,258},{2... | collective-permute-start | bytes 36872 | tf_op jit(solution)/shard_map/ppermute | solution.py:562
  105.2 4.6 %collective-permute-start.9 = (f32[12,128]{1,0:T(8,128)S(1)}, f32[12,128]{1,0:T(8,128)S(1)}, u32[]{:S(2)}, u32[]{:S(2)}) collective-permute-start(f32[12,128]{1,0:T(8,128)S(1)} %get-tuple-element.81), channel_id=1, source_target_pairs={{0,32},{32,64},{64,96},{96,128},{128,160},{160,192},{192,224},{1,3... | collective-permute-start | bytes 18440 | tf_op jit(solution)/shard_map/ppermute | solution.py:562
  145.2 16.2 %all-to-all-start.6 = ((f32[32,1,128]{2,1,0:T(1,128)}), f32[32,1,128]{2,1,0:T(1,128)S(1)}, u32[]{:S(2)}, u32[]{:S(2)}) async-start(f32[32,1,128]{2,1,0:T(1,128)} %shard_map.95), calls=%async_computation.6 | async-start | bytes 32768 | tf_op jit(solution)/shard_map/all_to_all | solution.py:639
  155.2 6.3 %collective-permute-start.10 = (f32[3,8,128]{2,1,0:T(8,128)S(1)}, f32[3,8,128]{2,1,0:T(8,128)S(1)}, u32[]{:S(2)}, u32[]{:S(2)}) collective-permute-start(f32[3,8,128]{2,1,0:T(8,128)S(1)} %get-tuple-element.86), channel_id=1, source_target_pairs={{256,0},{512,256},{768,512},{257,1},{513,257},{769,513},{258,2},{5... | collective-permute-start | bytes 36872 | tf_op jit(solution)/shard_map/ppermute | solution.py:567
  156.5 5.0 %collective-permute-start.11 = (f32[12,128]{1,0:T(8,128)S(1)}, f32[12,128]{1,0:T(8,128)S(1)}, u32[]{:S(2)}, u32[]{:S(2)}) collective-permute-start(f32[12,128]{1,0:T(8,128)S(1)} %get-tuple-element.87), channel_id=1, source_target_pairs={{32,0},{64,32},{96,64},{128,96},{160,128},{192,160},{224,192},{33,... | collective-permute-start | bytes 18440 | tf_op jit(solution)/shard_map/ppermute | solution.py:567

commit v11 on v9

--- a/solution.py
+++ b/solution.py
@@ -190,7 +190,7 @@
     return lax.div(at, NEAR), lax.rem(at, NEAR)
 
 
-FIRST = (5, 6, 4)
+FIRST = (5, 3, 4)
 
 
 def slot_of(group, count, step):

time: 161 us -> 160 us (level)
  waiting for transfers between devices: 12.4 us -> 10.3 us
    ppermute x6, waiting for transfers between devices: 11.4 us -> 9.49 us  [backward(): return lax.ppermute(piece, axis, [(i + 1, i) for i in range(count - 1)])]
  transfers between devices with their start and end apart: 15 -> 15, of which waited for: 5 -> 4; matrix products, arithmetic and copies ran while one was open for 0% -> 0% of each run, Pallas kernels for 0% -> 0%
where the time goes in v11:
time: 160 us; the launch traced here: 159 us
  starting transfers between devices  103 us (64%)
  blocking collectives  35.6 us (22%)
  waiting for transfers between devices  10.3 us (6%)
  Pallas kernels  8.33 us (5%)
    all_to_all x3, starting transfers between devices, far_slots(): return lax.all_to_all(sent, 'gz', 0, 0, axis_index_groups=groups)  65.6 us
    ppermute x6, starting transfers between devices, forward(): return lax.ppermute(piece, axis, [(i, i + 1) for i in range(count - 1)])  26.2 us
    all_to_all x3, blocking collectives, near_slots(): return lax.all_to_all(sent, 'gz', 0, 0, axis_index_groups=groups)  24.8 us
    ppermute x6, starting transfers between devices, backward(): return lax.ppermute(piece, axis, [(i + 1, i) for i in range(count - 1)])  11.5 us
    all_to_all x1, blocking collectives, body(): lines = lax.all_to_all(sent, ('gx', 'gy'), 0, 0, axis_index_groups=order)  10.8 us
    ppermute x6, waiting for transfers between devices, backward(): return lax.ppermute(piece, axis, [(i + 1, i) for i in range(count - 1)])  9.49 us
    pallas_call x12, Pallas kernels, call(): pl.pallas_call(kernel, out_shape=[jax.ShapeDtypeStruct(shape, F32) for sh...  8.33 us
  transfers between devices with their start and end apart: 15, of which 4 were waited for; matrix products, arithmetic and copies ran while one was open for 0% of the time, Pallas kernels for 0%

profile of v11, /device:TPU:1, one launch (start us, length us, event | category | flops | bytes accessed | tf_op | source)
XLA Modules:
  0.0 159.2 jit_solution(2607562912375922596)
XLA Ops:
  0.6 2.0 %shard_map.86 = (f32[4,24,128]{2,1,0:T(8,128)}, f32[6,8,128]{2,1,0:T(8,128)}, f32[6,8,128]{2,1,0:T(8,128)}, f32[24,128]{1,0:T(8,128)}, f32[24,128]{1,0:T(8,128)}) custom-call(f32[3,32,128]{2,1,0:T(8,128)} %bitcast.6, f32[3,32,128]{2,1,0:T(8,128)} %bitcast.19, s32[1,1,512]{2,1,0:T(1,128)} %cell.5, s32[1,1,512]{2,1,0:T(1,128)} %well.5, f32[1,1,512]{2,1,0:T(1,128)} %factor.5), custom_call_target="tpu_custom_call" | custom-call | tf_op jit(solution)/shard_map/pallas_call | solution.py:529
  2.7 11.0 %all_to_all.35.slots = f32[4,24,128]{2,1,0:T(8,128)S(1)} all-to-all(f32[4,24,128]{2,1,0:T(8,128)} %get-tuple-element.47), channel_id=1, replica_groups={{0,1,2,3},{4,5,6,7},{8,9,10,11},{12,13,14,15},{16,17,18,19},{20,21,22,2..., dimensions={0} | all-to-all | bytes 98304 | tf_op jit(solution)/shard_map/all_to_all | solution.py:545
  13.7 0.8 shard_map.87
  14.5 26.8 %all-to-all-start.1 = ((f32[8,24,128]{2,1,0:T(8,128)}), f32[8,24,128]{2,1,0:T(8,128)S(1)}, u32[]{:S(2)}, u32[]{:S(2)}) async-start(f32[8,24,128]{2,1,0:T(8,128)} %get-tuple-element.53), calls=%async_computation.1 | async-start | bytes 196608 | tf_op jit(solution)/shard_map/all_to_all | solution.py:557
  41.3 3.1 %collective-permute-start = (f32[6,8,128]{2,1,0:T(8,128)S(1)}, f32[6,8,128]{2,1,0:T(8,128)S(1)}, u32[]{:S(2)}, u32[]{:S(2)}) collective-permute-start(f32[6,8,128]{2,1,0:T(8,128)S(1)} %copy-done.8), channel_id=1, source_target_pairs={{0,256},{256,512},{512,768},{1,257},{257,513},{513,769},{2,258},{2... | collective-permute-start | bytes 73736 | tf_op jit(solution)/shard_map/ppermute | solution.py:562
  44.4 1.3 collective-permute-start.2
  45.7 5.9 %collective-permute-start.1 = (f32[24,128]{1,0:T(8,128)S(1)}, f32[24,128]{1,0:T(8,128)S(1)}, u32[]{:S(2)}, u32[]{:S(2)}) collective-permute-start(f32[24,128]{1,0:T(8,128)S(1)} %copy-done.10), channel_id=1, source_target_pairs={{0,32},{32,64},{64,96},{96,128},{128,160},{160,192},{192,224},{1,3... | collective-permute-start | bytes 36872 | tf_op jit(solution)/shard_map/ppermute | solution.py:562
  51.6 1.9 %collective-permute-start.3 = (f32[24,128]{1,0:T(8,128)S(1)}, f32[24,128]{1,0:T(8,128)S(1)}, u32[]{:S(2)}, u32[]{:S(2)}) collective-permute-start(f32[24,128]{1,0:T(8,128)S(1)} %copy-done.9), channel_id=1, source_target_pairs={{32,0},{64,32},{96,64},{128,96},{160,128},{192,160},{224,192},{33,... | collective-permute-start | bytes 36872 | tf_op jit(solution)/shard_map/ppermute | solution.py:567
  53.6 3.1 %collective-permute-done.3.yh = f32[24,128]{1,0:T(8,128)S(1)} collective-permute-done((f32[24,128]{1,0:T(8,128)S(1)}, f32[24,128]{1,0:T(8,128)S(1)}, u32[]{:S(2)}, u32[]{:S(2)}) %collective-permute-start.3) | collective-permute-done | bytes 12320 | tf_op jit(solution)/shard_map/ppermute | solution.py:567
  56.8 0.6 copy-done.5
  57.5 1.2 shard_map.89
  58.7 6.9 %all_to_all.36.slots = f32[4,24,128]{2,1,0:T(8,128)S(1)} all-to-all(f32[4,24,128]{2,1,0:T(8,128)S(1)} %broadcast_in_dim.4), channel_id=1, replica_groups={{0,1,2,3},{4,5,6,7},{8,9,10,11},{12,13,14,15},{16,17,18,19},{20,21,22,2..., dimensions={0} | all-to-all | bytes 98304 | tf_op jit(solution)/shard_map/all_to_all | solution.py:545
  65.6 0.7 shard_map.90
  66.3 17.7 %all-to-all-start.3 = ((f32[8,17,1,128]{3,2,1,0:T(1,128)}), f32[8,17,1,128]{3,2,1,0:T(1,128)S(1)}, u32[]{:S(2)}, u32[]{:S(2)}) async-start(f32[8,17,1,128]{3,2,1,0:T(1,128)} %get-tuple-element.66), calls=%async_computation.3 | async-start | bytes 139264 | tf_op jit(solution)/shard_map/all_to_all | solution.py:557
  84.1 3.1 %collective-permute-start.4 = (f32[3,8,128]{2,1,0:T(8,128)S(1)}, f32[3,8,128]{2,1,0:T(8,128)S(1)}, u32[]{:S(2)}, u32[]{:S(2)}) collective-permute-start(f32[3,8,128]{2,1,0:T(8,128)S(1)} %get-tuple-element.70), channel_id=1, source_target_pairs={{0,256},{256,512},{512,768},{1,257},{257,513},{513,769},{2,258},{2... | collective-permute-start | bytes 36872 | tf_op jit(solution)/shard_map/ppermute | solution.py:562
  87.2 1.3 collective-permute-start.6
  88.5 7.5 %collective-permute-start.5 = (f32[12,128]{1,0:T(8,128)S(1)}, f32[12,128]{1,0:T(8,128)S(1)}, u32[]{:S(2)}, u32[]{:S(2)}) collective-permute-start(f32[12,128]{1,0:T(8,128)S(1)} %get-tuple-element.71), channel_id=1, source_target_pairs={{0,32},{32,64},{64,96},{96,128},{128,160},{160,192},{192,224},{1,3... | collective-permute-start | bytes 18440 | tf_op jit(solution)/shard_map/ppermute | solution.py:562
  96.0 1.9 %collective-permute-start.7 = (f32[12,128]{1,0:T(8,128)S(1)}, f32[12,128]{1,0:T(8,128)S(1)}, u32[]{:S(2)}, u32[]{:S(2)}) collective-permute-start(f32[12,128]{1,0:T(8,128)S(1)} %get-tuple-element.73), channel_id=1, source_target_pairs={{32,0},{64,32},{96,64},{128,96},{160,128},{192,160},{224,192},{33,... | collective-permute-start | bytes 18440 | tf_op jit(solution)/shard_map/ppermute | solution.py:567
  98.0 3.0 %collective-permute-done.7.yh = f32[12,128]{1,0:T(8,128)S(1)} collective-permute-done((f32[12,128]{1,0:T(8,128)S(1)}, f32[12,128]{1,0:T(8,128)S(1)}, u32[]{:S(2)}, u32[]{:S(2)}) %collective-permute-start.7) | collective-permute-done | bytes 6176 | tf_op jit(solution)/shard_map/ppermute | solution.py:567
  101.1 1.1 shard_map.92
  102.2 4.3 %collective-permute-start.8 = (f32[3,8,128]{2,1,0:T(8,128)S(1)}, f32[3,8,128]{2,1,0:T(8,128)S(1)}, u32[]{:S(2)}, u32[]{:S(2)}) collective-permute-start(f32[3,8,128]{2,1,0:T(8,128)S(1)} %get-tuple-element.79), channel_id=1, source_target_pairs={{0,256},{256,512},{512,768},{1,257},{257,513},{513,769},{2,258},{2... | collective-permute-start | bytes 36872 | tf_op jit(solution)/shard_map/ppermute | solution.py:562
  106.5 2.2 %collective-permute-start.9 = (f32[12,128]{1,0:T(8,128)S(1)}, f32[12,128]{1,0:T(8,128)S(1)}, u32[]{:S(2)}, u32[]{:S(2)}) collective-permute-start(f32[12,128]{1,0:T(8,128)S(1)} %get-tuple-element.80), channel_id=1, source_target_pairs={{0,32},{32,64},{64,96},{96,128},{128,160},{160,192},{192,224},{1,3... | collective-permute-start | bytes 18440 | tf_op jit(solution)/shard_map/ppermute | solution.py:562
  108.7 0.8 collective-permute-done.9.yl
  109.7 6.9 %all_to_all.37.slots = f32[4,24,128]{2,1,0:T(8,128)S(1)} all-to-all(f32[4,24,128]{2,1,0:T(8,128)S(1)} %broadcast_in_dim.5), channel_id=1, replica_groups={{0,1,2,3},{4,5,6,7},{8,9,10,11},{12,13,14,15},{16,17,18,19},{20,21,22,2..., dimensions={0} | all-to-all | bytes 98304 | tf_op jit(solution)/shard_map/all_to_all | solution.py:545
  116.6 0.8 shard_map.94
  117.4 21.1 %all-to-all-start.5 = ((f32[8,20,1,128]{3,2,1,0:T(1,128)}), f32[8,20,1,128]{3,2,1,0:T(1,128)S(1)}, u32[]{:S(2)}, u32[]{:S(2)}) async-start(f32[8,20,1,128]{3,2,1,0:T(1,128)} %get-tuple-element.84), calls=%async_computation.5 | async-start | bytes 163840 | tf_op jit(solution)/shard_map/all_to_all | solution.py:557
  138.5 1.3 collective-permute-start.10
  139.8 3.8 %collective-permute-start.11 = (f32[12,128]{1,0:T(8,128)S(1)}, f32[12,128]{1,0:T(8,128)S(1)}, u32[]{:S(2)}, u32[]{:S(2)}) collective-permute-start(f32[12,128]{1,0:T(8,128)S(1)} %get-tuple-element.86), channel_id=1, source_target_pairs={{32,0},{64,32},{96,64},{128,96},{160,128},{192,160},{224,192},{33,... | collective-permute-start | bytes 18440 | tf_op jit(solution)/shard_map/ppermute | solution.py:567
  143.6 3.4 %collective-permute-done.11.yh = f32[12,128]{1,0:T(8,128)S(1)} collective-permute-done((f32[12,128]{1,0:T(8,128)S(1)}, f32[12,128]{1,0:T(8,128)S(1)}, u32[]{:S(2)}, u32[]{:S(2)}) %collective-permute-start.11) | collective-permute-done | bytes 6176 | tf_op jit(solution)/shard_map/ppermute | solution.py:567
  147.0 0.2 shard_map.96
  147.3 10.8 %all_to_all.38.lines = f32[32,1,128]{2,1,0:T(1,128)S(1)} all-to-all(f32[32,1,128]{2,1,0:T(1,128)S(1)} %shard_map.96), channel_id=1, replica_groups={{640,672,704,736,768,800,832,864,896,928,960,992,0,32,64,96,128,160,192..., dimensions={0} | all-to-all | bytes 32768 | tf_op jit(solution)/shard_map/all_to_all | solution.py:641
  158.1 1.2 shard_map.97
  (38 shorter events, 0.6 us)
Async XLA Ops:
  2.7 43.0 %copy-start.10 = (f32[24,128]{1,0:T(8,128)S(1)}, f32[24,128]{1,0:T(8,128)}, u32[]{:S(2)}) copy-start(f32[24,128]{1,0:T(8,128)} %get-tuple-element.56) | copy-start | bytes 36868
  13.7 27.6 %copy-start.8 = (f32[6,8,128]{2,1,0:T(8,128)S(1)}, f32[6,8,128]{2,1,0:T(8,128)}, u32[]{:S(2)}) copy-start(f32[6,8,128]{2,1,0:T(8,128)} %get-tuple-element.55) | copy-start | bytes 73732
  13.7 30.7 %copy-start.7 = (f32[6,8,128]{2,1,0:T(8,128)S(1)}, f32[6,8,128]{2,1,0:T(8,128)}, u32[]{:S(2)}) copy-start(f32[6,8,128]{2,1,0:T(8,128)} %get-tuple-element.57) | copy-start | bytes 73732
  13.7 37.9 %copy-start.9 = (f32[24,128]{1,0:T(8,128)S(1)}, f32[24,128]{1,0:T(8,128)}, u32[]{:S(2)}) copy-start(f32[24,128]{1,0:T(8,128)} %get-tuple-element.58) | copy-start | bytes 36868
  14.5 42.2 %copy-start = (f32[3,4,8,128]{3,2,1,0:T(8,128)S(1)}, f32[3,4,8,128]{3,2,1,0:T(8,128)}, u32[]{:S(2)}) copy-start(f32[3,4,8,128]{3,2,1,0:T(8,128)} %param.7) | copy-start | bytes 147460
  14.5 42.2 %copy-start.1 = (f32[3,4,8,128]{3,2,1,0:T(8,128)S(1)}, f32[3,4,8,128]{3,2,1,0:T(8,128)}, u32[]{:S(2)}) copy-start(f32[3,4,8,128]{3,2,1,0:T(8,128)} %param.8) | copy-start | bytes 147460
  14.5 42.2 %copy-start.2 = (f32[3,4,8,128]{3,2,1,0:T(8,128)S(1)}, f32[3,4,8,128]{3,2,1,0:T(8,128)}, u32[]{:S(2)}) copy-start(f32[3,4,8,128]{3,2,1,0:T(8,128)} %param.9) | copy-start | bytes 147460
  14.5 42.2 %copy-start.3 = (f32[3,4,8,128]{3,2,1,0:T(8,128)S(1)}, f32[3,4,8,128]{3,2,1,0:T(8,128)}, u32[]{:S(2)}) copy-start(f32[3,4,8,128]{3,2,1,0:T(8,128)} %param.10) | copy-start | bytes 147460
  14.5 42.3 %all-to-all-start.1 = ((f32[8,24,128]{2,1,0:T(8,128)}), f32[8,24,128]{2,1,0:T(8,128)S(1)}, u32[]{:S(2)}, u32[]{:S(2)}) async-start(f32[8,24,128]{2,1,0:T(8,128)} %get-tuple-element.53), calls=%async_computation.1 | async-start | bytes 196608 | tf_op jit(solution)/shard_map/all_to_all | solution.py:557
  41.3 15.4 %collective-permute-start = (f32[6,8,128]{2,1,0:T(8,128)S(1)}, f32[6,8,128]{2,1,0:T(8,128)S(1)}, u32[]{:S(2)}, u32[]{:S(2)}) collective-permute-start(f32[6,8,128]{2,1,0:T(8,128)S(1)} %copy-done.8), channel_id=1, source_target_pairs={{0,256},{256,512},{512,768},{1,257},{257,513},{513,769},{2,258},{2... | collective-permute-start | bytes 73736 | tf_op jit(solution)/shard_map/ppermute | solution.py:562
  44.4 12.3 %collective-permute-start.2 = (f32[6,8,128]{2,1,0:T(8,128)S(1)}, f32[6,8,128]{2,1,0:T(8,128)S(1)}, u32[]{:S(2)}, u32[]{:S(2)}) collective-permute-start(f32[6,8,128]{2,1,0:T(8,128)S(1)} %copy-done.7), channel_id=1, source_target_pairs={{256,0},{512,256},{768,512},{257,1},{513,257},{769,513},{258,2},{5... | collective-permute-start | bytes 73736 | tf_op jit(solution)/shard_map/ppermute | solution.py:567
  45.7 7.9 %collective-permute-start.1 = (f32[24,128]{1,0:T(8,128)S(1)}, f32[24,128]{1,0:T(8,128)S(1)}, u32[]{:S(2)}, u32[]{:S(2)}) collective-permute-start(f32[24,128]{1,0:T(8,128)S(1)} %copy-done.10), channel_id=1, source_target_pairs={{0,32},{32,64},{64,96},{96,128},{128,160},{160,192},{192,224},{1,3... | collective-permute-start | bytes 36872 | tf_op jit(solution)/shard_map/ppermute | solution.py:562
  51.6 5.0 %collective-permute-start.3 = (f32[24,128]{1,0:T(8,128)S(1)}, f32[24,128]{1,0:T(8,128)S(1)}, u32[]{:S(2)}, u32[]{:S(2)}) collective-permute-start(f32[24,128]{1,0:T(8,128)S(1)} %copy-done.9), channel_id=1, source_target_pairs={{32,0},{64,32},{96,64},{128,96},{160,128},{192,160},{224,192},{33,... | collective-permute-start | bytes 36872 | tf_op jit(solution)/shard_map/ppermute | solution.py:567
  56.7 0.7 copy-start.5
  56.7 0.7 copy-start.6
  56.8 0.7 copy-start.4
  66.3 34.7 %all-to-all-start.3 = ((f32[8,17,1,128]{3,2,1,0:T(1,128)}), f32[8,17,1,128]{3,2,1,0:T(1,128)S(1)}, u32[]{:S(2)}, u32[]{:S(2)}) async-start(f32[8,17,1,128]{3,2,1,0:T(1,128)} %get-tuple-element.66), calls=%async_computation.3 | async-start | bytes 139264 | tf_op jit(solution)/shard_map/all_to_all | solution.py:557
  84.1 16.9 %collective-permute-start.4 = (f32[3,8,128]{2,1,0:T(8,128)S(1)}, f32[3,8,128]{2,1,0:T(8,128)S(1)}, u32[]{:S(2)}, u32[]{:S(2)}) collective-permute-start(f32[3,8,128]{2,1,0:T(8,128)S(1)} %get-tuple-element.70), channel_id=1, source_target_pairs={{0,256},{256,512},{512,768},{1,257},{257,513},{513,769},{2,258},{2... | collective-permute-start | bytes 36872 | tf_op jit(solution)/shard_map/ppermute | solution.py:562
  87.2 13.8 %collective-permute-start.6 = (f32[3,8,128]{2,1,0:T(8,128)S(1)}, f32[3,8,128]{2,1,0:T(8,128)S(1)}, u32[]{:S(2)}, u32[]{:S(2)}) collective-permute-start(f32[3,8,128]{2,1,0:T(8,128)S(1)} %get-tuple-element.72), channel_id=1, source_target_pairs={{256,0},{512,256},{768,512},{257,1},{513,257},{769,513},{258,2},{5... | collective-permute-start | bytes 36872 | tf_op jit(solution)/shard_map/ppermute | solution.py:567
  88.5 9.5 %collective-permute-start.5 = (f32[12,128]{1,0:T(8,128)S(1)}, f32[12,128]{1,0:T(8,128)S(1)}, u32[]{:S(2)}, u32[]{:S(2)}) collective-permute-start(f32[12,128]{1,0:T(8,128)S(1)} %get-tuple-element.71), channel_id=1, source_target_pairs={{0,32},{32,64},{64,96},{96,128},{128,160},{160,192},{192,224},{1,3... | collective-permute-start | bytes 18440 | tf_op jit(solution)/shard_map/ppermute | solution.py:562
  96.0 5.0 %collective-permute-start.7 = (f32[12,128]{1,0:T(8,128)S(1)}, f32[12,128]{1,0:T(8,128)S(1)}, u32[]{:S(2)}, u32[]{:S(2)}) collective-permute-start(f32[12,128]{1,0:T(8,128)S(1)} %get-tuple-element.73), channel_id=1, source_target_pairs={{32,0},{64,32},{96,64},{128,96},{160,128},{192,160},{224,192},{33,... | collective-permute-start | bytes 18440 | tf_op jit(solution)/shard_map/ppermute | solution.py:567
  102.2 7.4 %collective-permute-start.8 = (f32[3,8,128]{2,1,0:T(8,128)S(1)}, f32[3,8,128]{2,1,0:T(8,128)S(1)}, u32[]{:S(2)}, u32[]{:S(2)}) collective-permute-start(f32[3,8,128]{2,1,0:T(8,128)S(1)} %get-tuple-element.79), channel_id=1, source_target_pairs={{0,256},{256,512},{512,768},{1,257},{257,513},{513,769},{2,258},{2... | collective-permute-start | bytes 36872 | tf_op jit(solution)/shard_map/ppermute | solution.py:562
  106.5 3.1 %collective-permute-start.9 = (f32[12,128]{1,0:T(8,128)S(1)}, f32[12,128]{1,0:T(8,128)S(1)}, u32[]{:S(2)}, u32[]{:S(2)}) collective-permute-start(f32[12,128]{1,0:T(8,128)S(1)} %get-tuple-element.80), channel_id=1, source_target_pairs={{0,32},{32,64},{64,96},{96,128},{128,160},{160,192},{192,224},{1,3... | collective-permute-start | bytes 18440 | tf_op jit(solution)/shard_map/ppermute | solution.py:562
  117.4 29.6 %all-to-all-start.5 = ((f32[8,20,1,128]{3,2,1,0:T(1,128)}), f32[8,20,1,128]{3,2,1,0:T(1,128)S(1)}, u32[]{:S(2)}, u32[]{:S(2)}) async-start(f32[8,20,1,128]{3,2,1,0:T(1,128)} %get-tuple-element.84), calls=%async_computation.5 | async-start | bytes 163840 | tf_op jit(solution)/shard_map/all_to_all | solution.py:557
  138.5 8.5 %collective-permute-start.10 = (f32[3,8,128]{2,1,0:T(8,128)S(1)}, f32[3,8,128]{2,1,0:T(8,128)S(1)}, u32[]{:S(2)}, u32[]{:S(2)}) collective-permute-start(f32[3,8,128]{2,1,0:T(8,128)S(1)} %get-tuple-element.85), channel_id=1, source_target_pairs={{256,0},{512,256},{768,512},{257,1},{513,257},{769,513},{258,2},{5... | collective-permute-start | bytes 36872 | tf_op jit(solution)/shard_map/ppermute | solution.py:567
  139.8 7.2 %collective-permute-start.11 = (f32[12,128]{1,0:T(8,128)S(1)}, f32[12,128]{1,0:T(8,128)S(1)}, u32[]{:S(2)}, u32[]{:S(2)}) collective-permute-start(f32[12,128]{1,0:T(8,128)S(1)} %get-tuple-element.86), channel_id=1, source_target_pairs={{32,0},{64,32},{96,64},{128,96},{160,128},{192,160},{224,192},{33,... | collective-permute-start | bytes 18440 | tf_op jit(solution)/shard_map/ppermute | solution.py:567

commit v12 on v11

--- a/solution.py
+++ b/solution.py
@@ -241,12 +241,16 @@
     ]
     for copy in copies:
         copy.start()
-    for copy in copies:
-        copy.wait()
+    copies[0].wait()
     row, lane = cell_masks(cell[0])
+    copies[3].wait()
+    wells = well_mask(well[0])
+    copies[1].wait()
     values = gather_cells([right[u] for u in range(3)], row, lane)
+    copies[2].wait()
     weight = factor[0]
-    sums = scatter_wells([weight * v for v in values] + [weight], well_mask(well[0]))
+    sums = scatter_wells([weight * v for v in values] + [weight], wells)
+    copies[4].wait()
     ends = fold(end_tile([(right, 0), (mobility, 32)], [(right, 16), (mobility, 48)]))
     for k in range(NEAR):
         put_well_rows(table.at[k], sums)

time: 160 us -> 161 us (level)
  no operation moved by 1% of the time
where the time goes in v12:
time: 161 us; the launch traced here: 160 us
  starting transfers between devices  103 us (64%)
  blocking collectives  35.6 us (22%)
  waiting for transfers between devices  10.3 us (6%)
  Pallas kernels  8.62 us (5%)
    all_to_all x3, starting transfers between devices, far_slots(): return lax.all_to_all(sent, 'gz', 0, 0, axis_index_groups=groups)  65.6 us
    ppermute x6, starting transfers between devices, forward(): return lax.ppermute(piece, axis, [(i, i + 1) for i in range(count - 1)])  26.2 us
    all_to_all x3, blocking collectives, near_slots(): return lax.all_to_all(sent, 'gz', 0, 0, axis_index_groups=groups)  24.8 us
    ppermute x6, starting transfers between devices, backward(): return lax.ppermute(piece, axis, [(i + 1, i) for i in range(count - 1)])  11.5 us
    all_to_all x1, blocking collectives, body(): lines = lax.all_to_all(sent, ('gx', 'gy'), 0, 0, axis_index_groups=order)  10.8 us
    ppermute x6, waiting for transfers between devices, backward(): return lax.ppermute(piece, axis, [(i + 1, i) for i in range(count - 1)])  9.49 us
    pallas_call x12, Pallas kernels, call(): pl.pallas_call(kernel, out_shape=[jax.ShapeDtypeStruct(shape, F32) for sh...  8.62 us
  transfers between devices with their start and end apart: 15, of which 4 were waited for; matrix products, arithmetic and copies ran while one was open for 0% of the time, Pallas kernels for 0%

profile of v12, /device:TPU:1, one launch (start us, length us, event | category | flops | bytes accessed | tf_op | source)
XLA Modules:
  0.0 159.5 jit_solution(1641077145664341614)
XLA Ops:
  0.6 2.3 %shard_map.86 = (f32[4,24,128]{2,1,0:T(8,128)}, f32[6,8,128]{2,1,0:T(8,128)}, f32[6,8,128]{2,1,0:T(8,128)}, f32[24,128]{1,0:T(8,128)}, f32[24,128]{1,0:T(8,128)}) custom-call(f32[3,32,128]{2,1,0:T(8,128)} %bitcast.6, f32[3,32,128]{2,1,0:T(8,128)} %bitcast.19, s32[1,1,512]{2,1,0:T(1,128)} %cell.5, s32[1,1,512]{2,1,0:T(1,128)} %well.5, f32[1,1,512]{2,1,0:T(1,128)} %factor.5), custom_call_target="tpu_custom_call" | custom-call | tf_op jit(solution)/shard_map/pallas_call | solution.py:533
  3.0 11.0 %all_to_all.35.slots = f32[4,24,128]{2,1,0:T(8,128)S(1)} all-to-all(f32[4,24,128]{2,1,0:T(8,128)} %get-tuple-element.47), channel_id=1, replica_groups={{0,1,2,3},{4,5,6,7},{8,9,10,11},{12,13,14,15},{16,17,18,19},{20,21,22,2..., dimensions={0} | all-to-all | bytes 98304 | tf_op jit(solution)/shard_map/all_to_all | solution.py:549
  14.0 0.8 shard_map.87
  14.8 26.8 %all-to-all-start.1 = ((f32[8,24,128]{2,1,0:T(8,128)}), f32[8,24,128]{2,1,0:T(8,128)S(1)}, u32[]{:S(2)}, u32[]{:S(2)}) async-start(f32[8,24,128]{2,1,0:T(8,128)} %get-tuple-element.53), calls=%async_computation.1 | async-start | bytes 196608 | tf_op jit(solution)/shard_map/all_to_all | solution.py:561
  41.5 3.1 %collective-permute-start = (f32[6,8,128]{2,1,0:T(8,128)S(1)}, f32[6,8,128]{2,1,0:T(8,128)S(1)}, u32[]{:S(2)}, u32[]{:S(2)}) collective-permute-start(f32[6,8,128]{2,1,0:T(8,128)S(1)} %copy-done.8), channel_id=1, source_target_pairs={{0,256},{256,512},{512,768},{1,257},{257,513},{513,769},{2,258},{2... | collective-permute-start | bytes 73736 | tf_op jit(solution)/shard_map/ppermute | solution.py:566
  44.7 1.3 collective-permute-start.2
  46.0 5.9 %collective-permute-start.1 = (f32[24,128]{1,0:T(8,128)S(1)}, f32[24,128]{1,0:T(8,128)S(1)}, u32[]{:S(2)}, u32[]{:S(2)}) collective-permute-start(f32[24,128]{1,0:T(8,128)S(1)} %copy-done.10), channel_id=1, source_target_pairs={{0,32},{32,64},{64,96},{96,128},{128,160},{160,192},{192,224},{1,3... | collective-permute-start | bytes 36872 | tf_op jit(solution)/shard_map/ppermute | solution.py:566
  51.9 1.9 %collective-permute-start.3 = (f32[24,128]{1,0:T(8,128)S(1)}, f32[24,128]{1,0:T(8,128)S(1)}, u32[]{:S(2)}, u32[]{:S(2)}) collective-permute-start(f32[24,128]{1,0:T(8,128)S(1)} %copy-done.9), channel_id=1, source_target_pairs={{32,0},{64,32},{96,64},{128,96},{160,128},{192,160},{224,192},{33,... | collective-permute-start | bytes 36872 | tf_op jit(solution)/shard_map/ppermute | solution.py:571
  53.9 3.1 %collective-permute-done.3.yh = f32[24,128]{1,0:T(8,128)S(1)} collective-permute-done((f32[24,128]{1,0:T(8,128)S(1)}, f32[24,128]{1,0:T(8,128)S(1)}, u32[]{:S(2)}, u32[]{:S(2)}) %collective-permute-start.3) | collective-permute-done | bytes 12320 | tf_op jit(solution)/shard_map/ppermute | solution.py:571
  57.1 0.6 copy-done.5
  57.8 1.2 shard_map.89
  59.0 6.9 %all_to_all.36.slots = f32[4,24,128]{2,1,0:T(8,128)S(1)} all-to-all(f32[4,24,128]{2,1,0:T(8,128)S(1)} %broadcast_in_dim.4), channel_id=1, replica_groups={{0,1,2,3},{4,5,6,7},{8,9,10,11},{12,13,14,15},{16,17,18,19},{20,21,22,2..., dimensions={0} | all-to-all | bytes 98304 | tf_op jit(solution)/shard_map/all_to_all | solution.py:549
  65.9 0.7 shard_map.90
  66.6 17.7 %all-to-all-start.3 = ((f32[8,17,1,128]{3,2,1,0:T(1,128)}), f32[8,17,1,128]{3,2,1,0:T(1,128)S(1)}, u32[]{:S(2)}, u32[]{:S(2)}) async-start(f32[8,17,1,128]{3,2,1,0:T(1,128)} %get-tuple-element.66), calls=%async_computation.3 | async-start | bytes 139264 | tf_op jit(solution)/shard_map/all_to_all | solution.py:561
  84.4 3.1 %collective-permute-start.4 = (f32[3,8,128]{2,1,0:T(8,128)S(1)}, f32[3,8,128]{2,1,0:T(8,128)S(1)}, u32[]{:S(2)}, u32[]{:S(2)}) collective-permute-start(f32[3,8,128]{2,1,0:T(8,128)S(1)} %get-tuple-element.70), channel_id=1, source_target_pairs={{0,256},{256,512},{512,768},{1,257},{257,513},{513,769},{2,258},{2... | collective-permute-start | bytes 36872 | tf_op jit(solution)/shard_map/ppermute | solution.py:566
  87.5 1.3 collective-permute-start.6
  88.8 7.5 %collective-permute-start.5 = (f32[12,128]{1,0:T(8,128)S(1)}, f32[12,128]{1,0:T(8,128)S(1)}, u32[]{:S(2)}, u32[]{:S(2)}) collective-permute-start(f32[12,128]{1,0:T(8,128)S(1)} %get-tuple-element.71), channel_id=1, source_target_pairs={{0,32},{32,64},{64,96},{96,128},{128,160},{160,192},{192,224},{1,3... | collective-permute-start | bytes 18440 | tf_op jit(solution)/shard_map/ppermute | solution.py:566
  96.3 1.9 %collective-permute-start.7 = (f32[12,128]{1,0:T(8,128)S(1)}, f32[12,128]{1,0:T(8,128)S(1)}, u32[]{:S(2)}, u32[]{:S(2)}) collective-permute-start(f32[12,128]{1,0:T(8,128)S(1)} %get-tuple-element.73), channel_id=1, source_target_pairs={{32,0},{64,32},{96,64},{128,96},{160,128},{192,160},{224,192},{33,... | collective-permute-start | bytes 18440 | tf_op jit(solution)/shard_map/ppermute | solution.py:571
  98.3 3.0 %collective-permute-done.7.yh = f32[12,128]{1,0:T(8,128)S(1)} collective-permute-done((f32[12,128]{1,0:T(8,128)S(1)}, f32[12,128]{1,0:T(8,128)S(1)}, u32[]{:S(2)}, u32[]{:S(2)}) %collective-permute-start.7) | collective-permute-done | bytes 6176 | tf_op jit(solution)/shard_map/ppermute | solution.py:571
  101.4 1.1 shard_map.92
  102.4 4.3 %collective-permute-start.8 = (f32[3,8,128]{2,1,0:T(8,128)S(1)}, f32[3,8,128]{2,1,0:T(8,128)S(1)}, u32[]{:S(2)}, u32[]{:S(2)}) collective-permute-start(f32[3,8,128]{2,1,0:T(8,128)S(1)} %get-tuple-element.79), channel_id=1, source_target_pairs={{0,256},{256,512},{512,768},{1,257},{257,513},{513,769},{2,258},{2... | collective-permute-start | bytes 36872 | tf_op jit(solution)/shard_map/ppermute | solution.py:566
  106.8 2.2 %collective-permute-start.9 = (f32[12,128]{1,0:T(8,128)S(1)}, f32[12,128]{1,0:T(8,128)S(1)}, u32[]{:S(2)}, u32[]{:S(2)}) collective-permute-start(f32[12,128]{1,0:T(8,128)S(1)} %get-tuple-element.80), channel_id=1, source_target_pairs={{0,32},{32,64},{64,96},{96,128},{128,160},{160,192},{192,224},{1,3... | collective-permute-start | bytes 18440 | tf_op jit(solution)/shard_map/ppermute | solution.py:566
  109.0 0.8 collective-permute-done.9.yl
  110.0 6.9 %all_to_all.37.slots = f32[4,24,128]{2,1,0:T(8,128)S(1)} all-to-all(f32[4,24,128]{2,1,0:T(8,128)S(1)} %broadcast_in_dim.5), channel_id=1, replica_groups={{0,1,2,3},{4,5,6,7},{8,9,10,11},{12,13,14,15},{16,17,18,19},{20,21,22,2..., dimensions={0} | all-to-all | bytes 98304 | tf_op jit(solution)/shard_map/all_to_all | solution.py:549
  116.9 0.8 shard_map.94
  117.7 21.1 %all-to-all-start.5 = ((f32[8,20,1,128]{3,2,1,0:T(1,128)}), f32[8,20,1,128]{3,2,1,0:T(1,128)S(1)}, u32[]{:S(2)}, u32[]{:S(2)}) async-start(f32[8,20,1,128]{3,2,1,0:T(1,128)} %get-tuple-element.84), calls=%async_computation.5 | async-start | bytes 163840 | tf_op jit(solution)/shard_map/all_to_all | solution.py:561
  138.8 1.3 collective-permute-start.10
  140.1 3.8 %collective-permute-start.11 = (f32[12,128]{1,0:T(8,128)S(1)}, f32[12,128]{1,0:T(8,128)S(1)}, u32[]{:S(2)}, u32[]{:S(2)}) collective-permute-start(f32[12,128]{1,0:T(8,128)S(1)} %get-tuple-element.86), channel_id=1, source_target_pairs={{32,0},{64,32},{96,64},{128,96},{160,128},{192,160},{224,192},{33,... | collective-permute-start | bytes 18440 | tf_op jit(solution)/shard_map/ppermute | solution.py:571
  143.9 3.4 %collective-permute-done.11.yh = f32[12,128]{1,0:T(8,128)S(1)} collective-permute-done((f32[12,128]{1,0:T(8,128)S(1)}, f32[12,128]{1,0:T(8,128)S(1)}, u32[]{:S(2)}, u32[]{:S(2)}) %collective-permute-start.11) | collective-permute-done | bytes 6176 | tf_op jit(solution)/shard_map/ppermute | solution.py:571
  147.3 0.2 shard_map.96
  147.5 10.8 %all_to_all.38.lines = f32[32,1,128]{2,1,0:T(1,128)S(1)} all-to-all(f32[32,1,128]{2,1,0:T(1,128)S(1)} %shard_map.96), channel_id=1, replica_groups={{640,672,704,736,768,800,832,864,896,928,960,992,0,32,64,96,128,160,192..., dimensions={0} | all-to-all | bytes 32768 | tf_op jit(solution)/shard_map/all_to_all | solution.py:645
  158.4 1.2 shard_map.97
  (38 shorter events, 0.6 us)
Async XLA Ops:
  3.0 43.0 %copy-start.10 = (f32[24,128]{1,0:T(8,128)S(1)}, f32[24,128]{1,0:T(8,128)}, u32[]{:S(2)}) copy-start(f32[24,128]{1,0:T(8,128)} %get-tuple-element.56) | copy-start | bytes 36868
  14.0 27.6 %copy-start.8 = (f32[6,8,128]{2,1,0:T(8,128)S(1)}, f32[6,8,128]{2,1,0:T(8,128)}, u32[]{:S(2)}) copy-start(f32[6,8,128]{2,1,0:T(8,128)} %get-tuple-element.55) | copy-start | bytes 73732
  14.0 30.7 %copy-start.7 = (f32[6,8,128]{2,1,0:T(8,128)S(1)}, f32[6,8,128]{2,1,0:T(8,128)}, u32[]{:S(2)}) copy-start(f32[6,8,128]{2,1,0:T(8,128)} %get-tuple-element.57) | copy-start | bytes 73732
  14.0 37.9 %copy-start.9 = (f32[24,128]{1,0:T(8,128)S(1)}, f32[24,128]{1,0:T(8,128)}, u32[]{:S(2)}) copy-start(f32[24,128]{1,0:T(8,128)} %get-tuple-element.58) | copy-start | bytes 36868
  14.8 42.2 %copy-start = (f32[3,4,8,128]{3,2,1,0:T(8,128)S(1)}, f32[3,4,8,128]{3,2,1,0:T(8,128)}, u32[]{:S(2)}) copy-start(f32[3,4,8,128]{3,2,1,0:T(8,128)} %param.7) | copy-start | bytes 147460
  14.8 42.2 %copy-start.1 = (f32[3,4,8,128]{3,2,1,0:T(8,128)S(1)}, f32[3,4,8,128]{3,2,1,0:T(8,128)}, u32[]{:S(2)}) copy-start(f32[3,4,8,128]{3,2,1,0:T(8,128)} %param.8) | copy-start | bytes 147460
  14.8 42.2 %copy-start.2 = (f32[3,4,8,128]{3,2,1,0:T(8,128)S(1)}, f32[3,4,8,128]{3,2,1,0:T(8,128)}, u32[]{:S(2)}) copy-start(f32[3,4,8,128]{3,2,1,0:T(8,128)} %param.9) | copy-start | bytes 147460
  14.8 42.2 %copy-start.3 = (f32[3,4,8,128]{3,2,1,0:T(8,128)S(1)}, f32[3,4,8,128]{3,2,1,0:T(8,128)}, u32[]{:S(2)}) copy-start(f32[3,4,8,128]{3,2,1,0:T(8,128)} %param.10) | copy-start | bytes 147460
  14.8 42.3 %all-to-all-start.1 = ((f32[8,24,128]{2,1,0:T(8,128)}), f32[8,24,128]{2,1,0:T(8,128)S(1)}, u32[]{:S(2)}, u32[]{:S(2)}) async-start(f32[8,24,128]{2,1,0:T(8,128)} %get-tuple-element.53), calls=%async_computation.1 | async-start | bytes 196608 | tf_op jit(solution)/shard_map/all_to_all | solution.py:561
  41.5 15.4 %collective-permute-start = (f32[6,8,128]{2,1,0:T(8,128)S(1)}, f32[6,8,128]{2,1,0:T(8,128)S(1)}, u32[]{:S(2)}, u32[]{:S(2)}) collective-permute-start(f32[6,8,128]{2,1,0:T(8,128)S(1)} %copy-done.8), channel_id=1, source_target_pairs={{0,256},{256,512},{512,768},{1,257},{257,513},{513,769},{2,258},{2... | collective-permute-start | bytes 73736 | tf_op jit(solution)/shard_map/ppermute | solution.py:566
  44.7 12.3 %collective-permute-start.2 = (f32[6,8,128]{2,1,0:T(8,128)S(1)}, f32[6,8,128]{2,1,0:T(8,128)S(1)}, u32[]{:S(2)}, u32[]{:S(2)}) collective-permute-start(f32[6,8,128]{2,1,0:T(8,128)S(1)} %copy-done.7), channel_id=1, source_target_pairs={{256,0},{512,256},{768,512},{257,1},{513,257},{769,513},{258,2},{5... | collective-permute-start | bytes 73736 | tf_op jit(solution)/shard_map/ppermute | solution.py:571
  46.0 7.9 %collective-permute-start.1 = (f32[24,128]{1,0:T(8,128)S(1)}, f32[24,128]{1,0:T(8,128)S(1)}, u32[]{:S(2)}, u32[]{:S(2)}) collective-permute-start(f32[24,128]{1,0:T(8,128)S(1)} %copy-done.10), channel_id=1, source_target_pairs={{0,32},{32,64},{64,96},{96,128},{128,160},{160,192},{192,224},{1,3... | collective-permute-start | bytes 36872 | tf_op jit(solution)/shard_map/ppermute | solution.py:566
  51.9 5.0 %collective-permute-start.3 = (f32[24,128]{1,0:T(8,128)S(1)}, f32[24,128]{1,0:T(8,128)S(1)}, u32[]{:S(2)}, u32[]{:S(2)}) collective-permute-start(f32[24,128]{1,0:T(8,128)S(1)} %copy-done.9), channel_id=1, source_target_pairs={{32,0},{64,32},{96,64},{128,96},{160,128},{192,160},{224,192},{33,... | collective-permute-start | bytes 36872 | tf_op jit(solution)/shard_map/ppermute | solution.py:571
  57.0 0.7 copy-start.5
  57.0 0.7 copy-start.6
  57.1 0.7 copy-start.4
  66.6 34.7 %all-to-all-start.3 = ((f32[8,17,1,128]{3,2,1,0:T(1,128)}), f32[8,17,1,128]{3,2,1,0:T(1,128)S(1)}, u32[]{:S(2)}, u32[]{:S(2)}) async-start(f32[8,17,1,128]{3,2,1,0:T(1,128)} %get-tuple-element.66), calls=%async_computation.3 | async-start | bytes 139264 | tf_op jit(solution)/shard_map/all_to_all | solution.py:561
  84.4 16.9 %collective-permute-start.4 = (f32[3,8,128]{2,1,0:T(8,128)S(1)}, f32[3,8,128]{2,1,0:T(8,128)S(1)}, u32[]{:S(2)}, u32[]{:S(2)}) collective-permute-start(f32[3,8,128]{2,1,0:T(8,128)S(1)} %get-tuple-element.70), channel_id=1, source_target_pairs={{0,256},{256,512},{512,768},{1,257},{257,513},{513,769},{2,258},{2... | collective-permute-start | bytes 36872 | tf_op jit(solution)/shard_map/ppermute | solution.py:566
  87.5 13.8 %collective-permute-start.6 = (f32[3,8,128]{2,1,0:T(8,128)S(1)}, f32[3,8,128]{2,1,0:T(8,128)S(1)}, u32[]{:S(2)}, u32[]{:S(2)}) collective-permute-start(f32[3,8,128]{2,1,0:T(8,128)S(1)} %get-tuple-element.72), channel_id=1, source_target_pairs={{256,0},{512,256},{768,512},{257,1},{513,257},{769,513},{258,2},{5... | collective-permute-start | bytes 36872 | tf_op jit(solution)/shard_map/ppermute | solution.py:571
  88.8 9.5 %collective-permute-start.5 = (f32[12,128]{1,0:T(8,128)S(1)}, f32[12,128]{1,0:T(8,128)S(1)}, u32[]{:S(2)}, u32[]{:S(2)}) collective-permute-start(f32[12,128]{1,0:T(8,128)S(1)} %get-tuple-element.71), channel_id=1, source_target_pairs={{0,32},{32,64},{64,96},{96,128},{128,160},{160,192},{192,224},{1,3... | collective-permute-start | bytes 18440 | tf_op jit(solution)/shard_map/ppermute | solution.py:566
  96.3 5.0 %collective-permute-start.7 = (f32[12,128]{1,0:T(8,128)S(1)}, f32[12,128]{1,0:T(8,128)S(1)}, u32[]{:S(2)}, u32[]{:S(2)}) collective-permute-start(f32[12,128]{1,0:T(8,128)S(1)} %get-tuple-element.73), channel_id=1, source_target_pairs={{32,0},{64,32},{96,64},{128,96},{160,128},{192,160},{224,192},{33,... | collective-permute-start | bytes 18440 | tf_op jit(solution)/shard_map/ppermute | solution.py:571
  102.4 7.4 %collective-permute-start.8 = (f32[3,8,128]{2,1,0:T(8,128)S(1)}, f32[3,8,128]{2,1,0:T(8,128)S(1)}, u32[]{:S(2)}, u32[]{:S(2)}) collective-permute-start(f32[3,8,128]{2,1,0:T(8,128)S(1)} %get-tuple-element.79), channel_id=1, source_target_pairs={{0,256},{256,512},{512,768},{1,257},{257,513},{513,769},{2,258},{2... | collective-permute-start | bytes 36872 | tf_op jit(solution)/shard_map/ppermute | solution.py:566
  106.8 3.1 %collective-permute-start.9 = (f32[12,128]{1,0:T(8,128)S(1)}, f32[12,128]{1,0:T(8,128)S(1)}, u32[]{:S(2)}, u32[]{:S(2)}) collective-permute-start(f32[12,128]{1,0:T(8,128)S(1)} %get-tuple-element.80), channel_id=1, source_target_pairs={{0,32},{32,64},{64,96},{96,128},{128,160},{160,192},{192,224},{1,3... | collective-permute-start | bytes 18440 | tf_op jit(solution)/shard_map/ppermute | solution.py:566
  117.7 29.6 %all-to-all-start.5 = ((f32[8,20,1,128]{3,2,1,0:T(1,128)}), f32[8,20,1,128]{3,2,1,0:T(1,128)S(1)}, u32[]{:S(2)}, u32[]{:S(2)}) async-start(f32[8,20,1,128]{3,2,1,0:T(1,128)} %get-tuple-element.84), calls=%async_computation.5 | async-start | bytes 163840 | tf_op jit(solution)/shard_map/all_to_all | solution.py:561
  138.8 8.5 %collective-permute-start.10 = (f32[3,8,128]{2,1,0:T(8,128)S(1)}, f32[3,8,128]{2,1,0:T(8,128)S(1)}, u32[]{:S(2)}, u32[]{:S(2)}) collective-permute-start(f32[3,8,128]{2,1,0:T(8,128)S(1)} %get-tuple-element.85), channel_id=1, source_target_pairs={{256,0},{512,256},{768,512},{257,1},{513,257},{769,513},{258,2},{5... | collective-permute-start | bytes 36872 | tf_op jit(solution)/shard_map/ppermute | solution.py:571
  140.1 7.2 %collective-permute-start.11 = (f32[12,128]{1,0:T(8,128)S(1)}, f32[12,128]{1,0:T(8,128)S(1)}, u32[]{:S(2)}, u32[]{:S(2)}) collective-permute-start(f32[12,128]{1,0:T(8,128)S(1)} %get-tuple-element.86), channel_id=1, source_target_pairs={{32,0},{64,32},{96,64},{128,96},{160,128},{192,160},{224,192},{33,... | collective-permute-start | bytes 18440 | tf_op jit(solution)/shard_map/ppermute | solution.py:571
